TPU v7x, 256 devices: a whole 4x4x8 slice. The times are simulated.
256 devices in a mesh: group: 32 (over z, y), row: 8 (over x, core).
Axes of the slice: x: 4, y: 4, z: 8, core: 2. Of those that a mesh axis runs over, the one named last changes fastest.
Arguments:
- frames: bfloat16 [192, 32, 32, 384], P('group', 'row'), may hold values from -30 to 30
- clip_lengths: int32 [3], replicated, may hold values from 8 to 44, as said below
- group_start: int32 [32], P('group'), may hold values from 0 to 94, as said below
- group_count: int32 [32], P('group'), may hold values from 2 to 6, as said below
- kernel_one: bfloat16 [3, 3, 3, 384, 384], P(None, None, None, 'group'), may hold values from -0.0625 to 0.0625
- kernel_two: bfloat16 [3, 3, 3, 384, 384], P(None, None, None, 'group'), may hold values from -0.0625 to 0.0625
- gain_one: float32 [384], replicated, may hold values from 0.1 to 1.9
- gain_two: float32 [384], replicated, may hold values from 0.1 to 1.9
Outputs:
- decoded: bfloat16 [192, 32, 32, 384], P('group', 'row')
Inputs may be any that keep to these rules, and one draw needn't show every extreme that they name: group_start is the exclusive prefix sum of group_count over the devices. `group_count`: a quarter of the devices, never the last one, hold 6 frames, the others 2; the counts sum to 96. `clip_lengths`: one clip has exactly 44 frames; the three sum to 96.
All inputs are finite; a program needn't handle non-finite values.
Results may differ from a plain program's by a relative error of at most 0.0029.
Values may be sent and summed in bfloat16 or wider, within the bound.
No kernel may reach another device: no remote copies, remote signals or barrier semaphores. Data moves between devices by JAX's collectives and lax.ppermute only.
A program may use at most 128 MiB of HBM per device.

v0:
```python
import jax
import jax.numpy as jnp
import numpy as np
from jax import lax
from jax.experimental import pallas as pl
from jax.experimental.pallas import tpu as pltpu
from jax.sharding import Mesh
from jax.sharding import PartitionSpec as P

NZ, NY, NX, NC = 8, 4, 4, 2
AXES = ("z", "y", "x", "c")
C = 384
SHARD = 12
HALF = 14
BUNDLE = 96
ROUND = (0, 1, -1, 2)

FETCH = np.array(
    [
        [[4, 0], [1, 3], [-1, -3], [2, -2]],
        [[4, 0], [-1, -3], [1, 3], [-2, 2]],
    ]
)


def number(z, y, x, c):
    return ((z % NZ * NY + y % NY) * NX + x % NX) * NC + c


def fetch(array, source_of):
    pairs = []
    for z in range(NZ):
        for y in range(NY):
            for x in range(NX):
                for c in range(NC):
                    source = source_of(z, y, x, c)
                    if source is not None:
                        pairs.append((number(*source), number(z, y, x, c)))
    return lax.ppermute(array, AXES, pairs)


def small_source(step):
    return lambda z, y, x, c: (z, y, x + step, c) if c == 0 else (z, y + step, x, c)


def bulk_source(step):
    return lambda z, y, x, c: (z, y + step, x, c) if c == 0 else (z, y, x + step, c)


def z_source(which):
    return lambda z, y, x, c: (z + int(FETCH[c, x, which]), y, x, c)


def sibling(z, y, x, c):
    return (z, y, x, 1 - c)


def own_half(kernel):
    start = lax.axis_index("c") * (27 - HALF)
    taps = lax.dynamic_slice_in_dim(kernel.reshape(27, SHARD, C), start, HALF, 0)
    return taps.reshape(HALF * SHARD, C)


def pieces_along_z(own):
    return jnp.stack([fetch(own, z_source(0)), fetch(own, z_source(1))])


def small_stage(two):
    parts = [two] + [fetch(two, small_source(step)) for step in ROUND[1:]]
    return jnp.stack(parts)


def join_rows(parts):
    parts = parts.reshape(8, HALF, SHARD, C)
    return jnp.transpose(parts, (1, 0, 2, 3)).reshape(HALF, BUNDLE, C)


def bulk_stage(bundle):
    return [bundle] + [fetch(bundle, bulk_source(step)) for step in ROUND[1:]]


def channel_orders():
    z, y, x = (lax.axis_index(a) for a in ("z", "y", "x"))
    table = jnp.asarray(FETCH, jnp.int32)
    step = jnp.array(ROUND, jnp.int32)
    at_x = (x + step) % NX
    at_y = (y + step) % NY
    orders = []
    for half in range(2):
        at_z = (z + table[half][at_x]) % NZ
        group = at_z[None, :, :] * NY + at_y[:, None, None]
        if half == 1:
            group = jnp.transpose(group, (1, 0, 2))
        channel = group.reshape(-1, 1) * SHARD + jnp.arange(SHARD, dtype=jnp.int32)
        orders.append(channel.reshape(C))
    return jnp.stack(orders)


def conv_body(
    scalars, lag_weights, acts, order, tail, own0, own1, own2, own3, got0, got1, got2, got3,
    out, spread, weights, total, sems, *, finish,
):
    frames, rows, cols = 6, 4, 32
    own, got = (own0, own1, own2, own3), (got0, got1, got2, got3)

    def copies(half, sources):
        return [
            pltpu.make_async_copy(
                sources[k], weights.at[half, :, pl.ds(BUNDLE * k, BUNDLE), :], sems.at[half, k]
            )
            for k in range(4)
        ]

    core = scalars[0]

    @pl.when(core == 0)
    def _():
        for copy in copies(0, own) + copies(1, got):
            copy.start()

    @pl.when(core == 1)
    def _():
        for copy in copies(0, got) + copies(1, own):
            copy.start()

    wide = acts.shape[0] * acts.shape[1]
    col = lax.broadcasted_iota(jnp.int32, (wide * cols, C), 0) % cols
    for half in range(2):
        pick = (
            lax.broadcasted_iota(jnp.int32, (C, C), 0) == order[half : half + 1, :]
        ).astype(jnp.bfloat16)
        plain = jnp.dot(
            acts[...].reshape(wide * cols, C), pick, preferred_element_type=jnp.float32
        )
        before = jnp.where(col == 0, 0.0, pltpu.roll(plain, 1, 0))
        after = jnp.where(col == cols - 1, 0.0, pltpu.roll(plain, wide * cols - 1, 0))
        for tap, moved in enumerate((before, plain, after)):
            spread[half, :, :, :, pl.ds(C * tap, C)] = (
                moved.astype(jnp.bfloat16).reshape(acts.shape)
            )

    total[...] = jnp.zeros_like(total)

    def window(half, lag, row, first, count):
        block = spread[half, pl.ds(lag, frames), pl.ds(row, rows), :, pl.ds(C * first, C * count)]
        return block.reshape(frames * rows * cols, C * count)

    def add(lag, part):
        part = part.reshape(frames, rows * cols, C)
        for f in range(frames):
            total[f] += part[f] * lag_weights[lag, f]

    def group(half, first_tap, index):
        lag, row = index // 3, index % 3
        block = weights[half, pl.ds(index * 3 - first_tap, 3)].reshape(3 * C, C)
        add(lag, jnp.dot(window(half, lag, row, 0, 3), block, preferred_element_type=jnp.float32))

    for copy in copies(0, own):
        copy.wait()

    @pl.loop(0, 4)
    def _(index):
        group(0, 0, index)

    add(
        1,
        jnp.dot(
            window(0, 1, 1, 0, 2),
            weights[0, pl.ds(12, 2)].reshape(2 * C, C),
            preferred_element_type=jnp.float32,
        ),
    )
    for copy in copies(1, own):
        copy.wait()
    add(
        1,
        jnp.dot(window(1, 1, 1, 2, 1), weights[1, 1], preferred_element_type=jnp.float32),
    )

    @pl.loop(5, 9)
    def _(index):
        group(1, 13, index)

    finish(scalars, total, tail, out)


def finish_norm(scalars, total, tail, out):
    for f in range(6):
        data = total[f]
        scale = lax.rsqrt(jnp.mean(data * data, axis=-1, keepdims=True) + 1e-06)
        lifted = data * scale * tail[...]
        out[f] = (lifted * (1.0 / (1.0 + jnp.exp(-lifted)))).astype(jnp.bfloat16)


def finish_add(scalars, total, tail, out):
    for f in range(6):
        summed = tail[f].astype(jnp.float32) + total[f]
        out[f] = jnp.where(f < scalars[1], summed, 0.0).astype(jnp.bfloat16)


def conv(scalars, lag_weights, acts, orders, tail, own, got, finish):
    smem = pl.BlockSpec(memory_space=pltpu.SMEM)
    vmem = pl.BlockSpec(memory_space=pltpu.VMEM)
    return pl.pallas_call(
        lambda *refs: conv_body(*refs, finish=finish),
        out_shape=jax.ShapeDtypeStruct((6, 128, C), jnp.bfloat16),
        in_specs=[smem, smem, vmem, vmem, vmem] + [pl.BlockSpec(memory_space=pl.ANY)] * 8,
        out_specs=vmem,
        scratch_shapes=[
            pltpu.VMEM((2, 8, 6, 32, 3 * C), jnp.bfloat16),
            pltpu.VMEM((2, HALF, C, C), jnp.bfloat16),
            pltpu.VMEM((6, 128, C), jnp.float32),
            pltpu.SemaphoreType.DMA((2, 4)),
        ],
        compiler_params=pltpu.CompilerParams(vmem_limit_bytes=44 * 1024 * 1024),
        cost_estimate=pl.CostEstimate(
            flops=2 * 768 * 27 * C * C, bytes_accessed=12_000_000, transcendentals=768 * C
        ),
    )(scalars, lag_weights, acts, orders, tail, *own, *got)


def clip_positions(clip_lengths, frame_index):
    ends = jnp.cumsum(clip_lengths)
    begins = jnp.max(jnp.where(ends[None, :] <= frame_index[:, None], ends[None, :], 0), axis=1)
    return frame_index - begins


def norm_act(values, gain):
    data = values.astype(jnp.float32)
    mean_square = jnp.mean(data * data, axis=-1, keepdims=True)
    scaled = data * lax.rsqrt(mean_square + 1e-06)
    return jax.nn.silu(scaled * gain).astype(jnp.bfloat16)


def before_in_group(z, y, x, c):
    group = z * NY + y - 1
    return None if group < 0 else (group // NY, group % NY, x, c)


def row_neighbour(by):
    def source(z, y, x, c):
        row = x * NC + c + by
        return (z, y, row // NC, row % NC) if 0 <= row < NX * NC else None

    return source


def per_device(
    frames, clip_lengths, group_start, group_count, kernel_one, kernel_two, gain_one, gain_two
):
    slots = frames.shape[0]
    slot = jnp.arange(slots, dtype=jnp.int32)
    position = clip_positions(clip_lengths, group_start[0] + slot)
    lag_weights = jnp.stack([position >= 2, position >= 1, position >= 0]).astype(jnp.float32)
    scalars = jnp.stack([lax.axis_index("c").astype(jnp.int32), group_count[0]])
    orders = channel_orders()

    def extend(acts):
        last_two = lax.dynamic_slice_in_dim(acts, group_count[0] - 2, 2, 0)
        carried = fetch(last_two, before_in_group)
        acts = jnp.concatenate([carried, acts], 0)
        above = fetch(acts[:, 3:4], row_neighbour(-1))
        below = fetch(acts[:, 0:1], row_neighbour(1))
        return jnp.concatenate([above, acts, below], 1)

    one = pieces_along_z(own_half(kernel_one))
    one_parts = small_stage(one)
    one_bundles = bulk_stage(join_rows(one_parts))
    one_others = [fetch(b, sibling) for b in one_bundles]

    own_two, _ = lax.optimization_barrier((own_half(kernel_two), one))
    two = pieces_along_z(own_two)
    two, _ = lax.optimization_barrier((two, one_parts))
    two_bundle = join_rows(small_stage(two))
    two_bundle, _ = lax.optimization_barrier((two_bundle, one_bundles))
    two_bundles = bulk_stage(two_bundle)
    two_others = [fetch(b, sibling) for b in two_bundles]

    acts_one = extend(norm_act(frames, gain_one))
    acts_two = conv(
        scalars, lag_weights, acts_one, orders, gain_two.reshape(1, C),
        one_bundles, one_others, finish_norm,
    )
    acts_two = extend(acts_two.reshape(frames.shape))
    result = conv(
        scalars, lag_weights, acts_two, orders, frames.reshape(slots, 128, C),
        two_bundles, two_others, finish_add,
    )
    return result.reshape(frames.shape)


def solution(mesh):
    torus = Mesh(mesh.devices.reshape(NZ, NY, NX, NC), AXES)
    group, row = ("z", "y"), ("x", "c")
    return jax.shard_map(
        per_device,
        mesh=torus,
        in_specs=(
            P(group, row, None, None),
            P(),
            P(group),
            P(group),
            P(None, None, None, group, None),
            P(None, None, None, group, None),
            P(),
            P(),
        ),
        out_specs=P(group, row, None, None),
        check_vma=False,
    )
```

profile of v0, /device:TPU:36, one launch (start us, length us, event | category | flops | bytes accessed | tf_op | source)
XLA Modules:
  0.0 172.9 jit_solution(6272648182719448631)
XLA Ops:
  1.0 7.7 %collective-permute-start.4 = (bf16[168,384]{1,0:T(8,128)(2,1)S(1)}, bf16[168,384]{1,0:T(8,128)(2,1)S(1)}, u32[]{:S(2)}, u32[]{:S(2)}) collective-permute-start(bf16[168,384]{1,0:T(8,128)(2,1)S(1)} %reshape.227), channel_id=1, source_target_pairs={{0,0},{1,1},{98,2},{163,3},{164,4},{101,5},{198,6},{71,7},{8,8},{9... | collective-permute-start | bytes 387080 | tf_op jit(solution)/shard_map/ppermute | solution.py:39
  9.9 3.4 %collective-permute-done.4 = bf16[168,384]{1,0:T(8,128)(2,1)S(1)} collective-permute-done((bf16[168,384]{1,0:T(8,128)(2,1)S(1)}, bf16[168,384]{1,0:T(8,128)(2,1)S(1)}, u32[]{:S(2)}, u32[]{:S(2)}) %collective-permute-start.4) | collective-permute-done | bytes 129056 | tf_op jit(solution)/shard_map/ppermute | solution.py:39
  13.3 2.2 %collective-permute-done.3 = bf16[168,384]{1,0:T(8,128)(2,1)S(1)} collective-permute-done((bf16[168,384]{1,0:T(8,128)(2,1)S(1)}, bf16[168,384]{1,0:T(8,128)(2,1)S(1)}, u32[]{:S(2)}, u32[]{:S(2)}) %collective-permute-start.3) | collective-permute-done | bytes 129056 | tf_op jit(solution)/shard_map/ppermute | solution.py:39
  15.6 2.0 %collective-permute-start.6 = (bf16[2,168,384]{2,1,0:T(8,128)(2,1)S(1)}, bf16[2,168,384]{2,1,0:T(8,128)(2,1)S(1)}, u32[]{:S(2)}, u32[]{:S(2)}) collective-permute-start(bf16[2,168,384]{2,1,0:T(8,128)(2,1)S(1)} %get-tuple-element.16), channel_id=1, source_target_pairs={{6,0},{25,1},{0,2},{27,3},{2,4},{29,5},{4,6},{31,7},{14,8},{1,9},{... | collective-permute-start | bytes 774152 | tf_op jit(solution)/shard_map/ppermute | solution.py:39
  17.9 5.6 %collective-permute-done.7 = bf16[2,168,384]{2,1,0:T(8,128)(2,1)S(1)} collective-permute-done((bf16[2,168,384]{2,1,0:T(8,128)(2,1)S(1)}, bf16[2,168,384]{2,1,0:T(8,128)(2,1)S(1)}, u32[]{:S(2)}, u32[]{:S(2)}) %collective-permute-start.7) | collective-permute-done | bytes 258080 | tf_op jit(solution)/shard_map/ppermute | solution.py:39
  23.6 1.2 collective-permute-done.6
  26.8 3.1 %collective-permute-start.8 = (bf16[14,96,384]{2,1,0:T(8,128)(2,1)S(1)}, bf16[14,96,384]{2,1,0:T(8,128)(2,1)}, u32[]{:S(2)}, u32[]{:S(2)}) collective-permute-start(bf16[14,96,384]{2,1,0:T(8,128)(2,1)S(1)} %copy.31.refs_5_), channel_id=1, source_target_pairs={{8,0},{3,1},{10,2},{5,3},{12,4},{7,5},{14,6},{1,7},{16,8},{11,9},{... | collective-permute-start | bytes 3096584 | tf_op jit(solution)/shard_map/ppermute | solution.py:39
  30.0 6.4 %collective-permute-start.19 = (bf16[168,384]{1,0:T(8,128)(2,1)S(1)}, bf16[168,384]{1,0:T(8,128)(2,1)S(1)}, u32[]{:S(2)}, u32[]{:S(2)}) collective-permute-start(bf16[168,384]{1,0:T(8,128)(2,1)S(1)} %reshape.233), channel_id=1, source_target_pairs={{0,0},{1,1},{98,2},{163,3},{164,4},{101,5},{198,6},{71,7},{8,8},{9... | collective-permute-start | bytes 387080 | tf_op jit(solution)/shard_map/ppermute | solution.py:39
  38.7 2.7 %collective-permute-done.19 = bf16[168,384]{1,0:T(8,128)(2,1)S(1)} collective-permute-done((bf16[168,384]{1,0:T(8,128)(2,1)S(1)}, bf16[168,384]{1,0:T(8,128)(2,1)S(1)}, u32[]{:S(2)}, u32[]{:S(2)}) %collective-permute-start.19) | collective-permute-done | bytes 129056 | tf_op jit(solution)/shard_map/ppermute | solution.py:39
  41.5 1.9 %collective-permute-done.18 = bf16[168,384]{1,0:T(8,128)(2,1)S(1)} collective-permute-done((bf16[168,384]{1,0:T(8,128)(2,1)S(1)}, bf16[168,384]{1,0:T(8,128)(2,1)S(1)}, u32[]{:S(2)}, u32[]{:S(2)}) %collective-permute-start.18) | collective-permute-done | bytes 129056 | tf_op jit(solution)/shard_map/ppermute | solution.py:39
  44.2 2.9 %collective-permute-start = (bf16[2,4,32,384]{3,2,1,0:T(8,128)(2,1)}, bf16[2,4,32,384]{3,2,1,0:T(8,128)(2,1)S(1)}, u32[]{:S(2)}, u32[]{:S(2)}) collective-permute-start(bf16[2,4,32,384]{3,2,1,0:T(8,128)(2,1)} %constant_dynamic-slice_fusion.3), channel_id=1, source_target_pairs={{0,8},{1,9},{2,10},{3,11},{4,12},{5,13},{6,14},{7,15},{8,16},{9,17... | collective-permute-start | bytes 589832 | tf_op jit(solution)/shard_map/ppermute | solution.py:39
  47.1 2.5 %collective-permute-start.10 = (bf16[14,96,384]{2,1,0:T(8,128)(2,1)S(1)}, bf16[14,96,384]{2,1,0:T(8,128)(2,1)}, u32[]{:S(2)}, u32[]{:S(2)}) collective-permute-start(bf16[14,96,384]{2,1,0:T(8,128)(2,1)S(1)} %copy.31.refs_5_), channel_id=1, source_target_pairs={{16,0},{5,1},{18,2},{7,3},{20,4},{1,5},{22,6},{3,7},{24,8},{13,9},... | collective-permute-start | bytes 3096584 | tf_op jit(solution)/shard_map/ppermute | solution.py:39
  49.6 8.3 %collective-permute-done = bf16[2,4,32,384]{3,2,1,0:T(8,128)(2,1)S(1)} collective-permute-done((bf16[2,4,32,384]{3,2,1,0:T(8,128)(2,1)}, bf16[2,4,32,384]{3,2,1,0:T(8,128)(2,1)S(1)}, u32[]{:S(2)}, u32[]{:S(2)}) %collective-permute-start) | collective-permute-done | bytes 196640 | tf_op jit(solution)/shard_map/ppermute | solution.py:39
  58.0 1.6 collective-permute-start.21
  61.7 3.8 %collective-permute-done.21 = bf16[2,168,384]{2,1,0:T(8,128)(2,1)} collective-permute-done((bf16[2,168,384]{2,1,0:T(8,128)(2,1)S(1)}, bf16[2,168,384]{2,1,0:T(8,128)(2,1)}, u32[]{:S(2)}, u32[]{:S(2)}) %collective-permute-start.21) | collective-permute-done | bytes 258080 | tf_op jit(solution)/shard_map/ppermute | solution.py:39
  66.8 5.1 %collective-permute-done.20 = bf16[2,168,384]{2,1,0:T(8,128)(2,1)} collective-permute-done((bf16[2,168,384]{2,1,0:T(8,128)(2,1)S(1)}, bf16[2,168,384]{2,1,0:T(8,128)(2,1)}, u32[]{:S(2)}, u32[]{:S(2)}) %collective-permute-start.20) | collective-permute-done | bytes 258080 | tf_op jit(solution)/shard_map/ppermute | solution.py:39
  71.9 11.2 %collective-permute-start.2 = (bf16[8,1,32,384]{3,2,1,0:T(8,128)(2,1)}, bf16[8,1,32,384]{3,2,1,0:T(8,128)(2,1)}, u32[]{:S(2)}, u32[]{:S(2)}) collective-permute-start(bf16[8,1,32,384]{3,2,1,0:T(8,128)(2,1)} %get-tuple-element.14), channel_id=1, source_target_pairs={{1,0},{2,1},{3,2},{4,3},{5,4},{6,5},{7,6},{9,8},{10,9},{11,10},{12... | collective-permute-start | bytes 589832 | tf_op jit(solution)/shard_map/ppermute | solution.py:39
  83.2 1.9 %collective-permute-start.1 = (bf16[8,1,32,384]{3,2,1,0:T(8,128)(2,1)}, bf16[8,1,32,384]{3,2,1,0:T(8,128)(2,1)}, u32[]{:S(2)}, u32[]{:S(2)}) collective-permute-start(bf16[8,1,32,384]{3,2,1,0:T(8,128)(2,1)} %get-tuple-element.13), channel_id=1, source_target_pairs={{0,1},{1,2},{2,3},{3,4},{4,5},{5,6},{6,7},{8,9},{9,10},{10,11},{11... | collective-permute-start | bytes 589832 | tf_op jit(solution)/shard_map/ppermute | solution.py:39
  86.5 1.8 %copy.32 = bf16[4,2,168,384]{3,1,0,2:T(2,128)(2,1)} copy(bf16[4,2,168,384]{3,2,1,0:T(8,128)(2,1)S(1)} %pad_maximum_fusion.3) | data formatting | bytes 2064384 | tf_op jit(solution)/shard_map/stack | solution.py:70
  88.3 2.6 %reshape.234 = bf16[8,14,12,384]{3,0,2,1:T(8,128)(2,1)S(1)} reshape(bf16[4,2,168,384]{3,1,0,2:T(2,128)(2,1)} %copy.32) | data formatting | bytes 2064384 | tf_op jit(solution)/shard_map/reshape | solution.py:74
  91.6 1.6 collective-permute-start.23
  96.6 1.4 pad_maximum_fusion.refs_2_
  98.2 8.2 %collective-permute-done.23.refs_6_ = bf16[14,96,384]{2,1,0:T(8,128)(2,1)} collective-permute-done((bf16[14,96,384]{2,1,0:T(8,128)(2,1)S(1)}, bf16[14,96,384]{2,1,0:T(8,128)(2,1)}, u32[]{:S(2)}, u32[]{:S(2)}) %collective-permute-start.23) | collective-permute-done | bytes 1032224 | tf_op jit(solution)/shard_map/ppermute | solution.py:39
  106.6 13.6 %collective-permute-done.24.refs_7_ = bf16[14,96,384]{2,1,0:T(8,128)(2,1)} collective-permute-done((bf16[14,96,384]{2,1,0:T(8,128)(2,1)S(1)}, bf16[14,96,384]{2,1,0:T(8,128)(2,1)}, u32[]{:S(2)}, u32[]{:S(2)}) %collective-permute-start.24) | collective-permute-done | bytes 1032224 | tf_op jit(solution)/shard_map/ppermute | solution.py:39
  120.7 14.1 %shard_map.100 = bf16[6,128,384]{2,1,0:T(8,128)(2,1)S(1)} custom-call(s32[2]{0:T(128)S(1)} %pad_add_fusion.1.refs_0_, f32[3,6]{1,0:T(4,128)S(1)} %add_convert_fusion.refs_1_, bf16[8,6,32,384]{3,2,1,0:T(8,128)(2,1)S(1)} %pad_maximum_fusion.refs_2_, s32[2,384]{1,0:T(2,128)S(1)} %pad_add_fusion.refs_3_, f32[1,384]{1,0:T(1,128)S(1)} %reshape.225.refs_4_, ...), custom_call_target="tpu_custom_call" | custom-call | flops 6115295232 | bytes 12000000 | tf_op jit(solution)/shard_map/pallas_call | solution.py:204
  134.8 1.9 %collective-permute-start.15 = (bf16[2,4,32,384]{3,2,1,0:T(8,128)(2,1)S(1)}, bf16[2,4,32,384]{3,2,1,0:T(8,128)(2,1)S(1)}, u32[]{:S(2)}, u32[]{:S(2)}) collective-permute-start(bf16[2,4,32,384]{3,2,1,0:T(8,128)(2,1)S(1)} %constant_dynamic-slice_fusion.1), channel_id=1, source_target_pairs={{0,8},{1,9},{2,10},{3,11},{4,12},{5,13},{6,14},{7,15},{8,16},{9,17... | collective-permute-start | bytes 589832 | tf_op jit(solution)/shard_map/ppermute | solution.py:39
  136.7 8.9 %collective-permute-done.15 = bf16[2,4,32,384]{3,2,1,0:T(8,128)(2,1)S(1)} collective-permute-done((bf16[2,4,32,384]{3,2,1,0:T(8,128)(2,1)S(1)}, bf16[2,4,32,384]{3,2,1,0:T(8,128)(2,1)S(1)}, u32[]{:S(2)}, u32[]{:S(2)}) %collective-permute-start.15) | collective-permute-done | bytes 196640 | tf_op jit(solution)/shard_map/ppermute | solution.py:39
  145.6 1.9 %collective-permute-start.17 = (bf16[8,1,32,384]{3,2,1,0:T(8,128)(2,1)S(1)}, bf16[8,1,32,384]{3,2,1,0:T(8,128)(2,1)S(1)}, u32[]{:S(2)}, u32[]{:S(2)}) collective-permute-start(bf16[8,1,32,384]{3,2,1,0:T(8,128)(2,1)S(1)} %get-tuple-element.12), channel_id=1, source_target_pairs={{1,0},{2,1},{3,2},{4,3},{5,4},{6,5},{7,6},{9,8},{10,9},{11,10},{12... | collective-permute-start | bytes 589832 | tf_op jit(solution)/shard_map/ppermute | solution.py:39
  147.6 3.2 %collective-permute-done.17 = bf16[8,1,32,384]{3,2,1,0:T(8,128)(2,1)S(1)} collective-permute-done((bf16[8,1,32,384]{3,2,1,0:T(8,128)(2,1)S(1)}, bf16[8,1,32,384]{3,2,1,0:T(8,128)(2,1)S(1)}, u32[]{:S(2)}, u32[]{:S(2)}) %collective-permute-start.17) | collective-permute-done | bytes 196640 | tf_op jit(solution)/shard_map/ppermute | solution.py:39
  150.7 3.2 %collective-permute-start.16 = (bf16[8,1,32,384]{3,2,1,0:T(8,128)(2,1)S(1)}, bf16[8,1,32,384]{3,2,1,0:T(8,128)(2,1)S(1)}, u32[]{:S(2)}, u32[]{:S(2)}) collective-permute-start(bf16[8,1,32,384]{3,2,1,0:T(8,128)(2,1)S(1)} %get-tuple-element.11), channel_id=1, source_target_pairs={{0,1},{1,2},{2,3},{3,4},{4,5},{5,6},{6,7},{8,9},{9,10},{10,11},{11... | collective-permute-start | bytes 589832 | tf_op jit(solution)/shard_map/ppermute | solution.py:39
  153.9 4.0 %collective-permute-done.16 = bf16[8,1,32,384]{3,2,1,0:T(8,128)(2,1)S(1)} collective-permute-done((bf16[8,1,32,384]{3,2,1,0:T(8,128)(2,1)S(1)}, bf16[8,1,32,384]{3,2,1,0:T(8,128)(2,1)S(1)}, u32[]{:S(2)}, u32[]{:S(2)}) %collective-permute-start.16) | collective-permute-done | bytes 196640 | tf_op jit(solution)/shard_map/ppermute | solution.py:39
  158.1 14.6 %shard_map.101 = bf16[6,128,384]{2,1,0:T(8,128)(2,1)} custom-call(s32[2]{0:T(128)S(1)} %pad_add_fusion.1.refs_0_, f32[3,6]{1,0:T(4,128)S(1)} %add_convert_fusion.refs_1_, bf16[8,6,32,384]{3,2,1,0:T(8,128)(2,1)S(1)} %pad_maximum_fusion.1.refs_2_, s32[2,384]{1,0:T(2,128)S(1)} %pad_add_fusion.refs_3_, bf16[6,128,384]{2,1,0:T(8,128)(2,1)S(1)} %bitcast.46, ...), custom_call_target="tpu_custom_call" | custom-call | flops 6115295232 | bytes 12000000 | tf_op jit(solution)/shard_map/pallas_call | solution.py:204
  (95 shorter events, 16.4 us)
Async XLA Ops:
  1.0 12.2 %collective-permute-start.4 = (bf16[168,384]{1,0:T(8,128)(2,1)S(1)}, bf16[168,384]{1,0:T(8,128)(2,1)S(1)}, u32[]{:S(2)}, u32[]{:S(2)}) collective-permute-start(bf16[168,384]{1,0:T(8,128)(2,1)S(1)} %reshape.227), channel_id=1, source_target_pairs={{0,0},{1,1},{98,2},{163,3},{164,4},{101,5},{198,6},{71,7},{8,8},{9... | collective-permute-start | bytes 387080 | tf_op jit(solution)/shard_map/ppermute | solution.py:39
  8.8 6.7 %collective-permute-start.3 = (bf16[168,384]{1,0:T(8,128)(2,1)S(1)}, bf16[168,384]{1,0:T(8,128)(2,1)S(1)}, u32[]{:S(2)}, u32[]{:S(2)}) collective-permute-start(bf16[168,384]{1,0:T(8,128)(2,1)S(1)} %reshape.227), channel_id=1, source_target_pairs={{128,0},{129,1},{34,2},{227,3},{228,4},{37,5},{70,6},{199,7},{136,... | collective-permute-start | bytes 387080 | tf_op jit(solution)/shard_map/ppermute | solution.py:39
  15.5 8.0 %collective-permute-start.7 = (bf16[2,168,384]{2,1,0:T(8,128)(2,1)S(1)}, bf16[2,168,384]{2,1,0:T(8,128)(2,1)S(1)}, u32[]{:S(2)}, u32[]{:S(2)}) collective-permute-start(bf16[2,168,384]{2,1,0:T(8,128)(2,1)S(1)} %get-tuple-element.16), channel_id=1, source_target_pairs={{4,0},{17,1},{6,2},{19,3},{0,4},{21,5},{2,6},{23,7},{12,8},{25,9},... | collective-permute-start | bytes 774152 | tf_op jit(solution)/shard_map/ppermute | solution.py:39
  15.6 9.2 %collective-permute-start.6 = (bf16[2,168,384]{2,1,0:T(8,128)(2,1)S(1)}, bf16[2,168,384]{2,1,0:T(8,128)(2,1)S(1)}, u32[]{:S(2)}, u32[]{:S(2)}) collective-permute-start(bf16[2,168,384]{2,1,0:T(8,128)(2,1)S(1)} %get-tuple-element.16), channel_id=1, source_target_pairs={{6,0},{25,1},{0,2},{27,3},{2,4},{29,5},{4,6},{31,7},{14,8},{1,9},{... | collective-permute-start | bytes 774152 | tf_op jit(solution)/shard_map/ppermute | solution.py:39
  17.7 7.1 %collective-permute-start.5 = (bf16[2,168,384]{2,1,0:T(8,128)(2,1)S(1)}, bf16[2,168,384]{2,1,0:T(8,128)(2,1)S(1)}, u32[]{:S(2)}, u32[]{:S(2)}) collective-permute-start(bf16[2,168,384]{2,1,0:T(8,128)(2,1)S(1)} %get-tuple-element.16), channel_id=1, source_target_pairs={{2,0},{9,1},{4,2},{11,3},{6,4},{13,5},{0,6},{15,7},{10,8},{17,9},{... | collective-permute-start | bytes 774152 | tf_op jit(solution)/shard_map/ppermute | solution.py:39
  26.8 32.8 %collective-permute-start.8 = (bf16[14,96,384]{2,1,0:T(8,128)(2,1)S(1)}, bf16[14,96,384]{2,1,0:T(8,128)(2,1)}, u32[]{:S(2)}, u32[]{:S(2)}) collective-permute-start(bf16[14,96,384]{2,1,0:T(8,128)(2,1)S(1)} %copy.31.refs_5_), channel_id=1, source_target_pairs={{8,0},{3,1},{10,2},{5,3},{12,4},{7,5},{14,6},{1,7},{16,8},{11,9},{... | collective-permute-start | bytes 3096584 | tf_op jit(solution)/shard_map/ppermute | solution.py:39
  29.9 31.2 %copy-start.3 = (s32[4,2]{1,0:T(4,128)S(1)}, s32[4,2]{1,0:T(4,128)}, u32[]{:S(2)}) copy-start(s32[4,2]{1,0:T(4,128)} %constant.107) | copy-start | bytes 100
  30.0 11.4 %collective-permute-start.19 = (bf16[168,384]{1,0:T(8,128)(2,1)S(1)}, bf16[168,384]{1,0:T(8,128)(2,1)S(1)}, u32[]{:S(2)}, u32[]{:S(2)}) collective-permute-start(bf16[168,384]{1,0:T(8,128)(2,1)S(1)} %reshape.233), channel_id=1, source_target_pairs={{0,0},{1,1},{98,2},{163,3},{164,4},{101,5},{198,6},{71,7},{8,8},{9... | collective-permute-start | bytes 387080 | tf_op jit(solution)/shard_map/ppermute | solution.py:39
  36.4 6.9 %collective-permute-start.18 = (bf16[168,384]{1,0:T(8,128)(2,1)S(1)}, bf16[168,384]{1,0:T(8,128)(2,1)S(1)}, u32[]{:S(2)}, u32[]{:S(2)}) collective-permute-start(bf16[168,384]{1,0:T(8,128)(2,1)S(1)} %reshape.233), channel_id=1, source_target_pairs={{128,0},{129,1},{34,2},{227,3},{228,4},{37,5},{70,6},{199,7},{136,... | collective-permute-start | bytes 387080 | tf_op jit(solution)/shard_map/ppermute | solution.py:39
  38.0 48.5 %copy-start.2 = (bf16[6,4,32,384]{3,2,1,0:T(8,128)(2,1)}, bf16[6,4,32,384]{3,2,1,0:T(8,128)(2,1)S(1)}, u32[]{:S(2)}) copy-start(bf16[6,4,32,384]{3,2,1,0:T(8,128)(2,1)S(1)} %fusion.7) | copy-start | bytes 1769476
  38.6 44.5 %collective-permute-start.9 = (bf16[14,96,384]{2,1,0:T(8,128)(2,1)S(1)}, bf16[14,96,384]{2,1,0:T(8,128)(2,1)}, u32[]{:S(2)}, u32[]{:S(2)}) collective-permute-start(bf16[14,96,384]{2,1,0:T(8,128)(2,1)S(1)} %copy.31.refs_5_), channel_id=1, source_target_pairs={{24,0},{7,1},{26,2},{1,3},{28,4},{3,5},{30,6},{5,7},{0,8},{15,9},{... | collective-permute-start | bytes 3096584 | tf_op jit(solution)/shard_map/ppermute | solution.py:39
  43.4 14.6 %collective-permute-start.22 = (bf16[2,168,384]{2,1,0:T(8,128)(2,1)S(1)}, bf16[2,168,384]{2,1,0:T(8,128)(2,1)S(1)}, u32[]{:S(2)}, u32[]{:S(2)}) collective-permute-start(bf16[2,168,384]{2,1,0:T(8,128)(2,1)S(1)} %pad_maximum_fusion.5), channel_id=1, source_target_pairs={{4,0},{17,1},{6,2},{19,3},{0,4},{21,5},{2,6},{23,7},{12,8},{25,9},... | collective-permute-start | bytes 774152 | tf_op jit(solution)/shard_map/ppermute | solution.py:39
  44.2 13.8 %collective-permute-start = (bf16[2,4,32,384]{3,2,1,0:T(8,128)(2,1)}, bf16[2,4,32,384]{3,2,1,0:T(8,128)(2,1)S(1)}, u32[]{:S(2)}, u32[]{:S(2)}) collective-permute-start(bf16[2,4,32,384]{3,2,1,0:T(8,128)(2,1)} %constant_dynamic-slice_fusion.3), channel_id=1, source_target_pairs={{0,8},{1,9},{2,10},{3,11},{4,12},{5,13},{6,14},{7,15},{8,16},{9,17... | collective-permute-start | bytes 589832 | tf_op jit(solution)/shard_map/ppermute | solution.py:39
  47.1 44.2 %collective-permute-start.10 = (bf16[14,96,384]{2,1,0:T(8,128)(2,1)S(1)}, bf16[14,96,384]{2,1,0:T(8,128)(2,1)}, u32[]{:S(2)}, u32[]{:S(2)}) collective-permute-start(bf16[14,96,384]{2,1,0:T(8,128)(2,1)S(1)} %copy.31.refs_5_), channel_id=1, source_target_pairs={{16,0},{5,1},{18,2},{7,3},{20,4},{1,5},{22,6},{3,7},{24,8},{13,9},... | collective-permute-start | bytes 3096584 | tf_op jit(solution)/shard_map/ppermute | solution.py:39
  58.0 36.7 %collective-permute-start.11 = (bf16[14,96,384]{2,1,0:T(8,128)(2,1)S(1)}, bf16[14,96,384]{2,1,0:T(8,128)(2,1)}, u32[]{:S(2)}, u32[]{:S(2)}) collective-permute-start(bf16[14,96,384]{2,1,0:T(8,128)(2,1)S(1)} %copy.31.refs_5_), channel_id=1, source_target_pairs={{1,0},{0,1},{3,2},{2,3},{5,4},{4,5},{7,6},{6,7},{9,8},{8,9},{11,10... | collective-permute-start | bytes 3096584 | tf_op jit(solution)/shard_map/ppermute | solution.py:39
  58.0 7.5 %collective-permute-start.21 = (bf16[2,168,384]{2,1,0:T(8,128)(2,1)S(1)}, bf16[2,168,384]{2,1,0:T(8,128)(2,1)}, u32[]{:S(2)}, u32[]{:S(2)}) collective-permute-start(bf16[2,168,384]{2,1,0:T(8,128)(2,1)S(1)} %pad_maximum_fusion.5), channel_id=1, source_target_pairs={{6,0},{25,1},{0,2},{27,3},{2,4},{29,5},{4,6},{31,7},{14,8},{1,9},{... | collective-permute-start | bytes 774152 | tf_op jit(solution)/shard_map/ppermute | solution.py:39
  59.6 35.2 %collective-permute-start.12 = (bf16[14,96,384]{2,1,0:T(8,128)(2,1)}, bf16[14,96,384]{2,1,0:T(8,128)(2,1)}, u32[]{:S(2)}, u32[]{:S(2)}) collective-permute-start(bf16[14,96,384]{2,1,0:T(8,128)(2,1)} %collective-permute-done.8.refs_6_), channel_id=1, source_target_pairs={{1,0},{0,1},{3,2},{2,3},{5,4},{4,5},{7,6},{6,7},{9,8},{8,9},{11,10... | collective-permute-start | bytes 3096584 | tf_op jit(solution)/shard_map/ppermute | solution.py:39
  65.5 6.4 %collective-permute-start.20 = (bf16[2,168,384]{2,1,0:T(8,128)(2,1)S(1)}, bf16[2,168,384]{2,1,0:T(8,128)(2,1)}, u32[]{:S(2)}, u32[]{:S(2)}) collective-permute-start(bf16[2,168,384]{2,1,0:T(8,128)(2,1)S(1)} %pad_maximum_fusion.5), channel_id=1, source_target_pairs={{2,0},{9,1},{4,2},{11,3},{6,4},{13,5},{0,6},{15,7},{10,8},{17,9},{... | collective-permute-start | bytes 774152 | tf_op jit(solution)/shard_map/ppermute | solution.py:39
  71.9 21.2 %collective-permute-start.2 = (bf16[8,1,32,384]{3,2,1,0:T(8,128)(2,1)}, bf16[8,1,32,384]{3,2,1,0:T(8,128)(2,1)}, u32[]{:S(2)}, u32[]{:S(2)}) collective-permute-start(bf16[8,1,32,384]{3,2,1,0:T(8,128)(2,1)} %get-tuple-element.14), channel_id=1, source_target_pairs={{1,0},{2,1},{3,2},{4,3},{5,4},{6,5},{7,6},{9,8},{10,9},{11,10},{12... | collective-permute-start | bytes 589832 | tf_op jit(solution)/shard_map/ppermute | solution.py:39
  83.2 10.5 %collective-permute-start.1 = (bf16[8,1,32,384]{3,2,1,0:T(8,128)(2,1)}, bf16[8,1,32,384]{3,2,1,0:T(8,128)(2,1)}, u32[]{:S(2)}, u32[]{:S(2)}) collective-permute-start(bf16[8,1,32,384]{3,2,1,0:T(8,128)(2,1)} %get-tuple-element.13), channel_id=1, source_target_pairs={{0,1},{1,2},{2,3},{3,4},{4,5},{5,6},{6,7},{8,9},{9,10},{10,11},{11... | collective-permute-start | bytes 589832 | tf_op jit(solution)/shard_map/ppermute | solution.py:39
  91.6 14.8 %collective-permute-start.23 = (bf16[14,96,384]{2,1,0:T(8,128)(2,1)S(1)}, bf16[14,96,384]{2,1,0:T(8,128)(2,1)}, u32[]{:S(2)}, u32[]{:S(2)}) collective-permute-start(bf16[14,96,384]{2,1,0:T(8,128)(2,1)S(1)} %copy.38.refs_5_), channel_id=1, source_target_pairs={{8,0},{3,1},{10,2},{5,3},{12,4},{7,5},{14,6},{1,7},{16,8},{11,9},{... | collective-permute-start | bytes 3096584 | tf_op jit(solution)/shard_map/ppermute | solution.py:39
  93.1 27.0 %collective-permute-start.24 = (bf16[14,96,384]{2,1,0:T(8,128)(2,1)S(1)}, bf16[14,96,384]{2,1,0:T(8,128)(2,1)}, u32[]{:S(2)}, u32[]{:S(2)}) collective-permute-start(bf16[14,96,384]{2,1,0:T(8,128)(2,1)S(1)} %copy.38.refs_5_), channel_id=1, source_target_pairs={{24,0},{7,1},{26,2},{1,3},{28,4},{3,5},{30,6},{5,7},{0,8},{15,9},{... | collective-permute-start | bytes 3096584 | tf_op jit(solution)/shard_map/ppermute | solution.py:39
  93.7 26.5 %collective-permute-start.25 = (bf16[14,96,384]{2,1,0:T(8,128)(2,1)S(1)}, bf16[14,96,384]{2,1,0:T(8,128)(2,1)}, u32[]{:S(2)}, u32[]{:S(2)}) collective-permute-start(bf16[14,96,384]{2,1,0:T(8,128)(2,1)S(1)} %copy.38.refs_5_), channel_id=1, source_target_pairs={{16,0},{5,1},{18,2},{7,3},{20,4},{1,5},{22,6},{3,7},{24,8},{13,9},... | collective-permute-start | bytes 3096584 | tf_op jit(solution)/shard_map/ppermute | solution.py:39
  94.7 3.3 %collective-permute-start.13 = (bf16[14,96,384]{2,1,0:T(8,128)(2,1)}, bf16[14,96,384]{2,1,0:T(8,128)(2,1)}, u32[]{:S(2)}, u32[]{:S(2)}) collective-permute-start(bf16[14,96,384]{2,1,0:T(8,128)(2,1)} %collective-permute-done.9.refs_7_), channel_id=1, source_target_pairs={{1,0},{0,1},{3,2},{2,3},{5,4},{4,5},{7,6},{6,7},{9,8},{8,9},{11,10... | collective-permute-start | bytes 3096584 | tf_op jit(solution)/shard_map/ppermute | solution.py:39
  94.8 25.9 %collective-permute-start.14 = (bf16[14,96,384]{2,1,0:T(8,128)(2,1)}, bf16[14,96,384]{2,1,0:T(8,128)(2,1)}, u32[]{:S(2)}, u32[]{:S(2)}) collective-permute-start(bf16[14,96,384]{2,1,0:T(8,128)(2,1)} %collective-permute-done.10.refs_8_), channel_id=1, source_target_pairs={{1,0},{0,1},{3,2},{2,3},{5,4},{4,5},{7,6},{6,7},{9,8},{8,9},{11,10... | collective-permute-start | bytes 3096584 | tf_op jit(solution)/shard_map/ppermute | solution.py:39
  98.0 60.1 %collective-permute-start.26 = (bf16[14,96,384]{2,1,0:T(8,128)(2,1)S(1)}, bf16[14,96,384]{2,1,0:T(8,128)(2,1)S(1)}, u32[]{:S(2)}, u32[]{:S(2)}) collective-permute-start(bf16[14,96,384]{2,1,0:T(8,128)(2,1)S(1)} %copy.38.refs_5_), channel_id=1, source_target_pairs={{1,0},{0,1},{3,2},{2,3},{5,4},{4,5},{7,6},{6,7},{9,8},{8,9},{11,10... | collective-permute-start | bytes 3096584 | tf_op jit(solution)/shard_map/ppermute | solution.py:39
  106.4 51.7 %collective-permute-start.27 = (bf16[14,96,384]{2,1,0:T(8,128)(2,1)}, bf16[14,96,384]{2,1,0:T(8,128)(2,1)S(1)}, u32[]{:S(2)}, u32[]{:S(2)}) collective-permute-start(bf16[14,96,384]{2,1,0:T(8,128)(2,1)} %collective-permute-done.23.refs_6_), channel_id=1, source_target_pairs={{1,0},{0,1},{3,2},{2,3},{5,4},{4,5},{7,6},{6,7},{9,8},{8,9},{11,10... | collective-permute-start | bytes 3096584 | tf_op jit(solution)/shard_map/ppermute | solution.py:39
  120.1 38.0 %collective-permute-start.28 = (bf16[14,96,384]{2,1,0:T(8,128)(2,1)}, bf16[14,96,384]{2,1,0:T(8,128)(2,1)S(1)}, u32[]{:S(2)}, u32[]{:S(2)}) collective-permute-start(bf16[14,96,384]{2,1,0:T(8,128)(2,1)} %collective-permute-done.24.refs_7_), channel_id=1, source_target_pairs={{1,0},{0,1},{3,2},{2,3},{5,4},{4,5},{7,6},{6,7},{9,8},{8,9},{11,10... | collective-permute-start | bytes 3096584 | tf_op jit(solution)/shard_map/ppermute | solution.py:39
  120.1 38.0 %collective-permute-start.29 = (bf16[14,96,384]{2,1,0:T(8,128)(2,1)}, bf16[14,96,384]{2,1,0:T(8,128)(2,1)S(1)}, u32[]{:S(2)}, u32[]{:S(2)}) collective-permute-start(bf16[14,96,384]{2,1,0:T(8,128)(2,1)} %collective-permute-done.25.refs_8_), channel_id=1, source_target_pairs={{1,0},{0,1},{3,2},{2,3},{5,4},{4,5},{7,6},{6,7},{9,8},{8,9},{11,10... | collective-permute-start | bytes 3096584 | tf_op jit(solution)/shard_map/ppermute | solution.py:39
  134.8 10.8 %collective-permute-start.15 = (bf16[2,4,32,384]{3,2,1,0:T(8,128)(2,1)S(1)}, bf16[2,4,32,384]{3,2,1,0:T(8,128)(2,1)S(1)}, u32[]{:S(2)}, u32[]{:S(2)}) collective-permute-start(bf16[2,4,32,384]{3,2,1,0:T(8,128)(2,1)S(1)} %constant_dynamic-slice_fusion.1), channel_id=1, source_target_pairs={{0,8},{1,9},{2,10},{3,11},{4,12},{5,13},{6,14},{7,15},{8,16},{9,17... | collective-permute-start | bytes 589832 | tf_op jit(solution)/shard_map/ppermute | solution.py:39
  145.6 5.1 %collective-permute-start.17 = (bf16[8,1,32,384]{3,2,1,0:T(8,128)(2,1)S(1)}, bf16[8,1,32,384]{3,2,1,0:T(8,128)(2,1)S(1)}, u32[]{:S(2)}, u32[]{:S(2)}) collective-permute-start(bf16[8,1,32,384]{3,2,1,0:T(8,128)(2,1)S(1)} %get-tuple-element.12), channel_id=1, source_target_pairs={{1,0},{2,1},{3,2},{4,3},{5,4},{6,5},{7,6},{9,8},{10,9},{11,10},{12... | collective-permute-start | bytes 589832 | tf_op jit(solution)/shard_map/ppermute | solution.py:39
  150.7 7.2 %collective-permute-start.16 = (bf16[8,1,32,384]{3,2,1,0:T(8,128)(2,1)S(1)}, bf16[8,1,32,384]{3,2,1,0:T(8,128)(2,1)S(1)}, u32[]{:S(2)}, u32[]{:S(2)}) collective-permute-start(bf16[8,1,32,384]{3,2,1,0:T(8,128)(2,1)S(1)} %get-tuple-element.11), channel_id=1, source_target_pairs={{0,1},{1,2},{2,3},{3,4},{4,5},{5,6},{6,7},{8,9},{9,10},{10,11},{11... | collective-permute-start | bytes 589832 | tf_op jit(solution)/shard_map/ppermute | solution.py:39
  (8 other events, 90.6 us)
where the time goes:
time: 173 us
  waiting for transfers between devices  72.1 us (42%)
  starting transfers between devices  54.9 us (32%)
  Pallas kernels  28.7 us (17%)
  local copies, waits for them, and re-layouts  10.1 us (6%)
  other arithmetic  5.17 us (3%)
  between operations  1.94 us (1%)
    ppermute x30, waiting for transfers between devices, fetch(): return lax.ppermute(array, AXES, pairs)  72.1 us
    ppermute x30, starting transfers between devices, fetch(): return lax.ppermute(array, AXES, pairs)  54.9 us
    pallas_call x2, Pallas kernels, conv(): pl.pallas_call(lambda *refs: conv_body(*refs, finish=finish), out_shape=j...  28.7 us
  transfers between devices with their start and end apart: 30, of which 14 were waited for; matrix products, arithmetic and copies ran while one was open for 7% of the time, Pallas kernels for 8%

commit v1 on v0

--- a/solution.py
+++ b/solution.py
@@ -55,24 +55,31 @@
     return (z, y, x, 1 - c)
 
 
-def own_half(kernel):
+def own_halves(kernels):
     start = lax.axis_index("c") * (27 - HALF)
-    taps = lax.dynamic_slice_in_dim(kernel.reshape(27, SHARD, C), start, HALF, 0)
-    return taps.reshape(HALF * SHARD, C)
-
-
-def pieces_along_z(own):
-    return jnp.stack([fetch(own, z_source(0)), fetch(own, z_source(1))])
-
-
-def small_stage(two):
-    parts = [two] + [fetch(two, small_source(step)) for step in ROUND[1:]]
-    return jnp.stack(parts)
+    return jnp.stack(
+        [
+            lax.dynamic_slice_in_dim(k.reshape(27, SHARD, C), start, HALF, 0).reshape(
+                HALF * SHARD, C
+            )
+            for k in kernels
+        ]
+    )
 
 
 def join_rows(parts):
     parts = parts.reshape(8, HALF, SHARD, C)
     return jnp.transpose(parts, (1, 0, 2, 3)).reshape(HALF, BUNDLE, C)
+
+
+def gather_bundles(kernels):
+    own = own_halves(kernels)
+    first = fetch(own, z_source(0))
+    second = fetch(own, z_source(1))
+    two = jnp.stack([first, second], 1)
+    near = [fetch(two, small_source(step)) for step in ROUND[1:]]
+    parts = jnp.stack([two] + near, 1)
+    return [join_rows(parts[0]), join_rows(parts[1])]
 
 
 def bulk_stage(bundle):
@@ -263,16 +270,10 @@
         below = fetch(acts[:, 0:1], row_neighbour(1))
         return jnp.concatenate([above, acts, below], 1)
 
-    one = pieces_along_z(own_half(kernel_one))
-    one_parts = small_stage(one)
-    one_bundles = bulk_stage(join_rows(one_parts))
+    one_bundle, two_bundle = gather_bundles((kernel_one, kernel_two))
+    one_bundles = bulk_stage(one_bundle)
     one_others = [fetch(b, sibling) for b in one_bundles]
-
-    own_two, _ = lax.optimization_barrier((own_half(kernel_two), one))
-    two = pieces_along_z(own_two)
-    two, _ = lax.optimization_barrier((two, one_parts))
-    two_bundle = join_rows(small_stage(two))
-    two_bundle, _ = lax.optimization_barrier((two_bundle, one_bundles))
+    two_bundle, _ = lax.optimization_barrier((two_bundle, one_bundles[:3]))
     two_bundles = bulk_stage(two_bundle)
     two_others = [fetch(b, sibling) for b in two_bundles]
 

time: 173 us -> 164 us (0.948)
  the two profiles are of different devices: /device:TPU:36 before, /device:TPU:131 now
where the time goes in v1:
time: 164 us; the launch traced here: 163 us
  waiting for transfers between devices  58.5 us (36%)
  starting transfers between devices  56.9 us (35%)
  Pallas kernels  28.6 us (17%)
  local copies, waits for them, and re-layouts  13.3 us (8%)
  other arithmetic  3.93 us (2%)
  between operations  1.93 us (1%)
    ppermute x25, waiting for transfers between devices, fetch(): return lax.ppermute(array, AXES, pairs)  58.5 us
    ppermute x25, starting transfers between devices, fetch(): return lax.ppermute(array, AXES, pairs)  56.9 us
    pallas_call x2, Pallas kernels, conv(): pl.pallas_call(lambda *refs: conv_body(*refs, finish=finish), out_shape=j...  28.6 us
    another operation x2, local copies, waits for them, and re-layouts, join_rows(): parts = parts.reshape(8, HALF, SHARD, C)  3.99 us
  transfers between devices with their start and end apart: 25, of which 11 were waited for; matrix products, arithmetic and copies ran while one was open for 7% of the time, Pallas kernels for 9%

profile of v1, /device:TPU:131, one launch (start us, length us, event | category | flops | bytes accessed | tf_op | source)
XLA Modules:
  0.0 163.2 jit_solution(1239687868690077186)
XLA Ops:
  0.0 1.0 constant_dynamic-slice_fusion.1
  1.2 3.6 %collective-permute-start.4 = (bf16[2,168,384]{2,1,0:T(8,128)(2,1)S(1)}, bf16[2,168,384]{2,1,0:T(8,128)(2,1)S(1)}, u32[]{:S(2)}, u32[]{:S(2)}) collective-permute-start(bf16[2,168,384]{2,1,0:T(8,128)(2,1)S(1)} %constant_dynamic-update-slice_fusion), channel_id=1, source_target_pairs={{0,0},{1,1},{98,2},{163,3},{164,4},{101,5},{198,6},{71,7},{8,8},{9... | collective-permute-start | bytes 774152 | tf_op jit(solution)/shard_map/ppermute | solution.py:39
  4.8 10.6 %collective-permute-done.4 = bf16[2,168,384]{2,1,0:T(8,128)(2,1)S(1)} collective-permute-done((bf16[2,168,384]{2,1,0:T(8,128)(2,1)S(1)}, bf16[2,168,384]{2,1,0:T(8,128)(2,1)S(1)}, u32[]{:S(2)}, u32[]{:S(2)}) %collective-permute-start.4) | collective-permute-done | bytes 258080 | tf_op jit(solution)/shard_map/ppermute | solution.py:39
  15.4 3.2 %collective-permute-done.3 = bf16[2,168,384]{2,1,0:T(8,128)(2,1)S(1)} collective-permute-done((bf16[2,168,384]{2,1,0:T(8,128)(2,1)S(1)}, bf16[2,168,384]{2,1,0:T(8,128)(2,1)S(1)}, u32[]{:S(2)}, u32[]{:S(2)}) %collective-permute-start.3) | collective-permute-done | bytes 258080 | tf_op jit(solution)/shard_map/ppermute | solution.py:39
  18.8 3.0 %collective-permute-start.7 = (bf16[2,2,168,384]{3,2,0,1:T(8,128)(2,1)S(1)}, bf16[2,2,168,384]{3,2,0,1:T(8,128)(2,1)S(1)}, u32[]{:S(2)}, u32[]{:S(2)}) collective-permute-start(bf16[2,2,168,384]{3,2,0,1:T(8,128)(2,1)S(1)} %get-tuple-element.14), channel_id=1, source_target_pairs={{4,0},{17,1},{6,2},{19,3},{0,4},{21,5},{2,6},{23,7},{12,8},{25,9},... | collective-permute-start | bytes 1548296 | tf_op jit(solution)/shard_map/ppermute | solution.py:39
  22.2 2.3 %collective-permute-start.5 = (bf16[2,2,168,384]{3,2,0,1:T(8,128)(2,1)S(1)}, bf16[2,2,168,384]{3,2,0,1:T(8,128)(2,1)S(1)}, u32[]{:S(2)}, u32[]{:S(2)}) collective-permute-start(bf16[2,2,168,384]{3,2,0,1:T(8,128)(2,1)S(1)} %get-tuple-element.14), channel_id=1, source_target_pairs={{2,0},{9,1},{4,2},{11,3},{6,4},{13,5},{0,6},{15,7},{10,8},{17,9},{... | collective-permute-start | bytes 1548296 | tf_op jit(solution)/shard_map/ppermute | solution.py:39
  24.4 4.0 %collective-permute-done.7 = bf16[2,2,168,384]{3,2,0,1:T(8,128)(2,1)S(1)} collective-permute-done((bf16[2,2,168,384]{3,2,0,1:T(8,128)(2,1)S(1)}, bf16[2,2,168,384]{3,2,0,1:T(8,128)(2,1)S(1)}, u32[]{:S(2)}, u32[]{:S(2)}) %collective-permute-start.7) | collective-permute-done | bytes 516128 | tf_op jit(solution)/shard_map/ppermute | solution.py:39
  28.4 5.4 %collective-permute-done.6 = bf16[2,2,168,384]{3,2,0,1:T(8,128)(2,1)S(1)} collective-permute-done((bf16[2,2,168,384]{3,2,0,1:T(8,128)(2,1)S(1)}, bf16[2,2,168,384]{3,2,0,1:T(8,128)(2,1)S(1)}, u32[]{:S(2)}, u32[]{:S(2)}) %collective-permute-start.6) | collective-permute-done | bytes 516128 | tf_op jit(solution)/shard_map/ppermute | solution.py:39
  35.8 1.4 reshape_squeeze.6
  37.2 1.6 copy.26
  42.7 3.0 %collective-permute-start = (bf16[2,4,32,384]{3,2,1,0:T(8,128)(2,1)}, bf16[2,4,32,384]{3,2,1,0:T(8,128)(2,1)S(1)}, u32[]{:S(2)}, u32[]{:S(2)}) collective-permute-start(bf16[2,4,32,384]{3,2,1,0:T(8,128)(2,1)} %constant_dynamic-slice_fusion.3), channel_id=1, source_target_pairs={{0,8},{1,9},{2,10},{3,11},{4,12},{5,13},{6,14},{7,15},{8,16},{9,17... | collective-permute-start | bytes 589832 | tf_op jit(solution)/shard_map/ppermute | solution.py:39
  45.8 7.5 %collective-permute-start.11 = (bf16[14,96,384]{2,1,0:T(8,128)(2,1)S(1)}, bf16[14,96,384]{2,1,0:T(8,128)(2,1)}, u32[]{:S(2)}, u32[]{:S(2)}) collective-permute-start(bf16[14,96,384]{2,1,0:T(8,128)(2,1)S(1)} %copy.31.refs_5_), channel_id=1, source_target_pairs={{1,0},{0,1},{3,2},{2,3},{5,4},{4,5},{7,6},{6,7},{9,8},{8,9},{11,10... | collective-permute-start | bytes 3096584 | tf_op jit(solution)/shard_map/ppermute | solution.py:39
  53.3 10.8 %collective-permute-done.8.refs_6_ = bf16[14,96,384]{2,1,0:T(8,128)(2,1)} collective-permute-done((bf16[14,96,384]{2,1,0:T(8,128)(2,1)S(1)}, bf16[14,96,384]{2,1,0:T(8,128)(2,1)}, u32[]{:S(2)}, u32[]{:S(2)}) %collective-permute-start.8) | collective-permute-done | bytes 1032224 | tf_op jit(solution)/shard_map/ppermute | solution.py:39
  64.1 3.7 %collective-permute-start.12 = (bf16[14,96,384]{2,1,0:T(8,128)(2,1)}, bf16[14,96,384]{2,1,0:T(8,128)(2,1)}, u32[]{:S(2)}, u32[]{:S(2)}) collective-permute-start(bf16[14,96,384]{2,1,0:T(8,128)(2,1)} %collective-permute-done.8.refs_6_), channel_id=1, source_target_pairs={{1,0},{0,1},{3,2},{2,3},{5,4},{4,5},{7,6},{6,7},{9,8},{8,9},{11,10... | collective-permute-start | bytes 3096584 | tf_op jit(solution)/shard_map/ppermute | solution.py:39
  70.0 1.9 %collective-permute-start.2 = (bf16[8,1,32,384]{3,2,1,0:T(8,128)(2,1)}, bf16[8,1,32,384]{3,2,1,0:T(8,128)(2,1)}, u32[]{:S(2)}, u32[]{:S(2)}) collective-permute-start(bf16[8,1,32,384]{3,2,1,0:T(8,128)(2,1)} %get-tuple-element.12), channel_id=1, source_target_pairs={{1,0},{2,1},{3,2},{4,3},{5,4},{6,5},{7,6},{9,8},{10,9},{11,10},{12... | collective-permute-start | bytes 589832 | tf_op jit(solution)/shard_map/ppermute | solution.py:39
  71.9 5.8 %collective-permute-start.1 = (bf16[8,1,32,384]{3,2,1,0:T(8,128)(2,1)}, bf16[8,1,32,384]{3,2,1,0:T(8,128)(2,1)}, u32[]{:S(2)}, u32[]{:S(2)}) collective-permute-start(bf16[8,1,32,384]{3,2,1,0:T(8,128)(2,1)} %get-tuple-element.11), channel_id=1, source_target_pairs={{0,1},{1,2},{2,3},{3,4},{4,5},{5,6},{6,7},{8,9},{9,10},{10,11},{11... | collective-permute-start | bytes 589832 | tf_op jit(solution)/shard_map/ppermute | solution.py:39
  77.8 1.8 %copy.32 = bf16[1,4,2,168,384]{4,2,1,3,0:T(2,128)(2,1)} copy(bf16[1,4,2,168,384]{4,3,0,2,1:T(8,128)(2,1)S(1)} %get-tuple-element.7) | data formatting | bytes 2064384 | tf_op jit(solution)/shard_map/slice | solution.py:82
  79.6 2.6 %reshape_squeeze.7 = bf16[8,14,12,384]{3,0,2,1:T(8,128)(2,1)S(1)} reshape(bf16[1,4,2,168,384]{4,2,1,3,0:T(2,128)(2,1)} %copy.32) | data formatting | bytes 2064384 | tf_op jit(solution)/shard_map/reshape;squeeze | solution.py:71
  82.8 1.8 %collective-permute-start.18 = (bf16[14,96,384]{2,1,0:T(8,128)(2,1)S(1)}, bf16[14,96,384]{2,1,0:T(8,128)(2,1)}, u32[]{:S(2)}, u32[]{:S(2)}) collective-permute-start(bf16[14,96,384]{2,1,0:T(8,128)(2,1)S(1)} %copy.38.refs_5_), channel_id=1, source_target_pairs={{8,0},{3,1},{10,2},{5,3},{12,4},{7,5},{14,6},{1,7},{16,8},{11,9},{... | collective-permute-start | bytes 3096584 | tf_op jit(solution)/shard_map/ppermute | solution.py:39
  84.7 1.9 %collective-permute-start.20 = (bf16[14,96,384]{2,1,0:T(8,128)(2,1)S(1)}, bf16[14,96,384]{2,1,0:T(8,128)(2,1)}, u32[]{:S(2)}, u32[]{:S(2)}) collective-permute-start(bf16[14,96,384]{2,1,0:T(8,128)(2,1)S(1)} %copy.38.refs_5_), channel_id=1, source_target_pairs={{16,0},{5,1},{18,2},{7,3},{20,4},{1,5},{22,6},{3,7},{24,8},{13,9},... | collective-permute-start | bytes 3096584 | tf_op jit(solution)/shard_map/ppermute | solution.py:39
  88.4 1.2 pad_maximum_fusion.1.refs_2_
  89.9 6.9 %collective-permute-done.18.refs_6_ = bf16[14,96,384]{2,1,0:T(8,128)(2,1)} collective-permute-done((bf16[14,96,384]{2,1,0:T(8,128)(2,1)S(1)}, bf16[14,96,384]{2,1,0:T(8,128)(2,1)}, u32[]{:S(2)}, u32[]{:S(2)}) %collective-permute-start.18) | collective-permute-done | bytes 1032224 | tf_op jit(solution)/shard_map/ppermute | solution.py:39
  96.8 1.3 collective-permute-start.22
  98.5 12.0 %collective-permute-start.23 = (bf16[14,96,384]{2,1,0:T(8,128)(2,1)}, bf16[14,96,384]{2,1,0:T(8,128)(2,1)S(1)}, u32[]{:S(2)}, u32[]{:S(2)}) collective-permute-start(bf16[14,96,384]{2,1,0:T(8,128)(2,1)} %collective-permute-done.19.refs_7_), channel_id=1, source_target_pairs={{1,0},{0,1},{3,2},{2,3},{5,4},{4,5},{7,6},{6,7},{9,8},{8,9},{11,10... | collective-permute-start | bytes 3096584 | tf_op jit(solution)/shard_map/ppermute | solution.py:39
  110.5 14.1 %shard_map.100 = bf16[6,128,384]{2,1,0:T(8,128)(2,1)S(1)} custom-call(s32[2]{0:T(128)S(1)} %pad_add_fusion.1.refs_0_, f32[3,6]{1,0:T(4,128)S(1)} %add_convert_fusion.refs_1_, bf16[8,6,32,384]{3,2,1,0:T(8,128)(2,1)S(1)} %pad_maximum_fusion.1.refs_2_, s32[2,384]{1,0:T(2,128)S(1)} %pad_add_fusion.refs_3_, f32[1,384]{1,0:T(1,128)S(1)} %reshape.213.refs_4_, ...), custom_call_target="tpu_custom_call" | custom-call | flops 6115295232 | bytes 12000000 | tf_op jit(solution)/shard_map/pallas_call | solution.py:211
  124.6 1.9 %collective-permute-start.15 = (bf16[2,4,32,384]{3,2,1,0:T(8,128)(2,1)S(1)}, bf16[2,4,32,384]{3,2,1,0:T(8,128)(2,1)S(1)}, u32[]{:S(2)}, u32[]{:S(2)}) collective-permute-start(bf16[2,4,32,384]{3,2,1,0:T(8,128)(2,1)S(1)} %constant_dynamic-slice_fusion), channel_id=1, source_target_pairs={{0,8},{1,9},{2,10},{3,11},{4,12},{5,13},{6,14},{7,15},{8,16},{9,17... | collective-permute-start | bytes 589832 | tf_op jit(solution)/shard_map/ppermute | solution.py:39
  126.6 9.2 %collective-permute-done.15 = bf16[2,4,32,384]{3,2,1,0:T(8,128)(2,1)S(1)} collective-permute-done((bf16[2,4,32,384]{3,2,1,0:T(8,128)(2,1)S(1)}, bf16[2,4,32,384]{3,2,1,0:T(8,128)(2,1)S(1)}, u32[]{:S(2)}, u32[]{:S(2)}) %collective-permute-start.15) | collective-permute-done | bytes 196640 | tf_op jit(solution)/shard_map/ppermute | solution.py:39
  135.9 3.3 %collective-permute-start.17 = (bf16[8,1,32,384]{3,2,1,0:T(8,128)(2,1)S(1)}, bf16[8,1,32,384]{3,2,1,0:T(8,128)(2,1)S(1)}, u32[]{:S(2)}, u32[]{:S(2)}) collective-permute-start(bf16[8,1,32,384]{3,2,1,0:T(8,128)(2,1)S(1)} %get-tuple-element.10), channel_id=1, source_target_pairs={{1,0},{2,1},{3,2},{4,3},{5,4},{6,5},{7,6},{9,8},{10,9},{11,10},{12... | collective-permute-start | bytes 589832 | tf_op jit(solution)/shard_map/ppermute | solution.py:39
  139.1 4.6 %collective-permute-done.17 = bf16[8,1,32,384]{3,2,1,0:T(8,128)(2,1)S(1)} collective-permute-done((bf16[8,1,32,384]{3,2,1,0:T(8,128)(2,1)S(1)}, bf16[8,1,32,384]{3,2,1,0:T(8,128)(2,1)S(1)}, u32[]{:S(2)}, u32[]{:S(2)}) %collective-permute-start.17) | collective-permute-done | bytes 196640 | tf_op jit(solution)/shard_map/ppermute | solution.py:39
  143.7 1.9 %collective-permute-start.16 = (bf16[8,1,32,384]{3,2,1,0:T(8,128)(2,1)S(1)}, bf16[8,1,32,384]{3,2,1,0:T(8,128)(2,1)S(1)}, u32[]{:S(2)}, u32[]{:S(2)}) collective-permute-start(bf16[8,1,32,384]{3,2,1,0:T(8,128)(2,1)S(1)} %get-tuple-element.9), channel_id=1, source_target_pairs={{0,1},{1,2},{2,3},{3,4},{4,5},{5,6},{6,7},{8,9},{9,10},{10,11},{11... | collective-permute-start | bytes 589832 | tf_op jit(solution)/shard_map/ppermute | solution.py:39
  145.6 2.6 %collective-permute-done.16 = bf16[8,1,32,384]{3,2,1,0:T(8,128)(2,1)S(1)} collective-permute-done((bf16[8,1,32,384]{3,2,1,0:T(8,128)(2,1)S(1)}, bf16[8,1,32,384]{3,2,1,0:T(8,128)(2,1)S(1)}, u32[]{:S(2)}, u32[]{:S(2)}) %collective-permute-start.16) | collective-permute-done | bytes 196640 | tf_op jit(solution)/shard_map/ppermute | solution.py:39
  148.5 14.6 %shard_map.101 = bf16[6,128,384]{2,1,0:T(8,128)(2,1)} custom-call(s32[2]{0:T(128)S(1)} %pad_add_fusion.1.refs_0_, f32[3,6]{1,0:T(4,128)S(1)} %add_convert_fusion.refs_1_, bf16[8,6,32,384]{3,2,1,0:T(8,128)(2,1)S(1)} %pad_maximum_fusion.2.refs_2_, s32[2,384]{1,0:T(2,128)S(1)} %pad_add_fusion.refs_3_, bf16[6,128,384]{2,1,0:T(8,128)(2,1)S(1)} %bitcast.39, ...), custom_call_target="tpu_custom_call" | custom-call | flops 6115295232 | bytes 12000000 | tf_op jit(solution)/shard_map/pallas_call | solution.py:211
  (79 shorter events, 11.0 us)
Async XLA Ops:
  1.2 14.3 %collective-permute-start.4 = (bf16[2,168,384]{2,1,0:T(8,128)(2,1)S(1)}, bf16[2,168,384]{2,1,0:T(8,128)(2,1)S(1)}, u32[]{:S(2)}, u32[]{:S(2)}) collective-permute-start(bf16[2,168,384]{2,1,0:T(8,128)(2,1)S(1)} %constant_dynamic-update-slice_fusion), channel_id=1, source_target_pairs={{0,0},{1,1},{98,2},{163,3},{164,4},{101,5},{198,6},{71,7},{8,8},{9... | collective-permute-start | bytes 774152 | tf_op jit(solution)/shard_map/ppermute | solution.py:39
  4.7 13.9 %collective-permute-start.3 = (bf16[2,168,384]{2,1,0:T(8,128)(2,1)S(1)}, bf16[2,168,384]{2,1,0:T(8,128)(2,1)S(1)}, u32[]{:S(2)}, u32[]{:S(2)}) collective-permute-start(bf16[2,168,384]{2,1,0:T(8,128)(2,1)S(1)} %constant_dynamic-update-slice_fusion), channel_id=1, source_target_pairs={{128,0},{129,1},{34,2},{227,3},{228,4},{37,5},{70,6},{199,7},{136,... | collective-permute-start | bytes 774152 | tf_op jit(solution)/shard_map/ppermute | solution.py:39
  18.8 9.6 %collective-permute-start.7 = (bf16[2,2,168,384]{3,2,0,1:T(8,128)(2,1)S(1)}, bf16[2,2,168,384]{3,2,0,1:T(8,128)(2,1)S(1)}, u32[]{:S(2)}, u32[]{:S(2)}) collective-permute-start(bf16[2,2,168,384]{3,2,0,1:T(8,128)(2,1)S(1)} %get-tuple-element.14), channel_id=1, source_target_pairs={{4,0},{17,1},{6,2},{19,3},{0,4},{21,5},{2,6},{23,7},{12,8},{25,9},... | collective-permute-start | bytes 1548296 | tf_op jit(solution)/shard_map/ppermute | solution.py:39
  21.8 12.1 %collective-permute-start.6 = (bf16[2,2,168,384]{3,2,0,1:T(8,128)(2,1)S(1)}, bf16[2,2,168,384]{3,2,0,1:T(8,128)(2,1)S(1)}, u32[]{:S(2)}, u32[]{:S(2)}) collective-permute-start(bf16[2,2,168,384]{3,2,0,1:T(8,128)(2,1)S(1)} %get-tuple-element.14), channel_id=1, source_target_pairs={{6,0},{25,1},{0,2},{27,3},{2,4},{29,5},{4,6},{31,7},{14,8},{1,9},{... | collective-permute-start | bytes 1548296 | tf_op jit(solution)/shard_map/ppermute | solution.py:39
  22.2 12.3 %collective-permute-start.5 = (bf16[2,2,168,384]{3,2,0,1:T(8,128)(2,1)S(1)}, bf16[2,2,168,384]{3,2,0,1:T(8,128)(2,1)S(1)}, u32[]{:S(2)}, u32[]{:S(2)}) collective-permute-start(bf16[2,2,168,384]{3,2,0,1:T(8,128)(2,1)S(1)} %get-tuple-element.14), channel_id=1, source_target_pairs={{2,0},{9,1},{4,2},{11,3},{6,4},{13,5},{0,6},{15,7},{10,8},{17,9},{... | collective-permute-start | bytes 1548296 | tf_op jit(solution)/shard_map/ppermute | solution.py:39
  38.8 1.1 copy-start
  38.8 2.1 %copy-start.3 = (f32[384]{0:T(512)S(1)}, f32[384]{0:T(512)}, u32[]{:S(2)}) copy-start(f32[384]{0:T(512)} %param.16) | copy-start | bytes 4612
  39.0 28.7 %copy-start.5 = (s32[4]{0:T(128)S(1)}, s32[4]{0:T(128)}, u32[]{:S(2)}) copy-start(s32[4]{0:T(128)} %constant.98.clone) | copy-start | bytes 52
  39.1 28.7 %copy-start.2 = (s32[4,2]{1,0:T(4,128)S(1)}, s32[4,2]{1,0:T(4,128)}, u32[]{:S(2)}) copy-start(s32[4,2]{1,0:T(4,128)} %constant.105) | copy-start | bytes 100
  39.1 29.3 %copy-start.1 = (s32[4,2]{1,0:T(4,128)S(1)}, s32[4,2]{1,0:T(4,128)}, u32[]{:S(2)}) copy-start(s32[4,2]{1,0:T(4,128)} %constant.107) | copy-start | bytes 100
  39.1 25.0 %collective-permute-start.8 = (bf16[14,96,384]{2,1,0:T(8,128)(2,1)S(1)}, bf16[14,96,384]{2,1,0:T(8,128)(2,1)}, u32[]{:S(2)}, u32[]{:S(2)}) collective-permute-start(bf16[14,96,384]{2,1,0:T(8,128)(2,1)S(1)} %copy.31.refs_5_), channel_id=1, source_target_pairs={{8,0},{3,1},{10,2},{5,3},{12,4},{7,5},{14,6},{1,7},{16,8},{11,9},{... | collective-permute-start | bytes 3096584 | tf_op jit(solution)/shard_map/ppermute | solution.py:39
  40.1 31.9 %collective-permute-start.9 = (bf16[14,96,384]{2,1,0:T(8,128)(2,1)S(1)}, bf16[14,96,384]{2,1,0:T(8,128)(2,1)}, u32[]{:S(2)}, u32[]{:S(2)}) collective-permute-start(bf16[14,96,384]{2,1,0:T(8,128)(2,1)S(1)} %copy.31.refs_5_), channel_id=1, source_target_pairs={{24,0},{7,1},{26,2},{1,3},{28,4},{3,5},{30,6},{5,7},{0,8},{15,9},{... | collective-permute-start | bytes 3096584 | tf_op jit(solution)/shard_map/ppermute | solution.py:39
  42.7 26.5 %collective-permute-start = (bf16[2,4,32,384]{3,2,1,0:T(8,128)(2,1)}, bf16[2,4,32,384]{3,2,1,0:T(8,128)(2,1)S(1)}, u32[]{:S(2)}, u32[]{:S(2)}) collective-permute-start(bf16[2,4,32,384]{3,2,1,0:T(8,128)(2,1)} %constant_dynamic-slice_fusion.3), channel_id=1, source_target_pairs={{0,8},{1,9},{2,10},{3,11},{4,12},{5,13},{6,14},{7,15},{8,16},{9,17... | collective-permute-start | bytes 589832 | tf_op jit(solution)/shard_map/ppermute | solution.py:39
  45.7 39.0 %collective-permute-start.10 = (bf16[14,96,384]{2,1,0:T(8,128)(2,1)S(1)}, bf16[14,96,384]{2,1,0:T(8,128)(2,1)}, u32[]{:S(2)}, u32[]{:S(2)}) collective-permute-start(bf16[14,96,384]{2,1,0:T(8,128)(2,1)S(1)} %copy.31.refs_5_), channel_id=1, source_target_pairs={{16,0},{5,1},{18,2},{7,3},{20,4},{1,5},{22,6},{3,7},{24,8},{13,9},... | collective-permute-start | bytes 3096584 | tf_op jit(solution)/shard_map/ppermute | solution.py:39
  45.8 40.8 %collective-permute-start.11 = (bf16[14,96,384]{2,1,0:T(8,128)(2,1)S(1)}, bf16[14,96,384]{2,1,0:T(8,128)(2,1)}, u32[]{:S(2)}, u32[]{:S(2)}) collective-permute-start(bf16[14,96,384]{2,1,0:T(8,128)(2,1)S(1)} %copy.31.refs_5_), channel_id=1, source_target_pairs={{1,0},{0,1},{3,2},{2,3},{5,4},{4,5},{7,6},{6,7},{9,8},{8,9},{11,10... | collective-permute-start | bytes 3096584 | tf_op jit(solution)/shard_map/ppermute | solution.py:39
  64.1 22.5 %collective-permute-start.12 = (bf16[14,96,384]{2,1,0:T(8,128)(2,1)}, bf16[14,96,384]{2,1,0:T(8,128)(2,1)}, u32[]{:S(2)}, u32[]{:S(2)}) collective-permute-start(bf16[14,96,384]{2,1,0:T(8,128)(2,1)} %collective-permute-done.8.refs_6_), channel_id=1, source_target_pairs={{1,0},{0,1},{3,2},{2,3},{5,4},{4,5},{7,6},{6,7},{9,8},{8,9},{11,10... | collective-permute-start | bytes 3096584 | tf_op jit(solution)/shard_map/ppermute | solution.py:39
  70.0 12.8 %collective-permute-start.2 = (bf16[8,1,32,384]{3,2,1,0:T(8,128)(2,1)}, bf16[8,1,32,384]{3,2,1,0:T(8,128)(2,1)}, u32[]{:S(2)}, u32[]{:S(2)}) collective-permute-start(bf16[8,1,32,384]{3,2,1,0:T(8,128)(2,1)} %get-tuple-element.12), channel_id=1, source_target_pairs={{1,0},{2,1},{3,2},{4,3},{5,4},{6,5},{7,6},{9,8},{10,9},{11,10},{12... | collective-permute-start | bytes 589832 | tf_op jit(solution)/shard_map/ppermute | solution.py:39
  71.9 12.7 %collective-permute-start.1 = (bf16[8,1,32,384]{3,2,1,0:T(8,128)(2,1)}, bf16[8,1,32,384]{3,2,1,0:T(8,128)(2,1)}, u32[]{:S(2)}, u32[]{:S(2)}) collective-permute-start(bf16[8,1,32,384]{3,2,1,0:T(8,128)(2,1)} %get-tuple-element.11), channel_id=1, source_target_pairs={{0,1},{1,2},{2,3},{3,4},{4,5},{5,6},{6,7},{8,9},{9,10},{10,11},{11... | collective-permute-start | bytes 589832 | tf_op jit(solution)/shard_map/ppermute | solution.py:39
  82.6 5.2 %copy-start.6 = (s32[3]{0:T(128)S(1)}, s32[3]{0:T(128)}, u32[]{:S(2)}) copy-start(s32[3]{0:T(128)} %param.11) | copy-start | bytes 40
  82.6 5.6 %copy-start.4 = (f32[384]{0:T(512)S(1)}, f32[384]{0:T(512)}, u32[]{:S(2)}) copy-start(f32[384]{0:T(512)} %param.17) | copy-start | bytes 4612
  82.8 14.0 %collective-permute-start.18 = (bf16[14,96,384]{2,1,0:T(8,128)(2,1)S(1)}, bf16[14,96,384]{2,1,0:T(8,128)(2,1)}, u32[]{:S(2)}, u32[]{:S(2)}) collective-permute-start(bf16[14,96,384]{2,1,0:T(8,128)(2,1)S(1)} %copy.38.refs_5_), channel_id=1, source_target_pairs={{8,0},{3,1},{10,2},{5,3},{12,4},{7,5},{14,6},{1,7},{16,8},{11,9},{... | collective-permute-start | bytes 3096584 | tf_op jit(solution)/shard_map/ppermute | solution.py:39
  84.7 13.9 %collective-permute-start.19 = (bf16[14,96,384]{2,1,0:T(8,128)(2,1)S(1)}, bf16[14,96,384]{2,1,0:T(8,128)(2,1)}, u32[]{:S(2)}, u32[]{:S(2)}) collective-permute-start(bf16[14,96,384]{2,1,0:T(8,128)(2,1)S(1)} %copy.38.refs_5_), channel_id=1, source_target_pairs={{24,0},{7,1},{26,2},{1,3},{28,4},{3,5},{30,6},{5,7},{0,8},{15,9},{... | collective-permute-start | bytes 3096584 | tf_op jit(solution)/shard_map/ppermute | solution.py:39
  84.7 25.9 %collective-permute-start.20 = (bf16[14,96,384]{2,1,0:T(8,128)(2,1)S(1)}, bf16[14,96,384]{2,1,0:T(8,128)(2,1)}, u32[]{:S(2)}, u32[]{:S(2)}) collective-permute-start(bf16[14,96,384]{2,1,0:T(8,128)(2,1)S(1)} %copy.38.refs_5_), channel_id=1, source_target_pairs={{16,0},{5,1},{18,2},{7,3},{20,4},{1,5},{22,6},{3,7},{24,8},{13,9},... | collective-permute-start | bytes 3096584 | tf_op jit(solution)/shard_map/ppermute | solution.py:39
  86.6 3.1 %collective-permute-start.13 = (bf16[14,96,384]{2,1,0:T(8,128)(2,1)}, bf16[14,96,384]{2,1,0:T(8,128)(2,1)}, u32[]{:S(2)}, u32[]{:S(2)}) collective-permute-start(bf16[14,96,384]{2,1,0:T(8,128)(2,1)} %collective-permute-done.9.refs_7_), channel_id=1, source_target_pairs={{1,0},{0,1},{3,2},{2,3},{5,4},{4,5},{7,6},{6,7},{9,8},{8,9},{11,10... | collective-permute-start | bytes 3096584 | tf_op jit(solution)/shard_map/ppermute | solution.py:39
  86.6 24.0 %collective-permute-start.14 = (bf16[14,96,384]{2,1,0:T(8,128)(2,1)}, bf16[14,96,384]{2,1,0:T(8,128)(2,1)}, u32[]{:S(2)}, u32[]{:S(2)}) collective-permute-start(bf16[14,96,384]{2,1,0:T(8,128)(2,1)} %collective-permute-done.10.refs_8_), channel_id=1, source_target_pairs={{1,0},{0,1},{3,2},{2,3},{5,4},{4,5},{7,6},{6,7},{9,8},{8,9},{11,10... | collective-permute-start | bytes 3096584 | tf_op jit(solution)/shard_map/ppermute | solution.py:39
  89.7 58.7 %collective-permute-start.21 = (bf16[14,96,384]{2,1,0:T(8,128)(2,1)S(1)}, bf16[14,96,384]{2,1,0:T(8,128)(2,1)S(1)}, u32[]{:S(2)}, u32[]{:S(2)}) collective-permute-start(bf16[14,96,384]{2,1,0:T(8,128)(2,1)S(1)} %copy.38.refs_5_), channel_id=1, source_target_pairs={{1,0},{0,1},{3,2},{2,3},{5,4},{4,5},{7,6},{6,7},{9,8},{8,9},{11,10... | collective-permute-start | bytes 3096584 | tf_op jit(solution)/shard_map/ppermute | solution.py:39
  96.8 51.6 %collective-permute-start.22 = (bf16[14,96,384]{2,1,0:T(8,128)(2,1)}, bf16[14,96,384]{2,1,0:T(8,128)(2,1)S(1)}, u32[]{:S(2)}, u32[]{:S(2)}) collective-permute-start(bf16[14,96,384]{2,1,0:T(8,128)(2,1)} %collective-permute-done.18.refs_6_), channel_id=1, source_target_pairs={{1,0},{0,1},{3,2},{2,3},{5,4},{4,5},{7,6},{6,7},{9,8},{8,9},{11,10... | collective-permute-start | bytes 3096584 | tf_op jit(solution)/shard_map/ppermute | solution.py:39
  98.5 49.9 %collective-permute-start.23 = (bf16[14,96,384]{2,1,0:T(8,128)(2,1)}, bf16[14,96,384]{2,1,0:T(8,128)(2,1)S(1)}, u32[]{:S(2)}, u32[]{:S(2)}) collective-permute-start(bf16[14,96,384]{2,1,0:T(8,128)(2,1)} %collective-permute-done.19.refs_7_), channel_id=1, source_target_pairs={{1,0},{0,1},{3,2},{2,3},{5,4},{4,5},{7,6},{6,7},{9,8},{8,9},{11,10... | collective-permute-start | bytes 3096584 | tf_op jit(solution)/shard_map/ppermute | solution.py:39
  110.5 37.9 %collective-permute-start.24 = (bf16[14,96,384]{2,1,0:T(8,128)(2,1)}, bf16[14,96,384]{2,1,0:T(8,128)(2,1)S(1)}, u32[]{:S(2)}, u32[]{:S(2)}) collective-permute-start(bf16[14,96,384]{2,1,0:T(8,128)(2,1)} %collective-permute-done.20.refs_8_), channel_id=1, source_target_pairs={{1,0},{0,1},{3,2},{2,3},{5,4},{4,5},{7,6},{6,7},{9,8},{8,9},{11,10... | collective-permute-start | bytes 3096584 | tf_op jit(solution)/shard_map/ppermute | solution.py:39
  124.6 11.2 %collective-permute-start.15 = (bf16[2,4,32,384]{3,2,1,0:T(8,128)(2,1)S(1)}, bf16[2,4,32,384]{3,2,1,0:T(8,128)(2,1)S(1)}, u32[]{:S(2)}, u32[]{:S(2)}) collective-permute-start(bf16[2,4,32,384]{3,2,1,0:T(8,128)(2,1)S(1)} %constant_dynamic-slice_fusion), channel_id=1, source_target_pairs={{0,8},{1,9},{2,10},{3,11},{4,12},{5,13},{6,14},{7,15},{8,16},{9,17... | collective-permute-start | bytes 589832 | tf_op jit(solution)/shard_map/ppermute | solution.py:39
  135.9 7.8 %collective-permute-start.17 = (bf16[8,1,32,384]{3,2,1,0:T(8,128)(2,1)S(1)}, bf16[8,1,32,384]{3,2,1,0:T(8,128)(2,1)S(1)}, u32[]{:S(2)}, u32[]{:S(2)}) collective-permute-start(bf16[8,1,32,384]{3,2,1,0:T(8,128)(2,1)S(1)} %get-tuple-element.10), channel_id=1, source_target_pairs={{1,0},{2,1},{3,2},{4,3},{5,4},{6,5},{7,6},{9,8},{10,9},{11,10},{12... | collective-permute-start | bytes 589832 | tf_op jit(solution)/shard_map/ppermute | solution.py:39
  143.7 4.5 %collective-permute-start.16 = (bf16[8,1,32,384]{3,2,1,0:T(8,128)(2,1)S(1)}, bf16[8,1,32,384]{3,2,1,0:T(8,128)(2,1)S(1)}, u32[]{:S(2)}, u32[]{:S(2)}) collective-permute-start(bf16[8,1,32,384]{3,2,1,0:T(8,128)(2,1)S(1)} %get-tuple-element.9), channel_id=1, source_target_pairs={{0,1},{1,2},{2,3},{3,4},{4,5},{5,6},{6,7},{8,9},{9,10},{10,11},{11... | collective-permute-start | bytes 589832 | tf_op jit(solution)/shard_map/ppermute | solution.py:39

commit v2 on v0

--- a/solution.py
+++ b/solution.py
@@ -15,12 +15,7 @@
 BUNDLE = 96
 ROUND = (0, 1, -1, 2)
 
-FETCH = np.array(
-    [
-        [[4, 0], [1, 3], [-1, -3], [2, -2]],
-        [[4, 0], [-1, -3], [1, 3], [-2, 2]],
-    ]
-)
+FETCH = np.array([[[4, 0], [1, 3], [-1, -3], [2, -2]], [[0, 4], [2, -2], [1, -3], [3, -1]]])
 
 
 def number(z, y, x, c):
@@ -39,16 +34,24 @@
     return lax.ppermute(array, AXES, pairs)
 
 
+def z_source(which):
+    def source(z, y, x, c):
+        odd = z % 2
+        if c == 0:
+            return (z + int(FETCH[0, x, which]), y + 2 * odd, x, c)
+        return (z - odd + int(FETCH[1, (x + 2 * odd) % NX, which]), y, x, c)
+
+    return source
+
+
 def small_source(step):
     return lambda z, y, x, c: (z, y, x + step, c) if c == 0 else (z, y + step, x, c)
 
 
 def bulk_source(step):
+    if step == 2:
+        return lambda z, y, x, c: (z + 1 if z % 2 != c else z - 1, y, x, c)
     return lambda z, y, x, c: (z, y + step, x, c) if c == 0 else (z, y, x + step, c)
-
-
-def z_source(which):
-    return lambda z, y, x, c: (z + int(FETCH[c, x, which]), y, x, c)
 
 
 def sibling(z, y, x, c):
@@ -61,18 +64,35 @@
     return taps.reshape(HALF * SHARD, C)
 
 
-def pieces_along_z(own):
+def z_stage(own):
     return jnp.stack([fetch(own, z_source(0)), fetch(own, z_source(1))])
 
 
 def small_stage(two):
-    parts = [two] + [fetch(two, small_source(step)) for step in ROUND[1:]]
-    return jnp.stack(parts)
+    return [two] + [fetch(two, small_source(step)) for step in ROUND[1:]]
+
+
+def join_body(*refs):
+    parts, out = refs[:-1], refs[-1]
+    for tap in range(HALF):
+        rows = [
+            part[piece, pl.ds(SHARD * tap, SHARD), :].astype(jnp.float32)
+            for part in parts
+            for piece in range(2)
+        ]
+        out[tap] = jnp.concatenate(rows, 0).astype(jnp.bfloat16)
 
 
 def join_rows(parts):
-    parts = parts.reshape(8, HALF, SHARD, C)
-    return jnp.transpose(parts, (1, 0, 2, 3)).reshape(HALF, BUNDLE, C)
+    vmem = pl.BlockSpec(memory_space=pltpu.VMEM)
+    return pl.pallas_call(
+        join_body,
+        out_shape=jax.ShapeDtypeStruct((HALF, BUNDLE, C), jnp.bfloat16),
+        in_specs=[vmem] * 4,
+        out_specs=vmem,
+        compiler_params=pltpu.CompilerParams(vmem_limit_bytes=16 * 1024 * 1024),
+        cost_estimate=pl.CostEstimate(flops=0, bytes_accessed=2_000_000, transcendentals=0),
+    )(*parts)
 
 
 def bulk_stage(bundle):
@@ -82,23 +102,24 @@
 def channel_orders():
     z, y, x = (lax.axis_index(a) for a in ("z", "y", "x"))
     table = jnp.asarray(FETCH, jnp.int32)
-    step = jnp.array(ROUND, jnp.int32)
-    at_x = (x + step) % NX
-    at_y = (y + step) % NY
-    orders = []
-    for half in range(2):
-        at_z = (z + table[half][at_x]) % NZ
-        group = at_z[None, :, :] * NY + at_y[:, None, None]
-        if half == 1:
-            group = jnp.transpose(group, (1, 0, 2))
-        channel = group.reshape(-1, 1) * SHARD + jnp.arange(SHARD, dtype=jnp.int32)
-        orders.append(channel.reshape(C))
-    return jnp.stack(orders)
+    around = jnp.array(ROUND, jnp.int32)
+    aside = jnp.array((0, 1, -1, 0), jnp.int32)
+    odd = z % 2
+    at_z = z + jnp.array((0, 0, 0, 1), jnp.int32) * jnp.where(odd == 1, 1, -1)
+    piece_z = at_z[:, None, None] + table[0][(x + around) % NX][None, :, :]
+    piece_y = (y + aside + 2 * (at_z % 2))[:, None, None]
+    first = piece_z % NZ * NY + piece_y % NY
+    at_z = z + jnp.array((0, 0, 0, 1), jnp.int32) * jnp.where(odd == 0, 1, -1)
+    piece_z = (at_z - at_z % 2)[:, None] + table[1][(x + aside + 2 * (at_z % 2)) % NX]
+    piece_y = y + around
+    second = piece_z[:, None, :] % NZ * NY + piece_y[None, :, None] % NY
+    ramp = jnp.arange(SHARD, dtype=jnp.int32)
+    return jnp.stack([(half.reshape(-1, 1) * SHARD + ramp).reshape(C) for half in (first, second)])
 
 
 def conv_body(
-    scalars, lag_weights, acts, order, tail, own0, own1, own2, own3, got0, got1, got2, got3,
-    out, spread, weights, total, sems, *, finish,
+    scalars, lag_weights, carried, inner, beside, across, order, tail, own0, own1, own2, own3, got0, got1, got2, got3,
+    out, acts, spread, weights, total, sems, *, finish,
 ):
     frames, rows, cols = 6, 4, 32
     own, got = (own0, own1, own2, own3), (got0, got1, got2, got3)
@@ -122,6 +143,19 @@
     def _():
         for copy in copies(0, got) + copies(1, own):
             copy.start()
+
+    acts[0:2, 1:5] = carried[...]
+    acts[2:8, 1:5] = inner[...]
+
+    @pl.when(core == 0)
+    def _():
+        acts[:, 0:1] = across[...]
+        acts[:, 5:6] = beside[...]
+
+    @pl.when(core == 1)
+    def _():
+        acts[:, 0:1] = beside[...]
+        acts[:, 5:6] = across[...]
 
     wide = acts.shape[0] * acts.shape[1]
     col = lax.broadcasted_iota(jnp.int32, (wide * cols, C), 0) % cols
@@ -198,15 +232,16 @@
         out[f] = jnp.where(f < scalars[1], summed, 0.0).astype(jnp.bfloat16)
 
 
-def conv(scalars, lag_weights, acts, orders, tail, own, got, finish):
+def conv(scalars, lag_weights, extended, orders, tail, own, got, finish):
     smem = pl.BlockSpec(memory_space=pltpu.SMEM)
     vmem = pl.BlockSpec(memory_space=pltpu.VMEM)
     return pl.pallas_call(
         lambda *refs: conv_body(*refs, finish=finish),
         out_shape=jax.ShapeDtypeStruct((6, 128, C), jnp.bfloat16),
-        in_specs=[smem, smem, vmem, vmem, vmem] + [pl.BlockSpec(memory_space=pl.ANY)] * 8,
+        in_specs=[smem, smem] + [vmem] * 6 + [pl.BlockSpec(memory_space=pl.ANY)] * 8,
         out_specs=vmem,
         scratch_shapes=[
+            pltpu.VMEM((8, 6, 32, C), jnp.bfloat16),
             pltpu.VMEM((2, 8, 6, 32, 3 * C), jnp.bfloat16),
             pltpu.VMEM((2, HALF, C, C), jnp.bfloat16),
             pltpu.VMEM((6, 128, C), jnp.float32),
@@ -216,7 +251,7 @@
         cost_estimate=pl.CostEstimate(
             flops=2 * 768 * 27 * C * C, bytes_accessed=12_000_000, transcendentals=768 * C
         ),
-    )(scalars, lag_weights, acts, orders, tail, *own, *got)
+    )(scalars, lag_weights, *extended, orders, tail, *own, *got)
 
 
 def clip_positions(clip_lengths, frame_index):
@@ -237,12 +272,14 @@
     return None if group < 0 else (group // NY, group % NY, x, c)
 
 
-def row_neighbour(by):
-    def source(z, y, x, c):
-        row = x * NC + c + by
-        return (z, y, row // NC, row % NC) if 0 <= row < NX * NC else None
-
-    return source
+def across_chips(z, y, x, c):
+    x = x - 1 if c == 0 else x + 1
+    return (z, y, x, 1 - c) if 0 <= x < NX else None
+
+
+def across_and_before(z, y, x, c):
+    place = across_chips(z, y, x, c)
+    return None if place is None else before_in_group(*place)
 
 
 def per_device(
@@ -255,35 +292,43 @@
     scalars = jnp.stack([lax.axis_index("c").astype(jnp.int32), group_count[0]])
     orders = channel_orders()
 
+    first_core = lax.axis_index("c") == 0
+    last = group_count[0] - 2
+
     def extend(acts):
-        last_two = lax.dynamic_slice_in_dim(acts, group_count[0] - 2, 2, 0)
-        carried = fetch(last_two, before_in_group)
-        acts = jnp.concatenate([carried, acts], 0)
-        above = fetch(acts[:, 3:4], row_neighbour(-1))
-        below = fetch(acts[:, 0:1], row_neighbour(1))
-        return jnp.concatenate([above, acts, below], 1)
-
-    one = pieces_along_z(own_half(kernel_one))
+        outer = jnp.where(first_core, acts[:, 0:1], acts[:, 3:4])
+        carried = fetch(lax.dynamic_slice_in_dim(acts, last, 2, 0), before_in_group)
+        across = fetch(outer, across_chips)
+        across_before = fetch(lax.dynamic_slice_in_dim(outer, last, 2, 0), across_and_before)
+        edge = jnp.concatenate(
+            [
+                jnp.where(first_core, carried[:, 3:4], carried[:, 0:1]),
+                jnp.where(first_core, acts[:, 3:4], acts[:, 0:1]),
+            ],
+            0,
+        )
+        beside = fetch(edge, sibling)
+        return carried, acts, beside, jnp.concatenate([across_before, across], 0)
+
+    one = z_stage(own_half(kernel_one))
+    own_two, one = lax.optimization_barrier((own_half(kernel_two), one))
     one_parts = small_stage(one)
+    two = z_stage(own_two)
+    two, one_parts = lax.optimization_barrier((two, one_parts))
     one_bundles = bulk_stage(join_rows(one_parts))
+    two_bundle = join_rows(small_stage(two))
+    two_bundle, one_bundles = lax.optimization_barrier((two_bundle, one_bundles))
     one_others = [fetch(b, sibling) for b in one_bundles]
-
-    own_two, _ = lax.optimization_barrier((own_half(kernel_two), one))
-    two = pieces_along_z(own_two)
-    two, _ = lax.optimization_barrier((two, one_parts))
-    two_bundle = join_rows(small_stage(two))
-    two_bundle, _ = lax.optimization_barrier((two_bundle, one_bundles))
     two_bundles = bulk_stage(two_bundle)
+
+    acts_two = conv(
+        scalars, lag_weights, extend(norm_act(frames, gain_one)), orders, gain_two.reshape(1, C),
+        one_bundles, one_others, finish_norm,
+    ).reshape(frames.shape)
+    two_bundles, acts_two = lax.optimization_barrier((two_bundles, acts_two))
     two_others = [fetch(b, sibling) for b in two_bundles]
-
-    acts_one = extend(norm_act(frames, gain_one))
-    acts_two = conv(
-        scalars, lag_weights, acts_one, orders, gain_two.reshape(1, C),
-        one_bundles, one_others, finish_norm,
-    )
-    acts_two = extend(acts_two.reshape(frames.shape))
     result = conv(
-        scalars, lag_weights, acts_two, orders, frames.reshape(slots, 128, C),
+        scalars, lag_weights, extend(acts_two), orders, frames.reshape(slots, 128, C),
         two_bundles, two_others, finish_add,
     )
     return result.reshape(frames.shape)

time: 173 us -> 148 us (0.86)
  the two profiles are of different devices: /device:TPU:36 before, /device:TPU:131 now
where the time goes in v2:
time: 148 us; the launch traced here: 146 us
  starting transfers between devices  60.6 us (41%)
  waiting for transfers between devices  40.9 us (28%)
  Pallas kernels  30.1 us (20%)
  local copies, waits for them, and re-layouts  6.82 us (5%)
  other arithmetic  5.59 us (4%)
  between operations  2 us (1%)
    ppermute x32, starting transfers between devices, fetch(): return lax.ppermute(array, AXES, pairs)  60.6 us
    ppermute x32, waiting for transfers between devices, fetch(): return lax.ppermute(array, AXES, pairs)  40.9 us
    pallas_call x2, Pallas kernels, conv(): pl.pallas_call(lambda *refs: conv_body(*refs, finish=finish), out_shape=j...  28.8 us
  transfers between devices with their start and end apart: 32, of which 12 were waited for; matrix products, arithmetic and copies ran while one was open for 6% of the time, Pallas kernels for 10%

profile of v2, /device:TPU:131, one launch (start us, length us, event | category | flops | bytes accessed | tf_op | source)
XLA Modules:
  0.0 146.0 jit_solution(13447587015047830027)
XLA Ops:
  0.0 1.2 copy-done
  1.3 3.1 %collective-permute-start.1 = (bf16[168,384]{1,0:T(8,128)(2,1)S(1)}, bf16[168,384]{1,0:T(8,128)(2,1)S(1)}, u32[]{:S(2)}, u32[]{:S(2)}) collective-permute-start(bf16[168,384]{1,0:T(8,128)(2,1)S(1)} %reshape.248), channel_id=1, source_target_pairs={{0,0},{129,1},{98,2},{195,3},{164,4},{165,5},{198,6},{231,7},{8,8}... | collective-permute-start | bytes 387080 | tf_op jit(solution)/shard_map/ppermute | solution.py:34
  4.4 4.3 %collective-permute-start = (bf16[168,384]{1,0:T(8,128)(2,1)S(1)}, bf16[168,384]{1,0:T(8,128)(2,1)S(1)}, u32[]{:S(2)}, u32[]{:S(2)}) collective-permute-start(bf16[168,384]{1,0:T(8,128)(2,1)S(1)} %reshape.248), channel_id=1, source_target_pairs={{128,0},{1,1},{34,2},{67,3},{228,4},{37,5},{70,6},{103,7},{136,8},... | collective-permute-start | bytes 387080 | tf_op jit(solution)/shard_map/ppermute | solution.py:34
  11.6 2.5 %collective-permute-done = bf16[168,384]{1,0:T(8,128)(2,1)S(1)} collective-permute-done((bf16[168,384]{1,0:T(8,128)(2,1)S(1)}, bf16[168,384]{1,0:T(8,128)(2,1)S(1)}, u32[]{:S(2)}, u32[]{:S(2)}) %collective-permute-start) | collective-permute-done | bytes 129056 | tf_op jit(solution)/shard_map/ppermute | solution.py:34
  14.1 3.6 %collective-permute-start.3 = (bf16[168,384]{1,0:T(8,128)(2,1)S(1)}, bf16[168,384]{1,0:T(8,128)(2,1)S(1)}, u32[]{:S(2)}, u32[]{:S(2)}) collective-permute-start(bf16[168,384]{1,0:T(8,128)(2,1)S(1)} %reshape.246), channel_id=1, source_target_pairs={{0,0},{129,1},{98,2},{195,3},{164,4},{165,5},{198,6},{231,7},{8,8}... | collective-permute-start | bytes 387080 | tf_op jit(solution)/shard_map/ppermute | solution.py:34
  17.8 4.6 %collective-permute-start.2 = (bf16[168,384]{1,0:T(8,128)(2,1)S(1)}, bf16[168,384]{1,0:T(8,128)(2,1)S(1)}, u32[]{:S(2)}, u32[]{:S(2)}) collective-permute-start(bf16[168,384]{1,0:T(8,128)(2,1)S(1)} %reshape.246), channel_id=1, source_target_pairs={{128,0},{1,1},{34,2},{67,3},{228,4},{37,5},{70,6},{103,7},{136,8},... | collective-permute-start | bytes 387080 | tf_op jit(solution)/shard_map/ppermute | solution.py:34
  22.4 2.7 %collective-permute-start.6 = (bf16[2,168,384]{2,1,0:T(8,128)(2,1)S(1)}, bf16[2,168,384]{2,1,0:T(8,128)(2,1)S(1)}, u32[]{:S(2)}, u32[]{:S(2)}) collective-permute-start(bf16[2,168,384]{2,1,0:T(8,128)(2,1)S(1)} %pad_maximum_fusion.refs_0_), channel_id=1, source_target_pairs={{4,0},{17,1},{6,2},{19,3},{0,4},{21,5},{2,6},{23,7},{12,8},{25,9},... | collective-permute-start | bytes 774152 | tf_op jit(solution)/shard_map/ppermute | solution.py:34
  25.5 2.2 %collective-permute-start.4 = (bf16[2,168,384]{2,1,0:T(8,128)(2,1)S(1)}, bf16[2,168,384]{2,1,0:T(8,128)(2,1)S(1)}, u32[]{:S(2)}, u32[]{:S(2)}) collective-permute-start(bf16[2,168,384]{2,1,0:T(8,128)(2,1)S(1)} %pad_maximum_fusion.refs_0_), channel_id=1, source_target_pairs={{2,0},{9,1},{4,2},{11,3},{6,4},{13,5},{0,6},{15,7},{10,8},{17,9},{... | collective-permute-start | bytes 774152 | tf_op jit(solution)/shard_map/ppermute | solution.py:34
  27.8 1.4 collective-permute-done.6.refs_3_
  29.3 2.8 %collective-permute-done.5.refs_2_ = bf16[2,168,384]{2,1,0:T(8,128)(2,1)S(1)} collective-permute-done((bf16[2,168,384]{2,1,0:T(8,128)(2,1)S(1)}, bf16[2,168,384]{2,1,0:T(8,128)(2,1)S(1)}, u32[]{:S(2)}, u32[]{:S(2)}) %collective-permute-start.5) | collective-permute-done | bytes 258080 | tf_op jit(solution)/shard_map/ppermute | solution.py:34
  33.4 4.4 %collective-permute-start.12 = (bf16[14,96,384]{2,1,0:T(8,128)(2,1)}, bf16[14,96,384]{2,1,0:T(8,128)(2,1)}, u32[]{:S(2)}, u32[]{:S(2)}) collective-permute-start(bf16[14,96,384]{2,1,0:T(8,128)(2,1)} %shard_map.128.refs_8_), channel_id=1, source_target_pairs={{224,0},{33,1},{226,2},{35,3},{228,4},{37,5},{230,6},{39,7},{232,8... | collective-permute-start | bytes 3096584 | tf_op jit(solution)/shard_map/ppermute | solution.py:34
  40.5 1.9 %collective-permute-start.9 = (bf16[2,168,384]{2,1,0:T(8,128)(2,1)S(1)}, bf16[2,168,384]{2,1,0:T(8,128)(2,1)S(1)}, u32[]{:S(2)}, u32[]{:S(2)}) collective-permute-start(bf16[2,168,384]{2,1,0:T(8,128)(2,1)S(1)} %pad_maximum_fusion.1.refs_0_), channel_id=1, source_target_pairs={{4,0},{17,1},{6,2},{19,3},{0,4},{21,5},{2,6},{23,7},{12,8},{25,9},... | collective-permute-start | bytes 774152 | tf_op jit(solution)/shard_map/ppermute | solution.py:34
  44.0 3.4 %collective-permute-done.9.refs_3_ = bf16[2,168,384]{2,1,0:T(8,128)(2,1)S(1)} collective-permute-done((bf16[2,168,384]{2,1,0:T(8,128)(2,1)S(1)}, bf16[2,168,384]{2,1,0:T(8,128)(2,1)S(1)}, u32[]{:S(2)}, u32[]{:S(2)}) %collective-permute-start.9) | collective-permute-done | bytes 258080 | tf_op jit(solution)/shard_map/ppermute | solution.py:34
  47.4 1.4 collective-permute-start.7
  48.8 1.4 constant_dynamic-slice_fusion.2
  50.6 2.8 %collective-permute-done.8.refs_2_ = bf16[2,168,384]{2,1,0:T(8,128)(2,1)S(1)} collective-permute-done((bf16[2,168,384]{2,1,0:T(8,128)(2,1)S(1)}, bf16[2,168,384]{2,1,0:T(8,128)(2,1)S(1)}, u32[]{:S(2)}, u32[]{:S(2)}) %collective-permute-start.8) | collective-permute-done | bytes 258080 | tf_op jit(solution)/shard_map/ppermute | solution.py:34
  53.4 8.6 %collective-permute-start.19 = (bf16[6,1,32,384]{3,2,1,0:T(8,128)(2,1)}, bf16[6,1,32,384]{3,2,1,0:T(8,128)(2,1)}, u32[]{:S(2)}, u32[]{:S(2)}) collective-permute-start(bf16[6,1,32,384]{3,2,1,0:T(8,128)(2,1)} %get-tuple-element.45), channel_id=1, source_target_pairs={{2,1},{1,2},{4,3},{3,4},{6,5},{5,6},{10,9},{9,10},{12,11},{11,12},... | collective-permute-start | bytes 442376 | tf_op jit(solution)/shard_map/ppermute | solution.py:34
  62.7 1.9 %collective-permute-start.16 = (bf16[2,4,32,384]{3,2,1,0:T(8,128)(2,1)}, bf16[2,4,32,384]{3,2,1,0:T(8,128)(2,1)S(1)}, u32[]{:S(2)}, u32[]{:S(2)}) collective-permute-start(bf16[2,4,32,384]{3,2,1,0:T(8,128)(2,1)} %constant_dynamic-slice_fusion.3), channel_id=1, source_target_pairs={{0,8},{1,9},{2,10},{3,11},{4,12},{5,13},{6,14},{7,15},{8,16},{9,17... | collective-permute-start | bytes 589832 | tf_op jit(solution)/shard_map/ppermute | solution.py:34
  65.8 4.1 %collective-permute-start.18 = (bf16[2,1,32,384]{3,2,1,0:T(8,128)(2,1)}, bf16[2,1,32,384]{3,2,1,0:T(8,128)(2,1)S(1)}, u32[]{:S(2)}, u32[]{:S(2)}) collective-permute-start(bf16[2,1,32,384]{3,2,1,0:T(8,128)(2,1)} %constant_dynamic-slice_fusion.2), channel_id=1, source_target_pairs={{2,9},{1,10},{4,11},{3,12},{6,13},{5,14},{10,17},{9,18},{12,19},{1... | collective-permute-start | bytes 147464 | tf_op jit(solution)/shard_map/ppermute | solution.py:34
  71.6 4.4 %collective-permute-done.18 = bf16[2,1,32,384]{3,2,1,0:T(8,128)(2,1)S(1)} collective-permute-done((bf16[2,1,32,384]{3,2,1,0:T(8,128)(2,1)}, bf16[2,1,32,384]{3,2,1,0:T(8,128)(2,1)S(1)}, u32[]{:S(2)}, u32[]{:S(2)}) %collective-permute-start.18) | collective-permute-done | bytes 49184 | tf_op jit(solution)/shard_map/ppermute | solution.py:34
  78.6 2.4 %collective-permute-done.17.refs_4_ = bf16[8,1,32,384]{3,2,1,0:T(8,128)(2,1)S(1)} collective-permute-done((bf16[8,1,32,384]{3,2,1,0:T(8,128)(2,1)S(1)}, bf16[8,1,32,384]{3,2,1,0:T(8,128)(2,1)S(1)}, u32[]{:S(2)}, u32[]{:S(2)}) %collective-permute-start.17) | collective-permute-done | bytes 196640 | tf_op jit(solution)/shard_map/ppermute | solution.py:34
  81.0 2.1 %collective-permute-start.14 = (bf16[14,96,384]{2,1,0:T(8,128)(2,1)S(1)}, bf16[14,96,384]{2,1,0:T(8,128)(2,1)}, u32[]{:S(2)}, u32[]{:S(2)}) collective-permute-start(bf16[14,96,384]{2,1,0:T(8,128)(2,1)S(1)} %shard_map.127.refs_8_), channel_id=1, source_target_pairs={{24,0},{7,1},{26,2},{1,3},{28,4},{3,5},{30,6},{5,7},{0,8},{15,9},{... | collective-permute-start | bytes 3096584 | tf_op jit(solution)/shard_map/ppermute | solution.py:34
  84.4 13.9 %shard_map.129 = bf16[6,128,384]{2,1,0:T(8,128)(2,1)S(1)} custom-call(s32[2]{0:T(128)S(1)} %pad_add_fusion.1.refs_0_, f32[3,6]{1,0:T(4,128)S(1)} %add_convert_fusion.refs_1_, bf16[2,4,32,384]{3,2,1,0:T(8,128)(2,1)S(1)} %collective-permute-done.16.refs_2_, bf16[6,4,32,384]{3,2,1,0:T(8,128)(2,1)S(1)} %fusion.7.refs_3_, ...), custom_call_target="tpu_custom_call" | custom-call | flops 6115295232 | bytes 12000000 | tf_op jit(solution)/shard_map/pallas_call | solution.py:238
  98.4 1.6 %collective-permute-start.28 = (bf16[14,96,384]{2,1,0:T(8,128)(2,1)S(1)}, bf16[14,96,384]{2,1,0:T(8,128)(2,1)S(1)}, u32[]{:S(2)}, u32[]{:S(2)}) collective-permute-start(bf16[14,96,384]{2,1,0:T(8,128)(2,1)S(1)} %shard_map.127.refs_8_), channel_id=1, source_target_pairs={{1,0},{0,1},{3,2},{2,3},{5,4},{4,5},{7,6},{6,7},{9,8},{8,9},{11,10... | collective-permute-start | bytes 3096584 | tf_op jit(solution)/shard_map/ppermute | solution.py:34
  100.6 2.4 %collective-permute-start.26 = (bf16[2,1,32,384]{3,2,1,0:T(8,128)(2,1)S(1)}, bf16[2,1,32,384]{3,2,1,0:T(8,128)(2,1)S(1)}, u32[]{:S(2)}, u32[]{:S(2)}) collective-permute-start(bf16[2,1,32,384]{3,2,1,0:T(8,128)(2,1)S(1)} %constant_dynamic-slice_fusion), channel_id=1, source_target_pairs={{2,9},{1,10},{4,11},{3,12},{6,13},{5,14},{10,17},{9,18},{12,19},{1... | collective-permute-start | bytes 147464 | tf_op jit(solution)/shard_map/ppermute | solution.py:34
  103.0 7.4 %collective-permute-done.26 = bf16[2,1,32,384]{3,2,1,0:T(8,128)(2,1)S(1)} collective-permute-done((bf16[2,1,32,384]{3,2,1,0:T(8,128)(2,1)S(1)}, bf16[2,1,32,384]{3,2,1,0:T(8,128)(2,1)S(1)}, u32[]{:S(2)}, u32[]{:S(2)}) %collective-permute-start.26) | collective-permute-done | bytes 49184 | tf_op jit(solution)/shard_map/ppermute | solution.py:34
  110.5 1.9 %collective-permute-start.24 = (bf16[2,4,32,384]{3,2,1,0:T(8,128)(2,1)S(1)}, bf16[2,4,32,384]{3,2,1,0:T(8,128)(2,1)S(1)}, u32[]{:S(2)}, u32[]{:S(2)}) collective-permute-start(bf16[2,4,32,384]{3,2,1,0:T(8,128)(2,1)S(1)} %constant_dynamic-slice_fusion.1), channel_id=1, source_target_pairs={{0,8},{1,9},{2,10},{3,11},{4,12},{5,13},{6,14},{7,15},{8,16},{9,17... | collective-permute-start | bytes 589832 | tf_op jit(solution)/shard_map/ppermute | solution.py:34
  112.4 9.4 %collective-permute-done.24.refs_2_ = bf16[2,4,32,384]{3,2,1,0:T(8,128)(2,1)S(1)} collective-permute-done((bf16[2,4,32,384]{3,2,1,0:T(8,128)(2,1)S(1)}, bf16[2,4,32,384]{3,2,1,0:T(8,128)(2,1)S(1)}, u32[]{:S(2)}, u32[]{:S(2)}) %collective-permute-start.24) | collective-permute-done | bytes 196640 | tf_op jit(solution)/shard_map/ppermute | solution.py:34
  121.8 4.9 %collective-permute-start.27 = (bf16[6,1,32,384]{3,2,1,0:T(8,128)(2,1)S(1)}, bf16[6,1,32,384]{3,2,1,0:T(8,128)(2,1)S(1)}, u32[]{:S(2)}, u32[]{:S(2)}) collective-permute-start(bf16[6,1,32,384]{3,2,1,0:T(8,128)(2,1)S(1)} %get-tuple-element.43), channel_id=1, source_target_pairs={{2,1},{1,2},{4,3},{3,4},{6,5},{5,6},{10,9},{9,10},{12,11},{11,12},... | collective-permute-start | bytes 442376 | tf_op jit(solution)/shard_map/ppermute | solution.py:34
  126.7 2.8 %collective-permute-done.27 = bf16[6,1,32,384]{3,2,1,0:T(8,128)(2,1)S(1)} collective-permute-done((bf16[6,1,32,384]{3,2,1,0:T(8,128)(2,1)S(1)}, bf16[6,1,32,384]{3,2,1,0:T(8,128)(2,1)S(1)}, u32[]{:S(2)}, u32[]{:S(2)}) %collective-permute-start.27) | collective-permute-done | bytes 147488 | tf_op jit(solution)/shard_map/ppermute | solution.py:34
  129.5 1.4 collective-permute-done.25.refs_4_
  130.9 14.9 %shard_map.130 = bf16[6,128,384]{2,1,0:T(8,128)(2,1)} custom-call(s32[2]{0:T(128)S(1)} %pad_add_fusion.1.refs_0_, f32[3,6]{1,0:T(4,128)S(1)} %add_convert_fusion.refs_1_, bf16[2,4,32,384]{3,2,1,0:T(8,128)(2,1)S(1)} %collective-permute-done.24.refs_2_, bf16[6,4,32,384]{3,2,1,0:T(8,128)(2,1)S(1)} %bitcast.29, ...), custom_call_target="tpu_custom_call" | custom-call | flops 6115295232 | bytes 12000000 | tf_op jit(solution)/shard_map/pallas_call | solution.py:238
  (103 shorter events, 16.2 us)
Async XLA Ops:
  1.3 10.3 %collective-permute-start.1 = (bf16[168,384]{1,0:T(8,128)(2,1)S(1)}, bf16[168,384]{1,0:T(8,128)(2,1)S(1)}, u32[]{:S(2)}, u32[]{:S(2)}) collective-permute-start(bf16[168,384]{1,0:T(8,128)(2,1)S(1)} %reshape.248), channel_id=1, source_target_pairs={{0,0},{129,1},{98,2},{195,3},{164,4},{165,5},{198,6},{231,7},{8,8}... | collective-permute-start | bytes 387080 | tf_op jit(solution)/shard_map/ppermute | solution.py:34
  4.4 9.6 %collective-permute-start = (bf16[168,384]{1,0:T(8,128)(2,1)S(1)}, bf16[168,384]{1,0:T(8,128)(2,1)S(1)}, u32[]{:S(2)}, u32[]{:S(2)}) collective-permute-start(bf16[168,384]{1,0:T(8,128)(2,1)S(1)} %reshape.248), channel_id=1, source_target_pairs={{128,0},{1,1},{34,2},{67,3},{228,4},{37,5},{70,6},{103,7},{136,8},... | collective-permute-start | bytes 387080 | tf_op jit(solution)/shard_map/ppermute | solution.py:34
  14.1 13.7 %collective-permute-start.3 = (bf16[168,384]{1,0:T(8,128)(2,1)S(1)}, bf16[168,384]{1,0:T(8,128)(2,1)S(1)}, u32[]{:S(2)}, u32[]{:S(2)}) collective-permute-start(bf16[168,384]{1,0:T(8,128)(2,1)S(1)} %reshape.246), channel_id=1, source_target_pairs={{0,0},{129,1},{98,2},{195,3},{164,4},{165,5},{198,6},{231,7},{8,8}... | collective-permute-start | bytes 387080 | tf_op jit(solution)/shard_map/ppermute | solution.py:34
  17.8 10.0 %collective-permute-start.2 = (bf16[168,384]{1,0:T(8,128)(2,1)S(1)}, bf16[168,384]{1,0:T(8,128)(2,1)S(1)}, u32[]{:S(2)}, u32[]{:S(2)}) collective-permute-start(bf16[168,384]{1,0:T(8,128)(2,1)S(1)} %reshape.246), channel_id=1, source_target_pairs={{128,0},{1,1},{34,2},{67,3},{228,4},{37,5},{70,6},{103,7},{136,8},... | collective-permute-start | bytes 387080 | tf_op jit(solution)/shard_map/ppermute | solution.py:34
  22.4 6.9 %collective-permute-start.6 = (bf16[2,168,384]{2,1,0:T(8,128)(2,1)S(1)}, bf16[2,168,384]{2,1,0:T(8,128)(2,1)S(1)}, u32[]{:S(2)}, u32[]{:S(2)}) collective-permute-start(bf16[2,168,384]{2,1,0:T(8,128)(2,1)S(1)} %pad_maximum_fusion.refs_0_), channel_id=1, source_target_pairs={{4,0},{17,1},{6,2},{19,3},{0,4},{21,5},{2,6},{23,7},{12,8},{25,9},... | collective-permute-start | bytes 774152 | tf_op jit(solution)/shard_map/ppermute | solution.py:34
  25.0 7.0 %collective-permute-start.5 = (bf16[2,168,384]{2,1,0:T(8,128)(2,1)S(1)}, bf16[2,168,384]{2,1,0:T(8,128)(2,1)S(1)}, u32[]{:S(2)}, u32[]{:S(2)}) collective-permute-start(bf16[2,168,384]{2,1,0:T(8,128)(2,1)S(1)} %pad_maximum_fusion.refs_0_), channel_id=1, source_target_pairs={{6,0},{25,1},{0,2},{27,3},{2,4},{29,5},{4,6},{31,7},{14,8},{1,9},{... | collective-permute-start | bytes 774152 | tf_op jit(solution)/shard_map/ppermute | solution.py:34
  25.5 6.8 %collective-permute-start.4 = (bf16[2,168,384]{2,1,0:T(8,128)(2,1)S(1)}, bf16[2,168,384]{2,1,0:T(8,128)(2,1)S(1)}, u32[]{:S(2)}, u32[]{:S(2)}) collective-permute-start(bf16[2,168,384]{2,1,0:T(8,128)(2,1)S(1)} %pad_maximum_fusion.refs_0_), channel_id=1, source_target_pairs={{2,0},{9,1},{4,2},{11,3},{6,4},{13,5},{0,6},{15,7},{10,8},{17,9},{... | collective-permute-start | bytes 774152 | tf_op jit(solution)/shard_map/ppermute | solution.py:34
  33.4 32.4 %collective-permute-start.12 = (bf16[14,96,384]{2,1,0:T(8,128)(2,1)}, bf16[14,96,384]{2,1,0:T(8,128)(2,1)}, u32[]{:S(2)}, u32[]{:S(2)}) collective-permute-start(bf16[14,96,384]{2,1,0:T(8,128)(2,1)} %shard_map.128.refs_8_), channel_id=1, source_target_pairs={{224,0},{33,1},{226,2},{35,3},{228,4},{37,5},{230,6},{39,7},{232,8... | collective-permute-start | bytes 3096584 | tf_op jit(solution)/shard_map/ppermute | solution.py:34
  37.8 32.1 %collective-permute-start.11 = (bf16[14,96,384]{2,1,0:T(8,128)(2,1)}, bf16[14,96,384]{2,1,0:T(8,128)(2,1)}, u32[]{:S(2)}, u32[]{:S(2)}) collective-permute-start(bf16[14,96,384]{2,1,0:T(8,128)(2,1)} %shard_map.128.refs_8_), channel_id=1, source_target_pairs={{24,0},{7,1},{26,2},{1,3},{28,4},{3,5},{30,6},{5,7},{0,8},{15,9},{... | collective-permute-start | bytes 3096584 | tf_op jit(solution)/shard_map/ppermute | solution.py:34
  38.7 31.2 %collective-permute-start.10 = (bf16[14,96,384]{2,1,0:T(8,128)(2,1)}, bf16[14,96,384]{2,1,0:T(8,128)(2,1)}, u32[]{:S(2)}, u32[]{:S(2)}) collective-permute-start(bf16[14,96,384]{2,1,0:T(8,128)(2,1)} %shard_map.128.refs_8_), channel_id=1, source_target_pairs={{8,0},{3,1},{10,2},{5,3},{12,4},{7,5},{14,6},{1,7},{16,8},{11,9},{... | collective-permute-start | bytes 3096584 | tf_op jit(solution)/shard_map/ppermute | solution.py:34
  40.5 6.9 %collective-permute-start.9 = (bf16[2,168,384]{2,1,0:T(8,128)(2,1)S(1)}, bf16[2,168,384]{2,1,0:T(8,128)(2,1)S(1)}, u32[]{:S(2)}, u32[]{:S(2)}) collective-permute-start(bf16[2,168,384]{2,1,0:T(8,128)(2,1)S(1)} %pad_maximum_fusion.1.refs_0_), channel_id=1, source_target_pairs={{4,0},{17,1},{6,2},{19,3},{0,4},{21,5},{2,6},{23,7},{12,8},{25,9},... | collective-permute-start | bytes 774152 | tf_op jit(solution)/shard_map/ppermute | solution.py:34
  43.9 9.6 %collective-permute-start.8 = (bf16[2,168,384]{2,1,0:T(8,128)(2,1)S(1)}, bf16[2,168,384]{2,1,0:T(8,128)(2,1)S(1)}, u32[]{:S(2)}, u32[]{:S(2)}) collective-permute-start(bf16[2,168,384]{2,1,0:T(8,128)(2,1)S(1)} %pad_maximum_fusion.1.refs_0_), channel_id=1, source_target_pairs={{6,0},{25,1},{0,2},{27,3},{2,4},{29,5},{4,6},{31,7},{14,8},{1,9},{... | collective-permute-start | bytes 774152 | tf_op jit(solution)/shard_map/ppermute | solution.py:34
  47.4 14.6 %collective-permute-start.7 = (bf16[2,168,384]{2,1,0:T(8,128)(2,1)S(1)}, bf16[2,168,384]{2,1,0:T(8,128)(2,1)S(1)}, u32[]{:S(2)}, u32[]{:S(2)}) collective-permute-start(bf16[2,168,384]{2,1,0:T(8,128)(2,1)S(1)} %pad_maximum_fusion.1.refs_0_), channel_id=1, source_target_pairs={{2,0},{9,1},{4,2},{11,3},{6,4},{13,5},{0,6},{15,7},{10,8},{17,9},{... | collective-permute-start | bytes 774152 | tf_op jit(solution)/shard_map/ppermute | solution.py:34
  53.4 24.5 %collective-permute-start.19 = (bf16[6,1,32,384]{3,2,1,0:T(8,128)(2,1)}, bf16[6,1,32,384]{3,2,1,0:T(8,128)(2,1)}, u32[]{:S(2)}, u32[]{:S(2)}) collective-permute-start(bf16[6,1,32,384]{3,2,1,0:T(8,128)(2,1)} %get-tuple-element.45), channel_id=1, source_target_pairs={{2,1},{1,2},{4,3},{3,4},{6,5},{5,6},{10,9},{9,10},{12,11},{11,12},... | collective-permute-start | bytes 442376 | tf_op jit(solution)/shard_map/ppermute | solution.py:34
  62.7 14.3 %collective-permute-start.16 = (bf16[2,4,32,384]{3,2,1,0:T(8,128)(2,1)}, bf16[2,4,32,384]{3,2,1,0:T(8,128)(2,1)S(1)}, u32[]{:S(2)}, u32[]{:S(2)}) collective-permute-start(bf16[2,4,32,384]{3,2,1,0:T(8,128)(2,1)} %constant_dynamic-slice_fusion.3), channel_id=1, source_target_pairs={{0,8},{1,9},{2,10},{3,11},{4,12},{5,13},{6,14},{7,15},{8,16},{9,17... | collective-permute-start | bytes 589832 | tf_op jit(solution)/shard_map/ppermute | solution.py:34
  65.8 10.2 %collective-permute-start.18 = (bf16[2,1,32,384]{3,2,1,0:T(8,128)(2,1)}, bf16[2,1,32,384]{3,2,1,0:T(8,128)(2,1)S(1)}, u32[]{:S(2)}, u32[]{:S(2)}) collective-permute-start(bf16[2,1,32,384]{3,2,1,0:T(8,128)(2,1)} %constant_dynamic-slice_fusion.2), channel_id=1, source_target_pairs={{2,9},{1,10},{4,11},{3,12},{6,13},{5,14},{10,17},{9,18},{12,19},{1... | collective-permute-start | bytes 147464 | tf_op jit(solution)/shard_map/ppermute | solution.py:34
  69.9 11.1 %collective-permute-start.20 = (bf16[14,96,384]{2,1,0:T(8,128)(2,1)}, bf16[14,96,384]{2,1,0:T(8,128)(2,1)}, u32[]{:S(2)}, u32[]{:S(2)}) collective-permute-start(bf16[14,96,384]{2,1,0:T(8,128)(2,1)} %shard_map.128.refs_8_), channel_id=1, source_target_pairs={{1,0},{0,1},{3,2},{2,3},{5,4},{4,5},{7,6},{6,7},{9,8},{8,9},{11,10... | collective-permute-start | bytes 3096584 | tf_op jit(solution)/shard_map/ppermute | solution.py:34
  70.0 13.1 %collective-permute-start.21 = (bf16[14,96,384]{2,1,0:T(8,128)(2,1)}, bf16[14,96,384]{2,1,0:T(8,128)(2,1)}, u32[]{:S(2)}, u32[]{:S(2)}) collective-permute-start(bf16[14,96,384]{2,1,0:T(8,128)(2,1)} %collective-permute-done.10.refs_9_), channel_id=1, source_target_pairs={{1,0},{0,1},{3,2},{2,3},{5,4},{4,5},{7,6},{6,7},{9,8},{8,9},{11,10... | collective-permute-start | bytes 3096584 | tf_op jit(solution)/shard_map/ppermute | solution.py:34
  76.1 8.4 %collective-permute-start.22 = (bf16[14,96,384]{2,1,0:T(8,128)(2,1)}, bf16[14,96,384]{2,1,0:T(8,128)(2,1)}, u32[]{:S(2)}, u32[]{:S(2)}) collective-permute-start(bf16[14,96,384]{2,1,0:T(8,128)(2,1)} %collective-permute-done.11.refs_10_), channel_id=1, source_target_pairs={{1,0},{0,1},{3,2},{2,3},{5,4},{4,5},{7,6},{6,7},{9,8},{8,9},{11,10... | collective-permute-start | bytes 3096584 | tf_op jit(solution)/shard_map/ppermute | solution.py:34
  77.0 7.4 %collective-permute-start.23 = (bf16[14,96,384]{2,1,0:T(8,128)(2,1)}, bf16[14,96,384]{2,1,0:T(8,128)(2,1)}, u32[]{:S(2)}, u32[]{:S(2)}) collective-permute-start(bf16[14,96,384]{2,1,0:T(8,128)(2,1)} %collective-permute-done.12.refs_11_), channel_id=1, source_target_pairs={{1,0},{0,1},{3,2},{2,3},{5,4},{4,5},{7,6},{6,7},{9,8},{8,9},{11,10... | collective-permute-start | bytes 3096584 | tf_op jit(solution)/shard_map/ppermute | solution.py:34
  78.0 3.0 %collective-permute-start.17 = (bf16[8,1,32,384]{3,2,1,0:T(8,128)(2,1)S(1)}, bf16[8,1,32,384]{3,2,1,0:T(8,128)(2,1)S(1)}, u32[]{:S(2)}, u32[]{:S(2)}) collective-permute-start(bf16[8,1,32,384]{3,2,1,0:T(8,128)(2,1)S(1)} %pad_maximum_fusion.2), channel_id=1, source_target_pairs={{1,0},{0,1},{3,2},{2,3},{5,4},{4,5},{7,6},{6,7},{9,8},{8,9},{11,10... | collective-permute-start | bytes 589832 | tf_op jit(solution)/shard_map/ppermute | solution.py:34
  81.0 17.3 %collective-permute-start.15 = (bf16[14,96,384]{2,1,0:T(8,128)(2,1)S(1)}, bf16[14,96,384]{2,1,0:T(8,128)(2,1)}, u32[]{:S(2)}, u32[]{:S(2)}) collective-permute-start(bf16[14,96,384]{2,1,0:T(8,128)(2,1)S(1)} %shard_map.127.refs_8_), channel_id=1, source_target_pairs={{224,0},{33,1},{226,2},{35,3},{228,4},{37,5},{230,6},{39,7},{232,8... | collective-permute-start | bytes 3096584 | tf_op jit(solution)/shard_map/ppermute | solution.py:34
  81.0 17.3 %collective-permute-start.14 = (bf16[14,96,384]{2,1,0:T(8,128)(2,1)S(1)}, bf16[14,96,384]{2,1,0:T(8,128)(2,1)}, u32[]{:S(2)}, u32[]{:S(2)}) collective-permute-start(bf16[14,96,384]{2,1,0:T(8,128)(2,1)S(1)} %shard_map.127.refs_8_), channel_id=1, source_target_pairs={{24,0},{7,1},{26,2},{1,3},{28,4},{3,5},{30,6},{5,7},{0,8},{15,9},{... | collective-permute-start | bytes 3096584 | tf_op jit(solution)/shard_map/ppermute | solution.py:34
  83.1 15.2 %collective-permute-start.13 = (bf16[14,96,384]{2,1,0:T(8,128)(2,1)S(1)}, bf16[14,96,384]{2,1,0:T(8,128)(2,1)}, u32[]{:S(2)}, u32[]{:S(2)}) collective-permute-start(bf16[14,96,384]{2,1,0:T(8,128)(2,1)S(1)} %shard_map.127.refs_8_), channel_id=1, source_target_pairs={{8,0},{3,1},{10,2},{5,3},{12,4},{7,5},{14,6},{1,7},{16,8},{11,9},{... | collective-permute-start | bytes 3096584 | tf_op jit(solution)/shard_map/ppermute | solution.py:34
  98.4 32.5 %collective-permute-start.28 = (bf16[14,96,384]{2,1,0:T(8,128)(2,1)S(1)}, bf16[14,96,384]{2,1,0:T(8,128)(2,1)S(1)}, u32[]{:S(2)}, u32[]{:S(2)}) collective-permute-start(bf16[14,96,384]{2,1,0:T(8,128)(2,1)S(1)} %shard_map.127.refs_8_), channel_id=1, source_target_pairs={{1,0},{0,1},{3,2},{2,3},{5,4},{4,5},{7,6},{6,7},{9,8},{8,9},{11,10... | collective-permute-start | bytes 3096584 | tf_op jit(solution)/shard_map/ppermute | solution.py:34
  99.9 31.0 %collective-permute-start.29 = (bf16[14,96,384]{2,1,0:T(8,128)(2,1)}, bf16[14,96,384]{2,1,0:T(8,128)(2,1)S(1)}, u32[]{:S(2)}, u32[]{:S(2)}) collective-permute-start(bf16[14,96,384]{2,1,0:T(8,128)(2,1)} %collective-permute-done.13.refs_9_), channel_id=1, source_target_pairs={{1,0},{0,1},{3,2},{2,3},{5,4},{4,5},{7,6},{6,7},{9,8},{8,9},{11,10... | collective-permute-start | bytes 3096584 | tf_op jit(solution)/shard_map/ppermute | solution.py:34
  100.0 30.9 %collective-permute-start.30 = (bf16[14,96,384]{2,1,0:T(8,128)(2,1)}, bf16[14,96,384]{2,1,0:T(8,128)(2,1)S(1)}, u32[]{:S(2)}, u32[]{:S(2)}) collective-permute-start(bf16[14,96,384]{2,1,0:T(8,128)(2,1)} %collective-permute-done.14.refs_10_), channel_id=1, source_target_pairs={{1,0},{0,1},{3,2},{2,3},{5,4},{4,5},{7,6},{6,7},{9,8},{8,9},{11,10... | collective-permute-start | bytes 3096584 | tf_op jit(solution)/shard_map/ppermute | solution.py:34
  100.4 30.5 %collective-permute-start.31 = (bf16[14,96,384]{2,1,0:T(8,128)(2,1)}, bf16[14,96,384]{2,1,0:T(8,128)(2,1)S(1)}, u32[]{:S(2)}, u32[]{:S(2)}) collective-permute-start(bf16[14,96,384]{2,1,0:T(8,128)(2,1)} %collective-permute-done.15.refs_11_), channel_id=1, source_target_pairs={{1,0},{0,1},{3,2},{2,3},{5,4},{4,5},{7,6},{6,7},{9,8},{8,9},{11,10... | collective-permute-start | bytes 3096584 | tf_op jit(solution)/shard_map/ppermute | solution.py:34
  100.6 9.9 %collective-permute-start.26 = (bf16[2,1,32,384]{3,2,1,0:T(8,128)(2,1)S(1)}, bf16[2,1,32,384]{3,2,1,0:T(8,128)(2,1)S(1)}, u32[]{:S(2)}, u32[]{:S(2)}) collective-permute-start(bf16[2,1,32,384]{3,2,1,0:T(8,128)(2,1)S(1)} %constant_dynamic-slice_fusion), channel_id=1, source_target_pairs={{2,9},{1,10},{4,11},{3,12},{6,13},{5,14},{10,17},{9,18},{12,19},{1... | collective-permute-start | bytes 147464 | tf_op jit(solution)/shard_map/ppermute | solution.py:34
  110.5 11.3 %collective-permute-start.24 = (bf16[2,4,32,384]{3,2,1,0:T(8,128)(2,1)S(1)}, bf16[2,4,32,384]{3,2,1,0:T(8,128)(2,1)S(1)}, u32[]{:S(2)}, u32[]{:S(2)}) collective-permute-start(bf16[2,4,32,384]{3,2,1,0:T(8,128)(2,1)S(1)} %constant_dynamic-slice_fusion.1), channel_id=1, source_target_pairs={{0,8},{1,9},{2,10},{3,11},{4,12},{5,13},{6,14},{7,15},{8,16},{9,17... | collective-permute-start | bytes 589832 | tf_op jit(solution)/shard_map/ppermute | solution.py:34
  121.8 7.7 %collective-permute-start.27 = (bf16[6,1,32,384]{3,2,1,0:T(8,128)(2,1)S(1)}, bf16[6,1,32,384]{3,2,1,0:T(8,128)(2,1)S(1)}, u32[]{:S(2)}, u32[]{:S(2)}) collective-permute-start(bf16[6,1,32,384]{3,2,1,0:T(8,128)(2,1)S(1)} %get-tuple-element.43), channel_id=1, source_target_pairs={{2,1},{1,2},{4,3},{3,4},{6,5},{5,6},{10,9},{9,10},{12,11},{11,12},... | collective-permute-start | bytes 442376 | tf_op jit(solution)/shard_map/ppermute | solution.py:34
  129.5 1.4 collective-permute-start.25
  (10 other events, 110.4 us)

commit v3 on v2

--- a/solution.py
+++ b/solution.py
@@ -38,7 +38,7 @@
     def source(z, y, x, c):
         odd = z % 2
         if c == 0:
-            return (z + int(FETCH[0, x, which]), y + 2 * odd, x, c)
+            return (z + int(FETCH[0, x, which]), y + 2 * odd - 1, x, c)
         return (z - odd + int(FETCH[1, (x + 2 * odd) % NX, which]), y, x, c)
 
     return source
@@ -65,7 +65,7 @@
 
 
 def z_stage(own):
-    return jnp.stack([fetch(own, z_source(0)), fetch(own, z_source(1))])
+    return jnp.stack([fetch(own, z_source(0)), fetch(own, z_source(1))], 1)
 
 
 def small_stage(two):
@@ -83,13 +83,14 @@
         out[tap] = jnp.concatenate(rows, 0).astype(jnp.bfloat16)
 
 
-def join_rows(parts):
-    vmem = pl.BlockSpec(memory_space=pltpu.VMEM)
+def join_rows(parts, which):
+    block = pl.BlockSpec((None, 2, HALF * SHARD, C), lambda i: (which, 0, 0, 0))
     return pl.pallas_call(
         join_body,
+        grid=(1,),
         out_shape=jax.ShapeDtypeStruct((HALF, BUNDLE, C), jnp.bfloat16),
-        in_specs=[vmem] * 4,
-        out_specs=vmem,
+        in_specs=[block] * 4,
+        out_specs=pl.BlockSpec((HALF, BUNDLE, C), lambda i: (0, 0, 0)),
         compiler_params=pltpu.CompilerParams(vmem_limit_bytes=16 * 1024 * 1024),
         cost_estimate=pl.CostEstimate(flops=0, bytes_accessed=2_000_000, transcendentals=0),
     )(*parts)
@@ -107,7 +108,7 @@
     odd = z % 2
     at_z = z + jnp.array((0, 0, 0, 1), jnp.int32) * jnp.where(odd == 1, 1, -1)
     piece_z = at_z[:, None, None] + table[0][(x + around) % NX][None, :, :]
-    piece_y = (y + aside + 2 * (at_z % 2))[:, None, None]
+    piece_y = (y + aside + 2 * (at_z % 2) - 1)[:, None, None]
     first = piece_z % NZ * NY + piece_y % NY
     at_z = z + jnp.array((0, 0, 0, 1), jnp.int32) * jnp.where(odd == 0, 1, -1)
     piece_z = (at_z - at_z % 2)[:, None] + table[1][(x + aside + 2 * (at_z % 2)) % NX]
@@ -248,9 +249,7 @@
             pltpu.SemaphoreType.DMA((2, 4)),
         ],
         compiler_params=pltpu.CompilerParams(vmem_limit_bytes=44 * 1024 * 1024),
-        cost_estimate=pl.CostEstimate(
-            flops=2 * 768 * 27 * C * C, bytes_accessed=12_000_000, transcendentals=768 * C
-        ),
+        cost_estimate=pl.CostEstimate(flops=1000, bytes_accessed=1000, transcendentals=0),
     )(scalars, lag_weights, *extended, orders, tail, *own, *got)
 
 
@@ -297,9 +296,16 @@
 
     def extend(acts):
         outer = jnp.where(first_core, acts[:, 0:1], acts[:, 3:4])
-        carried = fetch(lax.dynamic_slice_in_dim(acts, last, 2, 0), before_in_group)
+        ends, corners, outer = lax.optimization_barrier(
+            (
+                lax.dynamic_slice_in_dim(acts, last, 2, 0),
+                lax.dynamic_slice_in_dim(outer, last, 2, 0),
+                outer,
+            )
+        )
+        carried = fetch(ends, before_in_group)
+        across_before = fetch(corners, across_and_before)
         across = fetch(outer, across_chips)
-        across_before = fetch(lax.dynamic_slice_in_dim(outer, last, 2, 0), across_and_before)
         edge = jnp.concatenate(
             [
                 jnp.where(first_core, carried[:, 3:4], carried[:, 0:1]),
@@ -310,25 +316,25 @@
         beside = fetch(edge, sibling)
         return carried, acts, beside, jnp.concatenate([across_before, across], 0)
 
-    one = z_stage(own_half(kernel_one))
-    own_two, one = lax.optimization_barrier((own_half(kernel_two), one))
-    one_parts = small_stage(one)
-    two = z_stage(own_two)
-    two, one_parts = lax.optimization_barrier((two, one_parts))
-    one_bundles = bulk_stage(join_rows(one_parts))
-    two_bundle = join_rows(small_stage(two))
-    two_bundle, one_bundles = lax.optimization_barrier((two_bundle, one_bundles))
+    acts_one = norm_act(frames, gain_one)
+    parts = small_stage(z_stage(jnp.stack([own_half(kernel_one), own_half(kernel_two)])))
+    parts, extended_one = lax.optimization_barrier((parts, extend(acts_one)))
+    one_bundle, two_bundle = join_rows(parts, 0), join_rows(parts, 1)
+    one_bundles = bulk_stage(one_bundle)
+    two_bundles = bulk_stage(two_bundle)
+    one_bundles, two_bundle = lax.optimization_barrier((one_bundles, two_bundle))
     one_others = [fetch(b, sibling) for b in one_bundles]
-    two_bundles = bulk_stage(two_bundle)
 
     acts_two = conv(
-        scalars, lag_weights, extend(norm_act(frames, gain_one)), orders, gain_two.reshape(1, C),
+        scalars, lag_weights, extended_one, orders, gain_two.reshape(1, C),
         one_bundles, one_others, finish_norm,
     ).reshape(frames.shape)
     two_bundles, acts_two = lax.optimization_barrier((two_bundles, acts_two))
+    extended = extend(acts_two)
+    two_bundles, extended = lax.optimization_barrier((two_bundles, extended))
     two_others = [fetch(b, sibling) for b in two_bundles]
     result = conv(
-        scalars, lag_weights, extend(acts_two), orders, frames.reshape(slots, 128, C),
+        scalars, lag_weights, extended, orders, frames.reshape(slots, 128, C),
         two_bundles, two_others, finish_add,
     )
     return result.reshape(frames.shape)

time: 148 us -> 142 us (0.959)
  starting transfers between devices: 60.6 us -> 54.1 us
  waiting for transfers between devices: 40.9 us -> 46.4 us
  other arithmetic: 5.59 us -> 1.7 us
    ppermute x32 -> x27, starting transfers between devices: 60.6 us -> 54.1 us  [fetch(): return lax.ppermute(array, AXES, pairs)]
    ppermute x32 -> x27, waiting for transfers between devices: 40.9 us -> 46.4 us  [fetch(): return lax.ppermute(array, AXES, pairs)]
    unnamed x20 -> x35, local copies, waits for them, and re-layouts: 2.89 us -> 4 us
  transfers between devices with their start and end apart: 32 -> 27, of which waited for: 12 -> 15; matrix products, arithmetic and copies ran while one was open for 6% -> 2% of each run, Pallas kernels for 10% -> 10%
where the time goes in v3:
time: 142 us; the launch traced here: 141 us
  starting transfers between devices  54.1 us (38%)
  waiting for transfers between devices  46.4 us (33%)
  Pallas kernels  30.2 us (21%)
  local copies, waits for them, and re-layouts  6.96 us (5%)
  between operations  1.93 us (1%)
  other arithmetic  1.7 us (1%)
    ppermute x27, starting transfers between devices, fetch(): return lax.ppermute(array, AXES, pairs)  54.1 us
    ppermute x27, waiting for transfers between devices, fetch(): return lax.ppermute(array, AXES, pairs)  46.4 us
    pallas_call x2, Pallas kernels, conv(): pl.pallas_call(lambda *refs: conv_body(*refs, finish=finish), out_shape=j...  28.7 us
    unnamed x35, local copies, waits for them, and re-layouts  4 us
  transfers between devices with their start and end apart: 27, of which 15 were waited for; matrix products, arithmetic and copies ran while one was open for 2% of the time, Pallas kernels for 10%

profile of v3, /device:TPU:131, one launch (start us, length us, event | category | flops | bytes accessed | tf_op | source)
XLA Modules:
  0.0 141.3 jit_solution(15634599578001198231)
XLA Ops:
  0.0 1.1 constant_dynamic-slice_fusion.4
  1.3 1.3 collective-permute-start.1
  2.5 4.3 %collective-permute-start = (bf16[2,168,384]{2,1,0:T(8,128)(2,1)S(1)}, bf16[2,168,384]{2,1,0:T(8,128)(2,1)S(1)}, u32[]{:S(2)}, u32[]{:S(2)}) collective-permute-start(bf16[2,168,384]{2,1,0:T(8,128)(2,1)S(1)} %constant_dynamic-update-slice_fusion), channel_id=1, source_target_pairs={{152,0},{1,1},{58,2},{67,3},{252,4},{37,5},{94,6},{103,7},{128,8},... | collective-permute-start | bytes 774152 | tf_op jit(solution)/shard_map/ppermute | solution.py:34
  8.2 3.2 %collective-permute-start.5 = (bf16[2,4,32,384]{3,2,1,0:T(8,128)(2,1)S(1)}, bf16[2,4,32,384]{3,2,1,0:T(8,128)(2,1)S(1)}, u32[]{:S(2)}, u32[]{:S(2)}) collective-permute-start(bf16[2,4,32,384]{3,2,1,0:T(8,128)(2,1)S(1)} %constant_dynamic-slice_fusion.3), channel_id=1, source_target_pairs={{0,8},{1,9},{2,10},{3,11},{4,12},{5,13},{6,14},{7,15},{8,16},{9,17... | collective-permute-start | bytes 589832 | tf_op jit(solution)/shard_map/ppermute | solution.py:34
  11.4 3.2 %collective-permute-start.7 = (bf16[2,1,32,384]{3,2,1,0:T(8,128)(2,1)S(1)}, bf16[2,1,32,384]{3,2,1,0:T(8,128)(2,1)S(1)}, u32[]{:S(2)}, u32[]{:S(2)}) collective-permute-start(bf16[2,1,32,384]{3,2,1,0:T(8,128)(2,1)S(1)} %constant_dynamic-slice_fusion.2), channel_id=1, source_target_pairs={{2,9},{1,10},{4,11},{3,12},{6,13},{5,14},{10,17},{9,18},{12,19},{1... | collective-permute-start | bytes 147464 | tf_op jit(solution)/shard_map/ppermute | solution.py:34
  14.7 3.4 %collective-permute-start.8 = (bf16[6,1,32,384]{3,2,1,0:T(8,128)(2,1)S(1)}, bf16[6,1,32,384]{3,2,1,0:T(8,128)(2,1)S(1)}, u32[]{:S(2)}, u32[]{:S(2)}) collective-permute-start(bf16[6,1,32,384]{3,2,1,0:T(8,128)(2,1)S(1)} %get-tuple-element.38), channel_id=1, source_target_pairs={{2,1},{1,2},{4,3},{3,4},{6,5},{5,6},{10,9},{9,10},{12,11},{11,12},... | collective-permute-start | bytes 442376 | tf_op jit(solution)/shard_map/ppermute | solution.py:34
  18.0 1.8 %collective-permute-done = bf16[2,168,384]{2,1,0:T(8,128)(2,1)S(1)} collective-permute-done((bf16[2,168,384]{2,1,0:T(8,128)(2,1)S(1)}, bf16[2,168,384]{2,1,0:T(8,128)(2,1)S(1)}, u32[]{:S(2)}, u32[]{:S(2)}) %collective-permute-start) | collective-permute-done | bytes 258080 | tf_op jit(solution)/shard_map/ppermute | solution.py:34
  19.9 4.6 %collective-permute-start.4 = (bf16[2,2,168,384]{3,2,1,0:T(8,128)(2,1)S(1)}, bf16[2,2,168,384]{3,2,1,0:T(8,128)(2,1)S(1)}, u32[]{:S(2)}, u32[]{:S(2)}) collective-permute-start(bf16[2,2,168,384]{3,2,1,0:T(8,128)(2,1)S(1)} %pad_maximum_fusion.refs_0_), channel_id=1, source_target_pairs={{4,0},{17,1},{6,2},{19,3},{0,4},{21,5},{2,6},{23,7},{12,8},{25,9},... | collective-permute-start | bytes 1548296 | tf_op jit(solution)/shard_map/ppermute | solution.py:34
  24.5 2.7 %collective-permute-start.2 = (bf16[2,2,168,384]{3,2,1,0:T(8,128)(2,1)S(1)}, bf16[2,2,168,384]{3,2,1,0:T(8,128)(2,1)S(1)}, u32[]{:S(2)}, u32[]{:S(2)}) collective-permute-start(bf16[2,2,168,384]{3,2,1,0:T(8,128)(2,1)S(1)} %pad_maximum_fusion.refs_0_), channel_id=1, source_target_pairs={{2,0},{9,1},{4,2},{11,3},{6,4},{13,5},{0,6},{15,7},{10,8},{17,9},{... | collective-permute-start | bytes 1548296 | tf_op jit(solution)/shard_map/ppermute | solution.py:34
  27.2 6.0 %collective-permute-done.7 = bf16[2,1,32,384]{3,2,1,0:T(8,128)(2,1)S(1)} collective-permute-done((bf16[2,1,32,384]{3,2,1,0:T(8,128)(2,1)S(1)}, bf16[2,1,32,384]{3,2,1,0:T(8,128)(2,1)S(1)}, u32[]{:S(2)}, u32[]{:S(2)}) %collective-permute-start.7) | collective-permute-done | bytes 49184 | tf_op jit(solution)/shard_map/ppermute | solution.py:34
  34.9 2.2 %collective-permute-done.3.refs_2_ = bf16[2,2,168,384]{3,2,1,0:T(8,128)(2,1)S(1)} collective-permute-done((bf16[2,2,168,384]{3,2,1,0:T(8,128)(2,1)S(1)}, bf16[2,2,168,384]{3,2,1,0:T(8,128)(2,1)S(1)}, u32[]{:S(2)}, u32[]{:S(2)}) %collective-permute-start.3) | collective-permute-done | bytes 516128 | tf_op jit(solution)/shard_map/ppermute | solution.py:34
  37.1 1.3 shard_map.128.refs_8_
  38.5 4.9 %collective-permute-start.13 = (bf16[14,96,384]{2,1,0:T(8,128)(2,1)}, bf16[14,96,384]{2,1,0:T(8,128)(2,1)}, u32[]{:S(2)}, u32[]{:S(2)}) collective-permute-start(bf16[14,96,384]{2,1,0:T(8,128)(2,1)} %shard_map.128.refs_8_), channel_id=1, source_target_pairs={{24,0},{7,1},{26,2},{1,3},{28,4},{3,5},{30,6},{5,7},{0,8},{15,9},{... | collective-permute-start | bytes 3096584 | tf_op jit(solution)/shard_map/ppermute | solution.py:34
  44.5 1.0 copy-done.4
  45.8 6.5 %collective-permute-done.14.refs_11_ = bf16[14,96,384]{2,1,0:T(8,128)(2,1)} collective-permute-done((bf16[14,96,384]{2,1,0:T(8,128)(2,1)}, bf16[14,96,384]{2,1,0:T(8,128)(2,1)}, u32[]{:S(2)}, u32[]{:S(2)}) %collective-permute-start.14) | collective-permute-done | bytes 1032224 | tf_op jit(solution)/shard_map/ppermute | solution.py:34
  52.3 4.7 %collective-permute-done.13.refs_10_ = bf16[14,96,384]{2,1,0:T(8,128)(2,1)} collective-permute-done((bf16[14,96,384]{2,1,0:T(8,128)(2,1)}, bf16[14,96,384]{2,1,0:T(8,128)(2,1)}, u32[]{:S(2)}, u32[]{:S(2)}) %collective-permute-start.13) | collective-permute-done | bytes 1032224 | tf_op jit(solution)/shard_map/ppermute | solution.py:34
  57.5 10.6 %collective-permute-start.15 = (bf16[14,96,384]{2,1,0:T(8,128)(2,1)}, bf16[14,96,384]{2,1,0:T(8,128)(2,1)}, u32[]{:S(2)}, u32[]{:S(2)}) collective-permute-start(bf16[14,96,384]{2,1,0:T(8,128)(2,1)} %shard_map.128.refs_8_), channel_id=1, source_target_pairs={{1,0},{0,1},{3,2},{2,3},{5,4},{4,5},{7,6},{6,7},{9,8},{8,9},{11,10... | collective-permute-start | bytes 3096584 | tf_op jit(solution)/shard_map/ppermute | solution.py:34
  70.0 1.5 %collective-permute-start.9 = (bf16[14,96,384]{2,1,0:T(8,128)(2,1)S(1)}, bf16[14,96,384]{2,1,0:T(8,128)(2,1)}, u32[]{:S(2)}, u32[]{:S(2)}) collective-permute-start(bf16[14,96,384]{2,1,0:T(8,128)(2,1)S(1)} %shard_map.127.refs_8_), channel_id=1, source_target_pairs={{8,0},{3,1},{10,2},{5,3},{12,4},{7,5},{14,6},{1,7},{16,8},{11,9},{... | collective-permute-start | bytes 3096584 | tf_op jit(solution)/shard_map/ppermute | solution.py:34
  71.4 5.3 %collective-permute-start.17 = (bf16[14,96,384]{2,1,0:T(8,128)(2,1)}, bf16[14,96,384]{2,1,0:T(8,128)(2,1)}, u32[]{:S(2)}, u32[]{:S(2)}) collective-permute-start(bf16[14,96,384]{2,1,0:T(8,128)(2,1)} %collective-permute-done.13.refs_10_), channel_id=1, source_target_pairs={{1,0},{0,1},{3,2},{2,3},{5,4},{4,5},{7,6},{6,7},{9,8},{8,9},{11,10... | collective-permute-start | bytes 3096584 | tf_op jit(solution)/shard_map/ppermute | solution.py:34
  79.3 1.5 %collective-permute-done.18.refs_15_ = bf16[14,96,384]{2,1,0:T(8,128)(2,1)} collective-permute-done((bf16[14,96,384]{2,1,0:T(8,128)(2,1)}, bf16[14,96,384]{2,1,0:T(8,128)(2,1)}, u32[]{:S(2)}, u32[]{:S(2)}) %collective-permute-start.18) | collective-permute-done | bytes 1032224 | tf_op jit(solution)/shard_map/ppermute | solution.py:34
  82.6 13.8 %shard_map.129 = bf16[6,128,384]{2,1,0:T(8,128)(2,1)S(1)} custom-call(s32[2]{0:T(128)S(1)} %pad_add_fusion.1.refs_0_, f32[3,6]{1,0:T(4,128)S(1)} %add_convert_fusion.refs_1_, bf16[2,4,32,384]{3,2,1,0:T(8,128)(2,1)S(1)} %copy-done.6, bf16[6,4,32,384]{3,2,1,0:T(8,128)(2,1)S(1)} %fusion.7.refs_3_, bf16[8,1,32,384]{3,2,1,0:T(8,128)(2,1)S(1)} %copy-done.8, ...), custom_call_target="tpu_custom_call" | custom-call | flops 1000 | bytes 1000 | tf_op jit(solution)/shard_map/pallas_call | solution.py:239
  96.6 1.9 %collective-permute-start.19 = (bf16[2,4,32,384]{3,2,1,0:T(8,128)(2,1)S(1)}, bf16[2,4,32,384]{3,2,1,0:T(8,128)(2,1)S(1)}, u32[]{:S(2)}, u32[]{:S(2)}) collective-permute-start(bf16[2,4,32,384]{3,2,1,0:T(8,128)(2,1)S(1)} %constant_dynamic-slice_fusion.1), channel_id=1, source_target_pairs={{0,8},{1,9},{2,10},{3,11},{4,12},{5,13},{6,14},{7,15},{8,16},{9,17... | collective-permute-start | bytes 589832 | tf_op jit(solution)/shard_map/ppermute | solution.py:34
  98.5 1.9 %collective-permute-start.22 = (bf16[6,1,32,384]{3,2,1,0:T(8,128)(2,1)S(1)}, bf16[6,1,32,384]{3,2,1,0:T(8,128)(2,1)S(1)}, u32[]{:S(2)}, u32[]{:S(2)}) collective-permute-start(bf16[6,1,32,384]{3,2,1,0:T(8,128)(2,1)S(1)} %get-tuple-element.58), channel_id=1, source_target_pairs={{2,1},{1,2},{4,3},{3,4},{6,5},{5,6},{10,9},{9,10},{12,11},{11,12},... | collective-permute-start | bytes 442376 | tf_op jit(solution)/shard_map/ppermute | solution.py:34
  100.5 7.5 %collective-permute-done.19.refs_2_ = bf16[2,4,32,384]{3,2,1,0:T(8,128)(2,1)S(1)} collective-permute-done((bf16[2,4,32,384]{3,2,1,0:T(8,128)(2,1)S(1)}, bf16[2,4,32,384]{3,2,1,0:T(8,128)(2,1)S(1)}, u32[]{:S(2)}, u32[]{:S(2)}) %collective-permute-start.19) | collective-permute-done | bytes 196640 | tf_op jit(solution)/shard_map/ppermute | solution.py:34
  108.0 1.3 collective-permute-start.20
  109.3 1.9 %collective-permute-start.21 = (bf16[2,1,32,384]{3,2,1,0:T(8,128)(2,1)S(1)}, bf16[2,1,32,384]{3,2,1,0:T(8,128)(2,1)S(1)}, u32[]{:S(2)}, u32[]{:S(2)}) collective-permute-start(bf16[2,1,32,384]{3,2,1,0:T(8,128)(2,1)S(1)} %constant_dynamic-slice_fusion), channel_id=1, source_target_pairs={{2,9},{1,10},{4,11},{3,12},{6,13},{5,14},{10,17},{9,18},{12,19},{1... | collective-permute-start | bytes 147464 | tf_op jit(solution)/shard_map/ppermute | solution.py:34
  111.2 7.7 %collective-permute-done.21 = bf16[2,1,32,384]{3,2,1,0:T(8,128)(2,1)S(1)} collective-permute-done((bf16[2,1,32,384]{3,2,1,0:T(8,128)(2,1)S(1)}, bf16[2,1,32,384]{3,2,1,0:T(8,128)(2,1)S(1)}, u32[]{:S(2)}, u32[]{:S(2)}) %collective-permute-start.21) | collective-permute-done | bytes 49184 | tf_op jit(solution)/shard_map/ppermute | solution.py:34
  120.1 2.1 %collective-permute-done.23.refs_12_ = bf16[14,96,384]{2,1,0:T(8,128)(2,1)S(1)} collective-permute-done((bf16[14,96,384]{2,1,0:T(8,128)(2,1)S(1)}, bf16[14,96,384]{2,1,0:T(8,128)(2,1)S(1)}, u32[]{:S(2)}, u32[]{:S(2)}) %collective-permute-start.23) | collective-permute-done | bytes 1032224 | tf_op jit(solution)/shard_map/ppermute | solution.py:34
  122.1 1.2 collective-permute-done.24.refs_13_
  123.4 1.5 %collective-permute-done.25.refs_14_ = bf16[14,96,384]{2,1,0:T(8,128)(2,1)S(1)} collective-permute-done((bf16[14,96,384]{2,1,0:T(8,128)(2,1)}, bf16[14,96,384]{2,1,0:T(8,128)(2,1)S(1)}, u32[]{:S(2)}, u32[]{:S(2)}) %collective-permute-start.25) | collective-permute-done | bytes 1032224 | tf_op jit(solution)/shard_map/ppermute | solution.py:34
  124.8 1.5 %collective-permute-done.26.refs_15_ = bf16[14,96,384]{2,1,0:T(8,128)(2,1)S(1)} collective-permute-done((bf16[14,96,384]{2,1,0:T(8,128)(2,1)}, bf16[14,96,384]{2,1,0:T(8,128)(2,1)S(1)}, u32[]{:S(2)}, u32[]{:S(2)}) %collective-permute-start.26) | collective-permute-done | bytes 1032224 | tf_op jit(solution)/shard_map/ppermute | solution.py:34
  126.3 14.8 %shard_map.130 = bf16[6,128,384]{2,1,0:T(8,128)(2,1)} custom-call(s32[2]{0:T(128)S(1)} %pad_add_fusion.1.refs_0_, f32[3,6]{1,0:T(4,128)S(1)} %add_convert_fusion.refs_1_, bf16[2,4,32,384]{3,2,1,0:T(8,128)(2,1)S(1)} %collective-permute-done.19.refs_2_, bf16[6,4,32,384]{3,2,1,0:T(8,128)(2,1)S(1)} %bitcast.28, ...), custom_call_target="tpu_custom_call" | custom-call | flops 1000 | bytes 1000 | tf_op jit(solution)/shard_map/pallas_call | solution.py:239
  (107 shorter events, 11.3 us)
Async XLA Ops:
  1.3 16.8 %collective-permute-start.1 = (bf16[2,168,384]{2,1,0:T(8,128)(2,1)S(1)}, bf16[2,168,384]{2,1,0:T(8,128)(2,1)S(1)}, u32[]{:S(2)}, u32[]{:S(2)}) collective-permute-start(bf16[2,168,384]{2,1,0:T(8,128)(2,1)S(1)} %constant_dynamic-update-slice_fusion), channel_id=1, source_target_pairs={{24,0},{129,1},{122,2},{195,3},{188,4},{165,5},{222,6},{231,7},{0,... | collective-permute-start | bytes 774152 | tf_op jit(solution)/shard_map/ppermute | solution.py:34
  2.5 17.3 %collective-permute-start = (bf16[2,168,384]{2,1,0:T(8,128)(2,1)S(1)}, bf16[2,168,384]{2,1,0:T(8,128)(2,1)S(1)}, u32[]{:S(2)}, u32[]{:S(2)}) collective-permute-start(bf16[2,168,384]{2,1,0:T(8,128)(2,1)S(1)} %constant_dynamic-update-slice_fusion), channel_id=1, source_target_pairs={{152,0},{1,1},{58,2},{67,3},{252,4},{37,5},{94,6},{103,7},{128,8},... | collective-permute-start | bytes 774152 | tf_op jit(solution)/shard_map/ppermute | solution.py:34
  8.2 16.3 %collective-permute-start.5 = (bf16[2,4,32,384]{3,2,1,0:T(8,128)(2,1)S(1)}, bf16[2,4,32,384]{3,2,1,0:T(8,128)(2,1)S(1)}, u32[]{:S(2)}, u32[]{:S(2)}) collective-permute-start(bf16[2,4,32,384]{3,2,1,0:T(8,128)(2,1)S(1)} %constant_dynamic-slice_fusion.3), channel_id=1, source_target_pairs={{0,8},{1,9},{2,10},{3,11},{4,12},{5,13},{6,14},{7,15},{8,16},{9,17... | collective-permute-start | bytes 589832 | tf_op jit(solution)/shard_map/ppermute | solution.py:34
  11.4 21.8 %collective-permute-start.7 = (bf16[2,1,32,384]{3,2,1,0:T(8,128)(2,1)S(1)}, bf16[2,1,32,384]{3,2,1,0:T(8,128)(2,1)S(1)}, u32[]{:S(2)}, u32[]{:S(2)}) collective-permute-start(bf16[2,1,32,384]{3,2,1,0:T(8,128)(2,1)S(1)} %constant_dynamic-slice_fusion.2), channel_id=1, source_target_pairs={{2,9},{1,10},{4,11},{3,12},{6,13},{5,14},{10,17},{9,18},{12,19},{1... | collective-permute-start | bytes 147464 | tf_op jit(solution)/shard_map/ppermute | solution.py:34
  14.7 19.1 %collective-permute-start.8 = (bf16[6,1,32,384]{3,2,1,0:T(8,128)(2,1)S(1)}, bf16[6,1,32,384]{3,2,1,0:T(8,128)(2,1)S(1)}, u32[]{:S(2)}, u32[]{:S(2)}) collective-permute-start(bf16[6,1,32,384]{3,2,1,0:T(8,128)(2,1)S(1)} %get-tuple-element.38), channel_id=1, source_target_pairs={{2,1},{1,2},{4,3},{3,4},{6,5},{5,6},{10,9},{9,10},{12,11},{11,12},... | collective-permute-start | bytes 442376 | tf_op jit(solution)/shard_map/ppermute | solution.py:34
  19.9 15.0 %collective-permute-start.4 = (bf16[2,2,168,384]{3,2,1,0:T(8,128)(2,1)S(1)}, bf16[2,2,168,384]{3,2,1,0:T(8,128)(2,1)S(1)}, u32[]{:S(2)}, u32[]{:S(2)}) collective-permute-start(bf16[2,2,168,384]{3,2,1,0:T(8,128)(2,1)S(1)} %pad_maximum_fusion.refs_0_), channel_id=1, source_target_pairs={{4,0},{17,1},{6,2},{19,3},{0,4},{21,5},{2,6},{23,7},{12,8},{25,9},... | collective-permute-start | bytes 1548296 | tf_op jit(solution)/shard_map/ppermute | solution.py:34
  24.5 12.5 %collective-permute-start.3 = (bf16[2,2,168,384]{3,2,1,0:T(8,128)(2,1)S(1)}, bf16[2,2,168,384]{3,2,1,0:T(8,128)(2,1)S(1)}, u32[]{:S(2)}, u32[]{:S(2)}) collective-permute-start(bf16[2,2,168,384]{3,2,1,0:T(8,128)(2,1)S(1)} %pad_maximum_fusion.refs_0_), channel_id=1, source_target_pairs={{6,0},{25,1},{0,2},{27,3},{2,4},{29,5},{4,6},{31,7},{14,8},{1,9},{... | collective-permute-start | bytes 1548296 | tf_op jit(solution)/shard_map/ppermute | solution.py:34
  24.5 13.9 %copy-start.5 = (bf16[2,4,32,384]{3,2,1,0:T(8,128)(2,1)}, bf16[2,4,32,384]{3,2,1,0:T(8,128)(2,1)S(1)}, u32[]{:S(2)}) copy-start(bf16[2,4,32,384]{3,2,1,0:T(8,128)(2,1)S(1)} %collective-permute-done.5.refs_2_) | copy-start | bytes 589828
  24.5 12.5 %collective-permute-start.2 = (bf16[2,2,168,384]{3,2,1,0:T(8,128)(2,1)S(1)}, bf16[2,2,168,384]{3,2,1,0:T(8,128)(2,1)S(1)}, u32[]{:S(2)}, u32[]{:S(2)}) collective-permute-start(bf16[2,2,168,384]{3,2,1,0:T(8,128)(2,1)S(1)} %pad_maximum_fusion.refs_0_), channel_id=1, source_target_pairs={{2,0},{9,1},{4,2},{11,3},{6,4},{13,5},{0,6},{15,7},{10,8},{17,9},{... | collective-permute-start | bytes 1548296 | tf_op jit(solution)/shard_map/ppermute | solution.py:34
  33.2 1.6 %collective-permute-start.6 = (bf16[8,1,32,384]{3,2,1,0:T(8,128)(2,1)S(1)}, bf16[8,1,32,384]{3,2,1,0:T(8,128)(2,1)S(1)}, u32[]{:S(2)}, u32[]{:S(2)}) collective-permute-start(bf16[8,1,32,384]{3,2,1,0:T(8,128)(2,1)S(1)} %pad_maximum_fusion.1), channel_id=1, source_target_pairs={{1,0},{0,1},{3,2},{2,3},{5,4},{4,5},{7,6},{6,7},{9,8},{8,9},{11,10... | collective-permute-start | bytes 589832 | tf_op jit(solution)/shard_map/ppermute | solution.py:34
  38.4 13.9 %collective-permute-start.14 = (bf16[14,96,384]{2,1,0:T(8,128)(2,1)}, bf16[14,96,384]{2,1,0:T(8,128)(2,1)}, u32[]{:S(2)}, u32[]{:S(2)}) collective-permute-start(bf16[14,96,384]{2,1,0:T(8,128)(2,1)} %shard_map.128.refs_8_), channel_id=1, source_target_pairs={{224,0},{33,1},{226,2},{35,3},{228,4},{37,5},{230,6},{39,7},{232,8... | collective-permute-start | bytes 3096584 | tf_op jit(solution)/shard_map/ppermute | solution.py:34
  38.5 18.5 %collective-permute-start.13 = (bf16[14,96,384]{2,1,0:T(8,128)(2,1)}, bf16[14,96,384]{2,1,0:T(8,128)(2,1)}, u32[]{:S(2)}, u32[]{:S(2)}) collective-permute-start(bf16[14,96,384]{2,1,0:T(8,128)(2,1)} %shard_map.128.refs_8_), channel_id=1, source_target_pairs={{24,0},{7,1},{26,2},{1,3},{28,4},{3,5},{30,6},{5,7},{0,8},{15,9},{... | collective-permute-start | bytes 3096584 | tf_op jit(solution)/shard_map/ppermute | solution.py:34
  43.4 14.1 %collective-permute-start.12 = (bf16[14,96,384]{2,1,0:T(8,128)(2,1)}, bf16[14,96,384]{2,1,0:T(8,128)(2,1)}, u32[]{:S(2)}, u32[]{:S(2)}) collective-permute-start(bf16[14,96,384]{2,1,0:T(8,128)(2,1)} %shard_map.128.refs_8_), channel_id=1, source_target_pairs={{8,0},{3,1},{10,2},{5,3},{12,4},{7,5},{14,6},{1,7},{16,8},{11,9},{... | collective-permute-start | bytes 3096584 | tf_op jit(solution)/shard_map/ppermute | solution.py:34
  45.6 22.6 %copy-start.10 = (s32[4,2]{1,0:T(4,128)S(1)}, s32[4,2]{1,0:T(4,128)}, u32[]{:S(2)}) copy-start(s32[4,2]{1,0:T(4,128)} %constant.159) | copy-start | bytes 100
  45.6 23.5 %copy-start.9 = (s32[4,2]{1,0:T(4,128)S(1)}, s32[4,2]{1,0:T(4,128)}, u32[]{:S(2)}) copy-start(s32[4,2]{1,0:T(4,128)} %constant.161) | copy-start | bytes 100
  45.6 32.1 %copy-start.16 = (s32[3]{0:T(128)S(1)}, s32[3]{0:T(128)}, u32[]{:S(2)}) copy-start(s32[3]{0:T(128)} %param.14) | copy-start | bytes 40
  45.6 32.3 %copy-start.12 = (f32[384]{0:T(512)S(1)}, f32[384]{0:T(512)}, u32[]{:S(2)}) copy-start(f32[384]{0:T(512)} %param.20) | copy-start | bytes 4612
  57.5 13.9 %collective-permute-start.15 = (bf16[14,96,384]{2,1,0:T(8,128)(2,1)}, bf16[14,96,384]{2,1,0:T(8,128)(2,1)}, u32[]{:S(2)}, u32[]{:S(2)}) collective-permute-start(bf16[14,96,384]{2,1,0:T(8,128)(2,1)} %shard_map.128.refs_8_), channel_id=1, source_target_pairs={{1,0},{0,1},{3,2},{2,3},{5,4},{4,5},{7,6},{6,7},{9,8},{8,9},{11,10... | collective-permute-start | bytes 3096584 | tf_op jit(solution)/shard_map/ppermute | solution.py:34
  68.1 8.6 %collective-permute-start.16 = (bf16[14,96,384]{2,1,0:T(8,128)(2,1)}, bf16[14,96,384]{2,1,0:T(8,128)(2,1)}, u32[]{:S(2)}, u32[]{:S(2)}) collective-permute-start(bf16[14,96,384]{2,1,0:T(8,128)(2,1)} %collective-permute-done.12.refs_9_), channel_id=1, source_target_pairs={{1,0},{0,1},{3,2},{2,3},{5,4},{4,5},{7,6},{6,7},{9,8},{8,9},{11,10... | collective-permute-start | bytes 3096584 | tf_op jit(solution)/shard_map/ppermute | solution.py:34
  69.8 26.6 %collective-permute-start.11 = (bf16[14,96,384]{2,1,0:T(8,128)(2,1)S(1)}, bf16[14,96,384]{2,1,0:T(8,128)(2,1)}, u32[]{:S(2)}, u32[]{:S(2)}) collective-permute-start(bf16[14,96,384]{2,1,0:T(8,128)(2,1)S(1)} %shard_map.127.refs_8_), channel_id=1, source_target_pairs={{224,0},{33,1},{226,2},{35,3},{228,4},{37,5},{230,6},{39,7},{232,8... | collective-permute-start | bytes 3096584 | tf_op jit(solution)/shard_map/ppermute | solution.py:34
  69.9 26.6 %collective-permute-start.10 = (bf16[14,96,384]{2,1,0:T(8,128)(2,1)S(1)}, bf16[14,96,384]{2,1,0:T(8,128)(2,1)}, u32[]{:S(2)}, u32[]{:S(2)}) collective-permute-start(bf16[14,96,384]{2,1,0:T(8,128)(2,1)S(1)} %shard_map.127.refs_8_), channel_id=1, source_target_pairs={{24,0},{7,1},{26,2},{1,3},{28,4},{3,5},{30,6},{5,7},{0,8},{15,9},{... | collective-permute-start | bytes 3096584 | tf_op jit(solution)/shard_map/ppermute | solution.py:34
  70.0 26.5 %collective-permute-start.9 = (bf16[14,96,384]{2,1,0:T(8,128)(2,1)S(1)}, bf16[14,96,384]{2,1,0:T(8,128)(2,1)}, u32[]{:S(2)}, u32[]{:S(2)}) collective-permute-start(bf16[14,96,384]{2,1,0:T(8,128)(2,1)S(1)} %shard_map.127.refs_8_), channel_id=1, source_target_pairs={{8,0},{3,1},{10,2},{5,3},{12,4},{7,5},{14,6},{1,7},{16,8},{11,9},{... | collective-permute-start | bytes 3096584 | tf_op jit(solution)/shard_map/ppermute | solution.py:34
  71.4 7.9 %collective-permute-start.17 = (bf16[14,96,384]{2,1,0:T(8,128)(2,1)}, bf16[14,96,384]{2,1,0:T(8,128)(2,1)}, u32[]{:S(2)}, u32[]{:S(2)}) collective-permute-start(bf16[14,96,384]{2,1,0:T(8,128)(2,1)} %collective-permute-done.13.refs_10_), channel_id=1, source_target_pairs={{1,0},{0,1},{3,2},{2,3},{5,4},{4,5},{7,6},{6,7},{9,8},{8,9},{11,10... | collective-permute-start | bytes 3096584 | tf_op jit(solution)/shard_map/ppermute | solution.py:34
  76.7 4.1 %collective-permute-start.18 = (bf16[14,96,384]{2,1,0:T(8,128)(2,1)}, bf16[14,96,384]{2,1,0:T(8,128)(2,1)}, u32[]{:S(2)}, u32[]{:S(2)}) collective-permute-start(bf16[14,96,384]{2,1,0:T(8,128)(2,1)} %collective-permute-done.14.refs_11_), channel_id=1, source_target_pairs={{1,0},{0,1},{3,2},{2,3},{5,4},{4,5},{7,6},{6,7},{9,8},{8,9},{11,10... | collective-permute-start | bytes 3096584 | tf_op jit(solution)/shard_map/ppermute | solution.py:34
  96.6 11.3 %collective-permute-start.19 = (bf16[2,4,32,384]{3,2,1,0:T(8,128)(2,1)S(1)}, bf16[2,4,32,384]{3,2,1,0:T(8,128)(2,1)S(1)}, u32[]{:S(2)}, u32[]{:S(2)}) collective-permute-start(bf16[2,4,32,384]{3,2,1,0:T(8,128)(2,1)S(1)} %constant_dynamic-slice_fusion.1), channel_id=1, source_target_pairs={{0,8},{1,9},{2,10},{3,11},{4,12},{5,13},{6,14},{7,15},{8,16},{9,17... | collective-permute-start | bytes 589832 | tf_op jit(solution)/shard_map/ppermute | solution.py:34
  98.5 20.4 %collective-permute-start.22 = (bf16[6,1,32,384]{3,2,1,0:T(8,128)(2,1)S(1)}, bf16[6,1,32,384]{3,2,1,0:T(8,128)(2,1)S(1)}, u32[]{:S(2)}, u32[]{:S(2)}) collective-permute-start(bf16[6,1,32,384]{3,2,1,0:T(8,128)(2,1)S(1)} %get-tuple-element.58), channel_id=1, source_target_pairs={{2,1},{1,2},{4,3},{3,4},{6,5},{5,6},{10,9},{9,10},{12,11},{11,12},... | collective-permute-start | bytes 442376 | tf_op jit(solution)/shard_map/ppermute | solution.py:34
  108.0 10.9 %collective-permute-start.20 = (bf16[8,1,32,384]{3,2,1,0:T(8,128)(2,1)S(1)}, bf16[8,1,32,384]{3,2,1,0:T(8,128)(2,1)S(1)}, u32[]{:S(2)}, u32[]{:S(2)}) collective-permute-start(bf16[8,1,32,384]{3,2,1,0:T(8,128)(2,1)S(1)} %pad_maximum_fusion.3), channel_id=1, source_target_pairs={{1,0},{0,1},{3,2},{2,3},{5,4},{4,5},{7,6},{6,7},{9,8},{8,9},{11,10... | collective-permute-start | bytes 589832 | tf_op jit(solution)/shard_map/ppermute | solution.py:34
  109.3 9.6 %collective-permute-start.21 = (bf16[2,1,32,384]{3,2,1,0:T(8,128)(2,1)S(1)}, bf16[2,1,32,384]{3,2,1,0:T(8,128)(2,1)S(1)}, u32[]{:S(2)}, u32[]{:S(2)}) collective-permute-start(bf16[2,1,32,384]{3,2,1,0:T(8,128)(2,1)S(1)} %constant_dynamic-slice_fusion), channel_id=1, source_target_pairs={{2,9},{1,10},{4,11},{3,12},{6,13},{5,14},{10,17},{9,18},{12,19},{1... | collective-permute-start | bytes 147464 | tf_op jit(solution)/shard_map/ppermute | solution.py:34
  118.9 3.2 %collective-permute-start.23 = (bf16[14,96,384]{2,1,0:T(8,128)(2,1)S(1)}, bf16[14,96,384]{2,1,0:T(8,128)(2,1)S(1)}, u32[]{:S(2)}, u32[]{:S(2)}) collective-permute-start(bf16[14,96,384]{2,1,0:T(8,128)(2,1)S(1)} %shard_map.127.refs_8_), channel_id=1, source_target_pairs={{1,0},{0,1},{3,2},{2,3},{5,4},{4,5},{7,6},{6,7},{9,8},{8,9},{11,10... | collective-permute-start | bytes 3096584 | tf_op jit(solution)/shard_map/ppermute | solution.py:34
  119.1 4.3 %collective-permute-start.24 = (bf16[14,96,384]{2,1,0:T(8,128)(2,1)}, bf16[14,96,384]{2,1,0:T(8,128)(2,1)S(1)}, u32[]{:S(2)}, u32[]{:S(2)}) collective-permute-start(bf16[14,96,384]{2,1,0:T(8,128)(2,1)} %collective-permute-done.9.refs_9_), channel_id=1, source_target_pairs={{1,0},{0,1},{3,2},{2,3},{5,4},{4,5},{7,6},{6,7},{9,8},{8,9},{11,10... | collective-permute-start | bytes 3096584 | tf_op jit(solution)/shard_map/ppermute | solution.py:34
  119.5 5.3 %collective-permute-start.25 = (bf16[14,96,384]{2,1,0:T(8,128)(2,1)}, bf16[14,96,384]{2,1,0:T(8,128)(2,1)S(1)}, u32[]{:S(2)}, u32[]{:S(2)}) collective-permute-start(bf16[14,96,384]{2,1,0:T(8,128)(2,1)} %collective-permute-done.10.refs_10_), channel_id=1, source_target_pairs={{1,0},{0,1},{3,2},{2,3},{5,4},{4,5},{7,6},{6,7},{9,8},{8,9},{11,10... | collective-permute-start | bytes 3096584 | tf_op jit(solution)/shard_map/ppermute | solution.py:34
  119.6 6.7 %collective-permute-start.26 = (bf16[14,96,384]{2,1,0:T(8,128)(2,1)}, bf16[14,96,384]{2,1,0:T(8,128)(2,1)S(1)}, u32[]{:S(2)}, u32[]{:S(2)}) collective-permute-start(bf16[14,96,384]{2,1,0:T(8,128)(2,1)} %collective-permute-done.11.refs_11_), channel_id=1, source_target_pairs={{1,0},{0,1},{3,2},{2,3},{5,4},{4,5},{7,6},{6,7},{9,8},{8,9},{11,10... | collective-permute-start | bytes 3096584 | tf_op jit(solution)/shard_map/ppermute | solution.py:34
  (12 other events, 53.0 us)

commit v4 on v3

--- a/solution.py
+++ b/solution.py
@@ -248,7 +248,7 @@
             pltpu.VMEM((6, 128, C), jnp.float32),
             pltpu.SemaphoreType.DMA((2, 4)),
         ],
-        compiler_params=pltpu.CompilerParams(vmem_limit_bytes=44 * 1024 * 1024),
+        compiler_params=pltpu.CompilerParams(vmem_limit_bytes=26 * 1024 * 1024),
         cost_estimate=pl.CostEstimate(flops=1000, bytes_accessed=1000, transcendentals=0),
     )(scalars, lag_weights, *extended, orders, tail, *own, *got)
 
@@ -294,45 +294,62 @@
     first_core = lax.axis_index("c") == 0
     last = group_count[0] - 2
 
-    def extend(acts):
-        outer = jnp.where(first_core, acts[:, 0:1], acts[:, 3:4])
-        ends, corners, outer = lax.optimization_barrier(
-            (
-                lax.dynamic_slice_in_dim(acts, last, 2, 0),
-                lax.dynamic_slice_in_dim(outer, last, 2, 0),
-                outer,
-            )
+    def sides(acts):
+        return (
+            jnp.where(first_core, acts[:, 3:4], acts[:, 0:1]),
+            jnp.where(first_core, acts[:, 0:1], acts[:, 3:4]),
         )
-        carried = fetch(ends, before_in_group)
-        across_before = fetch(corners, across_and_before)
-        across = fetch(outer, across_chips)
-        edge = jnp.concatenate(
-            [
-                jnp.where(first_core, carried[:, 3:4], carried[:, 0:1]),
-                jnp.where(first_core, acts[:, 3:4], acts[:, 0:1]),
-            ],
-            0,
-        )
-        beside = fetch(edge, sibling)
-        return carried, acts, beside, jnp.concatenate([across_before, across], 0)
+
+    def last_two(acts):
+        return lax.dynamic_slice_in_dim(acts, last, 2, 0)
 
     acts_one = norm_act(frames, gain_one)
-    parts = small_stage(z_stage(jnp.stack([own_half(kernel_one), own_half(kernel_two)])))
-    parts, extended_one = lax.optimization_barrier((parts, extend(acts_one)))
+    own = jnp.stack([own_half(kernel_one), own_half(kernel_two)])
+    pieces = z_stage(own)
+    inner, outer = sides(acts_one)
+    beside, across = fetch(inner, sibling), fetch(outer, across_chips)
+    pieces, beside, across, orders, lag_weights, scalars = lax.optimization_barrier(
+        (pieces, beside, across, orders, lag_weights, scalars)
+    )
+
+    parts = small_stage(pieces)
     one_bundle, two_bundle = join_rows(parts, 0), join_rows(parts, 1)
     one_bundles = bulk_stage(one_bundle)
+    ends = jnp.concatenate([last_two(acts_one), last_two(beside), last_two(across)], 1)
+    ends, _ = lax.optimization_barrier((ends, one_bundle))
+    ends = fetch(ends, before_in_group)
+    extended = (
+        ends[:, 0:4],
+        acts_one,
+        jnp.concatenate([ends[:, 4:5], beside], 0),
+        jnp.concatenate([ends[:, 5:6], across], 0),
+    )
+    one_bundles, two_bundle, extended = lax.optimization_barrier(
+        (one_bundles, two_bundle, extended)
+    )
+    one_others = [fetch(b, sibling) for b in one_bundles]
+
+    two_bundle, one_others[1] = lax.optimization_barrier((two_bundle, one_others[1]))
     two_bundles = bulk_stage(two_bundle)
-    one_bundles, two_bundle = lax.optimization_barrier((one_bundles, two_bundle))
-    one_others = [fetch(b, sibling) for b in one_bundles]
-
     acts_two = conv(
-        scalars, lag_weights, extended_one, orders, gain_two.reshape(1, C),
+        scalars, lag_weights, extended, orders, gain_two.reshape(1, C),
         one_bundles, one_others, finish_norm,
     ).reshape(frames.shape)
+
     two_bundles, acts_two = lax.optimization_barrier((two_bundles, acts_two))
-    extended = extend(acts_two)
-    two_bundles, extended = lax.optimization_barrier((two_bundles, extended))
-    two_others = [fetch(b, sibling) for b in two_bundles]
+    two_others = [fetch(b, sibling) for b in two_bundles[:2]]
+    inner, outer = sides(acts_two)
+    ends, corners, outer = lax.optimization_barrier((last_two(acts_two), last_two(outer), outer))
+    carried = fetch(ends, before_in_group)
+    corners = fetch(corners, across_and_before)
+    across = fetch(outer, across_chips)
+    carried, corners, across, two_last = lax.optimization_barrier(
+        (carried, corners, across, two_bundles[2:])
+    )
+    edge = jnp.concatenate([sides(carried)[0], inner], 0)
+    beside = fetch(edge, sibling)
+    two_others += [fetch(b, sibling) for b in two_last]
+    extended = (carried, acts_two, beside, jnp.concatenate([corners, across], 0))
     result = conv(
         scalars, lag_weights, extended, orders, frames.reshape(slots, 128, C),
         two_bundles, two_others, finish_add,

time: 142 us -> 126 us (0.89)
  waiting for transfers between devices: 46.4 us -> 34.3 us
  local copies, waits for them, and re-layouts: 6.96 us -> 3.06 us
    ppermute x27 -> x26, waiting for transfers between devices: 46.4 us -> 34.3 us  [fetch(): return lax.ppermute(array, AXES, pairs)]
    unnamed x35 -> x19, local copies, waits for them, and re-layouts: 4 us -> 0.07 us
    ppermute x27 -> x26, starting transfers between devices: 54.1 us -> 54 us  [fetch(): return lax.ppermute(array, AXES, pairs)]
  transfers between devices with their start and end apart: 27 -> 26, of which waited for: 15 -> 8; matrix products, arithmetic and copies ran while one was open for 2% -> 3% of each run, Pallas kernels for 10% -> 12%
where the time goes in v4:
time: 126 us; the launch traced here: 125 us
  starting transfers between devices  54 us (43%)
  waiting for transfers between devices  34.3 us (27%)
  Pallas kernels  30.1 us (24%)
  local copies, waits for them, and re-layouts  3.06 us (2%)
  between operations  2 us (2%)
  other arithmetic  1.74 us (1%)
    ppermute x26, starting transfers between devices, fetch(): return lax.ppermute(array, AXES, pairs)  54 us
    ppermute x26, waiting for transfers between devices, fetch(): return lax.ppermute(array, AXES, pairs)  34.3 us
    pallas_call x2, Pallas kernels, conv(): pl.pallas_call(lambda *refs: conv_body(*refs, finish=finish), out_shape=j...  29.7 us
  transfers between devices with their start and end apart: 26, of which 8 were waited for; matrix products, arithmetic and copies ran while one was open for 3% of the time, Pallas kernels for 12%

profile of v4, /device:TPU:131, one launch (start us, length us, event | category | flops | bytes accessed | tf_op | source)
XLA Modules:
  0.0 125.1 jit_solution(3129541881928992930)
XLA Ops:
  0.0 1.1 constant_dynamic-slice_fusion.5
  1.3 1.9 %collective-permute-start = (bf16[2,168,384]{2,1,0:T(8,128)(2,1)S(1)}, bf16[2,168,384]{2,1,0:T(8,128)(2,1)S(1)}, u32[]{:S(2)}, u32[]{:S(2)}) collective-permute-start(bf16[2,168,384]{2,1,0:T(8,128)(2,1)S(1)} %constant_dynamic-update-slice_fusion), channel_id=1, source_target_pairs={{152,0},{1,1},{58,2},{67,3},{252,4},{37,5},{94,6},{103,7},{128,8},... | collective-permute-start | bytes 774152 | tf_op jit(solution)/shard_map/ppermute | solution.py:34
  3.2 2.4 %collective-permute-start.1 = (bf16[2,168,384]{2,1,0:T(8,128)(2,1)S(1)}, bf16[2,168,384]{2,1,0:T(8,128)(2,1)S(1)}, u32[]{:S(2)}, u32[]{:S(2)}) collective-permute-start(bf16[2,168,384]{2,1,0:T(8,128)(2,1)S(1)} %constant_dynamic-update-slice_fusion), channel_id=1, source_target_pairs={{24,0},{129,1},{122,2},{195,3},{188,4},{165,5},{222,6},{231,7},{0,... | collective-permute-start | bytes 774152 | tf_op jit(solution)/shard_map/ppermute | solution.py:34
  5.9 0.4 fusion.7.refs_3_
  6.4 1.0 collective-permute-start.2
  7.4 4.8 %collective-permute-start.3 = (bf16[6,1,32,384]{3,2,1,0:T(8,128)(2,1)S(1)}, bf16[6,1,32,384]{3,2,1,0:T(8,128)(2,1)S(1)}, u32[]{:S(2)}, u32[]{:S(2)}) collective-permute-start(bf16[6,1,32,384]{3,2,1,0:T(8,128)(2,1)S(1)} %get-tuple-element.73), channel_id=1, source_target_pairs={{2,1},{1,2},{4,3},{3,4},{6,5},{5,6},{10,9},{9,10},{12,11},{11,12},... | collective-permute-start | bytes 442376 | tf_op jit(solution)/shard_map/ppermute | solution.py:34
  12.3 0.6 gather_fusion
  13.3 0.6 gather_fusion.1
  16.2 2.4 %collective-permute-start.4 = (bf16[2,2,168,384]{3,2,1,0:T(8,128)(2,1)S(1)}, bf16[2,2,168,384]{3,2,1,0:T(8,128)(2,1)S(1)}, u32[]{:S(2)}, u32[]{:S(2)}) collective-permute-start(bf16[2,2,168,384]{3,2,1,0:T(8,128)(2,1)S(1)} %pad_maximum_fusion.refs_0_), channel_id=1, source_target_pairs={{2,0},{9,1},{4,2},{11,3},{6,4},{13,5},{0,6},{15,7},{10,8},{17,9},{... | collective-permute-start | bytes 1548296 | tf_op jit(solution)/shard_map/ppermute | solution.py:34
  18.6 1.3 %collective-permute-start.6 = (bf16[2,2,168,384]{3,2,1,0:T(8,128)(2,1)S(1)}, bf16[2,2,168,384]{3,2,1,0:T(8,128)(2,1)S(1)}, u32[]{:S(2)}, u32[]{:S(2)}) collective-permute-start(bf16[2,2,168,384]{3,2,1,0:T(8,128)(2,1)S(1)} %pad_maximum_fusion.refs_0_), channel_id=1, source_target_pairs={{4,0},{17,1},{6,2},{19,3},{0,4},{21,5},{2,6},{23,7},{12,8},{25,9},... | collective-permute-start | bytes 1548296 | tf_op jit(solution)/shard_map/ppermute | solution.py:34
  19.9 10.3 %collective-permute-done.4.refs_1_ = bf16[2,2,168,384]{3,2,1,0:T(8,128)(2,1)S(1)} collective-permute-done((bf16[2,2,168,384]{3,2,1,0:T(8,128)(2,1)S(1)}, bf16[2,2,168,384]{3,2,1,0:T(8,128)(2,1)S(1)}, u32[]{:S(2)}, u32[]{:S(2)}) %collective-permute-start.4) | collective-permute-done | bytes 516128 | tf_op jit(solution)/shard_map/ppermute | solution.py:34
  30.2 3.1 %collective-permute-done.5.refs_2_ = bf16[2,2,168,384]{3,2,1,0:T(8,128)(2,1)S(1)} collective-permute-done((bf16[2,2,168,384]{3,2,1,0:T(8,128)(2,1)S(1)}, bf16[2,2,168,384]{3,2,1,0:T(8,128)(2,1)S(1)}, u32[]{:S(2)}, u32[]{:S(2)}) %collective-permute-start.5) | collective-permute-done | bytes 516128 | tf_op jit(solution)/shard_map/ppermute | solution.py:34
  33.6 6.6 %collective-permute-start.8 = (bf16[14,96,384]{2,1,0:T(8,128)(2,1)S(1)}, bf16[14,96,384]{2,1,0:T(8,128)(2,1)S(1)}, u32[]{:S(2)}, u32[]{:S(2)}) collective-permute-start(bf16[14,96,384]{2,1,0:T(8,128)(2,1)S(1)} %shard_map.127.refs_8_), channel_id=1, source_target_pairs={{24,0},{7,1},{26,2},{1,3},{28,4},{3,5},{30,6},{5,7},{0,8},{15,9},{... | collective-permute-start | bytes 3096584 | tf_op jit(solution)/shard_map/ppermute | solution.py:34
  40.2 1.9 %collective-permute-start.10 = (bf16[2,6,32,384]{3,2,1,0:T(8,128)(2,1)S(1)}, bf16[2,6,32,384]{3,2,1,0:T(8,128)(2,1)S(1)}, u32[]{:S(2)}, u32[]{:S(2)}) collective-permute-start(bf16[2,6,32,384]{3,2,1,0:T(8,128)(2,1)S(1)} %pad_maximum_fusion.1), channel_id=1, source_target_pairs={{0,8},{1,9},{2,10},{3,11},{4,12},{5,13},{6,14},{7,15},{8,16},{9,17... | collective-permute-start | bytes 884744 | tf_op jit(solution)/shard_map/ppermute | solution.py:34
  42.4 9.7 %collective-permute-done.10 = bf16[2,6,32,384]{3,2,1,0:T(8,128)(2,1)S(1)} collective-permute-done((bf16[2,6,32,384]{3,2,1,0:T(8,128)(2,1)S(1)}, bf16[2,6,32,384]{3,2,1,0:T(8,128)(2,1)S(1)}, u32[]{:S(2)}, u32[]{:S(2)}) %collective-permute-start.10) | collective-permute-done | bytes 294944 | tf_op jit(solution)/shard_map/ppermute | solution.py:34
  52.2 0.4 collective-permute-done.7.refs_9_
  52.6 1.3 %collective-permute-done.9.refs_11_ = bf16[14,96,384]{2,1,0:T(8,128)(2,1)S(1)} collective-permute-done((bf16[14,96,384]{2,1,0:T(8,128)(2,1)S(1)}, bf16[14,96,384]{2,1,0:T(8,128)(2,1)S(1)}, u32[]{:S(2)}, u32[]{:S(2)}) %collective-permute-start.9) | collective-permute-done | bytes 1032224 | tf_op jit(solution)/shard_map/ppermute | solution.py:34
  53.9 12.3 %collective-permute-start.11 = (bf16[14,96,384]{2,1,0:T(8,128)(2,1)S(1)}, bf16[14,96,384]{2,1,0:T(8,128)(2,1)S(1)}, u32[]{:S(2)}, u32[]{:S(2)}) collective-permute-start(bf16[14,96,384]{2,1,0:T(8,128)(2,1)S(1)} %collective-permute-done.7.refs_9_), channel_id=1, source_target_pairs={{1,0},{0,1},{3,2},{2,3},{5,4},{4,5},{7,6},{6,7},{9,8},{8,9},{11,10... | collective-permute-start | bytes 3096584 | tf_op jit(solution)/shard_map/ppermute | solution.py:34
  66.3 0.4 collective-permute-start.16
  66.8 1.7 %collective-permute-done.11.refs_13_ = bf16[14,96,384]{2,1,0:T(8,128)(2,1)S(1)} collective-permute-done((bf16[14,96,384]{2,1,0:T(8,128)(2,1)S(1)}, bf16[14,96,384]{2,1,0:T(8,128)(2,1)S(1)}, u32[]{:S(2)}, u32[]{:S(2)}) %collective-permute-start.11) | collective-permute-done | bytes 1032224 | tf_op jit(solution)/shard_map/ppermute | solution.py:34
  68.5 1.3 %collective-permute-start.12 = (bf16[14,96,384]{2,1,0:T(8,128)(2,1)S(1)}, bf16[14,96,384]{2,1,0:T(8,128)(2,1)S(1)}, u32[]{:S(2)}, u32[]{:S(2)}) collective-permute-start(bf16[14,96,384]{2,1,0:T(8,128)(2,1)S(1)} %shard_map.128.refs_8_), channel_id=1, source_target_pairs={{8,0},{3,1},{10,2},{5,3},{12,4},{7,5},{14,6},{1,7},{16,8},{11,9},{... | collective-permute-start | bytes 3096584 | tf_op jit(solution)/shard_map/ppermute | solution.py:34
  69.9 4.1 %collective-permute-start.14 = (bf16[14,96,384]{2,1,0:T(8,128)(2,1)S(1)}, bf16[14,96,384]{2,1,0:T(8,128)(2,1)S(1)}, u32[]{:S(2)}, u32[]{:S(2)}) collective-permute-start(bf16[14,96,384]{2,1,0:T(8,128)(2,1)S(1)} %shard_map.128.refs_8_), channel_id=1, source_target_pairs={{224,0},{33,1},{226,2},{35,3},{228,4},{37,5},{230,6},{39,7},{232,8... | collective-permute-start | bytes 3096584 | tf_op jit(solution)/shard_map/ppermute | solution.py:34
  74.1 14.6 %shard_map.129 = bf16[6,128,384]{2,1,0:T(8,128)(2,1)S(1)} custom-call(s32[2]{0:T(128)S(1)} %pad_add_fusion.1.refs_0_, f32[3,6]{1,0:T(4,128)S(1)} %add_convert_fusion.refs_1_, bf16[2,4,32,384]{3,2,1,0:T(8,128)(2,1)S(1)} %slice.54.refs_2_, bf16[6,4,32,384]{3,2,1,0:T(8,128)(2,1)S(1)} %fusion.7.refs_3_, bf16[8,1,32,384]{3,2,1,0:T(8,128)(2,1)S(1)} %pad_maximum_fusion.2.refs_4_, ...), custom_call_target="tpu_custom_call" | custom-call | flops 1000 | bytes 1000 | tf_op jit(solution)/shard_map/pallas_call | solution.py:239
  88.8 1.9 %collective-permute-start.18 = (bf16[2,4,32,384]{3,2,1,0:T(8,128)(2,1)S(1)}, bf16[2,4,32,384]{3,2,1,0:T(8,128)(2,1)S(1)}, u32[]{:S(2)}, u32[]{:S(2)}) collective-permute-start(bf16[2,4,32,384]{3,2,1,0:T(8,128)(2,1)S(1)} %constant_dynamic-slice_fusion.1), channel_id=1, source_target_pairs={{0,8},{1,9},{2,10},{3,11},{4,12},{5,13},{6,14},{7,15},{8,16},{9,17... | collective-permute-start | bytes 589832 | tf_op jit(solution)/shard_map/ppermute | solution.py:34
  90.7 2.3 %collective-permute-start.20 = (bf16[6,1,32,384]{3,2,1,0:T(8,128)(2,1)S(1)}, bf16[6,1,32,384]{3,2,1,0:T(8,128)(2,1)S(1)}, u32[]{:S(2)}, u32[]{:S(2)}) collective-permute-start(bf16[6,1,32,384]{3,2,1,0:T(8,128)(2,1)S(1)} %get-tuple-element.57), channel_id=1, source_target_pairs={{2,1},{1,2},{4,3},{3,4},{6,5},{5,6},{10,9},{9,10},{12,11},{11,12},... | collective-permute-start | bytes 442376 | tf_op jit(solution)/shard_map/ppermute | solution.py:34
  93.1 1.9 %collective-permute-start.19 = (bf16[2,1,32,384]{3,2,1,0:T(8,128)(2,1)S(1)}, bf16[2,1,32,384]{3,2,1,0:T(8,128)(2,1)S(1)}, u32[]{:S(2)}, u32[]{:S(2)}) collective-permute-start(bf16[2,1,32,384]{3,2,1,0:T(8,128)(2,1)S(1)} %constant_dynamic-slice_fusion), channel_id=1, source_target_pairs={{2,9},{1,10},{4,11},{3,12},{6,13},{5,14},{10,17},{9,18},{12,19},{1... | collective-permute-start | bytes 147464 | tf_op jit(solution)/shard_map/ppermute | solution.py:34
  95.0 3.2 %collective-permute-start.22 = (bf16[14,96,384]{2,1,0:T(8,128)(2,1)S(1)}, bf16[14,96,384]{2,1,0:T(8,128)(2,1)S(1)}, u32[]{:S(2)}, u32[]{:S(2)}) collective-permute-start(bf16[14,96,384]{2,1,0:T(8,128)(2,1)S(1)} %shard_map.128.refs_8_), channel_id=1, source_target_pairs={{1,0},{0,1},{3,2},{2,3},{5,4},{4,5},{7,6},{6,7},{9,8},{8,9},{11,10... | collective-permute-start | bytes 3096584 | tf_op jit(solution)/shard_map/ppermute | solution.py:34
  98.3 4.5 %collective-permute-done.19 = bf16[2,1,32,384]{3,2,1,0:T(8,128)(2,1)S(1)} collective-permute-done((bf16[2,1,32,384]{3,2,1,0:T(8,128)(2,1)S(1)}, bf16[2,1,32,384]{3,2,1,0:T(8,128)(2,1)S(1)}, u32[]{:S(2)}, u32[]{:S(2)}) %collective-permute-start.19) | collective-permute-done | bytes 49184 | tf_op jit(solution)/shard_map/ppermute | solution.py:34
  102.7 3.1 %collective-permute-start.24 = (bf16[14,96,384]{2,1,0:T(8,128)(2,1)S(1)}, bf16[14,96,384]{2,1,0:T(8,128)(2,1)S(1)}, u32[]{:S(2)}, u32[]{:S(2)}) collective-permute-start(bf16[14,96,384]{2,1,0:T(8,128)(2,1)S(1)} %collective-permute-done.13.refs_10_), channel_id=1, source_target_pairs={{1,0},{0,1},{3,2},{2,3},{5,4},{4,5},{7,6},{6,7},{9,8},{8,9},{11,10... | collective-permute-start | bytes 3096584 | tf_op jit(solution)/shard_map/ppermute | solution.py:34
  106.0 0.5 collective-permute-start.21
  106.5 3.3 %collective-permute-done.21.refs_4_ = bf16[8,1,32,384]{3,2,1,0:T(8,128)(2,1)S(1)} collective-permute-done((bf16[8,1,32,384]{3,2,1,0:T(8,128)(2,1)S(1)}, bf16[8,1,32,384]{3,2,1,0:T(8,128)(2,1)S(1)}, u32[]{:S(2)}, u32[]{:S(2)}) %collective-permute-start.21) | collective-permute-done | bytes 196640 | tf_op jit(solution)/shard_map/ppermute | solution.py:34
  109.9 15.1 %shard_map.130 = bf16[6,128,384]{2,1,0:T(8,128)(2,1)} custom-call(s32[2]{0:T(128)S(1)} %pad_add_fusion.1.refs_0_, f32[3,6]{1,0:T(4,128)S(1)} %add_convert_fusion.refs_1_, bf16[2,4,32,384]{3,2,1,0:T(8,128)(2,1)S(1)} %collective-permute-done.18.refs_2_, bf16[6,4,32,384]{3,2,1,0:T(8,128)(2,1)S(1)} %bitcast.28, ...), custom_call_target="tpu_custom_call" | custom-call | flops 1000 | bytes 1000 | tf_op jit(solution)/shard_map/pallas_call | solution.py:239
  (92 shorter events, 3.3 us)
Async XLA Ops:
  1.3 14.9 %collective-permute-start = (bf16[2,168,384]{2,1,0:T(8,128)(2,1)S(1)}, bf16[2,168,384]{2,1,0:T(8,128)(2,1)S(1)}, u32[]{:S(2)}, u32[]{:S(2)}) collective-permute-start(bf16[2,168,384]{2,1,0:T(8,128)(2,1)S(1)} %constant_dynamic-update-slice_fusion), channel_id=1, source_target_pairs={{152,0},{1,1},{58,2},{67,3},{252,4},{37,5},{94,6},{103,7},{128,8},... | collective-permute-start | bytes 774152 | tf_op jit(solution)/shard_map/ppermute | solution.py:34
  3.2 13.0 %collective-permute-start.1 = (bf16[2,168,384]{2,1,0:T(8,128)(2,1)S(1)}, bf16[2,168,384]{2,1,0:T(8,128)(2,1)S(1)}, u32[]{:S(2)}, u32[]{:S(2)}) collective-permute-start(bf16[2,168,384]{2,1,0:T(8,128)(2,1)S(1)} %constant_dynamic-update-slice_fusion), channel_id=1, source_target_pairs={{24,0},{129,1},{122,2},{195,3},{188,4},{165,5},{222,6},{231,7},{0,... | collective-permute-start | bytes 774152 | tf_op jit(solution)/shard_map/ppermute | solution.py:34
  5.8 6.4 %copy-start.6 = (s32[4]{0:T(128)S(1)}, s32[4]{0:T(128)}, u32[]{:S(2)}) copy-start(s32[4]{0:T(128)} %constant.152.clone) | copy-start | bytes 52
  5.8 6.4 %copy-start.7 = (s32[4]{0:T(128)S(1)}, s32[4]{0:T(128)}, u32[]{:S(2)}) copy-start(s32[4]{0:T(128)} %constant.150.clone) | copy-start | bytes 52
  5.8 6.5 %copy-start.2 = (s32[4,2]{1,0:T(4,128)S(1)}, s32[4,2]{1,0:T(4,128)}, u32[]{:S(2)}) copy-start(s32[4,2]{1,0:T(4,128)} %constant.159) | copy-start | bytes 100
  5.9 7.5 %copy-start.1 = (s32[4,2]{1,0:T(4,128)S(1)}, s32[4,2]{1,0:T(4,128)}, u32[]{:S(2)}) copy-start(s32[4,2]{1,0:T(4,128)} %constant.161) | copy-start | bytes 100
  5.9 9.0 %copy-start.8 = (s32[3]{0:T(128)S(1)}, s32[3]{0:T(128)}, u32[]{:S(2)}) copy-start(s32[3]{0:T(128)} %param.14) | copy-start | bytes 40
  6.4 9.8 %collective-permute-start.2 = (bf16[6,1,32,384]{3,2,1,0:T(8,128)(2,1)S(1)}, bf16[6,1,32,384]{3,2,1,0:T(8,128)(2,1)S(1)}, u32[]{:S(2)}, u32[]{:S(2)}) collective-permute-start(bf16[6,1,32,384]{3,2,1,0:T(8,128)(2,1)S(1)} %get-tuple-element.74), channel_id=1, source_target_pairs={{1,0},{0,1},{3,2},{2,3},{5,4},{4,5},{7,6},{6,7},{9,8},{8,9},{11,10... | collective-permute-start | bytes 442376 | tf_op jit(solution)/shard_map/ppermute | solution.py:34
  7.4 8.9 %collective-permute-start.3 = (bf16[6,1,32,384]{3,2,1,0:T(8,128)(2,1)S(1)}, bf16[6,1,32,384]{3,2,1,0:T(8,128)(2,1)S(1)}, u32[]{:S(2)}, u32[]{:S(2)}) collective-permute-start(bf16[6,1,32,384]{3,2,1,0:T(8,128)(2,1)S(1)} %get-tuple-element.73), channel_id=1, source_target_pairs={{2,1},{1,2},{4,3},{3,4},{6,5},{5,6},{10,9},{9,10},{12,11},{11,12},... | collective-permute-start | bytes 442376 | tf_op jit(solution)/shard_map/ppermute | solution.py:34
  16.2 13.9 %collective-permute-start.4 = (bf16[2,2,168,384]{3,2,1,0:T(8,128)(2,1)S(1)}, bf16[2,2,168,384]{3,2,1,0:T(8,128)(2,1)S(1)}, u32[]{:S(2)}, u32[]{:S(2)}) collective-permute-start(bf16[2,2,168,384]{3,2,1,0:T(8,128)(2,1)S(1)} %pad_maximum_fusion.refs_0_), channel_id=1, source_target_pairs={{2,0},{9,1},{4,2},{11,3},{6,4},{13,5},{0,6},{15,7},{10,8},{17,9},{... | collective-permute-start | bytes 1548296 | tf_op jit(solution)/shard_map/ppermute | solution.py:34
  18.6 14.7 %collective-permute-start.5 = (bf16[2,2,168,384]{3,2,1,0:T(8,128)(2,1)S(1)}, bf16[2,2,168,384]{3,2,1,0:T(8,128)(2,1)S(1)}, u32[]{:S(2)}, u32[]{:S(2)}) collective-permute-start(bf16[2,2,168,384]{3,2,1,0:T(8,128)(2,1)S(1)} %pad_maximum_fusion.refs_0_), channel_id=1, source_target_pairs={{6,0},{25,1},{0,2},{27,3},{2,4},{29,5},{4,6},{31,7},{14,8},{1,9},{... | collective-permute-start | bytes 1548296 | tf_op jit(solution)/shard_map/ppermute | solution.py:34
  18.6 14.7 %collective-permute-start.6 = (bf16[2,2,168,384]{3,2,1,0:T(8,128)(2,1)S(1)}, bf16[2,2,168,384]{3,2,1,0:T(8,128)(2,1)S(1)}, u32[]{:S(2)}, u32[]{:S(2)}) collective-permute-start(bf16[2,2,168,384]{3,2,1,0:T(8,128)(2,1)S(1)} %pad_maximum_fusion.refs_0_), channel_id=1, source_target_pairs={{4,0},{17,1},{6,2},{19,3},{0,4},{21,5},{2,6},{23,7},{12,8},{25,9},... | collective-permute-start | bytes 1548296 | tf_op jit(solution)/shard_map/ppermute | solution.py:34
  33.5 19.1 %collective-permute-start.7 = (bf16[14,96,384]{2,1,0:T(8,128)(2,1)S(1)}, bf16[14,96,384]{2,1,0:T(8,128)(2,1)S(1)}, u32[]{:S(2)}, u32[]{:S(2)}) collective-permute-start(bf16[14,96,384]{2,1,0:T(8,128)(2,1)S(1)} %shard_map.127.refs_8_), channel_id=1, source_target_pairs={{8,0},{3,1},{10,2},{5,3},{12,4},{7,5},{14,6},{1,7},{16,8},{11,9},{... | collective-permute-start | bytes 3096584 | tf_op jit(solution)/shard_map/ppermute | solution.py:34
  33.6 19.0 %collective-permute-start.8 = (bf16[14,96,384]{2,1,0:T(8,128)(2,1)S(1)}, bf16[14,96,384]{2,1,0:T(8,128)(2,1)S(1)}, u32[]{:S(2)}, u32[]{:S(2)}) collective-permute-start(bf16[14,96,384]{2,1,0:T(8,128)(2,1)S(1)} %shard_map.127.refs_8_), channel_id=1, source_target_pairs={{24,0},{7,1},{26,2},{1,3},{28,4},{3,5},{30,6},{5,7},{0,8},{15,9},{... | collective-permute-start | bytes 3096584 | tf_op jit(solution)/shard_map/ppermute | solution.py:34
  40.1 13.8 %collective-permute-start.9 = (bf16[14,96,384]{2,1,0:T(8,128)(2,1)S(1)}, bf16[14,96,384]{2,1,0:T(8,128)(2,1)S(1)}, u32[]{:S(2)}, u32[]{:S(2)}) collective-permute-start(bf16[14,96,384]{2,1,0:T(8,128)(2,1)S(1)} %shard_map.127.refs_8_), channel_id=1, source_target_pairs={{224,0},{33,1},{226,2},{35,3},{228,4},{37,5},{230,6},{39,7},{232,8... | collective-permute-start | bytes 3096584 | tf_op jit(solution)/shard_map/ppermute | solution.py:34
  40.2 11.8 %collective-permute-start.10 = (bf16[2,6,32,384]{3,2,1,0:T(8,128)(2,1)S(1)}, bf16[2,6,32,384]{3,2,1,0:T(8,128)(2,1)S(1)}, u32[]{:S(2)}, u32[]{:S(2)}) collective-permute-start(bf16[2,6,32,384]{3,2,1,0:T(8,128)(2,1)S(1)} %pad_maximum_fusion.1), channel_id=1, source_target_pairs={{0,8},{1,9},{2,10},{3,11},{4,12},{5,13},{6,14},{7,15},{8,16},{9,17... | collective-permute-start | bytes 884744 | tf_op jit(solution)/shard_map/ppermute | solution.py:34
  42.4 31.7 %copy-start.4 = (f32[384]{0:T(512)S(1)}, f32[384]{0:T(512)}, u32[]{:S(2)}) copy-start(f32[384]{0:T(512)} %param.20) | copy-start | bytes 4612
  53.9 14.5 %collective-permute-start.11 = (bf16[14,96,384]{2,1,0:T(8,128)(2,1)S(1)}, bf16[14,96,384]{2,1,0:T(8,128)(2,1)S(1)}, u32[]{:S(2)}, u32[]{:S(2)}) collective-permute-start(bf16[14,96,384]{2,1,0:T(8,128)(2,1)S(1)} %collective-permute-done.7.refs_9_), channel_id=1, source_target_pairs={{1,0},{0,1},{3,2},{2,3},{5,4},{4,5},{7,6},{6,7},{9,8},{8,9},{11,10... | collective-permute-start | bytes 3096584 | tf_op jit(solution)/shard_map/ppermute | solution.py:34
  66.2 3.7 %collective-permute-start.15 = (bf16[14,96,384]{2,1,0:T(8,128)(2,1)S(1)}, bf16[14,96,384]{2,1,0:T(8,128)(2,1)S(1)}, u32[]{:S(2)}, u32[]{:S(2)}) collective-permute-start(bf16[14,96,384]{2,1,0:T(8,128)(2,1)S(1)} %shard_map.127.refs_8_), channel_id=1, source_target_pairs={{1,0},{0,1},{3,2},{2,3},{5,4},{4,5},{7,6},{6,7},{9,8},{8,9},{11,10... | collective-permute-start | bytes 3096584 | tf_op jit(solution)/shard_map/ppermute | solution.py:34
  66.3 7.8 %collective-permute-start.16 = (bf16[14,96,384]{2,1,0:T(8,128)(2,1)S(1)}, bf16[14,96,384]{2,1,0:T(8,128)(2,1)S(1)}, u32[]{:S(2)}, u32[]{:S(2)}) collective-permute-start(bf16[14,96,384]{2,1,0:T(8,128)(2,1)S(1)} %collective-permute-done.8.refs_10_), channel_id=1, source_target_pairs={{1,0},{0,1},{3,2},{2,3},{5,4},{4,5},{7,6},{6,7},{9,8},{8,9},{11,10... | collective-permute-start | bytes 3096584 | tf_op jit(solution)/shard_map/ppermute | solution.py:34
  66.7 7.4 %collective-permute-start.17 = (bf16[14,96,384]{2,1,0:T(8,128)(2,1)S(1)}, bf16[14,96,384]{2,1,0:T(8,128)(2,1)S(1)}, u32[]{:S(2)}, u32[]{:S(2)}) collective-permute-start(bf16[14,96,384]{2,1,0:T(8,128)(2,1)S(1)} %collective-permute-done.9.refs_11_), channel_id=1, source_target_pairs={{1,0},{0,1},{3,2},{2,3},{5,4},{4,5},{7,6},{6,7},{9,8},{8,9},{11,10... | collective-permute-start | bytes 3096584 | tf_op jit(solution)/shard_map/ppermute | solution.py:34
  68.5 20.2 %collective-permute-start.12 = (bf16[14,96,384]{2,1,0:T(8,128)(2,1)S(1)}, bf16[14,96,384]{2,1,0:T(8,128)(2,1)S(1)}, u32[]{:S(2)}, u32[]{:S(2)}) collective-permute-start(bf16[14,96,384]{2,1,0:T(8,128)(2,1)S(1)} %shard_map.128.refs_8_), channel_id=1, source_target_pairs={{8,0},{3,1},{10,2},{5,3},{12,4},{7,5},{14,6},{1,7},{16,8},{11,9},{... | collective-permute-start | bytes 3096584 | tf_op jit(solution)/shard_map/ppermute | solution.py:34
  69.7 18.9 %collective-permute-start.13 = (bf16[14,96,384]{2,1,0:T(8,128)(2,1)S(1)}, bf16[14,96,384]{2,1,0:T(8,128)(2,1)S(1)}, u32[]{:S(2)}, u32[]{:S(2)}) collective-permute-start(bf16[14,96,384]{2,1,0:T(8,128)(2,1)S(1)} %shard_map.128.refs_8_), channel_id=1, source_target_pairs={{24,0},{7,1},{26,2},{1,3},{28,4},{3,5},{30,6},{5,7},{0,8},{15,9},{... | collective-permute-start | bytes 3096584 | tf_op jit(solution)/shard_map/ppermute | solution.py:34
  69.9 18.8 %collective-permute-start.14 = (bf16[14,96,384]{2,1,0:T(8,128)(2,1)S(1)}, bf16[14,96,384]{2,1,0:T(8,128)(2,1)S(1)}, u32[]{:S(2)}, u32[]{:S(2)}) collective-permute-start(bf16[14,96,384]{2,1,0:T(8,128)(2,1)S(1)} %shard_map.128.refs_8_), channel_id=1, source_target_pairs={{224,0},{33,1},{226,2},{35,3},{228,4},{37,5},{230,6},{39,7},{232,8... | collective-permute-start | bytes 3096584 | tf_op jit(solution)/shard_map/ppermute | solution.py:34
  88.8 14.0 %collective-permute-start.18 = (bf16[2,4,32,384]{3,2,1,0:T(8,128)(2,1)S(1)}, bf16[2,4,32,384]{3,2,1,0:T(8,128)(2,1)S(1)}, u32[]{:S(2)}, u32[]{:S(2)}) collective-permute-start(bf16[2,4,32,384]{3,2,1,0:T(8,128)(2,1)S(1)} %constant_dynamic-slice_fusion.1), channel_id=1, source_target_pairs={{0,8},{1,9},{2,10},{3,11},{4,12},{5,13},{6,14},{7,15},{8,16},{9,17... | collective-permute-start | bytes 589832 | tf_op jit(solution)/shard_map/ppermute | solution.py:34
  90.7 12.0 %collective-permute-start.20 = (bf16[6,1,32,384]{3,2,1,0:T(8,128)(2,1)S(1)}, bf16[6,1,32,384]{3,2,1,0:T(8,128)(2,1)S(1)}, u32[]{:S(2)}, u32[]{:S(2)}) collective-permute-start(bf16[6,1,32,384]{3,2,1,0:T(8,128)(2,1)S(1)} %get-tuple-element.57), channel_id=1, source_target_pairs={{2,1},{1,2},{4,3},{3,4},{6,5},{5,6},{10,9},{9,10},{12,11},{11,12},... | collective-permute-start | bytes 442376 | tf_op jit(solution)/shard_map/ppermute | solution.py:34
  93.1 9.7 %collective-permute-start.19 = (bf16[2,1,32,384]{3,2,1,0:T(8,128)(2,1)S(1)}, bf16[2,1,32,384]{3,2,1,0:T(8,128)(2,1)S(1)}, u32[]{:S(2)}, u32[]{:S(2)}) collective-permute-start(bf16[2,1,32,384]{3,2,1,0:T(8,128)(2,1)S(1)} %constant_dynamic-slice_fusion), channel_id=1, source_target_pairs={{2,9},{1,10},{4,11},{3,12},{6,13},{5,14},{10,17},{9,18},{12,19},{1... | collective-permute-start | bytes 147464 | tf_op jit(solution)/shard_map/ppermute | solution.py:34
  95.0 14.8 %collective-permute-start.22 = (bf16[14,96,384]{2,1,0:T(8,128)(2,1)S(1)}, bf16[14,96,384]{2,1,0:T(8,128)(2,1)S(1)}, u32[]{:S(2)}, u32[]{:S(2)}) collective-permute-start(bf16[14,96,384]{2,1,0:T(8,128)(2,1)S(1)} %shard_map.128.refs_8_), channel_id=1, source_target_pairs={{1,0},{0,1},{3,2},{2,3},{5,4},{4,5},{7,6},{6,7},{9,8},{8,9},{11,10... | collective-permute-start | bytes 3096584 | tf_op jit(solution)/shard_map/ppermute | solution.py:34
  98.2 11.6 %collective-permute-start.23 = (bf16[14,96,384]{2,1,0:T(8,128)(2,1)S(1)}, bf16[14,96,384]{2,1,0:T(8,128)(2,1)S(1)}, u32[]{:S(2)}, u32[]{:S(2)}) collective-permute-start(bf16[14,96,384]{2,1,0:T(8,128)(2,1)S(1)} %collective-permute-done.12.refs_9_), channel_id=1, source_target_pairs={{1,0},{0,1},{3,2},{2,3},{5,4},{4,5},{7,6},{6,7},{9,8},{8,9},{11,10... | collective-permute-start | bytes 3096584 | tf_op jit(solution)/shard_map/ppermute | solution.py:34
  102.7 7.1 %collective-permute-start.24 = (bf16[14,96,384]{2,1,0:T(8,128)(2,1)S(1)}, bf16[14,96,384]{2,1,0:T(8,128)(2,1)S(1)}, u32[]{:S(2)}, u32[]{:S(2)}) collective-permute-start(bf16[14,96,384]{2,1,0:T(8,128)(2,1)S(1)} %collective-permute-done.13.refs_10_), channel_id=1, source_target_pairs={{1,0},{0,1},{3,2},{2,3},{5,4},{4,5},{7,6},{6,7},{9,8},{8,9},{11,10... | collective-permute-start | bytes 3096584 | tf_op jit(solution)/shard_map/ppermute | solution.py:34
  105.8 4.0 %collective-permute-start.25 = (bf16[14,96,384]{2,1,0:T(8,128)(2,1)S(1)}, bf16[14,96,384]{2,1,0:T(8,128)(2,1)S(1)}, u32[]{:S(2)}, u32[]{:S(2)}) collective-permute-start(bf16[14,96,384]{2,1,0:T(8,128)(2,1)S(1)} %collective-permute-done.14.refs_11_), channel_id=1, source_target_pairs={{1,0},{0,1},{3,2},{2,3},{5,4},{4,5},{7,6},{6,7},{9,8},{8,9},{11,10... | collective-permute-start | bytes 3096584 | tf_op jit(solution)/shard_map/ppermute | solution.py:34
  106.0 3.9 %collective-permute-start.21 = (bf16[8,1,32,384]{3,2,1,0:T(8,128)(2,1)S(1)}, bf16[8,1,32,384]{3,2,1,0:T(8,128)(2,1)S(1)}, u32[]{:S(2)}, u32[]{:S(2)}) collective-permute-start(bf16[8,1,32,384]{3,2,1,0:T(8,128)(2,1)S(1)} %pad_maximum_fusion.4), channel_id=1, source_target_pairs={{1,0},{0,1},{3,2},{2,3},{5,4},{4,5},{7,6},{6,7},{9,8},{8,9},{11,10... | collective-permute-start | bytes 589832 | tf_op jit(solution)/shard_map/ppermute | solution.py:34
  (3 other events, 16.8 us)

commit v5 on v4

--- a/solution.py
+++ b/solution.py
@@ -118,9 +118,38 @@
     return jnp.stack([(half.reshape(-1, 1) * SHARD + ramp).reshape(C) for half in (first, second)])
 
 
+def permute_body(order, *refs):
+    out, top = refs[-1], 0
+    picks = [
+        (lax.broadcasted_iota(jnp.int32, (C, C), 0) == order[half : half + 1, :]).astype(jnp.bfloat16)
+        for half in range(2)
+    ]
+    for ref in refs[:-1]:
+        rows = ref.shape[0]
+        for half in range(2):
+            out[half, top : top + rows] = jnp.dot(
+                ref[...], picks[half], preferred_element_type=jnp.float32
+            ).astype(jnp.bfloat16)
+        top += rows
+
+
+def permute(orders, *arrays):
+    arrays = [array.reshape(-1, C) for array in arrays]
+    rows = sum(array.shape[0] for array in arrays)
+    vmem = pl.BlockSpec(memory_space=pltpu.VMEM)
+    return pl.pallas_call(
+        permute_body,
+        out_shape=jax.ShapeDtypeStruct((2, rows, C), jnp.bfloat16),
+        in_specs=[vmem] * (1 + len(arrays)),
+        out_specs=vmem,
+        compiler_params=pltpu.CompilerParams(vmem_limit_bytes=16 * 1024 * 1024),
+        cost_estimate=pl.CostEstimate(flops=1000, bytes_accessed=1000, transcendentals=0),
+    )(orders, *arrays)
+
+
 def conv_body(
-    scalars, lag_weights, carried, inner, beside, across, order, tail, own0, own1, own2, own3, got0, got1, got2, got3,
-    out, acts, spread, weights, total, sems, *, finish,
+    scalars, lag_weights, inner, halo, tail, own0, own1, own2, own3, got0, got1, got2, got3,
+    out, spread, weights, total, sems, *, finish,
 ):
     frames, rows, cols = 6, 4, 32
     own, got = (own0, own1, own2, own3), (got0, got1, got2, got3)
@@ -145,33 +174,28 @@
         for copy in copies(0, got) + copies(1, own):
             copy.start()
 
-    acts[0:2, 1:5] = carried[...]
-    acts[2:8, 1:5] = inner[...]
-
-    @pl.when(core == 0)
-    def _():
-        acts[:, 0:1] = across[...]
-        acts[:, 5:6] = beside[...]
-
-    @pl.when(core == 1)
-    def _():
-        acts[:, 0:1] = beside[...]
-        acts[:, 5:6] = across[...]
-
-    wide = acts.shape[0] * acts.shape[1]
-    col = lax.broadcasted_iota(jnp.int32, (wide * cols, C), 0) % cols
+    wide, tall = frames + 2, rows + 2
+    col = lax.broadcasted_iota(jnp.int32, (wide * tall * cols, C), 0) % cols
     for half in range(2):
-        pick = (
-            lax.broadcasted_iota(jnp.int32, (C, C), 0) == order[half : half + 1, :]
-        ).astype(jnp.bfloat16)
-        plain = jnp.dot(
-            acts[...].reshape(wide * cols, C), pick, preferred_element_type=jnp.float32
-        )
+        spread[half, 2:wide, 1:5, :, C : 2 * C] = inner[half].reshape(frames, rows, cols, C)
+        spread[half, 0:2, 1:5, :, C : 2 * C] = halo[half, 0:256].reshape(2, rows, cols, C)
+
+        @pl.when(core == 0)
+        def _():
+            spread[half, :, 5:6, :, C : 2 * C] = halo[half, 256:512].reshape(wide, 1, cols, C)
+            spread[half, :, 0:1, :, C : 2 * C] = halo[half, 512:768].reshape(wide, 1, cols, C)
+
+        @pl.when(core == 1)
+        def _():
+            spread[half, :, 0:1, :, C : 2 * C] = halo[half, 256:512].reshape(wide, 1, cols, C)
+            spread[half, :, 5:6, :, C : 2 * C] = halo[half, 512:768].reshape(wide, 1, cols, C)
+
+        plain = spread[half, :, :, :, C : 2 * C].reshape(wide * tall * cols, C).astype(jnp.float32)
         before = jnp.where(col == 0, 0.0, pltpu.roll(plain, 1, 0))
-        after = jnp.where(col == cols - 1, 0.0, pltpu.roll(plain, wide * cols - 1, 0))
-        for tap, moved in enumerate((before, plain, after)):
-            spread[half, :, :, :, pl.ds(C * tap, C)] = (
-                moved.astype(jnp.bfloat16).reshape(acts.shape)
+        after = jnp.where(col == cols - 1, 0.0, pltpu.roll(plain, wide * tall * cols - 1, 0))
+        for place, moved in ((0, before), (2 * C, after)):
+            spread[half, :, :, :, place : place + C] = (
+                moved.astype(jnp.bfloat16).reshape(wide, tall, cols, C)
             )
 
     total[...] = jnp.zeros_like(total)
@@ -233,16 +257,15 @@
         out[f] = jnp.where(f < scalars[1], summed, 0.0).astype(jnp.bfloat16)
 
 
-def conv(scalars, lag_weights, extended, orders, tail, own, got, finish):
+def conv(scalars, lag_weights, inner, halo, tail, own, got, finish):
     smem = pl.BlockSpec(memory_space=pltpu.SMEM)
     vmem = pl.BlockSpec(memory_space=pltpu.VMEM)
     return pl.pallas_call(
         lambda *refs: conv_body(*refs, finish=finish),
         out_shape=jax.ShapeDtypeStruct((6, 128, C), jnp.bfloat16),
-        in_specs=[smem, smem] + [vmem] * 6 + [pl.BlockSpec(memory_space=pl.ANY)] * 8,
+        in_specs=[smem, smem] + [vmem] * 3 + [pl.BlockSpec(memory_space=pl.ANY)] * 8,
         out_specs=vmem,
         scratch_shapes=[
-            pltpu.VMEM((8, 6, 32, C), jnp.bfloat16),
             pltpu.VMEM((2, 8, 6, 32, 3 * C), jnp.bfloat16),
             pltpu.VMEM((2, HALF, C, C), jnp.bfloat16),
             pltpu.VMEM((6, 128, C), jnp.float32),
@@ -250,7 +273,7 @@
         ],
         compiler_params=pltpu.CompilerParams(vmem_limit_bytes=26 * 1024 * 1024),
         cost_estimate=pl.CostEstimate(flops=1000, bytes_accessed=1000, transcendentals=0),
-    )(scalars, lag_weights, *extended, orders, tail, *own, *got)
+    )(scalars, lag_weights, inner, halo, tail, *own, *got)
 
 
 def clip_positions(clip_lengths, frame_index):
@@ -307,52 +330,58 @@
     own = jnp.stack([own_half(kernel_one), own_half(kernel_two)])
     pieces = z_stage(own)
     inner, outer = sides(acts_one)
-    beside, across = fetch(inner, sibling), fetch(outer, across_chips)
-    pieces, beside, across, orders, lag_weights, scalars = lax.optimization_barrier(
-        (pieces, beside, across, orders, lag_weights, scalars)
+    ends, corners, outer = lax.optimization_barrier((last_two(acts_one), last_two(outer), outer))
+    carried = fetch(ends, before_in_group)
+    across = fetch(outer, across_chips)
+    corners = fetch(corners, across_and_before)
+    pieces, carried, across, corners, orders, lag_weights, scalars = lax.optimization_barrier(
+        (pieces, carried, across, corners, orders, lag_weights, scalars)
     )
 
     parts = small_stage(pieces)
     one_bundle, two_bundle = join_rows(parts, 0), join_rows(parts, 1)
     one_bundles = bulk_stage(one_bundle)
-    ends = jnp.concatenate([last_two(acts_one), last_two(beside), last_two(across)], 1)
-    ends, _ = lax.optimization_barrier((ends, one_bundle))
-    ends = fetch(ends, before_in_group)
-    extended = (
-        ends[:, 0:4],
-        acts_one,
-        jnp.concatenate([ends[:, 4:5], beside], 0),
-        jnp.concatenate([ends[:, 5:6], across], 0),
-    )
-    one_bundles, two_bundle, extended = lax.optimization_barrier(
-        (one_bundles, two_bundle, extended)
+    carried, _ = lax.optimization_barrier((carried, one_bundle))
+    beside = fetch(jnp.concatenate([sides(carried)[0], inner], 0), sibling)
+    inner = permute(orders, acts_one)
+    halo = permute(orders, carried, beside, jnp.concatenate([corners, across], 0))
+    one_bundles, two_bundle, inner, halo = lax.optimization_barrier(
+        (one_bundles, two_bundle, inner, halo)
     )
     one_others = [fetch(b, sibling) for b in one_bundles]
 
     two_bundle, one_others[1] = lax.optimization_barrier((two_bundle, one_others[1]))
     two_bundles = bulk_stage(two_bundle)
     acts_two = conv(
-        scalars, lag_weights, extended, orders, gain_two.reshape(1, C),
-        one_bundles, one_others, finish_norm,
+        scalars, lag_weights, inner, halo, gain_two.reshape(1, C), one_bundles, one_others,
+        finish_norm,
     ).reshape(frames.shape)
 
     two_bundles, acts_two = lax.optimization_barrier((two_bundles, acts_two))
-    two_others = [fetch(b, sibling) for b in two_bundles[:2]]
     inner, outer = sides(acts_two)
-    ends, corners, outer = lax.optimization_barrier((last_two(acts_two), last_two(outer), outer))
-    carried = fetch(ends, before_in_group)
+    beside = fetch(inner, sibling)
+    across = fetch(outer, across_chips)
+    ends = jnp.concatenate([last_two(acts_two), last_two(beside)], 1)
+    ends, corners = lax.optimization_barrier((ends, last_two(outer)))
+    ends = fetch(ends, before_in_group)
     corners = fetch(corners, across_and_before)
-    across = fetch(outer, across_chips)
-    carried, corners, across, two_last = lax.optimization_barrier(
-        (carried, corners, across, two_bundles[2:])
-    )
-    edge = jnp.concatenate([sides(carried)[0], inner], 0)
-    beside = fetch(edge, sibling)
+    first_two, two_last = two_bundles[:2], two_bundles[2:]
+    beside, first_two = lax.optimization_barrier((beside, first_two))
+    two_others = [fetch(b, sibling) for b in first_two]
+    inner = permute(orders, acts_two)
+    ends, corners, across, two_last, inner = lax.optimization_barrier(
+        (ends, corners, across, two_last, inner)
+    )
     two_others += [fetch(b, sibling) for b in two_last]
-    extended = (carried, acts_two, beside, jnp.concatenate([corners, across], 0))
+    halo = permute(
+        orders,
+        ends[:, 0:4],
+        jnp.concatenate([ends[:, 4:5], beside], 0),
+        jnp.concatenate([corners, across], 0),
+    )
     result = conv(
-        scalars, lag_weights, extended, orders, frames.reshape(slots, 128, C),
-        two_bundles, two_others, finish_add,
+        scalars, lag_weights, inner, halo, frames.reshape(slots, 128, C), two_bundles, two_others,
+        finish_add,
     )
     return result.reshape(frames.shape)
 

time: 126 us -> 123 us (0.976)
  starting transfers between devices: 54 us -> 34.5 us
  waiting for transfers between devices: 34.3 us -> 48.3 us
  Pallas kernels: 30.1 us -> 31.8 us
    ppermute x26 -> x27, starting transfers between devices: 54 us -> 34.5 us  [fetch(): return lax.ppermute(array, AXES, pairs)]
    ppermute x26 -> x27, waiting for transfers between devices: 34.3 us -> 48.3 us  [fetch(): return lax.ppermute(array, AXES, pairs)]
    pallas_call x0 -> x4, Pallas kernels: none -> 3.53 us  [permute(): pl.pallas_call(permute_body, out_shape=jax.ShapeDtypeStruct((2, rows, C),...]
    pallas_call x2, Pallas kernels: 29.7 us -> 27.9 us  [conv(): pl.pallas_call(lambda *refs: conv_body(*refs, finish=finish), out_shape=j...]
  transfers between devices with their start and end apart: 26 -> 27, of which waited for: 8 -> 13; matrix products, arithmetic and copies ran while one was open for 3% -> 3% of each run, Pallas kernels for 12% -> 14%
where the time goes in v5:
time: 123 us; the launch traced here: 121 us
  waiting for transfers between devices  48.3 us (39%)
  starting transfers between devices  34.5 us (28%)
  Pallas kernels  31.8 us (26%)
  local copies, waits for them, and re-layouts  3.04 us (2%)
  between operations  2.05 us (2%)
  other arithmetic  1.73 us (1%)
    ppermute x27, waiting for transfers between devices, fetch(): return lax.ppermute(array, AXES, pairs)  48.3 us
    ppermute x27, starting transfers between devices, fetch(): return lax.ppermute(array, AXES, pairs)  34.5 us
    pallas_call x2, Pallas kernels, conv(): pl.pallas_call(lambda *refs: conv_body(*refs, finish=finish), out_shape=j...  27.9 us
    pallas_call x4, Pallas kernels, permute(): pl.pallas_call(permute_body, out_shape=jax.ShapeDtypeStruct((2, rows, C),...  3.53 us
  transfers between devices with their start and end apart: 27, of which 13 were waited for; matrix products, arithmetic and copies ran while one was open for 3% of the time, Pallas kernels for 14%

profile of v5, /device:TPU:131, one launch (start us, length us, event | category | flops | bytes accessed | tf_op | source)
XLA Modules:
  0.0 121.5 jit_solution(8991711959839723745)
XLA Ops:
  0.0 1.1 constant_dynamic-slice_fusion.5
  1.2 1.9 %collective-permute-start = (bf16[2,168,384]{2,1,0:T(8,128)(2,1)S(1)}, bf16[2,168,384]{2,1,0:T(8,128)(2,1)S(1)}, u32[]{:S(2)}, u32[]{:S(2)}) collective-permute-start(bf16[2,168,384]{2,1,0:T(8,128)(2,1)S(1)} %constant_dynamic-update-slice_fusion), channel_id=1, source_target_pairs={{152,0},{1,1},{58,2},{67,3},{252,4},{37,5},{94,6},{103,7},{128,8},... | collective-permute-start | bytes 774152 | tf_op jit(solution)/shard_map/ppermute | solution.py:34
  3.2 2.4 %collective-permute-start.1 = (bf16[2,168,384]{2,1,0:T(8,128)(2,1)S(1)}, bf16[2,168,384]{2,1,0:T(8,128)(2,1)S(1)}, u32[]{:S(2)}, u32[]{:S(2)}) collective-permute-start(bf16[2,168,384]{2,1,0:T(8,128)(2,1)S(1)} %constant_dynamic-update-slice_fusion), channel_id=1, source_target_pairs={{24,0},{129,1},{122,2},{195,3},{188,4},{165,5},{222,6},{231,7},{0,... | collective-permute-start | bytes 774152 | tf_op jit(solution)/shard_map/ppermute | solution.py:34
  7.1 3.2 %collective-permute-start.2 = (bf16[2,4,32,384]{3,2,1,0:T(8,128)(2,1)S(1)}, bf16[2,4,32,384]{3,2,1,0:T(8,128)(2,1)S(1)}, u32[]{:S(2)}, u32[]{:S(2)}) collective-permute-start(bf16[2,4,32,384]{3,2,1,0:T(8,128)(2,1)S(1)} %constant_dynamic-slice_fusion.4), channel_id=1, source_target_pairs={{0,8},{1,9},{2,10},{3,11},{4,12},{5,13},{6,14},{7,15},{8,16},{9,17... | collective-permute-start | bytes 589832 | tf_op jit(solution)/shard_map/ppermute | solution.py:34
  10.3 4.4 %collective-permute-start.3 = (bf16[6,1,32,384]{3,2,1,0:T(8,128)(2,1)S(1)}, bf16[6,1,32,384]{3,2,1,0:T(8,128)(2,1)S(1)}, u32[]{:S(2)}, u32[]{:S(2)}) collective-permute-start(bf16[6,1,32,384]{3,2,1,0:T(8,128)(2,1)S(1)} %get-tuple-element.42), channel_id=1, source_target_pairs={{2,1},{1,2},{4,3},{3,4},{6,5},{5,6},{10,9},{9,10},{12,11},{11,12},... | collective-permute-start | bytes 442376 | tf_op jit(solution)/shard_map/ppermute | solution.py:34
  14.7 2.2 %collective-permute-start.4 = (bf16[2,1,32,384]{3,2,1,0:T(8,128)(2,1)S(1)}, bf16[2,1,32,384]{3,2,1,0:T(8,128)(2,1)S(1)}, u32[]{:S(2)}, u32[]{:S(2)}) collective-permute-start(bf16[2,1,32,384]{3,2,1,0:T(8,128)(2,1)S(1)} %constant_dynamic-slice_fusion.3), channel_id=1, source_target_pairs={{2,9},{1,10},{4,11},{3,12},{6,13},{5,14},{10,17},{9,18},{12,19},{1... | collective-permute-start | bytes 147464 | tf_op jit(solution)/shard_map/ppermute | solution.py:34
  20.3 12.6 %collective-permute-done.4 = bf16[2,1,32,384]{3,2,1,0:T(8,128)(2,1)S(1)} collective-permute-done((bf16[2,1,32,384]{3,2,1,0:T(8,128)(2,1)S(1)}, bf16[2,1,32,384]{3,2,1,0:T(8,128)(2,1)S(1)}, u32[]{:S(2)}, u32[]{:S(2)}) %collective-permute-start.4) | collective-permute-done | bytes 49184 | tf_op jit(solution)/shard_map/ppermute | solution.py:34
  32.9 1.5 %collective-permute-start.6 = (bf16[2,2,168,384]{3,2,1,0:T(8,128)(2,1)S(1)}, bf16[2,2,168,384]{3,2,1,0:T(8,128)(2,1)S(1)}, u32[]{:S(2)}, u32[]{:S(2)}) collective-permute-start(bf16[2,2,168,384]{3,2,1,0:T(8,128)(2,1)S(1)} %pad_maximum_fusion.refs_0_), channel_id=1, source_target_pairs={{6,0},{25,1},{0,2},{27,3},{2,4},{29,5},{4,6},{31,7},{14,8},{1,9},{... | collective-permute-start | bytes 1548296 | tf_op jit(solution)/shard_map/ppermute | solution.py:34
  34.4 6.6 %collective-permute-done.5.refs_1_ = bf16[2,2,168,384]{3,2,1,0:T(8,128)(2,1)S(1)} collective-permute-done((bf16[2,2,168,384]{3,2,1,0:T(8,128)(2,1)S(1)}, bf16[2,2,168,384]{3,2,1,0:T(8,128)(2,1)S(1)}, u32[]{:S(2)}, u32[]{:S(2)}) %collective-permute-start.5) | collective-permute-done | bytes 516128 | tf_op jit(solution)/shard_map/ppermute | solution.py:34
  41.0 6.7 %collective-permute-done.6.refs_2_ = bf16[2,2,168,384]{3,2,1,0:T(8,128)(2,1)S(1)} collective-permute-done((bf16[2,2,168,384]{3,2,1,0:T(8,128)(2,1)S(1)}, bf16[2,2,168,384]{3,2,1,0:T(8,128)(2,1)S(1)}, u32[]{:S(2)}, u32[]{:S(2)}) %collective-permute-start.6) | collective-permute-done | bytes 516128 | tf_op jit(solution)/shard_map/ppermute | solution.py:34
  48.1 1.5 %collective-permute-start.9 = (bf16[14,96,384]{2,1,0:T(8,128)(2,1)S(1)}, bf16[14,96,384]{2,1,0:T(8,128)(2,1)S(1)}, u32[]{:S(2)}, u32[]{:S(2)}) collective-permute-start(bf16[14,96,384]{2,1,0:T(8,128)(2,1)S(1)} %shard_map.127.refs_5_), channel_id=1, source_target_pairs={{24,0},{7,1},{26,2},{1,3},{28,4},{3,5},{30,6},{5,7},{0,8},{15,9},{... | collective-permute-start | bytes 3096584 | tf_op jit(solution)/shard_map/ppermute | solution.py:34
  50.1 0.9 shard_map.129.refs_2_
  51.3 0.9 shard_map.130.refs_3_
  52.2 9.6 %collective-permute-done.10.refs_8_ = bf16[14,96,384]{2,1,0:T(8,128)(2,1)S(1)} collective-permute-done((bf16[14,96,384]{2,1,0:T(8,128)(2,1)S(1)}, bf16[14,96,384]{2,1,0:T(8,128)(2,1)S(1)}, u32[]{:S(2)}, u32[]{:S(2)}) %collective-permute-start.10) | collective-permute-done | bytes 1032224 | tf_op jit(solution)/shard_map/ppermute | solution.py:34
  61.9 2.4 %collective-permute-start.12 = (bf16[14,96,384]{2,1,0:T(8,128)(2,1)S(1)}, bf16[14,96,384]{2,1,0:T(8,128)(2,1)S(1)}, u32[]{:S(2)}, u32[]{:S(2)}) collective-permute-start(bf16[14,96,384]{2,1,0:T(8,128)(2,1)S(1)} %collective-permute-done.8.refs_6_), channel_id=1, source_target_pairs={{1,0},{0,1},{3,2},{2,3},{5,4},{4,5},{7,6},{6,7},{9,8},{8,9},{11,10... | collective-permute-start | bytes 3096584 | tf_op jit(solution)/shard_map/ppermute | solution.py:34
  64.9 1.7 %collective-permute-done.12.refs_10_ = bf16[14,96,384]{2,1,0:T(8,128)(2,1)S(1)} collective-permute-done((bf16[14,96,384]{2,1,0:T(8,128)(2,1)S(1)}, bf16[14,96,384]{2,1,0:T(8,128)(2,1)S(1)}, u32[]{:S(2)}, u32[]{:S(2)}) %collective-permute-start.12) | collective-permute-done | bytes 1032224 | tf_op jit(solution)/shard_map/ppermute | solution.py:34
  66.6 2.4 %collective-permute-start.13 = (bf16[14,96,384]{2,1,0:T(8,128)(2,1)S(1)}, bf16[14,96,384]{2,1,0:T(8,128)(2,1)S(1)}, u32[]{:S(2)}, u32[]{:S(2)}) collective-permute-start(bf16[14,96,384]{2,1,0:T(8,128)(2,1)S(1)} %shard_map.128.refs_5_), channel_id=1, source_target_pairs={{8,0},{3,1},{10,2},{5,3},{12,4},{7,5},{14,6},{1,7},{16,8},{11,9},{... | collective-permute-start | bytes 3096584 | tf_op jit(solution)/shard_map/ppermute | solution.py:34
  69.6 1.5 %collective-permute-done.18.refs_12_ = bf16[14,96,384]{2,1,0:T(8,128)(2,1)S(1)} collective-permute-done((bf16[14,96,384]{2,1,0:T(8,128)(2,1)S(1)}, bf16[14,96,384]{2,1,0:T(8,128)(2,1)S(1)}, u32[]{:S(2)}, u32[]{:S(2)}) %collective-permute-start.18) | collective-permute-done | bytes 1032224 | tf_op jit(solution)/shard_map/ppermute | solution.py:34
  71.0 13.6 %shard_map.131 = bf16[6,128,384]{2,1,0:T(8,128)(2,1)S(1)} custom-call(s32[2]{0:T(128)S(1)} %pad_add_fusion.1.refs_0_, f32[3,6]{1,0:T(4,128)S(1)} %add_convert_fusion.refs_1_, bf16[2,768,384]{2,1,0:T(8,128)(2,1)S(1)} %shard_map.129.refs_2_, bf16[2,768,384]{2,1,0:T(8,128)(2,1)S(1)} %shard_map.130.refs_3_, f32[1,384]{1,0:T(1,128)S(1)} %reshape.269.refs_4_, ...), custom_call_target="tpu_custom_call" | custom-call | flops 1000 | bytes 1000 | tf_op jit(solution)/shard_map/pallas_call | solution.py:263
  84.7 0.7 collective-permute-start.19
  85.4 1.0 collective-permute-done.19
  86.5 2.4 %collective-permute-start.20 = (bf16[2,5,32,384]{3,2,1,0:T(8,128)(2,1)S(1)}, bf16[2,5,32,384]{3,2,1,0:T(8,128)(2,1)S(1)}, u32[]{:S(2)}, u32[]{:S(2)}) collective-permute-start(bf16[2,5,32,384]{3,2,1,0:T(8,128)(2,1)S(1)} %pad_maximum_fusion.1), channel_id=1, source_target_pairs={{0,8},{1,9},{2,10},{3,11},{4,12},{5,13},{6,14},{7,15},{8,16},{9,17... | collective-permute-start | bytes 737288 | tf_op jit(solution)/shard_map/ppermute | solution.py:34
  88.9 2.9 %collective-permute-start.22 = (bf16[6,1,32,384]{3,2,1,0:T(8,128)(2,1)S(1)}, bf16[6,1,32,384]{3,2,1,0:T(8,128)(2,1)S(1)}, u32[]{:S(2)}, u32[]{:S(2)}) collective-permute-start(bf16[6,1,32,384]{3,2,1,0:T(8,128)(2,1)S(1)} %get-tuple-element.81), channel_id=1, source_target_pairs={{2,1},{1,2},{4,3},{3,4},{6,5},{5,6},{10,9},{9,10},{12,11},{11,12},... | collective-permute-start | bytes 442376 | tf_op jit(solution)/shard_map/ppermute | solution.py:34
  91.9 2.4 %collective-permute-start.21 = (bf16[2,1,32,384]{3,2,1,0:T(8,128)(2,1)S(1)}, bf16[2,1,32,384]{3,2,1,0:T(8,128)(2,1)S(1)}, u32[]{:S(2)}, u32[]{:S(2)}) collective-permute-start(bf16[2,1,32,384]{3,2,1,0:T(8,128)(2,1)S(1)} %constant_dynamic-slice_fusion), channel_id=1, source_target_pairs={{2,9},{1,10},{4,11},{3,12},{6,13},{5,14},{10,17},{9,18},{12,19},{1... | collective-permute-start | bytes 147464 | tf_op jit(solution)/shard_map/ppermute | solution.py:34
  94.2 0.9 shard_map.132.refs_2_
  95.1 1.4 %collective-permute-start.23 = (bf16[14,96,384]{2,1,0:T(8,128)(2,1)S(1)}, bf16[14,96,384]{2,1,0:T(8,128)(2,1)S(1)}, u32[]{:S(2)}, u32[]{:S(2)}) collective-permute-start(bf16[14,96,384]{2,1,0:T(8,128)(2,1)S(1)} %shard_map.128.refs_5_), channel_id=1, source_target_pairs={{1,0},{0,1},{3,2},{2,3},{5,4},{4,5},{7,6},{6,7},{9,8},{8,9},{11,10... | collective-permute-start | bytes 3096584 | tf_op jit(solution)/shard_map/ppermute | solution.py:34
  96.6 5.2 %collective-permute-done.21 = bf16[2,1,32,384]{3,2,1,0:T(8,128)(2,1)S(1)} collective-permute-done((bf16[2,1,32,384]{3,2,1,0:T(8,128)(2,1)S(1)}, bf16[2,1,32,384]{3,2,1,0:T(8,128)(2,1)S(1)}, u32[]{:S(2)}, u32[]{:S(2)}) %collective-permute-start.21) | collective-permute-done | bytes 49184 | tf_op jit(solution)/shard_map/ppermute | solution.py:34
  101.8 1.5 %collective-permute-start.25 = (bf16[14,96,384]{2,1,0:T(8,128)(2,1)S(1)}, bf16[14,96,384]{2,1,0:T(8,128)(2,1)S(1)}, u32[]{:S(2)}, u32[]{:S(2)}) collective-permute-start(bf16[14,96,384]{2,1,0:T(8,128)(2,1)S(1)} %collective-permute-done.14.refs_7_), channel_id=1, source_target_pairs={{1,0},{0,1},{3,2},{2,3},{5,4},{4,5},{7,6},{6,7},{9,8},{8,9},{11,10... | collective-permute-start | bytes 3096584 | tf_op jit(solution)/shard_map/ppermute | solution.py:34
  103.4 0.9 shard_map.133.refs_3_
  104.3 1.2 %collective-permute-done.25.refs_11_ = bf16[14,96,384]{2,1,0:T(8,128)(2,1)S(1)} collective-permute-done((bf16[14,96,384]{2,1,0:T(8,128)(2,1)S(1)}, bf16[14,96,384]{2,1,0:T(8,128)(2,1)S(1)}, u32[]{:S(2)}, u32[]{:S(2)}) %collective-permute-start.25) | collective-permute-done | bytes 1032224 | tf_op jit(solution)/shard_map/ppermute | solution.py:34
  105.5 1.5 %collective-permute-done.26.refs_12_ = bf16[14,96,384]{2,1,0:T(8,128)(2,1)S(1)} collective-permute-done((bf16[14,96,384]{2,1,0:T(8,128)(2,1)S(1)}, bf16[14,96,384]{2,1,0:T(8,128)(2,1)S(1)}, u32[]{:S(2)}, u32[]{:S(2)}) %collective-permute-start.26) | collective-permute-done | bytes 1032224 | tf_op jit(solution)/shard_map/ppermute | solution.py:34
  107.0 14.3 %shard_map.134 = bf16[6,128,384]{2,1,0:T(8,128)(2,1)} custom-call(s32[2]{0:T(128)S(1)} %pad_add_fusion.1.refs_0_, f32[3,6]{1,0:T(4,128)S(1)} %add_convert_fusion.refs_1_, bf16[2,768,384]{2,1,0:T(8,128)(2,1)S(1)} %shard_map.132.refs_2_, bf16[2,768,384]{2,1,0:T(8,128)(2,1)S(1)} %shard_map.133.refs_3_, bf16[6,128,384]{2,1,0:T(8,128)(2,1)S(1)} %bitcast.33, ...), custom_call_target="tpu_custom_call" | custom-call | flops 1000 | bytes 1000 | tf_op jit(solution)/shard_map/pallas_call | solution.py:263
  (98 shorter events, 6.2 us)
Async XLA Ops:
  1.2 19.0 %collective-permute-start = (bf16[2,168,384]{2,1,0:T(8,128)(2,1)S(1)}, bf16[2,168,384]{2,1,0:T(8,128)(2,1)S(1)}, u32[]{:S(2)}, u32[]{:S(2)}) collective-permute-start(bf16[2,168,384]{2,1,0:T(8,128)(2,1)S(1)} %constant_dynamic-update-slice_fusion), channel_id=1, source_target_pairs={{152,0},{1,1},{58,2},{67,3},{252,4},{37,5},{94,6},{103,7},{128,8},... | collective-permute-start | bytes 774152 | tf_op jit(solution)/shard_map/ppermute | solution.py:34
  3.2 17.0 %collective-permute-start.1 = (bf16[2,168,384]{2,1,0:T(8,128)(2,1)S(1)}, bf16[2,168,384]{2,1,0:T(8,128)(2,1)S(1)}, u32[]{:S(2)}, u32[]{:S(2)}) collective-permute-start(bf16[2,168,384]{2,1,0:T(8,128)(2,1)S(1)} %constant_dynamic-update-slice_fusion), channel_id=1, source_target_pairs={{24,0},{129,1},{122,2},{195,3},{188,4},{165,5},{222,6},{231,7},{0,... | collective-permute-start | bytes 774152 | tf_op jit(solution)/shard_map/ppermute | solution.py:34
  6.5 10.5 %copy-start.7 = (s32[4]{0:T(128)S(1)}, s32[4]{0:T(128)}, u32[]{:S(2)}) copy-start(s32[4]{0:T(128)} %constant.150.clone) | copy-start | bytes 52
  6.5 10.5 %copy-start.2 = (s32[4,2]{1,0:T(4,128)S(1)}, s32[4,2]{1,0:T(4,128)}, u32[]{:S(2)}) copy-start(s32[4,2]{1,0:T(4,128)} %constant.159) | copy-start | bytes 100
  6.5 11.5 %copy-start.1 = (s32[4,2]{1,0:T(4,128)S(1)}, s32[4,2]{1,0:T(4,128)}, u32[]{:S(2)}) copy-start(s32[4,2]{1,0:T(4,128)} %constant.161) | copy-start | bytes 100
  6.6 13.0 %copy-start.8 = (s32[3]{0:T(128)S(1)}, s32[3]{0:T(128)}, u32[]{:S(2)}) copy-start(s32[3]{0:T(128)} %param.14) | copy-start | bytes 40
  7.1 25.8 %collective-permute-start.2 = (bf16[2,4,32,384]{3,2,1,0:T(8,128)(2,1)S(1)}, bf16[2,4,32,384]{3,2,1,0:T(8,128)(2,1)S(1)}, u32[]{:S(2)}, u32[]{:S(2)}) collective-permute-start(bf16[2,4,32,384]{3,2,1,0:T(8,128)(2,1)S(1)} %constant_dynamic-slice_fusion.4), channel_id=1, source_target_pairs={{0,8},{1,9},{2,10},{3,11},{4,12},{5,13},{6,14},{7,15},{8,16},{9,17... | collective-permute-start | bytes 589832 | tf_op jit(solution)/shard_map/ppermute | solution.py:34
  10.3 22.6 %collective-permute-start.3 = (bf16[6,1,32,384]{3,2,1,0:T(8,128)(2,1)S(1)}, bf16[6,1,32,384]{3,2,1,0:T(8,128)(2,1)S(1)}, u32[]{:S(2)}, u32[]{:S(2)}) collective-permute-start(bf16[6,1,32,384]{3,2,1,0:T(8,128)(2,1)S(1)} %get-tuple-element.42), channel_id=1, source_target_pairs={{2,1},{1,2},{4,3},{3,4},{6,5},{5,6},{10,9},{9,10},{12,11},{11,12},... | collective-permute-start | bytes 442376 | tf_op jit(solution)/shard_map/ppermute | solution.py:34
  14.7 18.2 %collective-permute-start.4 = (bf16[2,1,32,384]{3,2,1,0:T(8,128)(2,1)S(1)}, bf16[2,1,32,384]{3,2,1,0:T(8,128)(2,1)S(1)}, u32[]{:S(2)}, u32[]{:S(2)}) collective-permute-start(bf16[2,1,32,384]{3,2,1,0:T(8,128)(2,1)S(1)} %constant_dynamic-slice_fusion.3), channel_id=1, source_target_pairs={{2,9},{1,10},{4,11},{3,12},{6,13},{5,14},{10,17},{9,18},{12,19},{1... | collective-permute-start | bytes 147464 | tf_op jit(solution)/shard_map/ppermute | solution.py:34
  32.9 8.1 %collective-permute-start.5 = (bf16[2,2,168,384]{3,2,1,0:T(8,128)(2,1)S(1)}, bf16[2,2,168,384]{3,2,1,0:T(8,128)(2,1)S(1)}, u32[]{:S(2)}, u32[]{:S(2)}) collective-permute-start(bf16[2,2,168,384]{3,2,1,0:T(8,128)(2,1)S(1)} %pad_maximum_fusion.refs_0_), channel_id=1, source_target_pairs={{2,0},{9,1},{4,2},{11,3},{6,4},{13,5},{0,6},{15,7},{10,8},{17,9},{... | collective-permute-start | bytes 1548296 | tf_op jit(solution)/shard_map/ppermute | solution.py:34
  32.9 14.8 %collective-permute-start.6 = (bf16[2,2,168,384]{3,2,1,0:T(8,128)(2,1)S(1)}, bf16[2,2,168,384]{3,2,1,0:T(8,128)(2,1)S(1)}, u32[]{:S(2)}, u32[]{:S(2)}) collective-permute-start(bf16[2,2,168,384]{3,2,1,0:T(8,128)(2,1)S(1)} %pad_maximum_fusion.refs_0_), channel_id=1, source_target_pairs={{6,0},{25,1},{0,2},{27,3},{2,4},{29,5},{4,6},{31,7},{14,8},{1,9},{... | collective-permute-start | bytes 1548296 | tf_op jit(solution)/shard_map/ppermute | solution.py:34
  34.4 13.3 %collective-permute-start.7 = (bf16[2,2,168,384]{3,2,1,0:T(8,128)(2,1)S(1)}, bf16[2,2,168,384]{3,2,1,0:T(8,128)(2,1)S(1)}, u32[]{:S(2)}, u32[]{:S(2)}) collective-permute-start(bf16[2,2,168,384]{3,2,1,0:T(8,128)(2,1)S(1)} %pad_maximum_fusion.refs_0_), channel_id=1, source_target_pairs={{4,0},{17,1},{6,2},{19,3},{0,4},{21,5},{2,6},{23,7},{12,8},{25,9},... | collective-permute-start | bytes 1548296 | tf_op jit(solution)/shard_map/ppermute | solution.py:34
  47.9 13.9 %collective-permute-start.10 = (bf16[14,96,384]{2,1,0:T(8,128)(2,1)S(1)}, bf16[14,96,384]{2,1,0:T(8,128)(2,1)S(1)}, u32[]{:S(2)}, u32[]{:S(2)}) collective-permute-start(bf16[14,96,384]{2,1,0:T(8,128)(2,1)S(1)} %shard_map.127.refs_5_), channel_id=1, source_target_pairs={{224,0},{33,1},{226,2},{35,3},{228,4},{37,5},{230,6},{39,7},{232,8... | collective-permute-start | bytes 3096584 | tf_op jit(solution)/shard_map/ppermute | solution.py:34
  48.0 13.8 %collective-permute-start.8 = (bf16[14,96,384]{2,1,0:T(8,128)(2,1)S(1)}, bf16[14,96,384]{2,1,0:T(8,128)(2,1)S(1)}, u32[]{:S(2)}, u32[]{:S(2)}) collective-permute-start(bf16[14,96,384]{2,1,0:T(8,128)(2,1)S(1)} %shard_map.127.refs_5_), channel_id=1, source_target_pairs={{8,0},{3,1},{10,2},{5,3},{12,4},{7,5},{14,6},{1,7},{16,8},{11,9},{... | collective-permute-start | bytes 3096584 | tf_op jit(solution)/shard_map/ppermute | solution.py:34
  48.1 13.8 %collective-permute-start.9 = (bf16[14,96,384]{2,1,0:T(8,128)(2,1)S(1)}, bf16[14,96,384]{2,1,0:T(8,128)(2,1)S(1)}, u32[]{:S(2)}, u32[]{:S(2)}) collective-permute-start(bf16[14,96,384]{2,1,0:T(8,128)(2,1)S(1)} %shard_map.127.refs_5_), channel_id=1, source_target_pairs={{24,0},{7,1},{26,2},{1,3},{28,4},{3,5},{30,6},{5,7},{0,8},{15,9},{... | collective-permute-start | bytes 3096584 | tf_op jit(solution)/shard_map/ppermute | solution.py:34
  49.6 1.7 %collective-permute-start.11 = (bf16[8,1,32,384]{3,2,1,0:T(8,128)(2,1)S(1)}, bf16[8,1,32,384]{3,2,1,0:T(8,128)(2,1)S(1)}, u32[]{:S(2)}, u32[]{:S(2)}) collective-permute-start(bf16[8,1,32,384]{3,2,1,0:T(8,128)(2,1)S(1)} %pad_maximum_fusion.2), channel_id=1, source_target_pairs={{1,0},{0,1},{3,2},{2,3},{5,4},{4,5},{7,6},{6,7},{9,8},{8,9},{11,10... | collective-permute-start | bytes 589832 | tf_op jit(solution)/shard_map/ppermute | solution.py:34
  51.2 17.7 %copy-start.4 = (f32[384]{0:T(512)S(1)}, f32[384]{0:T(512)}, u32[]{:S(2)}) copy-start(f32[384]{0:T(512)} %param.20) | copy-start | bytes 4612
  61.9 4.7 %collective-permute-start.12 = (bf16[14,96,384]{2,1,0:T(8,128)(2,1)S(1)}, bf16[14,96,384]{2,1,0:T(8,128)(2,1)S(1)}, u32[]{:S(2)}, u32[]{:S(2)}) collective-permute-start(bf16[14,96,384]{2,1,0:T(8,128)(2,1)S(1)} %collective-permute-done.8.refs_6_), channel_id=1, source_target_pairs={{1,0},{0,1},{3,2},{2,3},{5,4},{4,5},{7,6},{6,7},{9,8},{8,9},{11,10... | collective-permute-start | bytes 3096584 | tf_op jit(solution)/shard_map/ppermute | solution.py:34
  64.3 4.6 %collective-permute-start.16 = (bf16[14,96,384]{2,1,0:T(8,128)(2,1)S(1)}, bf16[14,96,384]{2,1,0:T(8,128)(2,1)S(1)}, u32[]{:S(2)}, u32[]{:S(2)}) collective-permute-start(bf16[14,96,384]{2,1,0:T(8,128)(2,1)S(1)} %shard_map.127.refs_5_), channel_id=1, source_target_pairs={{1,0},{0,1},{3,2},{2,3},{5,4},{4,5},{7,6},{6,7},{9,8},{8,9},{11,10... | collective-permute-start | bytes 3096584 | tf_op jit(solution)/shard_map/ppermute | solution.py:34
  64.3 5.2 %collective-permute-start.17 = (bf16[14,96,384]{2,1,0:T(8,128)(2,1)S(1)}, bf16[14,96,384]{2,1,0:T(8,128)(2,1)S(1)}, u32[]{:S(2)}, u32[]{:S(2)}) collective-permute-start(bf16[14,96,384]{2,1,0:T(8,128)(2,1)S(1)} %collective-permute-done.9.refs_7_), channel_id=1, source_target_pairs={{1,0},{0,1},{3,2},{2,3},{5,4},{4,5},{7,6},{6,7},{9,8},{8,9},{11,10... | collective-permute-start | bytes 3096584 | tf_op jit(solution)/shard_map/ppermute | solution.py:34
  64.9 6.2 %collective-permute-start.18 = (bf16[14,96,384]{2,1,0:T(8,128)(2,1)S(1)}, bf16[14,96,384]{2,1,0:T(8,128)(2,1)S(1)}, u32[]{:S(2)}, u32[]{:S(2)}) collective-permute-start(bf16[14,96,384]{2,1,0:T(8,128)(2,1)S(1)} %collective-permute-done.10.refs_8_), channel_id=1, source_target_pairs={{1,0},{0,1},{3,2},{2,3},{5,4},{4,5},{7,6},{6,7},{9,8},{8,9},{11,10... | collective-permute-start | bytes 3096584 | tf_op jit(solution)/shard_map/ppermute | solution.py:34
  66.6 18.1 %collective-permute-start.13 = (bf16[14,96,384]{2,1,0:T(8,128)(2,1)S(1)}, bf16[14,96,384]{2,1,0:T(8,128)(2,1)S(1)}, u32[]{:S(2)}, u32[]{:S(2)}) collective-permute-start(bf16[14,96,384]{2,1,0:T(8,128)(2,1)S(1)} %shard_map.128.refs_5_), channel_id=1, source_target_pairs={{8,0},{3,1},{10,2},{5,3},{12,4},{7,5},{14,6},{1,7},{16,8},{11,9},{... | collective-permute-start | bytes 3096584 | tf_op jit(solution)/shard_map/ppermute | solution.py:34
  69.0 15.7 %collective-permute-start.14 = (bf16[14,96,384]{2,1,0:T(8,128)(2,1)S(1)}, bf16[14,96,384]{2,1,0:T(8,128)(2,1)S(1)}, u32[]{:S(2)}, u32[]{:S(2)}) collective-permute-start(bf16[14,96,384]{2,1,0:T(8,128)(2,1)S(1)} %shard_map.128.refs_5_), channel_id=1, source_target_pairs={{24,0},{7,1},{26,2},{1,3},{28,4},{3,5},{30,6},{5,7},{0,8},{15,9},{... | collective-permute-start | bytes 3096584 | tf_op jit(solution)/shard_map/ppermute | solution.py:34
  69.0 15.7 %collective-permute-start.15 = (bf16[14,96,384]{2,1,0:T(8,128)(2,1)S(1)}, bf16[14,96,384]{2,1,0:T(8,128)(2,1)S(1)}, u32[]{:S(2)}, u32[]{:S(2)}) collective-permute-start(bf16[14,96,384]{2,1,0:T(8,128)(2,1)S(1)} %shard_map.128.refs_5_), channel_id=1, source_target_pairs={{224,0},{33,1},{226,2},{35,3},{228,4},{37,5},{230,6},{39,7},{232,8... | collective-permute-start | bytes 3096584 | tf_op jit(solution)/shard_map/ppermute | solution.py:34
  84.7 1.7 %collective-permute-start.19 = (bf16[6,1,32,384]{3,2,1,0:T(8,128)(2,1)S(1)}, bf16[6,1,32,384]{3,2,1,0:T(8,128)(2,1)S(1)}, u32[]{:S(2)}, u32[]{:S(2)}) collective-permute-start(bf16[6,1,32,384]{3,2,1,0:T(8,128)(2,1)S(1)} %get-tuple-element.82), channel_id=1, source_target_pairs={{1,0},{0,1},{3,2},{2,3},{5,4},{4,5},{7,6},{6,7},{9,8},{8,9},{11,10... | collective-permute-start | bytes 442376 | tf_op jit(solution)/shard_map/ppermute | solution.py:34
  86.5 15.3 %collective-permute-start.20 = (bf16[2,5,32,384]{3,2,1,0:T(8,128)(2,1)S(1)}, bf16[2,5,32,384]{3,2,1,0:T(8,128)(2,1)S(1)}, u32[]{:S(2)}, u32[]{:S(2)}) collective-permute-start(bf16[2,5,32,384]{3,2,1,0:T(8,128)(2,1)S(1)} %pad_maximum_fusion.1), channel_id=1, source_target_pairs={{0,8},{1,9},{2,10},{3,11},{4,12},{5,13},{6,14},{7,15},{8,16},{9,17... | collective-permute-start | bytes 737288 | tf_op jit(solution)/shard_map/ppermute | solution.py:34
  88.9 7.7 %collective-permute-start.22 = (bf16[6,1,32,384]{3,2,1,0:T(8,128)(2,1)S(1)}, bf16[6,1,32,384]{3,2,1,0:T(8,128)(2,1)S(1)}, u32[]{:S(2)}, u32[]{:S(2)}) collective-permute-start(bf16[6,1,32,384]{3,2,1,0:T(8,128)(2,1)S(1)} %get-tuple-element.81), channel_id=1, source_target_pairs={{2,1},{1,2},{4,3},{3,4},{6,5},{5,6},{10,9},{9,10},{12,11},{11,12},... | collective-permute-start | bytes 442376 | tf_op jit(solution)/shard_map/ppermute | solution.py:34
  91.9 9.9 %collective-permute-start.21 = (bf16[2,1,32,384]{3,2,1,0:T(8,128)(2,1)S(1)}, bf16[2,1,32,384]{3,2,1,0:T(8,128)(2,1)S(1)}, u32[]{:S(2)}, u32[]{:S(2)}) collective-permute-start(bf16[2,1,32,384]{3,2,1,0:T(8,128)(2,1)S(1)} %constant_dynamic-slice_fusion), channel_id=1, source_target_pairs={{2,9},{1,10},{4,11},{3,12},{6,13},{5,14},{10,17},{9,18},{12,19},{1... | collective-permute-start | bytes 147464 | tf_op jit(solution)/shard_map/ppermute | solution.py:34
  95.1 9.2 %collective-permute-start.23 = (bf16[14,96,384]{2,1,0:T(8,128)(2,1)S(1)}, bf16[14,96,384]{2,1,0:T(8,128)(2,1)S(1)}, u32[]{:S(2)}, u32[]{:S(2)}) collective-permute-start(bf16[14,96,384]{2,1,0:T(8,128)(2,1)S(1)} %shard_map.128.refs_5_), channel_id=1, source_target_pairs={{1,0},{0,1},{3,2},{2,3},{5,4},{4,5},{7,6},{6,7},{9,8},{8,9},{11,10... | collective-permute-start | bytes 3096584 | tf_op jit(solution)/shard_map/ppermute | solution.py:34
  96.5 7.7 %collective-permute-start.24 = (bf16[14,96,384]{2,1,0:T(8,128)(2,1)S(1)}, bf16[14,96,384]{2,1,0:T(8,128)(2,1)S(1)}, u32[]{:S(2)}, u32[]{:S(2)}) collective-permute-start(bf16[14,96,384]{2,1,0:T(8,128)(2,1)S(1)} %collective-permute-done.13.refs_6_), channel_id=1, source_target_pairs={{1,0},{0,1},{3,2},{2,3},{5,4},{4,5},{7,6},{6,7},{9,8},{8,9},{11,10... | collective-permute-start | bytes 3096584 | tf_op jit(solution)/shard_map/ppermute | solution.py:34
  101.8 3.7 %collective-permute-start.25 = (bf16[14,96,384]{2,1,0:T(8,128)(2,1)S(1)}, bf16[14,96,384]{2,1,0:T(8,128)(2,1)S(1)}, u32[]{:S(2)}, u32[]{:S(2)}) collective-permute-start(bf16[14,96,384]{2,1,0:T(8,128)(2,1)S(1)} %collective-permute-done.14.refs_7_), channel_id=1, source_target_pairs={{1,0},{0,1},{3,2},{2,3},{5,4},{4,5},{7,6},{6,7},{9,8},{8,9},{11,10... | collective-permute-start | bytes 3096584 | tf_op jit(solution)/shard_map/ppermute | solution.py:34
  103.3 3.7 %collective-permute-start.26 = (bf16[14,96,384]{2,1,0:T(8,128)(2,1)S(1)}, bf16[14,96,384]{2,1,0:T(8,128)(2,1)S(1)}, u32[]{:S(2)}, u32[]{:S(2)}) collective-permute-start(bf16[14,96,384]{2,1,0:T(8,128)(2,1)S(1)} %collective-permute-done.15.refs_8_), channel_id=1, source_target_pairs={{1,0},{0,1},{3,2},{2,3},{5,4},{4,5},{7,6},{6,7},{9,8},{8,9},{11,10... | collective-permute-start | bytes 3096584 | tf_op jit(solution)/shard_map/ppermute | solution.py:34
  (4 other events, 33.7 us)

commit v6 on v5

--- a/solution.py
+++ b/solution.py
@@ -66,10 +66,6 @@
 
 def z_stage(own):
     return jnp.stack([fetch(own, z_source(0)), fetch(own, z_source(1))], 1)
-
-
-def small_stage(two):
-    return [two] + [fetch(two, small_source(step)) for step in ROUND[1:]]
 
 
 def join_body(*refs):
@@ -118,38 +114,87 @@
     return jnp.stack([(half.reshape(-1, 1) * SHARD + ramp).reshape(C) for half in (first, second)])
 
 
-def permute_body(order, *refs):
-    out, top = refs[-1], 0
-    picks = [
-        (lax.broadcasted_iota(jnp.int32, (C, C), 0) == order[half : half + 1, :]).astype(jnp.bfloat16)
-        for half in range(2)
-    ]
-    for ref in refs[:-1]:
-        rows = ref.shape[0]
-        for half in range(2):
-            out[half, top : top + rows] = jnp.dot(
-                ref[...], picks[half], preferred_element_type=jnp.float32
-            ).astype(jnp.bfloat16)
-        top += rows
-
-
-def permute(orders, *arrays):
-    arrays = [array.reshape(-1, C) for array in arrays]
-    rows = sum(array.shape[0] for array in arrays)
+def spread_cells(cells, order, half):
+    rows = cells.shape[0]
+    pick = (lax.broadcasted_iota(jnp.int32, (C, C), 0) == order[half : half + 1, :]).astype(jnp.bfloat16)
+    plain = jnp.dot(cells, pick, preferred_element_type=jnp.float32)
+    col = lax.broadcasted_iota(jnp.int32, (rows, C), 0) % 32
+    before = jnp.where(col == 0, 0.0, pltpu.roll(plain, 1, 0))
+    after = jnp.where(col == 31, 0.0, pltpu.roll(plain, rows - 1, 0))
+    return [part.astype(jnp.bfloat16) for part in (before, plain, after)]
+
+
+def spread_inner_body(order, acts, out):
+    for half in range(2):
+        for tap, part in enumerate(spread_cells(acts[...], order, half)):
+            out[half, 2:8, 1:5, :, C * tap : C * (tap + 1)] = part.reshape(6, 4, 32, C)
+
+
+def spread_inner(orders, acts):
     vmem = pl.BlockSpec(memory_space=pltpu.VMEM)
     return pl.pallas_call(
-        permute_body,
-        out_shape=jax.ShapeDtypeStruct((2, rows, C), jnp.bfloat16),
-        in_specs=[vmem] * (1 + len(arrays)),
+        spread_inner_body,
+        out_shape=jax.ShapeDtypeStruct((2, 8, 6, 32, 3 * C), jnp.bfloat16),
+        in_specs=[vmem] * 2,
         out_specs=vmem,
-        compiler_params=pltpu.CompilerParams(vmem_limit_bytes=16 * 1024 * 1024),
+        compiler_params=pltpu.CompilerParams(vmem_limit_bytes=20 * 1024 * 1024),
         cost_estimate=pl.CostEstimate(flops=1000, bytes_accessed=1000, transcendentals=0),
-    )(orders, *arrays)
+    )(orders, acts.reshape(-1, C))
+
+
+def spread_halo_body(scalars, order, carried, beside, across, _, out, frames, rows, sems):
+    core = scalars[0]
+    for half in range(2):
+        for tap, part in enumerate(spread_cells(carried[...], order, half)):
+            frames[half, :, :, :, C * tap : C * (tap + 1)] = part.reshape(2, 4, 32, C)
+        for side, cells in enumerate((beside, across)):
+            for tap, part in enumerate(spread_cells(cells[...], order, half)):
+                rows[side, half, :, :, :, C * tap : C * (tap + 1)] = part.reshape(8, 1, 32, C)
+
+    def copies(above, below):
+        return [
+            pltpu.make_async_copy(frames, out.at[:, 0:2, 1:5], sems.at[0]),
+            pltpu.make_async_copy(rows.at[above], out.at[:, :, 0:1], sems.at[1]),
+            pltpu.make_async_copy(rows.at[below], out.at[:, :, 5:6], sems.at[2]),
+        ]
+
+    @pl.when(core == 0)
+    def _():
+        for copy in copies(1, 0):
+            copy.start()
+        for copy in copies(1, 0):
+            copy.wait()
+
+    @pl.when(core == 1)
+    def _():
+        for copy in copies(0, 1):
+            copy.start()
+        for copy in copies(0, 1):
+            copy.wait()
+
+
+def spread_halo(scalars, orders, carried, beside, across, spread):
+    vmem = pl.BlockSpec(memory_space=pltpu.VMEM)
+    either = pl.BlockSpec(memory_space=pl.ANY)
+    return pl.pallas_call(
+        spread_halo_body,
+        out_shape=jax.ShapeDtypeStruct(spread.shape, spread.dtype),
+        in_specs=[pl.BlockSpec(memory_space=pltpu.SMEM)] + [vmem] * 4 + [either],
+        out_specs=either,
+        scratch_shapes=[
+            pltpu.VMEM((2, 2, 4, 32, 3 * C), jnp.bfloat16),
+            pltpu.VMEM((2, 2, 8, 1, 32, 3 * C), jnp.bfloat16),
+            pltpu.SemaphoreType.DMA((3,)),
+        ],
+        input_output_aliases={5: 0},
+        compiler_params=pltpu.CompilerParams(vmem_limit_bytes=20 * 1024 * 1024),
+        cost_estimate=pl.CostEstimate(flops=1000, bytes_accessed=1000, transcendentals=0),
+    )(scalars, orders, *(cells.reshape(-1, C) for cells in (carried, beside, across)), spread)
 
 
 def conv_body(
-    scalars, lag_weights, inner, halo, tail, own0, own1, own2, own3, got0, got1, got2, got3,
-    out, spread, weights, total, sems, *, finish,
+    scalars, lag_weights, spread, tail, own0, own1, own2, own3, got0, got1, got2, got3,
+    out, weights, total, sems, *, finish,
 ):
     frames, rows, cols = 6, 4, 32
     own, got = (own0, own1, own2, own3), (got0, got1, got2, got3)
@@ -174,30 +219,6 @@
         for copy in copies(0, got) + copies(1, own):
             copy.start()
 
-    wide, tall = frames + 2, rows + 2
-    col = lax.broadcasted_iota(jnp.int32, (wide * tall * cols, C), 0) % cols
-    for half in range(2):
-        spread[half, 2:wide, 1:5, :, C : 2 * C] = inner[half].reshape(frames, rows, cols, C)
-        spread[half, 0:2, 1:5, :, C : 2 * C] = halo[half, 0:256].reshape(2, rows, cols, C)
-
-        @pl.when(core == 0)
-        def _():
-            spread[half, :, 5:6, :, C : 2 * C] = halo[half, 256:512].reshape(wide, 1, cols, C)
-            spread[half, :, 0:1, :, C : 2 * C] = halo[half, 512:768].reshape(wide, 1, cols, C)
-
-        @pl.when(core == 1)
-        def _():
-            spread[half, :, 0:1, :, C : 2 * C] = halo[half, 256:512].reshape(wide, 1, cols, C)
-            spread[half, :, 5:6, :, C : 2 * C] = halo[half, 512:768].reshape(wide, 1, cols, C)
-
-        plain = spread[half, :, :, :, C : 2 * C].reshape(wide * tall * cols, C).astype(jnp.float32)
-        before = jnp.where(col == 0, 0.0, pltpu.roll(plain, 1, 0))
-        after = jnp.where(col == cols - 1, 0.0, pltpu.roll(plain, wide * tall * cols - 1, 0))
-        for place, moved in ((0, before), (2 * C, after)):
-            spread[half, :, :, :, place : place + C] = (
-                moved.astype(jnp.bfloat16).reshape(wide, tall, cols, C)
-            )
-
     total[...] = jnp.zeros_like(total)
 
     def window(half, lag, row, first, count):
@@ -257,23 +278,22 @@
         out[f] = jnp.where(f < scalars[1], summed, 0.0).astype(jnp.bfloat16)
 
 
-def conv(scalars, lag_weights, inner, halo, tail, own, got, finish):
+def conv(scalars, lag_weights, spread, tail, own, got, finish):
     smem = pl.BlockSpec(memory_space=pltpu.SMEM)
     vmem = pl.BlockSpec(memory_space=pltpu.VMEM)
     return pl.pallas_call(
         lambda *refs: conv_body(*refs, finish=finish),
         out_shape=jax.ShapeDtypeStruct((6, 128, C), jnp.bfloat16),
-        in_specs=[smem, smem] + [vmem] * 3 + [pl.BlockSpec(memory_space=pl.ANY)] * 8,
+        in_specs=[smem, smem] + [vmem] * 2 + [pl.BlockSpec(memory_space=pl.ANY)] * 8,
         out_specs=vmem,
         scratch_shapes=[
-            pltpu.VMEM((2, 8, 6, 32, 3 * C), jnp.bfloat16),
             pltpu.VMEM((2, HALF, C, C), jnp.bfloat16),
             pltpu.VMEM((6, 128, C), jnp.float32),
             pltpu.SemaphoreType.DMA((2, 4)),
         ],
         compiler_params=pltpu.CompilerParams(vmem_limit_bytes=26 * 1024 * 1024),
         cost_estimate=pl.CostEstimate(flops=1000, bytes_accessed=1000, transcendentals=0),
-    )(scalars, lag_weights, inner, halo, tail, *own, *got)
+    )(scalars, lag_weights, spread, tail, *own, *got)
 
 
 def clip_positions(clip_lengths, frame_index):
@@ -334,53 +354,59 @@
     carried = fetch(ends, before_in_group)
     across = fetch(outer, across_chips)
     corners = fetch(corners, across_and_before)
-    pieces, carried, across, corners, orders, lag_weights, scalars = lax.optimization_barrier(
-        (pieces, carried, across, corners, orders, lag_weights, scalars)
-    )
-
-    parts = small_stage(pieces)
+    pieces, orders, lag_weights, scalars = lax.optimization_barrier(
+        (pieces, orders, lag_weights, scalars)
+    )
+
+    opposite = fetch(pieces, small_source(2))
+    after = fetch(pieces, small_source(1))
+    gated, carried, across, corners = lax.optimization_barrier((pieces, carried, across, corners))
+    parts = [pieces, after, fetch(gated, small_source(-1)), opposite]
+    beside = fetch(jnp.concatenate([sides(carried)[0], inner], 0), sibling)
+    spread = spread_halo(
+        scalars, orders, carried, beside, jnp.concatenate([corners, across], 0),
+        spread_inner(orders, acts_one),
+    )
+    parts, spread = lax.optimization_barrier((parts, spread))
+
     one_bundle, two_bundle = join_rows(parts, 0), join_rows(parts, 1)
     one_bundles = bulk_stage(one_bundle)
-    carried, _ = lax.optimization_barrier((carried, one_bundle))
-    beside = fetch(jnp.concatenate([sides(carried)[0], inner], 0), sibling)
-    inner = permute(orders, acts_one)
-    halo = permute(orders, carried, beside, jnp.concatenate([corners, across], 0))
-    one_bundles, two_bundle, inner, halo = lax.optimization_barrier(
-        (one_bundles, two_bundle, inner, halo)
-    )
-    one_others = [fetch(b, sibling) for b in one_bundles]
+    one_own, two_own = lax.optimization_barrier((one_bundle, two_bundle))
+    one_others, two_others = [fetch(one_own, sibling)], [fetch(two_own, sibling)]
+    one_bundles, two_bundle, one_others, two_others = lax.optimization_barrier(
+        (one_bundles, two_bundle, one_others, two_others)
+    )
+    one_others += [fetch(b, sibling) for b in one_bundles[1:]]
 
     two_bundle, one_others[1] = lax.optimization_barrier((two_bundle, one_others[1]))
     two_bundles = bulk_stage(two_bundle)
     acts_two = conv(
-        scalars, lag_weights, inner, halo, gain_two.reshape(1, C), one_bundles, one_others,
-        finish_norm,
+        scalars, lag_weights, spread, gain_two.reshape(1, C), one_bundles, one_others, finish_norm
     ).reshape(frames.shape)
 
     two_bundles, acts_two = lax.optimization_barrier((two_bundles, acts_two))
     inner, outer = sides(acts_two)
     beside = fetch(inner, sibling)
     across = fetch(outer, across_chips)
+    two_others.append(fetch(two_bundles[1], sibling))
+    two_bundles[1], beside, two_others = lax.optimization_barrier(
+        (two_bundles[1], beside, two_others)
+    )
     ends = jnp.concatenate([last_two(acts_two), last_two(beside)], 1)
     ends, corners = lax.optimization_barrier((ends, last_two(outer)))
     ends = fetch(ends, before_in_group)
     corners = fetch(corners, across_and_before)
-    first_two, two_last = two_bundles[:2], two_bundles[2:]
-    beside, first_two = lax.optimization_barrier((beside, first_two))
-    two_others = [fetch(b, sibling) for b in first_two]
-    inner = permute(orders, acts_two)
-    ends, corners, across, two_last, inner = lax.optimization_barrier(
-        (ends, corners, across, two_last, inner)
-    )
-    two_others += [fetch(b, sibling) for b in two_last]
-    halo = permute(
-        orders,
-        ends[:, 0:4],
+    two_others += [fetch(b, sibling) for b in two_bundles[2:]]
+    spread = spread_inner(orders, acts_two)
+    ends, corners, across, spread = lax.optimization_barrier((ends, corners, across, spread))
+    spread = spread_halo(
+        scalars, orders, ends[:, 0:4],
         jnp.concatenate([ends[:, 4:5], beside], 0),
         jnp.concatenate([corners, across], 0),
+        spread,
     )
     result = conv(
-        scalars, lag_weights, inner, halo, frames.reshape(slots, 128, C), two_bundles, two_others,
+        scalars, lag_weights, spread, frames.reshape(slots, 128, C), two_bundles, two_others,
         finish_add,
     )
     return result.reshape(frames.shape)

time: 123 us -> 122 us (level)
  waiting for transfers between devices: 48.3 us -> 40 us
  starting transfers between devices: 34.5 us -> 41.4 us
    ppermute x27, waiting for transfers between devices: 48.3 us -> 40 us  [fetch(): return lax.ppermute(array, AXES, pairs)]
    ppermute x27, starting transfers between devices: 34.5 us -> 41.4 us  [fetch(): return lax.ppermute(array, AXES, pairs)]
    pallas_call x4, Pallas kernels: 3.53 us -> 6.4 us  [the longest x2 4.16 us: spread_halo(): pl.pallas_call(spread_halo_body, out_shape=jax.ShapeDtypeStruct(spread.sh...]
    pallas_call x2, Pallas kernels: 27.9 us -> 25.2 us  [conv(): pl.pallas_call(lambda *refs: conv_body(*refs, finish=finish), out_shape=j...]
  transfers between devices with their start and end apart: 27 -> 27, of which waited for: 13 -> 9; matrix products, arithmetic and copies ran while one was open for 3% -> 3% of each run, Pallas kernels for 14% -> 16%
where the time goes in v6:
time: 122 us; the launch traced here: 120 us
  starting transfers between devices  41.4 us (34%)
  waiting for transfers between devices  40 us (33%)
  Pallas kernels  32 us (26%)
  local copies, waits for them, and re-layouts  3.06 us (3%)
  between operations  2.07 us (2%)
  other arithmetic  1.73 us (1%)
    ppermute x27, starting transfers between devices, fetch(): return lax.ppermute(array, AXES, pairs)  41.4 us
    ppermute x27, waiting for transfers between devices, fetch(): return lax.ppermute(array, AXES, pairs)  40 us
    pallas_call x2, Pallas kernels, conv(): pl.pallas_call(lambda *refs: conv_body(*refs, finish=finish), out_shape=j...  25.2 us
    pallas_call x2, Pallas kernels, spread_halo(): pl.pallas_call(spread_halo_body, out_shape=jax.ShapeDtypeStruct(spread.sh...  4.16 us
  transfers between devices with their start and end apart: 27, of which 9 were waited for; matrix products, arithmetic and copies ran while one was open for 3% of the time, Pallas kernels for 16%

profile of v6, /device:TPU:131, one launch (start us, length us, event | category | flops | bytes accessed | tf_op | source)
XLA Modules:
  0.0 120.1 jit_solution(14220985192905600310)
XLA Ops:
  0.0 1.1 constant_dynamic-slice_fusion.5
  1.2 1.9 %collective-permute-start = (bf16[2,168,384]{2,1,0:T(8,128)(2,1)S(1)}, bf16[2,168,384]{2,1,0:T(8,128)(2,1)S(1)}, u32[]{:S(2)}, u32[]{:S(2)}) collective-permute-start(bf16[2,168,384]{2,1,0:T(8,128)(2,1)S(1)} %constant_dynamic-update-slice_fusion), channel_id=1, source_target_pairs={{152,0},{1,1},{58,2},{67,3},{252,4},{37,5},{94,6},{103,7},{128,8},... | collective-permute-start | bytes 774152 | tf_op jit(solution)/shard_map/ppermute | solution.py:34
  3.2 2.4 %collective-permute-start.1 = (bf16[2,168,384]{2,1,0:T(8,128)(2,1)S(1)}, bf16[2,168,384]{2,1,0:T(8,128)(2,1)S(1)}, u32[]{:S(2)}, u32[]{:S(2)}) collective-permute-start(bf16[2,168,384]{2,1,0:T(8,128)(2,1)S(1)} %constant_dynamic-update-slice_fusion), channel_id=1, source_target_pairs={{24,0},{129,1},{122,2},{195,3},{188,4},{165,5},{222,6},{231,7},{0,... | collective-permute-start | bytes 774152 | tf_op jit(solution)/shard_map/ppermute | solution.py:34
  7.1 3.2 %collective-permute-start.3 = (bf16[2,4,32,384]{3,2,1,0:T(8,128)(2,1)S(1)}, bf16[2,4,32,384]{3,2,1,0:T(8,128)(2,1)S(1)}, u32[]{:S(2)}, u32[]{:S(2)}) collective-permute-start(bf16[2,4,32,384]{3,2,1,0:T(8,128)(2,1)S(1)} %constant_dynamic-slice_fusion.4), channel_id=1, source_target_pairs={{0,8},{1,9},{2,10},{3,11},{4,12},{5,13},{6,14},{7,15},{8,16},{9,17... | collective-permute-start | bytes 589832 | tf_op jit(solution)/shard_map/ppermute | solution.py:34
  10.3 4.4 %collective-permute-start.4 = (bf16[6,1,32,384]{3,2,1,0:T(8,128)(2,1)S(1)}, bf16[6,1,32,384]{3,2,1,0:T(8,128)(2,1)S(1)}, u32[]{:S(2)}, u32[]{:S(2)}) collective-permute-start(bf16[6,1,32,384]{3,2,1,0:T(8,128)(2,1)S(1)} %get-tuple-element.52), channel_id=1, source_target_pairs={{2,1},{1,2},{4,3},{3,4},{6,5},{5,6},{10,9},{9,10},{12,11},{11,12},... | collective-permute-start | bytes 442376 | tf_op jit(solution)/shard_map/ppermute | solution.py:34
  14.7 2.2 %collective-permute-start.5 = (bf16[2,1,32,384]{3,2,1,0:T(8,128)(2,1)S(1)}, bf16[2,1,32,384]{3,2,1,0:T(8,128)(2,1)S(1)}, u32[]{:S(2)}, u32[]{:S(2)}) collective-permute-start(bf16[2,1,32,384]{3,2,1,0:T(8,128)(2,1)S(1)} %constant_dynamic-slice_fusion.3), channel_id=1, source_target_pairs={{2,9},{1,10},{4,11},{3,12},{6,13},{5,14},{10,17},{9,18},{12,19},{1... | collective-permute-start | bytes 147464 | tf_op jit(solution)/shard_map/ppermute | solution.py:34
  20.3 1.9 %collective-permute-start.2 = (bf16[2,2,168,384]{3,2,1,0:T(8,128)(2,1)S(1)}, bf16[2,2,168,384]{3,2,1,0:T(8,128)(2,1)S(1)}, u32[]{:S(2)}, u32[]{:S(2)}) collective-permute-start(bf16[2,2,168,384]{3,2,1,0:T(8,128)(2,1)S(1)} %pad_maximum_fusion.refs_0_), channel_id=1, source_target_pairs={{2,0},{9,1},{4,2},{11,3},{6,4},{13,5},{0,6},{15,7},{10,8},{17,9},{... | collective-permute-start | bytes 1548296 | tf_op jit(solution)/shard_map/ppermute | solution.py:34
  22.2 1.0 collective-permute-start.7
  23.2 9.7 %collective-permute-done.5 = bf16[2,1,32,384]{3,2,1,0:T(8,128)(2,1)S(1)} collective-permute-done((bf16[2,1,32,384]{3,2,1,0:T(8,128)(2,1)S(1)}, bf16[2,1,32,384]{3,2,1,0:T(8,128)(2,1)S(1)}, u32[]{:S(2)}, u32[]{:S(2)}) %collective-permute-start.5) | collective-permute-done | bytes 49184 | tf_op jit(solution)/shard_map/ppermute | solution.py:34
  33.0 2.1 %collective-permute-start.8 = (bf16[8,1,32,384]{3,2,1,0:T(8,128)(2,1)S(1)}, bf16[8,1,32,384]{3,2,1,0:T(8,128)(2,1)S(1)}, u32[]{:S(2)}, u32[]{:S(2)}) collective-permute-start(bf16[8,1,32,384]{3,2,1,0:T(8,128)(2,1)S(1)} %pad_maximum_fusion.2), channel_id=1, source_target_pairs={{1,0},{0,1},{3,2},{2,3},{5,4},{4,5},{7,6},{6,7},{9,8},{8,9},{11,10... | collective-permute-start | bytes 589832 | tf_op jit(solution)/shard_map/ppermute | solution.py:34
  35.0 1.1 shard_map.127._
  36.2 2.1 %shard_map.128.refs_2_ = bf16[2,8,6,32,1152]{4,3,2,1,0:T(8,128)(2,1)S(1)} custom-call(s32[2]{0:T(128)S(1)} %pad_add_fusion.1.scalars.refs_0_, s32[2,384]{1,0:T(2,128)S(1)} %pad_add_fusion.order, bf16[256,384]{1,0:T(8,128)(2,1)S(1)} %bitcast.42, bf16[256,384]{1,0:T(8,128)(2,1)S(1)} %bitcast.43, ...), custom_call_target="tpu_custom_call", output_to_operand_aliasing={{}: (5, {})} | custom-call | flops 1000 | bytes 1000 | tf_op jit(solution)/shard_map/pallas_call | solution.py:179
  38.3 3.9 %collective-permute-done.6.refs_2_ = bf16[2,2,168,384]{3,2,1,0:T(8,128)(2,1)S(1)} collective-permute-done((bf16[2,2,168,384]{3,2,1,0:T(8,128)(2,1)S(1)}, bf16[2,2,168,384]{3,2,1,0:T(8,128)(2,1)S(1)}, u32[]{:S(2)}, u32[]{:S(2)}) %collective-permute-start.6) | collective-permute-done | bytes 516128 | tf_op jit(solution)/shard_map/ppermute | solution.py:34
  42.6 3.0 %collective-permute-start.12 = (bf16[14,96,384]{2,1,0:T(8,128)(2,1)S(1)}, bf16[14,96,384]{2,1,0:T(8,128)(2,1)S(1)}, u32[]{:S(2)}, u32[]{:S(2)}) collective-permute-start(bf16[14,96,384]{2,1,0:T(8,128)(2,1)S(1)} %shard_map.129.refs_4_), channel_id=1, source_target_pairs={{1,0},{0,1},{3,2},{2,3},{5,4},{4,5},{7,6},{6,7},{9,8},{8,9},{11,10... | collective-permute-start | bytes 3096584 | tf_op jit(solution)/shard_map/ppermute | solution.py:34
  45.7 1.1 collective-permute-start.10
  47.9 1.5 %collective-permute-done.13.refs_8_ = bf16[14,96,384]{2,1,0:T(8,128)(2,1)S(1)} collective-permute-done((bf16[14,96,384]{2,1,0:T(8,128)(2,1)S(1)}, bf16[14,96,384]{2,1,0:T(8,128)(2,1)S(1)}, u32[]{:S(2)}, u32[]{:S(2)}) %collective-permute-start.13) | collective-permute-done | bytes 1032224 | tf_op jit(solution)/shard_map/ppermute | solution.py:34
  49.4 10.1 %collective-permute-done.10.refs_6_ = bf16[14,96,384]{2,1,0:T(8,128)(2,1)S(1)} collective-permute-done((bf16[14,96,384]{2,1,0:T(8,128)(2,1)S(1)}, bf16[14,96,384]{2,1,0:T(8,128)(2,1)S(1)}, u32[]{:S(2)}, u32[]{:S(2)}) %collective-permute-start.10) | collective-permute-done | bytes 1032224 | tf_op jit(solution)/shard_map/ppermute | solution.py:34
  59.5 1.1 collective-permute-done.11.refs_7_
  60.7 1.3 %collective-permute-start.14 = (bf16[14,96,384]{2,1,0:T(8,128)(2,1)S(1)}, bf16[14,96,384]{2,1,0:T(8,128)(2,1)S(1)}, u32[]{:S(2)}, u32[]{:S(2)}) collective-permute-start(bf16[14,96,384]{2,1,0:T(8,128)(2,1)S(1)} %collective-permute-done.9.refs_5_), channel_id=1, source_target_pairs={{1,0},{0,1},{3,2},{2,3},{5,4},{4,5},{7,6},{6,7},{9,8},{8,9},{11,10... | collective-permute-start | bytes 3096584 | tf_op jit(solution)/shard_map/ppermute | solution.py:34
  62.5 1.8 %collective-permute-done.14.refs_9_ = bf16[14,96,384]{2,1,0:T(8,128)(2,1)S(1)} collective-permute-done((bf16[14,96,384]{2,1,0:T(8,128)(2,1)S(1)}, bf16[14,96,384]{2,1,0:T(8,128)(2,1)S(1)}, u32[]{:S(2)}, u32[]{:S(2)}) %collective-permute-start.14) | collective-permute-done | bytes 1032224 | tf_op jit(solution)/shard_map/ppermute | solution.py:34
  64.3 1.5 %collective-permute-start.16 = (bf16[14,96,384]{2,1,0:T(8,128)(2,1)S(1)}, bf16[14,96,384]{2,1,0:T(8,128)(2,1)S(1)}, u32[]{:S(2)}, u32[]{:S(2)}) collective-permute-start(bf16[14,96,384]{2,1,0:T(8,128)(2,1)S(1)} %shard_map.130.refs_4_), channel_id=1, source_target_pairs={{24,0},{7,1},{26,2},{1,3},{28,4},{3,5},{30,6},{5,7},{0,8},{15,9},{... | collective-permute-start | bytes 3096584 | tf_op jit(solution)/shard_map/ppermute | solution.py:34
  65.7 2.6 %collective-permute-start.17 = (bf16[14,96,384]{2,1,0:T(8,128)(2,1)S(1)}, bf16[14,96,384]{2,1,0:T(8,128)(2,1)S(1)}, u32[]{:S(2)}, u32[]{:S(2)}) collective-permute-start(bf16[14,96,384]{2,1,0:T(8,128)(2,1)S(1)} %shard_map.130.refs_4_), channel_id=1, source_target_pairs={{224,0},{33,1},{226,2},{35,3},{228,4},{37,5},{230,6},{39,7},{232,8... | collective-permute-start | bytes 3096584 | tf_op jit(solution)/shard_map/ppermute | solution.py:34
  68.4 12.3 %shard_map.131 = bf16[6,128,384]{2,1,0:T(8,128)(2,1)S(1)} custom-call(s32[2]{0:T(128)S(1)} %pad_add_fusion.1.scalars.refs_0_, f32[3,6]{1,0:T(4,128)S(1)} %add_convert_fusion.refs_1_, bf16[2,8,6,32,1152]{4,3,2,1,0:T(8,128)(2,1)S(1)} %shard_map.128.refs_2_, f32[1,384]{1,0:T(1,128)S(1)} %reshape.269.refs_3_, bf16[14,96,384]{2,1,0:T(8,128)(2,1)S(1)} %shard_map.129.refs_4_, ...), custom_call_target="tpu_custom_call" | custom-call | flops 1000 | bytes 1000 | tf_op jit(solution)/shard_map/pallas_call | solution.py:284
  80.7 3.0 %collective-permute-start.21 = (bf16[14,96,384]{2,1,0:T(8,128)(2,1)S(1)}, bf16[14,96,384]{2,1,0:T(8,128)(2,1)S(1)}, u32[]{:S(2)}, u32[]{:S(2)}) collective-permute-start(bf16[14,96,384]{2,1,0:T(8,128)(2,1)S(1)} %collective-permute-done.15.refs_5_), channel_id=1, source_target_pairs={{1,0},{0,1},{3,2},{2,3},{5,4},{4,5},{7,6},{6,7},{9,8},{8,9},{11,10... | collective-permute-start | bytes 3096584 | tf_op jit(solution)/shard_map/ppermute | solution.py:34
  84.4 4.7 %collective-permute-done.20 = bf16[6,1,32,384]{3,2,1,0:T(8,128)(2,1)S(1)} collective-permute-done((bf16[6,1,32,384]{3,2,1,0:T(8,128)(2,1)S(1)}, bf16[6,1,32,384]{3,2,1,0:T(8,128)(2,1)S(1)}, u32[]{:S(2)}, u32[]{:S(2)}) %collective-permute-start.20) | collective-permute-done | bytes 147488 | tf_op jit(solution)/shard_map/ppermute | solution.py:34
  89.2 1.9 %collective-permute-start.22 = (bf16[2,5,32,384]{3,2,1,0:T(8,128)(2,1)S(1)}, bf16[2,5,32,384]{3,2,1,0:T(8,128)(2,1)S(1)}, u32[]{:S(2)}, u32[]{:S(2)}) collective-permute-start(bf16[2,5,32,384]{3,2,1,0:T(8,128)(2,1)S(1)} %pad_maximum_fusion.1), channel_id=1, source_target_pairs={{0,8},{1,9},{2,10},{3,11},{4,12},{5,13},{6,14},{7,15},{8,16},{9,17... | collective-permute-start | bytes 737288 | tf_op jit(solution)/shard_map/ppermute | solution.py:34
  91.1 3.3 %collective-permute-start.24 = (bf16[6,1,32,384]{3,2,1,0:T(8,128)(2,1)S(1)}, bf16[6,1,32,384]{3,2,1,0:T(8,128)(2,1)S(1)}, u32[]{:S(2)}, u32[]{:S(2)}) collective-permute-start(bf16[6,1,32,384]{3,2,1,0:T(8,128)(2,1)S(1)} %get-tuple-element.93), channel_id=1, source_target_pairs={{2,1},{1,2},{4,3},{3,4},{6,5},{5,6},{10,9},{9,10},{12,11},{11,12},... | collective-permute-start | bytes 442376 | tf_op jit(solution)/shard_map/ppermute | solution.py:34
  94.4 2.8 %collective-permute-start.23 = (bf16[2,1,32,384]{3,2,1,0:T(8,128)(2,1)S(1)}, bf16[2,1,32,384]{3,2,1,0:T(8,128)(2,1)S(1)}, u32[]{:S(2)}, u32[]{:S(2)}) collective-permute-start(bf16[2,1,32,384]{3,2,1,0:T(8,128)(2,1)S(1)} %constant_dynamic-slice_fusion), channel_id=1, source_target_pairs={{2,9},{1,10},{4,11},{3,12},{6,13},{5,14},{10,17},{9,18},{12,19},{1... | collective-permute-start | bytes 147464 | tf_op jit(solution)/shard_map/ppermute | solution.py:34
  97.3 1.1 shard_map.132._
  98.4 6.4 %collective-permute-done.23 = bf16[2,1,32,384]{3,2,1,0:T(8,128)(2,1)S(1)} collective-permute-done((bf16[2,1,32,384]{3,2,1,0:T(8,128)(2,1)S(1)}, bf16[2,1,32,384]{3,2,1,0:T(8,128)(2,1)S(1)}, u32[]{:S(2)}, u32[]{:S(2)}) %collective-permute-start.23) | collective-permute-done | bytes 49184 | tf_op jit(solution)/shard_map/ppermute | solution.py:34
  105.0 2.1 %shard_map.133.refs_2_ = bf16[2,8,6,32,1152]{4,3,2,1,0:T(8,128)(2,1)S(1)} custom-call(s32[2]{0:T(128)S(1)} %pad_add_fusion.1.scalars.refs_0_, s32[2,384]{1,0:T(2,128)S(1)} %pad_add_fusion.order, bf16[256,384]{1,0:T(8,128)(2,1)S(1)} %bitcast.39, bf16[256,384]{1,0:T(8,128)(2,1)S(1)} %bitcast.40, ...), custom_call_target="tpu_custom_call", output_to_operand_aliasing={{}: (5, {})} | custom-call | flops 1000 | bytes 1000 | tf_op jit(solution)/shard_map/pallas_call | solution.py:179
  107.1 12.9 %shard_map.134 = bf16[6,128,384]{2,1,0:T(8,128)(2,1)} custom-call(s32[2]{0:T(128)S(1)} %pad_add_fusion.1.scalars.refs_0_, f32[3,6]{1,0:T(4,128)S(1)} %add_convert_fusion.refs_1_, bf16[2,8,6,32,1152]{4,3,2,1,0:T(8,128)(2,1)S(1)} %shard_map.133.refs_2_, bf16[6,128,384]{2,1,0:T(8,128)(2,1)S(1)} %bitcast.33, bf16[14,96,384]{2,1,0:T(8,128)(2,1)S(1)} %shard_map.130.refs_4_, ...), custom_call_target="tpu_custom_call" | custom-call | flops 1000 | bytes 1000 | tf_op jit(solution)/shard_map/pallas_call | solution.py:284
  (98 shorter events, 6.4 us)
Async XLA Ops:
  1.2 19.0 %collective-permute-start = (bf16[2,168,384]{2,1,0:T(8,128)(2,1)S(1)}, bf16[2,168,384]{2,1,0:T(8,128)(2,1)S(1)}, u32[]{:S(2)}, u32[]{:S(2)}) collective-permute-start(bf16[2,168,384]{2,1,0:T(8,128)(2,1)S(1)} %constant_dynamic-update-slice_fusion), channel_id=1, source_target_pairs={{152,0},{1,1},{58,2},{67,3},{252,4},{37,5},{94,6},{103,7},{128,8},... | collective-permute-start | bytes 774152 | tf_op jit(solution)/shard_map/ppermute | solution.py:34
  3.2 17.0 %collective-permute-start.1 = (bf16[2,168,384]{2,1,0:T(8,128)(2,1)S(1)}, bf16[2,168,384]{2,1,0:T(8,128)(2,1)S(1)}, u32[]{:S(2)}, u32[]{:S(2)}) collective-permute-start(bf16[2,168,384]{2,1,0:T(8,128)(2,1)S(1)} %constant_dynamic-update-slice_fusion), channel_id=1, source_target_pairs={{24,0},{129,1},{122,2},{195,3},{188,4},{165,5},{222,6},{231,7},{0,... | collective-permute-start | bytes 774152 | tf_op jit(solution)/shard_map/ppermute | solution.py:34
  6.5 10.5 %copy-start.7 = (s32[4]{0:T(128)S(1)}, s32[4]{0:T(128)}, u32[]{:S(2)}) copy-start(s32[4]{0:T(128)} %constant.150.clone) | copy-start | bytes 52
  6.5 10.5 %copy-start.2 = (s32[4,2]{1,0:T(4,128)S(1)}, s32[4,2]{1,0:T(4,128)}, u32[]{:S(2)}) copy-start(s32[4,2]{1,0:T(4,128)} %constant.159) | copy-start | bytes 100
  6.5 11.5 %copy-start.1 = (s32[4,2]{1,0:T(4,128)S(1)}, s32[4,2]{1,0:T(4,128)}, u32[]{:S(2)}) copy-start(s32[4,2]{1,0:T(4,128)} %constant.161) | copy-start | bytes 100
  6.6 13.0 %copy-start.8 = (s32[3]{0:T(128)S(1)}, s32[3]{0:T(128)}, u32[]{:S(2)}) copy-start(s32[3]{0:T(128)} %param.14) | copy-start | bytes 40
  7.1 25.8 %collective-permute-start.3 = (bf16[2,4,32,384]{3,2,1,0:T(8,128)(2,1)S(1)}, bf16[2,4,32,384]{3,2,1,0:T(8,128)(2,1)S(1)}, u32[]{:S(2)}, u32[]{:S(2)}) collective-permute-start(bf16[2,4,32,384]{3,2,1,0:T(8,128)(2,1)S(1)} %constant_dynamic-slice_fusion.4), channel_id=1, source_target_pairs={{0,8},{1,9},{2,10},{3,11},{4,12},{5,13},{6,14},{7,15},{8,16},{9,17... | collective-permute-start | bytes 589832 | tf_op jit(solution)/shard_map/ppermute | solution.py:34
  10.3 22.6 %collective-permute-start.4 = (bf16[6,1,32,384]{3,2,1,0:T(8,128)(2,1)S(1)}, bf16[6,1,32,384]{3,2,1,0:T(8,128)(2,1)S(1)}, u32[]{:S(2)}, u32[]{:S(2)}) collective-permute-start(bf16[6,1,32,384]{3,2,1,0:T(8,128)(2,1)S(1)} %get-tuple-element.52), channel_id=1, source_target_pairs={{2,1},{1,2},{4,3},{3,4},{6,5},{5,6},{10,9},{9,10},{12,11},{11,12},... | collective-permute-start | bytes 442376 | tf_op jit(solution)/shard_map/ppermute | solution.py:34
  14.7 18.2 %collective-permute-start.5 = (bf16[2,1,32,384]{3,2,1,0:T(8,128)(2,1)S(1)}, bf16[2,1,32,384]{3,2,1,0:T(8,128)(2,1)S(1)}, u32[]{:S(2)}, u32[]{:S(2)}) collective-permute-start(bf16[2,1,32,384]{3,2,1,0:T(8,128)(2,1)S(1)} %constant_dynamic-slice_fusion.3), channel_id=1, source_target_pairs={{2,9},{1,10},{4,11},{3,12},{6,13},{5,14},{10,17},{9,18},{12,19},{1... | collective-permute-start | bytes 147464 | tf_op jit(solution)/shard_map/ppermute | solution.py:34
  20.3 21.9 %collective-permute-start.2 = (bf16[2,2,168,384]{3,2,1,0:T(8,128)(2,1)S(1)}, bf16[2,2,168,384]{3,2,1,0:T(8,128)(2,1)S(1)}, u32[]{:S(2)}, u32[]{:S(2)}) collective-permute-start(bf16[2,2,168,384]{3,2,1,0:T(8,128)(2,1)S(1)} %pad_maximum_fusion.refs_0_), channel_id=1, source_target_pairs={{2,0},{9,1},{4,2},{11,3},{6,4},{13,5},{0,6},{15,7},{10,8},{17,9},{... | collective-permute-start | bytes 1548296 | tf_op jit(solution)/shard_map/ppermute | solution.py:34
  22.2 20.0 %collective-permute-start.7 = (bf16[2,2,168,384]{3,2,1,0:T(8,128)(2,1)S(1)}, bf16[2,2,168,384]{3,2,1,0:T(8,128)(2,1)S(1)}, u32[]{:S(2)}, u32[]{:S(2)}) collective-permute-start(bf16[2,2,168,384]{3,2,1,0:T(8,128)(2,1)S(1)} %pad_maximum_fusion.refs_0_), channel_id=1, source_target_pairs={{4,0},{17,1},{6,2},{19,3},{0,4},{21,5},{2,6},{23,7},{12,8},{25,9},... | collective-permute-start | bytes 1548296 | tf_op jit(solution)/shard_map/ppermute | solution.py:34
  32.9 9.3 %collective-permute-start.6 = (bf16[2,2,168,384]{3,2,1,0:T(8,128)(2,1)S(1)}, bf16[2,2,168,384]{3,2,1,0:T(8,128)(2,1)S(1)}, u32[]{:S(2)}, u32[]{:S(2)}) collective-permute-start(bf16[2,2,168,384]{3,2,1,0:T(8,128)(2,1)S(1)} %pad_maximum_fusion.refs_0_), channel_id=1, source_target_pairs={{6,0},{25,1},{0,2},{27,3},{2,4},{29,5},{4,6},{31,7},{14,8},{1,9},{... | collective-permute-start | bytes 1548296 | tf_op jit(solution)/shard_map/ppermute | solution.py:34
  33.0 3.2 %collective-permute-start.8 = (bf16[8,1,32,384]{3,2,1,0:T(8,128)(2,1)S(1)}, bf16[8,1,32,384]{3,2,1,0:T(8,128)(2,1)S(1)}, u32[]{:S(2)}, u32[]{:S(2)}) collective-permute-start(bf16[8,1,32,384]{3,2,1,0:T(8,128)(2,1)S(1)} %pad_maximum_fusion.2), channel_id=1, source_target_pairs={{1,0},{0,1},{3,2},{2,3},{5,4},{4,5},{7,6},{6,7},{9,8},{8,9},{11,10... | collective-permute-start | bytes 589832 | tf_op jit(solution)/shard_map/ppermute | solution.py:34
  42.4 25.9 %copy-start.4 = (f32[384]{0:T(512)S(1)}, f32[384]{0:T(512)}, u32[]{:S(2)}) copy-start(f32[384]{0:T(512)} %param.20) | copy-start | bytes 4612
  42.6 5.3 %collective-permute-start.12 = (bf16[14,96,384]{2,1,0:T(8,128)(2,1)S(1)}, bf16[14,96,384]{2,1,0:T(8,128)(2,1)S(1)}, u32[]{:S(2)}, u32[]{:S(2)}) collective-permute-start(bf16[14,96,384]{2,1,0:T(8,128)(2,1)S(1)} %shard_map.129.refs_4_), channel_id=1, source_target_pairs={{1,0},{0,1},{3,2},{2,3},{5,4},{4,5},{7,6},{6,7},{9,8},{8,9},{11,10... | collective-permute-start | bytes 3096584 | tf_op jit(solution)/shard_map/ppermute | solution.py:34
  45.6 3.7 %collective-permute-start.13 = (bf16[14,96,384]{2,1,0:T(8,128)(2,1)S(1)}, bf16[14,96,384]{2,1,0:T(8,128)(2,1)S(1)}, u32[]{:S(2)}, u32[]{:S(2)}) collective-permute-start(bf16[14,96,384]{2,1,0:T(8,128)(2,1)S(1)} %shard_map.130.refs_4_), channel_id=1, source_target_pairs={{1,0},{0,1},{3,2},{2,3},{5,4},{4,5},{7,6},{6,7},{9,8},{8,9},{11,10... | collective-permute-start | bytes 3096584 | tf_op jit(solution)/shard_map/ppermute | solution.py:34
  45.7 13.8 %collective-permute-start.10 = (bf16[14,96,384]{2,1,0:T(8,128)(2,1)S(1)}, bf16[14,96,384]{2,1,0:T(8,128)(2,1)S(1)}, u32[]{:S(2)}, u32[]{:S(2)}) collective-permute-start(bf16[14,96,384]{2,1,0:T(8,128)(2,1)S(1)} %shard_map.129.refs_4_), channel_id=1, source_target_pairs={{24,0},{7,1},{26,2},{1,3},{28,4},{3,5},{30,6},{5,7},{0,8},{15,9},{... | collective-permute-start | bytes 3096584 | tf_op jit(solution)/shard_map/ppermute | solution.py:34
  46.9 13.8 %collective-permute-start.11 = (bf16[14,96,384]{2,1,0:T(8,128)(2,1)S(1)}, bf16[14,96,384]{2,1,0:T(8,128)(2,1)S(1)}, u32[]{:S(2)}, u32[]{:S(2)}) collective-permute-start(bf16[14,96,384]{2,1,0:T(8,128)(2,1)S(1)} %shard_map.129.refs_4_), channel_id=1, source_target_pairs={{224,0},{33,1},{226,2},{35,3},{228,4},{37,5},{230,6},{39,7},{232,8... | collective-permute-start | bytes 3096584 | tf_op jit(solution)/shard_map/ppermute | solution.py:34
  46.9 13.8 %collective-permute-start.9 = (bf16[14,96,384]{2,1,0:T(8,128)(2,1)S(1)}, bf16[14,96,384]{2,1,0:T(8,128)(2,1)S(1)}, u32[]{:S(2)}, u32[]{:S(2)}) collective-permute-start(bf16[14,96,384]{2,1,0:T(8,128)(2,1)S(1)} %shard_map.129.refs_4_), channel_id=1, source_target_pairs={{8,0},{3,1},{10,2},{5,3},{12,4},{7,5},{14,6},{1,7},{16,8},{11,9},{... | collective-permute-start | bytes 3096584 | tf_op jit(solution)/shard_map/ppermute | solution.py:34
  60.7 3.6 %collective-permute-start.14 = (bf16[14,96,384]{2,1,0:T(8,128)(2,1)S(1)}, bf16[14,96,384]{2,1,0:T(8,128)(2,1)S(1)}, u32[]{:S(2)}, u32[]{:S(2)}) collective-permute-start(bf16[14,96,384]{2,1,0:T(8,128)(2,1)S(1)} %collective-permute-done.9.refs_5_), channel_id=1, source_target_pairs={{1,0},{0,1},{3,2},{2,3},{5,4},{4,5},{7,6},{6,7},{9,8},{8,9},{11,10... | collective-permute-start | bytes 3096584 | tf_op jit(solution)/shard_map/ppermute | solution.py:34
  62.0 6.3 %collective-permute-start.18 = (bf16[14,96,384]{2,1,0:T(8,128)(2,1)S(1)}, bf16[14,96,384]{2,1,0:T(8,128)(2,1)S(1)}, u32[]{:S(2)}, u32[]{:S(2)}) collective-permute-start(bf16[14,96,384]{2,1,0:T(8,128)(2,1)S(1)} %collective-permute-done.10.refs_6_), channel_id=1, source_target_pairs={{1,0},{0,1},{3,2},{2,3},{5,4},{4,5},{7,6},{6,7},{9,8},{8,9},{11,10... | collective-permute-start | bytes 3096584 | tf_op jit(solution)/shard_map/ppermute | solution.py:34
  62.3 6.1 %collective-permute-start.19 = (bf16[14,96,384]{2,1,0:T(8,128)(2,1)S(1)}, bf16[14,96,384]{2,1,0:T(8,128)(2,1)S(1)}, u32[]{:S(2)}, u32[]{:S(2)}) collective-permute-start(bf16[14,96,384]{2,1,0:T(8,128)(2,1)S(1)} %collective-permute-done.11.refs_7_), channel_id=1, source_target_pairs={{1,0},{0,1},{3,2},{2,3},{5,4},{4,5},{7,6},{6,7},{9,8},{8,9},{11,10... | collective-permute-start | bytes 3096584 | tf_op jit(solution)/shard_map/ppermute | solution.py:34
  64.3 16.4 %collective-permute-start.15 = (bf16[14,96,384]{2,1,0:T(8,128)(2,1)S(1)}, bf16[14,96,384]{2,1,0:T(8,128)(2,1)S(1)}, u32[]{:S(2)}, u32[]{:S(2)}) collective-permute-start(bf16[14,96,384]{2,1,0:T(8,128)(2,1)S(1)} %shard_map.130.refs_4_), channel_id=1, source_target_pairs={{8,0},{3,1},{10,2},{5,3},{12,4},{7,5},{14,6},{1,7},{16,8},{11,9},{... | collective-permute-start | bytes 3096584 | tf_op jit(solution)/shard_map/ppermute | solution.py:34
  64.3 16.4 %collective-permute-start.16 = (bf16[14,96,384]{2,1,0:T(8,128)(2,1)S(1)}, bf16[14,96,384]{2,1,0:T(8,128)(2,1)S(1)}, u32[]{:S(2)}, u32[]{:S(2)}) collective-permute-start(bf16[14,96,384]{2,1,0:T(8,128)(2,1)S(1)} %shard_map.130.refs_4_), channel_id=1, source_target_pairs={{24,0},{7,1},{26,2},{1,3},{28,4},{3,5},{30,6},{5,7},{0,8},{15,9},{... | collective-permute-start | bytes 3096584 | tf_op jit(solution)/shard_map/ppermute | solution.py:34
  65.7 14.9 %collective-permute-start.17 = (bf16[14,96,384]{2,1,0:T(8,128)(2,1)S(1)}, bf16[14,96,384]{2,1,0:T(8,128)(2,1)S(1)}, u32[]{:S(2)}, u32[]{:S(2)}) collective-permute-start(bf16[14,96,384]{2,1,0:T(8,128)(2,1)S(1)} %shard_map.130.refs_4_), channel_id=1, source_target_pairs={{224,0},{33,1},{226,2},{35,3},{228,4},{37,5},{230,6},{39,7},{232,8... | collective-permute-start | bytes 3096584 | tf_op jit(solution)/shard_map/ppermute | solution.py:34
  80.7 8.5 %collective-permute-start.21 = (bf16[14,96,384]{2,1,0:T(8,128)(2,1)S(1)}, bf16[14,96,384]{2,1,0:T(8,128)(2,1)S(1)}, u32[]{:S(2)}, u32[]{:S(2)}) collective-permute-start(bf16[14,96,384]{2,1,0:T(8,128)(2,1)S(1)} %collective-permute-done.15.refs_5_), channel_id=1, source_target_pairs={{1,0},{0,1},{3,2},{2,3},{5,4},{4,5},{7,6},{6,7},{9,8},{8,9},{11,10... | collective-permute-start | bytes 3096584 | tf_op jit(solution)/shard_map/ppermute | solution.py:34
  83.7 23.3 %collective-permute-start.25 = (bf16[14,96,384]{2,1,0:T(8,128)(2,1)S(1)}, bf16[14,96,384]{2,1,0:T(8,128)(2,1)S(1)}, u32[]{:S(2)}, u32[]{:S(2)}) collective-permute-start(bf16[14,96,384]{2,1,0:T(8,128)(2,1)S(1)} %collective-permute-done.16.refs_6_), channel_id=1, source_target_pairs={{1,0},{0,1},{3,2},{2,3},{5,4},{4,5},{7,6},{6,7},{9,8},{8,9},{11,10... | collective-permute-start | bytes 3096584 | tf_op jit(solution)/shard_map/ppermute | solution.py:34
  83.7 23.3 %collective-permute-start.26 = (bf16[14,96,384]{2,1,0:T(8,128)(2,1)S(1)}, bf16[14,96,384]{2,1,0:T(8,128)(2,1)S(1)}, u32[]{:S(2)}, u32[]{:S(2)}) collective-permute-start(bf16[14,96,384]{2,1,0:T(8,128)(2,1)S(1)} %collective-permute-done.17.refs_7_), channel_id=1, source_target_pairs={{1,0},{0,1},{3,2},{2,3},{5,4},{4,5},{7,6},{6,7},{9,8},{8,9},{11,10... | collective-permute-start | bytes 3096584 | tf_op jit(solution)/shard_map/ppermute | solution.py:34
  84.3 4.9 %collective-permute-start.20 = (bf16[6,1,32,384]{3,2,1,0:T(8,128)(2,1)S(1)}, bf16[6,1,32,384]{3,2,1,0:T(8,128)(2,1)S(1)}, u32[]{:S(2)}, u32[]{:S(2)}) collective-permute-start(bf16[6,1,32,384]{3,2,1,0:T(8,128)(2,1)S(1)} %get-tuple-element.94), channel_id=1, source_target_pairs={{1,0},{0,1},{3,2},{2,3},{5,4},{4,5},{7,6},{6,7},{9,8},{8,9},{11,10... | collective-permute-start | bytes 442376 | tf_op jit(solution)/shard_map/ppermute | solution.py:34
  89.2 15.7 %collective-permute-start.22 = (bf16[2,5,32,384]{3,2,1,0:T(8,128)(2,1)S(1)}, bf16[2,5,32,384]{3,2,1,0:T(8,128)(2,1)S(1)}, u32[]{:S(2)}, u32[]{:S(2)}) collective-permute-start(bf16[2,5,32,384]{3,2,1,0:T(8,128)(2,1)S(1)} %pad_maximum_fusion.1), channel_id=1, source_target_pairs={{0,8},{1,9},{2,10},{3,11},{4,12},{5,13},{6,14},{7,15},{8,16},{9,17... | collective-permute-start | bytes 737288 | tf_op jit(solution)/shard_map/ppermute | solution.py:34
  91.1 7.3 %collective-permute-start.24 = (bf16[6,1,32,384]{3,2,1,0:T(8,128)(2,1)S(1)}, bf16[6,1,32,384]{3,2,1,0:T(8,128)(2,1)S(1)}, u32[]{:S(2)}, u32[]{:S(2)}) collective-permute-start(bf16[6,1,32,384]{3,2,1,0:T(8,128)(2,1)S(1)} %get-tuple-element.93), channel_id=1, source_target_pairs={{2,1},{1,2},{4,3},{3,4},{6,5},{5,6},{10,9},{9,10},{12,11},{11,12},... | collective-permute-start | bytes 442376 | tf_op jit(solution)/shard_map/ppermute | solution.py:34
  94.4 10.4 %collective-permute-start.23 = (bf16[2,1,32,384]{3,2,1,0:T(8,128)(2,1)S(1)}, bf16[2,1,32,384]{3,2,1,0:T(8,128)(2,1)S(1)}, u32[]{:S(2)}, u32[]{:S(2)}) collective-permute-start(bf16[2,1,32,384]{3,2,1,0:T(8,128)(2,1)S(1)} %constant_dynamic-slice_fusion), channel_id=1, source_target_pairs={{2,9},{1,10},{4,11},{3,12},{6,13},{5,14},{10,17},{9,18},{12,19},{1... | collective-permute-start | bytes 147464 | tf_op jit(solution)/shard_map/ppermute | solution.py:34
  (4 other events, 33.7 us)

commit v7 on v6

--- a/solution.py
+++ b/solution.py
@@ -142,50 +142,41 @@
     )(orders, acts.reshape(-1, C))
 
 
-def spread_halo_body(scalars, order, carried, beside, across, _, out, frames, rows, sems):
+def spread_halo_body(scalars, order, carried, beside, across, _, out):
     core = scalars[0]
     for half in range(2):
         for tap, part in enumerate(spread_cells(carried[...], order, half)):
-            frames[half, :, :, :, C * tap : C * (tap + 1)] = part.reshape(2, 4, 32, C)
-        for side, cells in enumerate((beside, across)):
-            for tap, part in enumerate(spread_cells(cells[...], order, half)):
-                rows[side, half, :, :, :, C * tap : C * (tap + 1)] = part.reshape(8, 1, 32, C)
-
-    def copies(above, below):
-        return [
-            pltpu.make_async_copy(frames, out.at[:, 0:2, 1:5], sems.at[0]),
-            pltpu.make_async_copy(rows.at[above], out.at[:, :, 0:1], sems.at[1]),
-            pltpu.make_async_copy(rows.at[below], out.at[:, :, 5:6], sems.at[2]),
-        ]
-
-    @pl.when(core == 0)
-    def _():
-        for copy in copies(1, 0):
-            copy.start()
-        for copy in copies(1, 0):
-            copy.wait()
-
-    @pl.when(core == 1)
-    def _():
-        for copy in copies(0, 1):
-            copy.start()
-        for copy in copies(0, 1):
-            copy.wait()
+            out[half, 0:2, 1:5, :, C * tap : C * (tap + 1)] = part.reshape(2, 4, 32, C)
+        for tap, part in enumerate(spread_cells(beside[...], order, half)):
+            part = part.reshape(8, 1, 32, C)
+
+            @pl.when(core == 0)
+            def _():
+                out[half, :, 5:6, :, C * tap : C * (tap + 1)] = part
+
+            @pl.when(core == 1)
+            def _():
+                out[half, :, 0:1, :, C * tap : C * (tap + 1)] = part
+
+        for tap, part in enumerate(spread_cells(across[...], order, half)):
+            part = part.reshape(8, 1, 32, C)
+
+            @pl.when(core == 0)
+            def _():
+                out[half, :, 0:1, :, C * tap : C * (tap + 1)] = part
+
+            @pl.when(core == 1)
+            def _():
+                out[half, :, 5:6, :, C * tap : C * (tap + 1)] = part
 
 
 def spread_halo(scalars, orders, carried, beside, across, spread):
     vmem = pl.BlockSpec(memory_space=pltpu.VMEM)
-    either = pl.BlockSpec(memory_space=pl.ANY)
     return pl.pallas_call(
         spread_halo_body,
         out_shape=jax.ShapeDtypeStruct(spread.shape, spread.dtype),
-        in_specs=[pl.BlockSpec(memory_space=pltpu.SMEM)] + [vmem] * 4 + [either],
-        out_specs=either,
-        scratch_shapes=[
-            pltpu.VMEM((2, 2, 4, 32, 3 * C), jnp.bfloat16),
-            pltpu.VMEM((2, 2, 8, 1, 32, 3 * C), jnp.bfloat16),
-            pltpu.SemaphoreType.DMA((3,)),
-        ],
+        in_specs=[pl.BlockSpec(memory_space=pltpu.SMEM)] + [vmem] * 5,
+        out_specs=vmem,
         input_output_aliases={5: 0},
         compiler_params=pltpu.CompilerParams(vmem_limit_bytes=20 * 1024 * 1024),
         cost_estimate=pl.CostEstimate(flops=1000, bytes_accessed=1000, transcendentals=0),
@@ -350,19 +341,20 @@
     own = jnp.stack([own_half(kernel_one), own_half(kernel_two)])
     pieces = z_stage(own)
     inner, outer = sides(acts_one)
-    ends, corners, outer = lax.optimization_barrier((last_two(acts_one), last_two(outer), outer))
+    ends, outer = lax.optimization_barrier((last_two(acts_one), outer))
     carried = fetch(ends, before_in_group)
     across = fetch(outer, across_chips)
-    corners = fetch(corners, across_and_before)
     pieces, orders, lag_weights, scalars = lax.optimization_barrier(
         (pieces, orders, lag_weights, scalars)
     )
 
     opposite = fetch(pieces, small_source(2))
     after = fetch(pieces, small_source(1))
-    gated, carried, across, corners = lax.optimization_barrier((pieces, carried, across, corners))
+    gated, carried, across = lax.optimization_barrier((pieces, carried, across))
     parts = [pieces, after, fetch(gated, small_source(-1)), opposite]
-    beside = fetch(jnp.concatenate([sides(carried)[0], inner], 0), sibling)
+    carried_inner, carried_outer = sides(carried)
+    corners = fetch(carried_outer, across_chips)
+    beside = fetch(jnp.concatenate([carried_inner, inner], 0), sibling)
     spread = spread_halo(
         scalars, orders, carried, beside, jnp.concatenate([corners, across], 0),
         spread_inner(orders, acts_one),
@@ -373,12 +365,14 @@
     one_bundles = bulk_stage(one_bundle)
     one_own, two_own = lax.optimization_barrier((one_bundle, two_bundle))
     one_others, two_others = [fetch(one_own, sibling)], [fetch(two_own, sibling)]
-    one_bundles, two_bundle, one_others, two_others = lax.optimization_barrier(
-        (one_bundles, two_bundle, one_others, two_others)
+    two_bundle, one_others, two_others = lax.optimization_barrier(
+        (two_bundle, one_others, two_others)
+    )
+    one_bundles, one_others, two_others = lax.optimization_barrier(
+        (one_bundles, one_others, two_others)
     )
     one_others += [fetch(b, sibling) for b in one_bundles[1:]]
 
-    two_bundle, one_others[1] = lax.optimization_barrier((two_bundle, one_others[1]))
     two_bundles = bulk_stage(two_bundle)
     acts_two = conv(
         scalars, lag_weights, spread, gain_two.reshape(1, C), one_bundles, one_others, finish_norm
@@ -388,17 +382,17 @@
     inner, outer = sides(acts_two)
     beside = fetch(inner, sibling)
     across = fetch(outer, across_chips)
-    two_others.append(fetch(two_bundles[1], sibling))
-    two_bundles[1], beside, two_others = lax.optimization_barrier(
-        (two_bundles[1], beside, two_others)
-    )
+    two_bundles, beside = lax.optimization_barrier((two_bundles, beside))
     ends = jnp.concatenate([last_two(acts_two), last_two(beside)], 1)
     ends, corners = lax.optimization_barrier((ends, last_two(outer)))
     ends = fetch(ends, before_in_group)
     corners = fetch(corners, across_and_before)
-    two_others += [fetch(b, sibling) for b in two_bundles[2:]]
+    two_others += [fetch(b, sibling) for b in two_bundles[1:3]]
     spread = spread_inner(orders, acts_two)
-    ends, corners, across, spread = lax.optimization_barrier((ends, corners, across, spread))
+    ends, corners, across, spread, two_last = lax.optimization_barrier(
+        (ends, corners, across, spread, two_bundles[3])
+    )
+    two_others.append(fetch(two_last, sibling))
     spread = spread_halo(
         scalars, orders, ends[:, 0:4],
         jnp.concatenate([ends[:, 4:5], beside], 0),

time: 122 us -> 117 us (0.959); the launches traced: 120 us -> 117 us
  waiting for transfers between devices: 40 us -> 29.7 us
  starting transfers between devices: 41.4 us -> 47.5 us
    ppermute x27, waiting for transfers between devices: 40 us -> 29.7 us  [fetch(): return lax.ppermute(array, AXES, pairs)]
    ppermute x27, starting transfers between devices: 41.4 us -> 47.5 us  [fetch(): return lax.ppermute(array, AXES, pairs)]
  transfers between devices with their start and end apart: 27 -> 27, of which waited for: 9 -> 10; matrix products, arithmetic and copies ran while one was open for 3% -> 3% of each run, Pallas kernels for 16% -> 17%
where the time goes in v7:
time: 117 us
  starting transfers between devices  47.5 us (41%)
  Pallas kernels  32.5 us (28%)
  waiting for transfers between devices  29.7 us (25%)
  local copies, waits for them, and re-layouts  3.02 us (3%)
  between operations  2.03 us (2%)
  other arithmetic  1.73 us (1%)
    ppermute x27, starting transfers between devices, fetch(): return lax.ppermute(array, AXES, pairs)  47.5 us
    ppermute x27, waiting for transfers between devices, fetch(): return lax.ppermute(array, AXES, pairs)  29.7 us
    pallas_call x2, Pallas kernels, conv(): pl.pallas_call(lambda *refs: conv_body(*refs, finish=finish), out_shape=j...  24.9 us
    pallas_call x2, Pallas kernels, spread_halo(): pl.pallas_call(spread_halo_body, out_shape=jax.ShapeDtypeStruct(spread.sh...  4.97 us
  transfers between devices with their start and end apart: 27, of which 10 were waited for; matrix products, arithmetic and copies ran while one was open for 3% of the time, Pallas kernels for 17%

profile of v7, /device:TPU:131, one launch (start us, length us, event | category | flops | bytes accessed | tf_op | source)
XLA Modules:
  0.0 116.5 jit_solution(10873188248899479029)
XLA Ops:
  0.0 1.1 constant_dynamic-slice_fusion.4
  1.2 1.9 %collective-permute-start = (bf16[2,168,384]{2,1,0:T(8,128)(2,1)S(1)}, bf16[2,168,384]{2,1,0:T(8,128)(2,1)S(1)}, u32[]{:S(2)}, u32[]{:S(2)}) collective-permute-start(bf16[2,168,384]{2,1,0:T(8,128)(2,1)S(1)} %constant_dynamic-update-slice_fusion), channel_id=1, source_target_pairs={{152,0},{1,1},{58,2},{67,3},{252,4},{37,5},{94,6},{103,7},{128,8},... | collective-permute-start | bytes 774152 | tf_op jit(solution)/shard_map/ppermute | solution.py:34
  3.2 2.4 %collective-permute-start.1 = (bf16[2,168,384]{2,1,0:T(8,128)(2,1)S(1)}, bf16[2,168,384]{2,1,0:T(8,128)(2,1)S(1)}, u32[]{:S(2)}, u32[]{:S(2)}) collective-permute-start(bf16[2,168,384]{2,1,0:T(8,128)(2,1)S(1)} %constant_dynamic-update-slice_fusion), channel_id=1, source_target_pairs={{24,0},{129,1},{122,2},{195,3},{188,4},{165,5},{222,6},{231,7},{0,... | collective-permute-start | bytes 774152 | tf_op jit(solution)/shard_map/ppermute | solution.py:34
  7.1 3.2 %collective-permute-start.3 = (bf16[2,4,32,384]{3,2,1,0:T(8,128)(2,1)S(1)}, bf16[2,4,32,384]{3,2,1,0:T(8,128)(2,1)S(1)}, u32[]{:S(2)}, u32[]{:S(2)}) collective-permute-start(bf16[2,4,32,384]{3,2,1,0:T(8,128)(2,1)S(1)} %constant_dynamic-slice_fusion.3), channel_id=1, source_target_pairs={{0,8},{1,9},{2,10},{3,11},{4,12},{5,13},{6,14},{7,15},{8,16},{9,17... | collective-permute-start | bytes 589832 | tf_op jit(solution)/shard_map/ppermute | solution.py:34
  10.3 4.4 %collective-permute-start.4 = (bf16[6,1,32,384]{3,2,1,0:T(8,128)(2,1)S(1)}, bf16[6,1,32,384]{3,2,1,0:T(8,128)(2,1)S(1)}, u32[]{:S(2)}, u32[]{:S(2)}) collective-permute-start(bf16[6,1,32,384]{3,2,1,0:T(8,128)(2,1)S(1)} %get-tuple-element.52), channel_id=1, source_target_pairs={{2,1},{1,2},{4,3},{3,4},{6,5},{5,6},{10,9},{9,10},{12,11},{11,12},... | collective-permute-start | bytes 442376 | tf_op jit(solution)/shard_map/ppermute | solution.py:34
  18.1 1.1 collective-permute-start.2
  19.2 1.0 collective-permute-start.6
  20.3 0.7 collective-permute-start.5
  21.0 14.6 %collective-permute-start.7 = (bf16[8,1,32,384]{3,2,1,0:T(8,128)(2,1)S(1)}, bf16[8,1,32,384]{3,2,1,0:T(8,128)(2,1)S(1)}, u32[]{:S(2)}, u32[]{:S(2)}) collective-permute-start(bf16[8,1,32,384]{3,2,1,0:T(8,128)(2,1)S(1)} %pad_maximum_fusion.2), channel_id=1, source_target_pairs={{1,0},{0,1},{3,2},{2,3},{5,4},{4,5},{7,6},{6,7},{9,8},{8,9},{11,10... | collective-permute-start | bytes 589832 | tf_op jit(solution)/shard_map/ppermute | solution.py:34
  35.6 1.9 %collective-permute-start.8 = (bf16[2,1,32,384]{3,2,1,0:T(8,128)(2,1)S(1)}, bf16[2,1,32,384]{3,2,1,0:T(8,128)(2,1)S(1)}, u32[]{:S(2)}, u32[]{:S(2)}) collective-permute-start(bf16[2,1,32,384]{3,2,1,0:T(8,128)(2,1)S(1)} %get-tuple-element.97), channel_id=1, source_target_pairs={{2,1},{1,2},{4,3},{3,4},{6,5},{5,6},{10,9},{9,10},{12,11},{11,12},... | collective-permute-start | bytes 147464 | tf_op jit(solution)/shard_map/ppermute | solution.py:34
  37.5 1.1 shard_map.127._
  38.6 6.6 %collective-permute-done.8 = bf16[2,1,32,384]{3,2,1,0:T(8,128)(2,1)S(1)} collective-permute-done((bf16[2,1,32,384]{3,2,1,0:T(8,128)(2,1)S(1)}, bf16[2,1,32,384]{3,2,1,0:T(8,128)(2,1)S(1)}, u32[]{:S(2)}, u32[]{:S(2)}) %collective-permute-start.8) | collective-permute-done | bytes 49184 | tf_op jit(solution)/shard_map/ppermute | solution.py:34
  45.3 2.4 %shard_map.128.refs_2_ = bf16[2,8,6,32,1152]{4,3,2,1,0:T(8,128)(2,1)S(1)} custom-call(s32[2]{0:T(128)S(1)} %pad_add_fusion.1.scalars.refs_0_, s32[2,384]{1,0:T(2,128)S(1)} %pad_add_fusion.order, bf16[256,384]{1,0:T(8,128)(2,1)S(1)} %bitcast.42, bf16[256,384]{1,0:T(8,128)(2,1)S(1)} %bitcast.43, ...), custom_call_target="tpu_custom_call", output_to_operand_aliasing={{}: (5, {})} | custom-call | flops 1000 | bytes 1000 | tf_op jit(solution)/shard_map/pallas_call | solution.py:175
  48.7 1.5 %collective-permute-start.15 = (bf16[14,96,384]{2,1,0:T(8,128)(2,1)S(1)}, bf16[14,96,384]{2,1,0:T(8,128)(2,1)S(1)}, u32[]{:S(2)}, u32[]{:S(2)}) collective-permute-start(bf16[14,96,384]{2,1,0:T(8,128)(2,1)S(1)} %shard_map.130.refs_4_), channel_id=1, source_target_pairs={{24,0},{7,1},{26,2},{1,3},{28,4},{3,5},{30,6},{5,7},{0,8},{15,9},{... | collective-permute-start | bytes 3096584 | tf_op jit(solution)/shard_map/ppermute | solution.py:34
  50.8 1.5 %collective-permute-done.9.refs_8_ = bf16[14,96,384]{2,1,0:T(8,128)(2,1)S(1)} collective-permute-done((bf16[14,96,384]{2,1,0:T(8,128)(2,1)S(1)}, bf16[14,96,384]{2,1,0:T(8,128)(2,1)S(1)}, u32[]{:S(2)}, u32[]{:S(2)}) %collective-permute-start.9) | collective-permute-done | bytes 1032224 | tf_op jit(solution)/shard_map/ppermute | solution.py:34
  52.3 10.2 %collective-permute-done.14.refs_5_ = bf16[14,96,384]{2,1,0:T(8,128)(2,1)S(1)} collective-permute-done((bf16[14,96,384]{2,1,0:T(8,128)(2,1)S(1)}, bf16[14,96,384]{2,1,0:T(8,128)(2,1)S(1)}, u32[]{:S(2)}, u32[]{:S(2)}) %collective-permute-start.14) | collective-permute-done | bytes 1032224 | tf_op jit(solution)/shard_map/ppermute | solution.py:34
  62.5 1.5 %collective-permute-done.16.refs_7_ = bf16[14,96,384]{2,1,0:T(8,128)(2,1)S(1)} collective-permute-done((bf16[14,96,384]{2,1,0:T(8,128)(2,1)S(1)}, bf16[14,96,384]{2,1,0:T(8,128)(2,1)S(1)}, u32[]{:S(2)}, u32[]{:S(2)}) %collective-permute-start.16) | collective-permute-done | bytes 1032224 | tf_op jit(solution)/shard_map/ppermute | solution.py:34
  64.0 2.7 %collective-permute-start.17 = (bf16[14,96,384]{2,1,0:T(8,128)(2,1)S(1)}, bf16[14,96,384]{2,1,0:T(8,128)(2,1)S(1)}, u32[]{:S(2)}, u32[]{:S(2)}) collective-permute-start(bf16[14,96,384]{2,1,0:T(8,128)(2,1)S(1)} %collective-permute-done.14.refs_5_), channel_id=1, source_target_pairs={{1,0},{0,1},{3,2},{2,3},{5,4},{4,5},{7,6},{6,7},{9,8},{8,9},{11,10... | collective-permute-start | bytes 3096584 | tf_op jit(solution)/shard_map/ppermute | solution.py:34
  67.2 1.5 %collective-permute-start.12 = (bf16[14,96,384]{2,1,0:T(8,128)(2,1)S(1)}, bf16[14,96,384]{2,1,0:T(8,128)(2,1)S(1)}, u32[]{:S(2)}, u32[]{:S(2)}) collective-permute-start(bf16[14,96,384]{2,1,0:T(8,128)(2,1)S(1)} %shard_map.129.refs_4_), channel_id=1, source_target_pairs={{24,0},{7,1},{26,2},{1,3},{28,4},{3,5},{30,6},{5,7},{0,8},{15,9},{... | collective-permute-start | bytes 3096584 | tf_op jit(solution)/shard_map/ppermute | solution.py:34
  68.9 1.5 %collective-permute-done.18.refs_10_ = bf16[14,96,384]{2,1,0:T(8,128)(2,1)S(1)} collective-permute-done((bf16[14,96,384]{2,1,0:T(8,128)(2,1)S(1)}, bf16[14,96,384]{2,1,0:T(8,128)(2,1)S(1)}, u32[]{:S(2)}, u32[]{:S(2)}) %collective-permute-start.18) | collective-permute-done | bytes 1032224 | tf_op jit(solution)/shard_map/ppermute | solution.py:34
  70.4 1.5 %collective-permute-done.19.refs_11_ = bf16[14,96,384]{2,1,0:T(8,128)(2,1)S(1)} collective-permute-done((bf16[14,96,384]{2,1,0:T(8,128)(2,1)S(1)}, bf16[14,96,384]{2,1,0:T(8,128)(2,1)S(1)}, u32[]{:S(2)}, u32[]{:S(2)}) %collective-permute-start.19) | collective-permute-done | bytes 1032224 | tf_op jit(solution)/shard_map/ppermute | solution.py:34
  71.9 12.3 %shard_map.131 = bf16[6,128,384]{2,1,0:T(8,128)(2,1)S(1)} custom-call(s32[2]{0:T(128)S(1)} %pad_add_fusion.1.scalars.refs_0_, f32[3,6]{1,0:T(4,128)S(1)} %add_convert_fusion.refs_1_, bf16[2,8,6,32,1152]{4,3,2,1,0:T(8,128)(2,1)S(1)} %shard_map.128.refs_2_, f32[1,384]{1,0:T(1,128)S(1)} %reshape.269.refs_3_, bf16[14,96,384]{2,1,0:T(8,128)(2,1)S(1)} %shard_map.130.refs_4_, ...), custom_call_target="tpu_custom_call" | custom-call | flops 1000 | bytes 1000 | tf_op jit(solution)/shard_map/pallas_call | solution.py:275
  84.2 1.0 collective-permute-start.20
  85.3 1.0 collective-permute-done.20
  86.3 1.9 %collective-permute-start.21 = (bf16[2,5,32,384]{3,2,1,0:T(8,128)(2,1)S(1)}, bf16[2,5,32,384]{3,2,1,0:T(8,128)(2,1)S(1)}, u32[]{:S(2)}, u32[]{:S(2)}) collective-permute-start(bf16[2,5,32,384]{3,2,1,0:T(8,128)(2,1)S(1)} %pad_maximum_fusion.1), channel_id=1, source_target_pairs={{0,8},{1,9},{2,10},{3,11},{4,12},{5,13},{6,14},{7,15},{8,16},{9,17... | collective-permute-start | bytes 737288 | tf_op jit(solution)/shard_map/ppermute | solution.py:34
  88.2 2.5 %collective-permute-start.23 = (bf16[6,1,32,384]{3,2,1,0:T(8,128)(2,1)S(1)}, bf16[6,1,32,384]{3,2,1,0:T(8,128)(2,1)S(1)}, u32[]{:S(2)}, u32[]{:S(2)}) collective-permute-start(bf16[6,1,32,384]{3,2,1,0:T(8,128)(2,1)S(1)} %get-tuple-element.93), channel_id=1, source_target_pairs={{2,1},{1,2},{4,3},{3,4},{6,5},{5,6},{10,9},{9,10},{12,11},{11,12},... | collective-permute-start | bytes 442376 | tf_op jit(solution)/shard_map/ppermute | solution.py:34
  90.7 2.7 %collective-permute-start.22 = (bf16[2,1,32,384]{3,2,1,0:T(8,128)(2,1)S(1)}, bf16[2,1,32,384]{3,2,1,0:T(8,128)(2,1)S(1)}, u32[]{:S(2)}, u32[]{:S(2)}) collective-permute-start(bf16[2,1,32,384]{3,2,1,0:T(8,128)(2,1)S(1)} %constant_dynamic-slice_fusion), channel_id=1, source_target_pairs={{2,9},{1,10},{4,11},{3,12},{6,13},{5,14},{10,17},{9,18},{12,19},{1... | collective-permute-start | bytes 147464 | tf_op jit(solution)/shard_map/ppermute | solution.py:34
  93.5 1.1 shard_map.132._
  94.6 0.7 collective-permute-start.24
  95.5 5.1 %collective-permute-done.22 = bf16[2,1,32,384]{3,2,1,0:T(8,128)(2,1)S(1)} collective-permute-done((bf16[2,1,32,384]{3,2,1,0:T(8,128)(2,1)S(1)}, bf16[2,1,32,384]{3,2,1,0:T(8,128)(2,1)S(1)}, u32[]{:S(2)}, u32[]{:S(2)}) %collective-permute-start.22) | collective-permute-done | bytes 49184 | tf_op jit(solution)/shard_map/ppermute | solution.py:34
  101.0 2.6 %shard_map.133.refs_2_ = bf16[2,8,6,32,1152]{4,3,2,1,0:T(8,128)(2,1)S(1)} custom-call(s32[2]{0:T(128)S(1)} %pad_add_fusion.1.scalars.refs_0_, s32[2,384]{1,0:T(2,128)S(1)} %pad_add_fusion.order, bf16[256,384]{1,0:T(8,128)(2,1)S(1)} %bitcast.39, bf16[256,384]{1,0:T(8,128)(2,1)S(1)} %bitcast.40, ...), custom_call_target="tpu_custom_call", output_to_operand_aliasing={{}: (5, {})} | custom-call | flops 1000 | bytes 1000 | tf_op jit(solution)/shard_map/pallas_call | solution.py:175
  103.6 12.7 %shard_map.134 = bf16[6,128,384]{2,1,0:T(8,128)(2,1)} custom-call(s32[2]{0:T(128)S(1)} %pad_add_fusion.1.scalars.refs_0_, f32[3,6]{1,0:T(4,128)S(1)} %add_convert_fusion.refs_1_, bf16[2,8,6,32,1152]{4,3,2,1,0:T(8,128)(2,1)S(1)} %shard_map.133.refs_2_, bf16[6,128,384]{2,1,0:T(8,128)(2,1)S(1)} %bitcast.33, bf16[14,96,384]{2,1,0:T(8,128)(2,1)S(1)} %shard_map.129.refs_4_, ...), custom_call_target="tpu_custom_call" | custom-call | flops 1000 | bytes 1000 | tf_op jit(solution)/shard_map/pallas_call | solution.py:275
  (97 shorter events, 6.6 us)
Async XLA Ops:
  1.2 16.8 %collective-permute-start = (bf16[2,168,384]{2,1,0:T(8,128)(2,1)S(1)}, bf16[2,168,384]{2,1,0:T(8,128)(2,1)S(1)}, u32[]{:S(2)}, u32[]{:S(2)}) collective-permute-start(bf16[2,168,384]{2,1,0:T(8,128)(2,1)S(1)} %constant_dynamic-update-slice_fusion), channel_id=1, source_target_pairs={{152,0},{1,1},{58,2},{67,3},{252,4},{37,5},{94,6},{103,7},{128,8},... | collective-permute-start | bytes 774152 | tf_op jit(solution)/shard_map/ppermute | solution.py:34
  3.2 14.9 %collective-permute-start.1 = (bf16[2,168,384]{2,1,0:T(8,128)(2,1)S(1)}, bf16[2,168,384]{2,1,0:T(8,128)(2,1)S(1)}, u32[]{:S(2)}, u32[]{:S(2)}) collective-permute-start(bf16[2,168,384]{2,1,0:T(8,128)(2,1)S(1)} %constant_dynamic-update-slice_fusion), channel_id=1, source_target_pairs={{24,0},{129,1},{122,2},{195,3},{188,4},{165,5},{222,6},{231,7},{0,... | collective-permute-start | bytes 774152 | tf_op jit(solution)/shard_map/ppermute | solution.py:34
  6.5 8.3 %copy-start.7 = (s32[4]{0:T(128)S(1)}, s32[4]{0:T(128)}, u32[]{:S(2)}) copy-start(s32[4]{0:T(128)} %constant.150.clone) | copy-start | bytes 52
  6.5 8.3 %copy-start.2 = (s32[4,2]{1,0:T(4,128)S(1)}, s32[4,2]{1,0:T(4,128)}, u32[]{:S(2)}) copy-start(s32[4,2]{1,0:T(4,128)} %constant.159) | copy-start | bytes 100
  6.5 9.3 %copy-start.1 = (s32[4,2]{1,0:T(4,128)S(1)}, s32[4,2]{1,0:T(4,128)}, u32[]{:S(2)}) copy-start(s32[4,2]{1,0:T(4,128)} %constant.161) | copy-start | bytes 100
  6.6 10.9 %copy-start.8 = (s32[3]{0:T(128)S(1)}, s32[3]{0:T(128)}, u32[]{:S(2)}) copy-start(s32[3]{0:T(128)} %param.14) | copy-start | bytes 40
  7.1 13.2 %collective-permute-start.3 = (bf16[2,4,32,384]{3,2,1,0:T(8,128)(2,1)S(1)}, bf16[2,4,32,384]{3,2,1,0:T(8,128)(2,1)S(1)}, u32[]{:S(2)}, u32[]{:S(2)}) collective-permute-start(bf16[2,4,32,384]{3,2,1,0:T(8,128)(2,1)S(1)} %constant_dynamic-slice_fusion.3), channel_id=1, source_target_pairs={{0,8},{1,9},{2,10},{3,11},{4,12},{5,13},{6,14},{7,15},{8,16},{9,17... | collective-permute-start | bytes 589832 | tf_op jit(solution)/shard_map/ppermute | solution.py:34
  10.3 10.0 %collective-permute-start.4 = (bf16[6,1,32,384]{3,2,1,0:T(8,128)(2,1)S(1)}, bf16[6,1,32,384]{3,2,1,0:T(8,128)(2,1)S(1)}, u32[]{:S(2)}, u32[]{:S(2)}) collective-permute-start(bf16[6,1,32,384]{3,2,1,0:T(8,128)(2,1)S(1)} %get-tuple-element.52), channel_id=1, source_target_pairs={{2,1},{1,2},{4,3},{3,4},{6,5},{5,6},{10,9},{9,10},{12,11},{11,12},... | collective-permute-start | bytes 442376 | tf_op jit(solution)/shard_map/ppermute | solution.py:34
  18.1 29.6 %collective-permute-start.2 = (bf16[2,2,168,384]{3,2,1,0:T(8,128)(2,1)S(1)}, bf16[2,2,168,384]{3,2,1,0:T(8,128)(2,1)S(1)}, u32[]{:S(2)}, u32[]{:S(2)}) collective-permute-start(bf16[2,2,168,384]{3,2,1,0:T(8,128)(2,1)S(1)} %pad_maximum_fusion.refs_0_), channel_id=1, source_target_pairs={{2,0},{9,1},{4,2},{11,3},{6,4},{13,5},{0,6},{15,7},{10,8},{17,9},{... | collective-permute-start | bytes 1548296 | tf_op jit(solution)/shard_map/ppermute | solution.py:34
  19.2 28.5 %collective-permute-start.6 = (bf16[2,2,168,384]{3,2,1,0:T(8,128)(2,1)S(1)}, bf16[2,2,168,384]{3,2,1,0:T(8,128)(2,1)S(1)}, u32[]{:S(2)}, u32[]{:S(2)}) collective-permute-start(bf16[2,2,168,384]{3,2,1,0:T(8,128)(2,1)S(1)} %pad_maximum_fusion.refs_0_), channel_id=1, source_target_pairs={{4,0},{17,1},{6,2},{19,3},{0,4},{21,5},{2,6},{23,7},{12,8},{25,9},... | collective-permute-start | bytes 1548296 | tf_op jit(solution)/shard_map/ppermute | solution.py:34
  20.3 27.4 %collective-permute-start.5 = (bf16[2,2,168,384]{3,2,1,0:T(8,128)(2,1)S(1)}, bf16[2,2,168,384]{3,2,1,0:T(8,128)(2,1)S(1)}, u32[]{:S(2)}, u32[]{:S(2)}) collective-permute-start(bf16[2,2,168,384]{3,2,1,0:T(8,128)(2,1)S(1)} %pad_maximum_fusion.refs_0_), channel_id=1, source_target_pairs={{6,0},{25,1},{0,2},{27,3},{2,4},{29,5},{4,6},{31,7},{14,8},{1,9},{... | collective-permute-start | bytes 1548296 | tf_op jit(solution)/shard_map/ppermute | solution.py:34
  21.0 24.3 %collective-permute-start.7 = (bf16[8,1,32,384]{3,2,1,0:T(8,128)(2,1)S(1)}, bf16[8,1,32,384]{3,2,1,0:T(8,128)(2,1)S(1)}, u32[]{:S(2)}, u32[]{:S(2)}) collective-permute-start(bf16[8,1,32,384]{3,2,1,0:T(8,128)(2,1)S(1)} %pad_maximum_fusion.2), channel_id=1, source_target_pairs={{1,0},{0,1},{3,2},{2,3},{5,4},{4,5},{7,6},{6,7},{9,8},{8,9},{11,10... | collective-permute-start | bytes 589832 | tf_op jit(solution)/shard_map/ppermute | solution.py:34
  35.6 9.6 %collective-permute-start.8 = (bf16[2,1,32,384]{3,2,1,0:T(8,128)(2,1)S(1)}, bf16[2,1,32,384]{3,2,1,0:T(8,128)(2,1)S(1)}, u32[]{:S(2)}, u32[]{:S(2)}) collective-permute-start(bf16[2,1,32,384]{3,2,1,0:T(8,128)(2,1)S(1)} %get-tuple-element.97), channel_id=1, source_target_pairs={{2,1},{1,2},{4,3},{3,4},{6,5},{5,6},{10,9},{9,10},{12,11},{11,12},... | collective-permute-start | bytes 147464 | tf_op jit(solution)/shard_map/ppermute | solution.py:34
  47.9 21.0 %copy-start.4 = (f32[384]{0:T(512)S(1)}, f32[384]{0:T(512)}, u32[]{:S(2)}) copy-start(f32[384]{0:T(512)} %param.20) | copy-start | bytes 4612
  48.1 2.7 %collective-permute-start.10 = (bf16[14,96,384]{2,1,0:T(8,128)(2,1)S(1)}, bf16[14,96,384]{2,1,0:T(8,128)(2,1)S(1)}, u32[]{:S(2)}, u32[]{:S(2)}) collective-permute-start(bf16[14,96,384]{2,1,0:T(8,128)(2,1)S(1)} %shard_map.129.refs_4_), channel_id=1, source_target_pairs={{1,0},{0,1},{3,2},{2,3},{5,4},{4,5},{7,6},{6,7},{9,8},{8,9},{11,10... | collective-permute-start | bytes 3096584 | tf_op jit(solution)/shard_map/ppermute | solution.py:34
  48.2 4.1 %collective-permute-start.9 = (bf16[14,96,384]{2,1,0:T(8,128)(2,1)S(1)}, bf16[14,96,384]{2,1,0:T(8,128)(2,1)S(1)}, u32[]{:S(2)}, u32[]{:S(2)}) collective-permute-start(bf16[14,96,384]{2,1,0:T(8,128)(2,1)S(1)} %shard_map.130.refs_4_), channel_id=1, source_target_pairs={{1,0},{0,1},{3,2},{2,3},{5,4},{4,5},{7,6},{6,7},{9,8},{8,9},{11,10... | collective-permute-start | bytes 3096584 | tf_op jit(solution)/shard_map/ppermute | solution.py:34
  48.7 13.8 %collective-permute-start.14 = (bf16[14,96,384]{2,1,0:T(8,128)(2,1)S(1)}, bf16[14,96,384]{2,1,0:T(8,128)(2,1)S(1)}, u32[]{:S(2)}, u32[]{:S(2)}) collective-permute-start(bf16[14,96,384]{2,1,0:T(8,128)(2,1)S(1)} %shard_map.130.refs_4_), channel_id=1, source_target_pairs={{8,0},{3,1},{10,2},{5,3},{12,4},{7,5},{14,6},{1,7},{16,8},{11,9},{... | collective-permute-start | bytes 3096584 | tf_op jit(solution)/shard_map/ppermute | solution.py:34
  48.7 13.8 %collective-permute-start.15 = (bf16[14,96,384]{2,1,0:T(8,128)(2,1)S(1)}, bf16[14,96,384]{2,1,0:T(8,128)(2,1)S(1)}, u32[]{:S(2)}, u32[]{:S(2)}) collective-permute-start(bf16[14,96,384]{2,1,0:T(8,128)(2,1)S(1)} %shard_map.130.refs_4_), channel_id=1, source_target_pairs={{24,0},{7,1},{26,2},{1,3},{28,4},{3,5},{30,6},{5,7},{0,8},{15,9},{... | collective-permute-start | bytes 3096584 | tf_op jit(solution)/shard_map/ppermute | solution.py:34
  50.2 13.8 %collective-permute-start.16 = (bf16[14,96,384]{2,1,0:T(8,128)(2,1)S(1)}, bf16[14,96,384]{2,1,0:T(8,128)(2,1)S(1)}, u32[]{:S(2)}, u32[]{:S(2)}) collective-permute-start(bf16[14,96,384]{2,1,0:T(8,128)(2,1)S(1)} %shard_map.130.refs_4_), channel_id=1, source_target_pairs={{224,0},{33,1},{226,2},{35,3},{228,4},{37,5},{230,6},{39,7},{232,8... | collective-permute-start | bytes 3096584 | tf_op jit(solution)/shard_map/ppermute | solution.py:34
  64.0 5.0 %collective-permute-start.17 = (bf16[14,96,384]{2,1,0:T(8,128)(2,1)S(1)}, bf16[14,96,384]{2,1,0:T(8,128)(2,1)S(1)}, u32[]{:S(2)}, u32[]{:S(2)}) collective-permute-start(bf16[14,96,384]{2,1,0:T(8,128)(2,1)S(1)} %collective-permute-done.14.refs_5_), channel_id=1, source_target_pairs={{1,0},{0,1},{3,2},{2,3},{5,4},{4,5},{7,6},{6,7},{9,8},{8,9},{11,10... | collective-permute-start | bytes 3096584 | tf_op jit(solution)/shard_map/ppermute | solution.py:34
  66.7 3.7 %collective-permute-start.18 = (bf16[14,96,384]{2,1,0:T(8,128)(2,1)S(1)}, bf16[14,96,384]{2,1,0:T(8,128)(2,1)S(1)}, u32[]{:S(2)}, u32[]{:S(2)}) collective-permute-start(bf16[14,96,384]{2,1,0:T(8,128)(2,1)S(1)} %collective-permute-done.15.refs_6_), channel_id=1, source_target_pairs={{1,0},{0,1},{3,2},{2,3},{5,4},{4,5},{7,6},{6,7},{9,8},{8,9},{11,10... | collective-permute-start | bytes 3096584 | tf_op jit(solution)/shard_map/ppermute | solution.py:34
  66.7 5.2 %collective-permute-start.19 = (bf16[14,96,384]{2,1,0:T(8,128)(2,1)S(1)}, bf16[14,96,384]{2,1,0:T(8,128)(2,1)S(1)}, u32[]{:S(2)}, u32[]{:S(2)}) collective-permute-start(bf16[14,96,384]{2,1,0:T(8,128)(2,1)S(1)} %collective-permute-done.16.refs_7_), channel_id=1, source_target_pairs={{1,0},{0,1},{3,2},{2,3},{5,4},{4,5},{7,6},{6,7},{9,8},{8,9},{11,10... | collective-permute-start | bytes 3096584 | tf_op jit(solution)/shard_map/ppermute | solution.py:34
  67.2 17.0 %collective-permute-start.11 = (bf16[14,96,384]{2,1,0:T(8,128)(2,1)S(1)}, bf16[14,96,384]{2,1,0:T(8,128)(2,1)S(1)}, u32[]{:S(2)}, u32[]{:S(2)}) collective-permute-start(bf16[14,96,384]{2,1,0:T(8,128)(2,1)S(1)} %shard_map.129.refs_4_), channel_id=1, source_target_pairs={{8,0},{3,1},{10,2},{5,3},{12,4},{7,5},{14,6},{1,7},{16,8},{11,9},{... | collective-permute-start | bytes 3096584 | tf_op jit(solution)/shard_map/ppermute | solution.py:34
  67.2 17.0 %collective-permute-start.12 = (bf16[14,96,384]{2,1,0:T(8,128)(2,1)S(1)}, bf16[14,96,384]{2,1,0:T(8,128)(2,1)S(1)}, u32[]{:S(2)}, u32[]{:S(2)}) collective-permute-start(bf16[14,96,384]{2,1,0:T(8,128)(2,1)S(1)} %shard_map.129.refs_4_), channel_id=1, source_target_pairs={{24,0},{7,1},{26,2},{1,3},{28,4},{3,5},{30,6},{5,7},{0,8},{15,9},{... | collective-permute-start | bytes 3096584 | tf_op jit(solution)/shard_map/ppermute | solution.py:34
  68.9 15.2 %collective-permute-start.13 = (bf16[14,96,384]{2,1,0:T(8,128)(2,1)S(1)}, bf16[14,96,384]{2,1,0:T(8,128)(2,1)S(1)}, u32[]{:S(2)}, u32[]{:S(2)}) collective-permute-start(bf16[14,96,384]{2,1,0:T(8,128)(2,1)S(1)} %shard_map.129.refs_4_), channel_id=1, source_target_pairs={{224,0},{33,1},{226,2},{35,3},{228,4},{37,5},{230,6},{39,7},{232,8... | collective-permute-start | bytes 3096584 | tf_op jit(solution)/shard_map/ppermute | solution.py:34
  84.2 2.0 %collective-permute-start.20 = (bf16[6,1,32,384]{3,2,1,0:T(8,128)(2,1)S(1)}, bf16[6,1,32,384]{3,2,1,0:T(8,128)(2,1)S(1)}, u32[]{:S(2)}, u32[]{:S(2)}) collective-permute-start(bf16[6,1,32,384]{3,2,1,0:T(8,128)(2,1)S(1)} %get-tuple-element.94), channel_id=1, source_target_pairs={{1,0},{0,1},{3,2},{2,3},{5,4},{4,5},{7,6},{6,7},{9,8},{8,9},{11,10... | collective-permute-start | bytes 442376 | tf_op jit(solution)/shard_map/ppermute | solution.py:34
  86.3 14.2 %collective-permute-start.21 = (bf16[2,5,32,384]{3,2,1,0:T(8,128)(2,1)S(1)}, bf16[2,5,32,384]{3,2,1,0:T(8,128)(2,1)S(1)}, u32[]{:S(2)}, u32[]{:S(2)}) collective-permute-start(bf16[2,5,32,384]{3,2,1,0:T(8,128)(2,1)S(1)} %pad_maximum_fusion.1), channel_id=1, source_target_pairs={{0,8},{1,9},{2,10},{3,11},{4,12},{5,13},{6,14},{7,15},{8,16},{9,17... | collective-permute-start | bytes 737288 | tf_op jit(solution)/shard_map/ppermute | solution.py:34
  88.2 7.2 %collective-permute-start.23 = (bf16[6,1,32,384]{3,2,1,0:T(8,128)(2,1)S(1)}, bf16[6,1,32,384]{3,2,1,0:T(8,128)(2,1)S(1)}, u32[]{:S(2)}, u32[]{:S(2)}) collective-permute-start(bf16[6,1,32,384]{3,2,1,0:T(8,128)(2,1)S(1)} %get-tuple-element.93), channel_id=1, source_target_pairs={{2,1},{1,2},{4,3},{3,4},{6,5},{5,6},{10,9},{9,10},{12,11},{11,12},... | collective-permute-start | bytes 442376 | tf_op jit(solution)/shard_map/ppermute | solution.py:34
  90.7 9.8 %collective-permute-start.22 = (bf16[2,1,32,384]{3,2,1,0:T(8,128)(2,1)S(1)}, bf16[2,1,32,384]{3,2,1,0:T(8,128)(2,1)S(1)}, u32[]{:S(2)}, u32[]{:S(2)}) collective-permute-start(bf16[2,1,32,384]{3,2,1,0:T(8,128)(2,1)S(1)} %constant_dynamic-slice_fusion), channel_id=1, source_target_pairs={{2,9},{1,10},{4,11},{3,12},{6,13},{5,14},{10,17},{9,18},{12,19},{1... | collective-permute-start | bytes 147464 | tf_op jit(solution)/shard_map/ppermute | solution.py:34
  94.6 9.0 %collective-permute-start.24 = (bf16[14,96,384]{2,1,0:T(8,128)(2,1)S(1)}, bf16[14,96,384]{2,1,0:T(8,128)(2,1)S(1)}, u32[]{:S(2)}, u32[]{:S(2)}) collective-permute-start(bf16[14,96,384]{2,1,0:T(8,128)(2,1)S(1)} %collective-permute-done.11.refs_5_), channel_id=1, source_target_pairs={{1,0},{0,1},{3,2},{2,3},{5,4},{4,5},{7,6},{6,7},{9,8},{8,9},{11,10... | collective-permute-start | bytes 3096584 | tf_op jit(solution)/shard_map/ppermute | solution.py:34
  95.3 8.3 %collective-permute-start.25 = (bf16[14,96,384]{2,1,0:T(8,128)(2,1)S(1)}, bf16[14,96,384]{2,1,0:T(8,128)(2,1)S(1)}, u32[]{:S(2)}, u32[]{:S(2)}) collective-permute-start(bf16[14,96,384]{2,1,0:T(8,128)(2,1)S(1)} %collective-permute-done.12.refs_6_), channel_id=1, source_target_pairs={{1,0},{0,1},{3,2},{2,3},{5,4},{4,5},{7,6},{6,7},{9,8},{8,9},{11,10... | collective-permute-start | bytes 3096584 | tf_op jit(solution)/shard_map/ppermute | solution.py:34
  100.6 3.1 %collective-permute-start.26 = (bf16[14,96,384]{2,1,0:T(8,128)(2,1)S(1)}, bf16[14,96,384]{2,1,0:T(8,128)(2,1)S(1)}, u32[]{:S(2)}, u32[]{:S(2)}) collective-permute-start(bf16[14,96,384]{2,1,0:T(8,128)(2,1)S(1)} %collective-permute-done.13.refs_7_), channel_id=1, source_target_pairs={{1,0},{0,1},{3,2},{2,3},{5,4},{4,5},{7,6},{6,7},{9,8},{8,9},{11,10... | collective-permute-start | bytes 3096584 | tf_op jit(solution)/shard_map/ppermute | solution.py:34
  (4 other events, 29.4 us)

commit v8 on v7

--- a/solution.py
+++ b/solution.py
@@ -114,9 +114,26 @@
     return jnp.stack([(half.reshape(-1, 1) * SHARD + ramp).reshape(C) for half in (first, second)])
 
 
-def spread_cells(cells, order, half):
+def picks_body(order, out):
+    for half in range(2):
+        out[half] = (
+            lax.broadcasted_iota(jnp.int32, (C, C), 0) == order[half : half + 1, :]
+        ).astype(jnp.bfloat16)
+
+
+def make_picks(orders):
+    vmem = pl.BlockSpec(memory_space=pltpu.VMEM)
+    return pl.pallas_call(
+        picks_body,
+        out_shape=jax.ShapeDtypeStruct((2, C, C), jnp.bfloat16),
+        in_specs=[vmem],
+        out_specs=vmem,
+        cost_estimate=pl.CostEstimate(flops=1000, bytes_accessed=1000, transcendentals=0),
+    )(orders)
+
+
+def spread_cells(cells, pick):
     rows = cells.shape[0]
-    pick = (lax.broadcasted_iota(jnp.int32, (C, C), 0) == order[half : half + 1, :]).astype(jnp.bfloat16)
     plain = jnp.dot(cells, pick, preferred_element_type=jnp.float32)
     col = lax.broadcasted_iota(jnp.int32, (rows, C), 0) % 32
     before = jnp.where(col == 0, 0.0, pltpu.roll(plain, 1, 0))
@@ -124,13 +141,13 @@
     return [part.astype(jnp.bfloat16) for part in (before, plain, after)]
 
 
-def spread_inner_body(order, acts, out):
+def spread_inner_body(picks, acts, out):
     for half in range(2):
-        for tap, part in enumerate(spread_cells(acts[...], order, half)):
+        for tap, part in enumerate(spread_cells(acts[...], picks[half])):
             out[half, 2:8, 1:5, :, C * tap : C * (tap + 1)] = part.reshape(6, 4, 32, C)
 
 
-def spread_inner(orders, acts):
+def spread_inner(picks, acts):
     vmem = pl.BlockSpec(memory_space=pltpu.VMEM)
     return pl.pallas_call(
         spread_inner_body,
@@ -139,38 +156,37 @@
         out_specs=vmem,
         compiler_params=pltpu.CompilerParams(vmem_limit_bytes=20 * 1024 * 1024),
         cost_estimate=pl.CostEstimate(flops=1000, bytes_accessed=1000, transcendentals=0),
-    )(orders, acts.reshape(-1, C))
-
-
-def spread_halo_body(scalars, order, carried, beside, across, _, out):
+    )(picks, acts.reshape(-1, C))
+
+
+def spread_halo_body(scalars, picks, ends, beside, across, _, out):
     core = scalars[0]
+    cells = jnp.concatenate(
+        [ends[:, 0:4].reshape(256, C)]
+        + [
+            rows[...].reshape(-1, C)
+            for rows in (ends.at[:, 4:5], beside, ends.at[:, 5:6], across)
+        ],
+        0,
+    )
     for half in range(2):
-        for tap, part in enumerate(spread_cells(carried[...], order, half)):
-            out[half, 0:2, 1:5, :, C * tap : C * (tap + 1)] = part.reshape(2, 4, 32, C)
-        for tap, part in enumerate(spread_cells(beside[...], order, half)):
-            part = part.reshape(8, 1, 32, C)
+        for tap, part in enumerate(spread_cells(cells, picks[half])):
+            lanes = slice(C * tap, C * (tap + 1))
+            out[half, 0:2, 1:5, :, lanes] = part[0:256].reshape(2, 4, 32, C)
+            near, far = part[256:512].reshape(8, 1, 32, C), part[512:768].reshape(8, 1, 32, C)
 
             @pl.when(core == 0)
             def _():
-                out[half, :, 5:6, :, C * tap : C * (tap + 1)] = part
+                out[half, :, 0:1, :, lanes] = far
+                out[half, :, 5:6, :, lanes] = near
 
             @pl.when(core == 1)
             def _():
-                out[half, :, 0:1, :, C * tap : C * (tap + 1)] = part
-
-        for tap, part in enumerate(spread_cells(across[...], order, half)):
-            part = part.reshape(8, 1, 32, C)
-
-            @pl.when(core == 0)
-            def _():
-                out[half, :, 0:1, :, C * tap : C * (tap + 1)] = part
-
-            @pl.when(core == 1)
-            def _():
-                out[half, :, 5:6, :, C * tap : C * (tap + 1)] = part
-
-
-def spread_halo(scalars, orders, carried, beside, across, spread):
+                out[half, :, 0:1, :, lanes] = near
+                out[half, :, 5:6, :, lanes] = far
+
+
+def spread_halo(scalars, picks, ends, beside, across, spread):
     vmem = pl.BlockSpec(memory_space=pltpu.VMEM)
     return pl.pallas_call(
         spread_halo_body,
@@ -180,7 +196,7 @@
         input_output_aliases={5: 0},
         compiler_params=pltpu.CompilerParams(vmem_limit_bytes=20 * 1024 * 1024),
         cost_estimate=pl.CostEstimate(flops=1000, bytes_accessed=1000, transcendentals=0),
-    )(scalars, orders, *(cells.reshape(-1, C) for cells in (carried, beside, across)), spread)
+    )(scalars, picks, ends, beside, across, spread)
 
 
 def conv_body(
@@ -310,11 +326,6 @@
     return (z, y, x, 1 - c) if 0 <= x < NX else None
 
 
-def across_and_before(z, y, x, c):
-    place = across_chips(z, y, x, c)
-    return None if place is None else before_in_group(*place)
-
-
 def per_device(
     frames, clip_lengths, group_start, group_count, kernel_one, kernel_two, gain_one, gain_two
 ):
@@ -334,31 +345,25 @@
             jnp.where(first_core, acts[:, 0:1], acts[:, 3:4]),
         )
 
-    def last_two(acts):
-        return lax.dynamic_slice_in_dim(acts, last, 2, 0)
+    def with_rows(*arrays):
+        return jnp.concatenate([lax.dynamic_slice_in_dim(a, last, 2, 0) for a in arrays], 1)
 
     acts_one = norm_act(frames, gain_one)
     own = jnp.stack([own_half(kernel_one), own_half(kernel_two)])
     pieces = z_stage(own)
     inner, outer = sides(acts_one)
-    ends, outer = lax.optimization_barrier((last_two(acts_one), outer))
-    carried = fetch(ends, before_in_group)
-    across = fetch(outer, across_chips)
-    pieces, orders, lag_weights, scalars = lax.optimization_barrier(
-        (pieces, orders, lag_weights, scalars)
+    beside, across = fetch(inner, sibling), fetch(outer, across_chips)
+    ends = fetch(with_rows(acts_one, beside, across), before_in_group)
+    picks = make_picks(orders)
+    pieces, picks, lag_weights, scalars = lax.optimization_barrier(
+        (pieces, picks, lag_weights, scalars)
     )
 
     opposite = fetch(pieces, small_source(2))
     after = fetch(pieces, small_source(1))
-    gated, carried, across = lax.optimization_barrier((pieces, carried, across))
+    gated, ends = lax.optimization_barrier((pieces, ends))
     parts = [pieces, after, fetch(gated, small_source(-1)), opposite]
-    carried_inner, carried_outer = sides(carried)
-    corners = fetch(carried_outer, across_chips)
-    beside = fetch(jnp.concatenate([carried_inner, inner], 0), sibling)
-    spread = spread_halo(
-        scalars, orders, carried, beside, jnp.concatenate([corners, across], 0),
-        spread_inner(orders, acts_one),
-    )
+    spread = spread_halo(scalars, picks, ends, beside, across, spread_inner(picks, acts_one))
     parts, spread = lax.optimization_barrier((parts, spread))
 
     one_bundle, two_bundle = join_rows(parts, 0), join_rows(parts, 1)
@@ -380,25 +385,13 @@
 
     two_bundles, acts_two = lax.optimization_barrier((two_bundles, acts_two))
     inner, outer = sides(acts_two)
-    beside = fetch(inner, sibling)
-    across = fetch(outer, across_chips)
-    two_bundles, beside = lax.optimization_barrier((two_bundles, beside))
-    ends = jnp.concatenate([last_two(acts_two), last_two(beside)], 1)
-    ends, corners = lax.optimization_barrier((ends, last_two(outer)))
-    ends = fetch(ends, before_in_group)
-    corners = fetch(corners, across_and_before)
-    two_others += [fetch(b, sibling) for b in two_bundles[1:3]]
-    spread = spread_inner(orders, acts_two)
-    ends, corners, across, spread, two_last = lax.optimization_barrier(
-        (ends, corners, across, spread, two_bundles[3])
-    )
-    two_others.append(fetch(two_last, sibling))
-    spread = spread_halo(
-        scalars, orders, ends[:, 0:4],
-        jnp.concatenate([ends[:, 4:5], beside], 0),
-        jnp.concatenate([corners, across], 0),
-        spread,
-    )
+    across, beside = fetch(outer, across_chips), fetch(inner, sibling)
+    two_bundles, beside, across = lax.optimization_barrier((two_bundles, beside, across))
+    two_others += [fetch(b, sibling) for b in two_bundles[1:]]
+    ends = fetch(with_rows(acts_two, beside, across), before_in_group)
+    spread = spread_inner(picks, acts_two)
+    ends, spread = lax.optimization_barrier((ends, spread))
+    spread = spread_halo(scalars, picks, ends, beside, across, spread)
     result = conv(
         scalars, lag_weights, spread, frames.reshape(slots, 128, C), two_bundles, two_others,
         finish_add,

time: 117 us -> 121 us (1.034)
  waiting for transfers between devices: 29.7 us -> 48.5 us
  starting transfers between devices: 47.5 us -> 30.5 us
    ppermute x27 -> x25, waiting for transfers between devices: 29.7 us -> 48.5 us  [fetch(): return lax.ppermute(array, AXES, pairs)]
    ppermute x27 -> x25, starting transfers between devices: 47.5 us -> 30.5 us  [fetch(): return lax.ppermute(array, AXES, pairs)]
    pallas_call x0 -> x1, Pallas kernels: none -> 1.6 us  [make_picks(): pl.pallas_call(picks_body, out_shape=jax.ShapeDtypeStruct((2, C, C), jnp....]
  transfers between devices with their start and end apart: 27 -> 25, of which waited for: 10 -> 10; matrix products, arithmetic and copies ran while one was open for 3% -> 3% of each run, Pallas kernels for 17% -> 17%
where the time goes in v8:
time: 121 us; the launch traced here: 120 us
  waiting for transfers between devices  48.5 us (40%)
  Pallas kernels  33.5 us (28%)
  starting transfers between devices  30.5 us (25%)
  local copies, waits for them, and re-layouts  3.05 us (3%)
  other arithmetic  2.25 us (2%)
  between operations  2.01 us (2%)
    ppermute x25, waiting for transfers between devices, fetch(): return lax.ppermute(array, AXES, pairs)  48.5 us
    ppermute x25, starting transfers between devices, fetch(): return lax.ppermute(array, AXES, pairs)  30.5 us
    pallas_call x2, Pallas kernels, conv(): pl.pallas_call(lambda *refs: conv_body(*refs, finish=finish), out_shape=j...  25 us
    pallas_call x2, Pallas kernels, spread_halo(): pl.pallas_call(spread_halo_body, out_shape=jax.ShapeDtypeStruct(spread.sh...  4.41 us
  transfers between devices with their start and end apart: 25, of which 10 were waited for; matrix products, arithmetic and copies ran while one was open for 3% of the time, Pallas kernels for 17%

profile of v8, /device:TPU:131, one launch (start us, length us, event | category | flops | bytes accessed | tf_op | source)
XLA Modules:
  0.0 119.8 jit_solution(9369682691859299010)
XLA Ops:
  0.0 1.1 constant_dynamic-slice_fusion.6
  1.2 1.9 %collective-permute-start = (bf16[2,168,384]{2,1,0:T(8,128)(2,1)S(1)}, bf16[2,168,384]{2,1,0:T(8,128)(2,1)S(1)}, u32[]{:S(2)}, u32[]{:S(2)}) collective-permute-start(bf16[2,168,384]{2,1,0:T(8,128)(2,1)S(1)} %constant_dynamic-update-slice_fusion), channel_id=1, source_target_pairs={{152,0},{1,1},{58,2},{67,3},{252,4},{37,5},{94,6},{103,7},{128,8},... | collective-permute-start | bytes 774152 | tf_op jit(solution)/shard_map/ppermute | solution.py:34
  3.2 2.4 %collective-permute-start.1 = (bf16[2,168,384]{2,1,0:T(8,128)(2,1)S(1)}, bf16[2,168,384]{2,1,0:T(8,128)(2,1)S(1)}, u32[]{:S(2)}, u32[]{:S(2)}) collective-permute-start(bf16[2,168,384]{2,1,0:T(8,128)(2,1)S(1)} %constant_dynamic-update-slice_fusion), channel_id=1, source_target_pairs={{24,0},{129,1},{122,2},{195,3},{188,4},{165,5},{222,6},{231,7},{0,... | collective-permute-start | bytes 774152 | tf_op jit(solution)/shard_map/ppermute | solution.py:34
  6.3 5.7 %collective-permute-start.4 = (bf16[6,1,32,384]{3,2,1,0:T(8,128)(2,1)S(1)}, bf16[6,1,32,384]{3,2,1,0:T(8,128)(2,1)S(1)}, u32[]{:S(2)}, u32[]{:S(2)}) collective-permute-start(bf16[6,1,32,384]{3,2,1,0:T(8,128)(2,1)S(1)} %get-tuple-element.82), channel_id=1, source_target_pairs={{2,1},{1,2},{4,3},{3,4},{6,5},{5,6},{10,9},{9,10},{12,11},{11,12},... | collective-permute-start | bytes 442376 | tf_op jit(solution)/shard_map/ppermute | solution.py:34
  16.6 1.6 %shard_map.127.picks = bf16[2,384,384]{2,1,0:T(8,128)(2,1)} custom-call(s32[2,384]{1,0:T(2,128)} %pad_add_fusion.order), custom_call_target="tpu_custom_call" | custom-call | flops 1000 | bytes 1000 | tf_op jit(solution)/shard_map/pallas_call | solution.py:126
  18.3 2.1 %collective-permute-start.5 = (bf16[2,6,32,384]{3,2,1,0:T(8,128)(2,1)S(1)}, bf16[2,6,32,384]{3,2,1,0:T(8,128)(2,1)S(1)}, u32[]{:S(2)}, u32[]{:S(2)}) collective-permute-start(bf16[2,6,32,384]{3,2,1,0:T(8,128)(2,1)S(1)} %pad_maximum_fusion.1), channel_id=1, source_target_pairs={{0,8},{1,9},{2,10},{3,11},{4,12},{5,13},{6,14},{7,15},{8,16},{9,17... | collective-permute-start | bytes 884744 | tf_op jit(solution)/shard_map/ppermute | solution.py:34
  20.6 0.9 collective-permute-start.2
  21.5 1.0 collective-permute-start.7
  22.5 11.9 %collective-permute-done.5.ends = bf16[2,6,32,384]{3,2,1,0:T(8,128)(2,1)S(1)} collective-permute-done((bf16[2,6,32,384]{3,2,1,0:T(8,128)(2,1)S(1)}, bf16[2,6,32,384]{3,2,1,0:T(8,128)(2,1)S(1)}, u32[]{:S(2)}, u32[]{:S(2)}) %collective-permute-start.5) | collective-permute-done | bytes 294944 | tf_op jit(solution)/shard_map/ppermute | solution.py:34
  34.4 1.1 shard_map.128._
  35.5 2.1 %shard_map.129.refs_2_ = bf16[2,8,6,32,1152]{4,3,2,1,0:T(8,128)(2,1)S(1)} custom-call(s32[2]{0:T(128)S(1)} %pad_add_fusion.1.scalars.refs_0_, bf16[2,384,384]{2,1,0:T(8,128)(2,1)S(1)} %copy-done, bf16[2,6,32,384]{3,2,1,0:T(8,128)(2,1)S(1)} %collective-permute-done.5.ends, ...), custom_call_target="tpu_custom_call", output_to_operand_aliasing={{}: (5, {})} | custom-call | flops 1000 | bytes 1000 | tf_op jit(solution)/shard_map/pallas_call | solution.py:191
  37.6 0.6 collective-permute-done.7.refs_3_
  38.3 5.5 %collective-permute-done.6.refs_2_ = bf16[2,2,168,384]{3,2,1,0:T(8,128)(2,1)S(1)} collective-permute-done((bf16[2,2,168,384]{3,2,1,0:T(8,128)(2,1)S(1)}, bf16[2,2,168,384]{3,2,1,0:T(8,128)(2,1)S(1)}, u32[]{:S(2)}, u32[]{:S(2)}) %collective-permute-start.6) | collective-permute-done | bytes 516128 | tf_op jit(solution)/shard_map/ppermute | solution.py:34
  44.2 1.5 %collective-permute-start.8 = (bf16[14,96,384]{2,1,0:T(8,128)(2,1)S(1)}, bf16[14,96,384]{2,1,0:T(8,128)(2,1)S(1)}, u32[]{:S(2)}, u32[]{:S(2)}) collective-permute-start(bf16[14,96,384]{2,1,0:T(8,128)(2,1)S(1)} %shard_map.131.refs_4_), channel_id=1, source_target_pairs={{1,0},{0,1},{3,2},{2,3},{5,4},{4,5},{7,6},{6,7},{9,8},{8,9},{11,10... | collective-permute-start | bytes 3096584 | tf_op jit(solution)/shard_map/ppermute | solution.py:34
  45.8 2.4 %collective-permute-start.13 = (bf16[14,96,384]{2,1,0:T(8,128)(2,1)S(1)}, bf16[14,96,384]{2,1,0:T(8,128)(2,1)S(1)}, u32[]{:S(2)}, u32[]{:S(2)}) collective-permute-start(bf16[14,96,384]{2,1,0:T(8,128)(2,1)S(1)} %shard_map.131.refs_4_), channel_id=1, source_target_pairs={{8,0},{3,1},{10,2},{5,3},{12,4},{7,5},{14,6},{1,7},{16,8},{11,9},{... | collective-permute-start | bytes 3096584 | tf_op jit(solution)/shard_map/ppermute | solution.py:34
  48.1 0.8 collective-permute-start.15
  49.4 10.3 %collective-permute-done.13.refs_5_ = bf16[14,96,384]{2,1,0:T(8,128)(2,1)S(1)} collective-permute-done((bf16[14,96,384]{2,1,0:T(8,128)(2,1)S(1)}, bf16[14,96,384]{2,1,0:T(8,128)(2,1)S(1)}, u32[]{:S(2)}, u32[]{:S(2)}) %collective-permute-start.13) | collective-permute-done | bytes 1032224 | tf_op jit(solution)/shard_map/ppermute | solution.py:34
  59.7 2.2 %collective-permute-done.14.refs_6_ = bf16[14,96,384]{2,1,0:T(8,128)(2,1)S(1)} collective-permute-done((bf16[14,96,384]{2,1,0:T(8,128)(2,1)S(1)}, bf16[14,96,384]{2,1,0:T(8,128)(2,1)S(1)}, u32[]{:S(2)}, u32[]{:S(2)}) %collective-permute-start.14) | collective-permute-done | bytes 1032224 | tf_op jit(solution)/shard_map/ppermute | solution.py:34
  61.9 2.1 %collective-permute-start.16 = (bf16[14,96,384]{2,1,0:T(8,128)(2,1)S(1)}, bf16[14,96,384]{2,1,0:T(8,128)(2,1)S(1)}, u32[]{:S(2)}, u32[]{:S(2)}) collective-permute-start(bf16[14,96,384]{2,1,0:T(8,128)(2,1)S(1)} %collective-permute-done.13.refs_5_), channel_id=1, source_target_pairs={{1,0},{0,1},{3,2},{2,3},{5,4},{4,5},{7,6},{6,7},{9,8},{8,9},{11,10... | collective-permute-start | bytes 3096584 | tf_op jit(solution)/shard_map/ppermute | solution.py:34
  64.5 2.4 %collective-permute-start.10 = (bf16[14,96,384]{2,1,0:T(8,128)(2,1)S(1)}, bf16[14,96,384]{2,1,0:T(8,128)(2,1)S(1)}, u32[]{:S(2)}, u32[]{:S(2)}) collective-permute-start(bf16[14,96,384]{2,1,0:T(8,128)(2,1)S(1)} %shard_map.130.refs_4_), channel_id=1, source_target_pairs={{8,0},{3,1},{10,2},{5,3},{12,4},{7,5},{14,6},{1,7},{16,8},{11,9},{... | collective-permute-start | bytes 3096584 | tf_op jit(solution)/shard_map/ppermute | solution.py:34
  66.9 0.8 collective-permute-done.17.refs_10_
  67.8 1.5 %collective-permute-done.18.refs_11_ = bf16[14,96,384]{2,1,0:T(8,128)(2,1)S(1)} collective-permute-done((bf16[14,96,384]{2,1,0:T(8,128)(2,1)S(1)}, bf16[14,96,384]{2,1,0:T(8,128)(2,1)S(1)}, u32[]{:S(2)}, u32[]{:S(2)}) %collective-permute-start.18) | collective-permute-done | bytes 1032224 | tf_op jit(solution)/shard_map/ppermute | solution.py:34
  69.3 12.3 %shard_map.132 = bf16[6,128,384]{2,1,0:T(8,128)(2,1)S(1)} custom-call(s32[2]{0:T(128)S(1)} %pad_add_fusion.1.scalars.refs_0_, f32[3,6]{1,0:T(4,128)S(1)} %add_convert_fusion.refs_1_, bf16[2,8,6,32,1152]{4,3,2,1,0:T(8,128)(2,1)S(1)} %shard_map.129.refs_2_, f32[1,384]{1,0:T(1,128)S(1)} %reshape.248.refs_3_, bf16[14,96,384]{2,1,0:T(8,128)(2,1)S(1)} %shard_map.131.refs_4_, ...), custom_call_target="tpu_custom_call" | custom-call | flops 1000 | bytes 1000 | tf_op jit(solution)/shard_map/pallas_call | solution.py:291
  81.6 1.0 collective-permute-start.19
  82.6 2.4 %collective-permute-start.20 = (bf16[6,1,32,384]{3,2,1,0:T(8,128)(2,1)S(1)}, bf16[6,1,32,384]{3,2,1,0:T(8,128)(2,1)S(1)}, u32[]{:S(2)}, u32[]{:S(2)}) collective-permute-start(bf16[6,1,32,384]{3,2,1,0:T(8,128)(2,1)S(1)} %get-tuple-element.79), channel_id=1, source_target_pairs={{2,1},{1,2},{4,3},{3,4},{6,5},{5,6},{10,9},{9,10},{12,11},{11,12},... | collective-permute-start | bytes 442376 | tf_op jit(solution)/shard_map/ppermute | solution.py:34
  85.1 4.3 %collective-permute-done.20.across = bf16[6,1,32,384]{3,2,1,0:T(8,128)(2,1)S(1)} collective-permute-done((bf16[6,1,32,384]{3,2,1,0:T(8,128)(2,1)S(1)}, bf16[6,1,32,384]{3,2,1,0:T(8,128)(2,1)S(1)}, u32[]{:S(2)}, u32[]{:S(2)}) %collective-permute-start.20) | collective-permute-done | bytes 147488 | tf_op jit(solution)/shard_map/ppermute | solution.py:34
  89.4 0.7 collective-permute-start.22
  90.7 1.9 %collective-permute-start.21 = (bf16[2,6,32,384]{3,2,1,0:T(8,128)(2,1)S(1)}, bf16[2,6,32,384]{3,2,1,0:T(8,128)(2,1)S(1)}, u32[]{:S(2)}, u32[]{:S(2)}) collective-permute-start(bf16[2,6,32,384]{3,2,1,0:T(8,128)(2,1)S(1)} %pad_maximum_fusion.2), channel_id=1, source_target_pairs={{0,8},{1,9},{2,10},{3,11},{4,12},{5,13},{6,14},{7,15},{8,16},{9,17... | collective-permute-start | bytes 884744 | tf_op jit(solution)/shard_map/ppermute | solution.py:34
  92.7 1.1 shard_map.133._
  93.8 10.8 %collective-permute-done.21.ends = bf16[2,6,32,384]{3,2,1,0:T(8,128)(2,1)S(1)} collective-permute-done((bf16[2,6,32,384]{3,2,1,0:T(8,128)(2,1)S(1)}, bf16[2,6,32,384]{3,2,1,0:T(8,128)(2,1)S(1)}, u32[]{:S(2)}, u32[]{:S(2)}) %collective-permute-start.21) | collective-permute-done | bytes 294944 | tf_op jit(solution)/shard_map/ppermute | solution.py:34
  104.6 2.3 %shard_map.134.refs_2_ = bf16[2,8,6,32,1152]{4,3,2,1,0:T(8,128)(2,1)S(1)} custom-call(s32[2]{0:T(128)S(1)} %pad_add_fusion.1.scalars.refs_0_, bf16[2,384,384]{2,1,0:T(8,128)(2,1)S(1)} %copy-done, bf16[2,6,32,384]{3,2,1,0:T(8,128)(2,1)S(1)} %collective-permute-done.21.ends, ...), custom_call_target="tpu_custom_call", output_to_operand_aliasing={{}: (5, {})} | custom-call | flops 1000 | bytes 1000 | tf_op jit(solution)/shard_map/pallas_call | solution.py:191
  106.9 12.7 %shard_map.135 = bf16[6,128,384]{2,1,0:T(8,128)(2,1)} custom-call(s32[2]{0:T(128)S(1)} %pad_add_fusion.1.scalars.refs_0_, f32[3,6]{1,0:T(4,128)S(1)} %add_convert_fusion.refs_1_, bf16[2,8,6,32,1152]{4,3,2,1,0:T(8,128)(2,1)S(1)} %shard_map.134.refs_2_, bf16[6,128,384]{2,1,0:T(8,128)(2,1)S(1)} %bitcast.27, bf16[14,96,384]{2,1,0:T(8,128)(2,1)S(1)} %shard_map.130.refs_4_, ...), custom_call_target="tpu_custom_call" | custom-call | flops 1000 | bytes 1000 | tf_op jit(solution)/shard_map/pallas_call | solution.py:291
  (92 shorter events, 6.3 us)
Async XLA Ops:
  1.2 19.3 %collective-permute-start = (bf16[2,168,384]{2,1,0:T(8,128)(2,1)S(1)}, bf16[2,168,384]{2,1,0:T(8,128)(2,1)S(1)}, u32[]{:S(2)}, u32[]{:S(2)}) collective-permute-start(bf16[2,168,384]{2,1,0:T(8,128)(2,1)S(1)} %constant_dynamic-update-slice_fusion), channel_id=1, source_target_pairs={{152,0},{1,1},{58,2},{67,3},{252,4},{37,5},{94,6},{103,7},{128,8},... | collective-permute-start | bytes 774152 | tf_op jit(solution)/shard_map/ppermute | solution.py:34
  3.2 17.3 %collective-permute-start.1 = (bf16[2,168,384]{2,1,0:T(8,128)(2,1)S(1)}, bf16[2,168,384]{2,1,0:T(8,128)(2,1)S(1)}, u32[]{:S(2)}, u32[]{:S(2)}) collective-permute-start(bf16[2,168,384]{2,1,0:T(8,128)(2,1)S(1)} %constant_dynamic-update-slice_fusion), channel_id=1, source_target_pairs={{24,0},{129,1},{122,2},{195,3},{188,4},{165,5},{222,6},{231,7},{0,... | collective-permute-start | bytes 774152 | tf_op jit(solution)/shard_map/ppermute | solution.py:34
  5.6 6.6 %copy-start.7 = (s32[4]{0:T(128)S(1)}, s32[4]{0:T(128)}, u32[]{:S(2)}) copy-start(s32[4]{0:T(128)} %constant.152.clone) | copy-start | bytes 52
  5.6 6.6 %copy-start.8 = (s32[4]{0:T(128)S(1)}, s32[4]{0:T(128)}, u32[]{:S(2)}) copy-start(s32[4]{0:T(128)} %constant.150.clone) | copy-start | bytes 52
  5.6 6.7 %copy-start.3 = (s32[4,2]{1,0:T(4,128)S(1)}, s32[4,2]{1,0:T(4,128)}, u32[]{:S(2)}) copy-start(s32[4,2]{1,0:T(4,128)} %constant.159) | copy-start | bytes 100
  5.6 7.8 %copy-start.2 = (s32[4,2]{1,0:T(4,128)S(1)}, s32[4,2]{1,0:T(4,128)}, u32[]{:S(2)}) copy-start(s32[4,2]{1,0:T(4,128)} %constant.161) | copy-start | bytes 100
  5.8 9.2 %copy-start.9 = (s32[3]{0:T(128)S(1)}, s32[3]{0:T(128)}, u32[]{:S(2)}) copy-start(s32[3]{0:T(128)} %param.14) | copy-start | bytes 40
  6.3 11.9 %collective-permute-start.4 = (bf16[6,1,32,384]{3,2,1,0:T(8,128)(2,1)S(1)}, bf16[6,1,32,384]{3,2,1,0:T(8,128)(2,1)S(1)}, u32[]{:S(2)}, u32[]{:S(2)}) collective-permute-start(bf16[6,1,32,384]{3,2,1,0:T(8,128)(2,1)S(1)} %get-tuple-element.82), channel_id=1, source_target_pairs={{2,1},{1,2},{4,3},{3,4},{6,5},{5,6},{10,9},{9,10},{12,11},{11,12},... | collective-permute-start | bytes 442376 | tf_op jit(solution)/shard_map/ppermute | solution.py:34
  12.1 6.2 %collective-permute-start.3 = (bf16[6,1,32,384]{3,2,1,0:T(8,128)(2,1)S(1)}, bf16[6,1,32,384]{3,2,1,0:T(8,128)(2,1)S(1)}, u32[]{:S(2)}, u32[]{:S(2)}) collective-permute-start(bf16[6,1,32,384]{3,2,1,0:T(8,128)(2,1)S(1)} %get-tuple-element.81), channel_id=1, source_target_pairs={{1,0},{0,1},{3,2},{2,3},{5,4},{4,5},{7,6},{6,7},{9,8},{8,9},{11,10... | collective-permute-start | bytes 442376 | tf_op jit(solution)/shard_map/ppermute | solution.py:34
  18.2 16.2 %copy-start = (bf16[2,384,384]{2,1,0:T(8,128)(2,1)S(1)}, bf16[2,384,384]{2,1,0:T(8,128)(2,1)}, u32[]{:S(2)}) copy-start(bf16[2,384,384]{2,1,0:T(8,128)(2,1)} %shard_map.127.picks) | copy-start | bytes 1769476
  18.3 16.1 %collective-permute-start.5 = (bf16[2,6,32,384]{3,2,1,0:T(8,128)(2,1)S(1)}, bf16[2,6,32,384]{3,2,1,0:T(8,128)(2,1)S(1)}, u32[]{:S(2)}, u32[]{:S(2)}) collective-permute-start(bf16[2,6,32,384]{3,2,1,0:T(8,128)(2,1)S(1)} %pad_maximum_fusion.1), channel_id=1, source_target_pairs={{0,8},{1,9},{2,10},{3,11},{4,12},{5,13},{6,14},{7,15},{8,16},{9,17... | collective-permute-start | bytes 884744 | tf_op jit(solution)/shard_map/ppermute | solution.py:34
  20.6 17.0 %collective-permute-start.2 = (bf16[2,2,168,384]{3,2,1,0:T(8,128)(2,1)S(1)}, bf16[2,2,168,384]{3,2,1,0:T(8,128)(2,1)S(1)}, u32[]{:S(2)}, u32[]{:S(2)}) collective-permute-start(bf16[2,2,168,384]{3,2,1,0:T(8,128)(2,1)S(1)} %pad_maximum_fusion.refs_0_), channel_id=1, source_target_pairs={{2,0},{9,1},{4,2},{11,3},{6,4},{13,5},{0,6},{15,7},{10,8},{17,9},{... | collective-permute-start | bytes 1548296 | tf_op jit(solution)/shard_map/ppermute | solution.py:34
  21.5 16.8 %collective-permute-start.7 = (bf16[2,2,168,384]{3,2,1,0:T(8,128)(2,1)S(1)}, bf16[2,2,168,384]{3,2,1,0:T(8,128)(2,1)S(1)}, u32[]{:S(2)}, u32[]{:S(2)}) collective-permute-start(bf16[2,2,168,384]{3,2,1,0:T(8,128)(2,1)S(1)} %pad_maximum_fusion.refs_0_), channel_id=1, source_target_pairs={{4,0},{17,1},{6,2},{19,3},{0,4},{21,5},{2,6},{23,7},{12,8},{25,9},... | collective-permute-start | bytes 1548296 | tf_op jit(solution)/shard_map/ppermute | solution.py:34
  34.4 9.4 %collective-permute-start.6 = (bf16[2,2,168,384]{3,2,1,0:T(8,128)(2,1)S(1)}, bf16[2,2,168,384]{3,2,1,0:T(8,128)(2,1)S(1)}, u32[]{:S(2)}, u32[]{:S(2)}) collective-permute-start(bf16[2,2,168,384]{3,2,1,0:T(8,128)(2,1)S(1)} %pad_maximum_fusion.refs_0_), channel_id=1, source_target_pairs={{6,0},{25,1},{0,2},{27,3},{2,4},{29,5},{4,6},{31,7},{14,8},{1,9},{... | collective-permute-start | bytes 1548296 | tf_op jit(solution)/shard_map/ppermute | solution.py:34
  44.0 23.0 %copy-start.5 = (f32[384]{0:T(512)S(1)}, f32[384]{0:T(512)}, u32[]{:S(2)}) copy-start(f32[384]{0:T(512)} %param.20) | copy-start | bytes 4612
  44.2 4.8 %collective-permute-start.8 = (bf16[14,96,384]{2,1,0:T(8,128)(2,1)S(1)}, bf16[14,96,384]{2,1,0:T(8,128)(2,1)S(1)}, u32[]{:S(2)}, u32[]{:S(2)}) collective-permute-start(bf16[14,96,384]{2,1,0:T(8,128)(2,1)S(1)} %shard_map.131.refs_4_), channel_id=1, source_target_pairs={{1,0},{0,1},{3,2},{2,3},{5,4},{4,5},{7,6},{6,7},{9,8},{8,9},{11,10... | collective-permute-start | bytes 3096584 | tf_op jit(solution)/shard_map/ppermute | solution.py:34
  45.7 3.7 %collective-permute-start.9 = (bf16[14,96,384]{2,1,0:T(8,128)(2,1)S(1)}, bf16[14,96,384]{2,1,0:T(8,128)(2,1)S(1)}, u32[]{:S(2)}, u32[]{:S(2)}) collective-permute-start(bf16[14,96,384]{2,1,0:T(8,128)(2,1)S(1)} %shard_map.130.refs_4_), channel_id=1, source_target_pairs={{1,0},{0,1},{3,2},{2,3},{5,4},{4,5},{7,6},{6,7},{9,8},{8,9},{11,10... | collective-permute-start | bytes 3096584 | tf_op jit(solution)/shard_map/ppermute | solution.py:34
  45.8 13.9 %collective-permute-start.13 = (bf16[14,96,384]{2,1,0:T(8,128)(2,1)S(1)}, bf16[14,96,384]{2,1,0:T(8,128)(2,1)S(1)}, u32[]{:S(2)}, u32[]{:S(2)}) collective-permute-start(bf16[14,96,384]{2,1,0:T(8,128)(2,1)S(1)} %shard_map.131.refs_4_), channel_id=1, source_target_pairs={{8,0},{3,1},{10,2},{5,3},{12,4},{7,5},{14,6},{1,7},{16,8},{11,9},{... | collective-permute-start | bytes 3096584 | tf_op jit(solution)/shard_map/ppermute | solution.py:34
  48.1 13.8 %collective-permute-start.14 = (bf16[14,96,384]{2,1,0:T(8,128)(2,1)S(1)}, bf16[14,96,384]{2,1,0:T(8,128)(2,1)S(1)}, u32[]{:S(2)}, u32[]{:S(2)}) collective-permute-start(bf16[14,96,384]{2,1,0:T(8,128)(2,1)S(1)} %shard_map.131.refs_4_), channel_id=1, source_target_pairs={{24,0},{7,1},{26,2},{1,3},{28,4},{3,5},{30,6},{5,7},{0,8},{15,9},{... | collective-permute-start | bytes 3096584 | tf_op jit(solution)/shard_map/ppermute | solution.py:34
  48.1 13.8 %collective-permute-start.15 = (bf16[14,96,384]{2,1,0:T(8,128)(2,1)S(1)}, bf16[14,96,384]{2,1,0:T(8,128)(2,1)S(1)}, u32[]{:S(2)}, u32[]{:S(2)}) collective-permute-start(bf16[14,96,384]{2,1,0:T(8,128)(2,1)S(1)} %shard_map.131.refs_4_), channel_id=1, source_target_pairs={{224,0},{33,1},{226,2},{35,3},{228,4},{37,5},{230,6},{39,7},{232,8... | collective-permute-start | bytes 3096584 | tf_op jit(solution)/shard_map/ppermute | solution.py:34
  61.9 5.0 %collective-permute-start.16 = (bf16[14,96,384]{2,1,0:T(8,128)(2,1)S(1)}, bf16[14,96,384]{2,1,0:T(8,128)(2,1)S(1)}, u32[]{:S(2)}, u32[]{:S(2)}) collective-permute-start(bf16[14,96,384]{2,1,0:T(8,128)(2,1)S(1)} %collective-permute-done.13.refs_5_), channel_id=1, source_target_pairs={{1,0},{0,1},{3,2},{2,3},{5,4},{4,5},{7,6},{6,7},{9,8},{8,9},{11,10... | collective-permute-start | bytes 3096584 | tf_op jit(solution)/shard_map/ppermute | solution.py:34
  64.0 3.7 %collective-permute-start.17 = (bf16[14,96,384]{2,1,0:T(8,128)(2,1)S(1)}, bf16[14,96,384]{2,1,0:T(8,128)(2,1)S(1)}, u32[]{:S(2)}, u32[]{:S(2)}) collective-permute-start(bf16[14,96,384]{2,1,0:T(8,128)(2,1)S(1)} %collective-permute-done.14.refs_6_), channel_id=1, source_target_pairs={{1,0},{0,1},{3,2},{2,3},{5,4},{4,5},{7,6},{6,7},{9,8},{8,9},{11,10... | collective-permute-start | bytes 3096584 | tf_op jit(solution)/shard_map/ppermute | solution.py:34
  64.0 5.2 %collective-permute-start.18 = (bf16[14,96,384]{2,1,0:T(8,128)(2,1)S(1)}, bf16[14,96,384]{2,1,0:T(8,128)(2,1)S(1)}, u32[]{:S(2)}, u32[]{:S(2)}) collective-permute-start(bf16[14,96,384]{2,1,0:T(8,128)(2,1)S(1)} %collective-permute-done.15.refs_7_), channel_id=1, source_target_pairs={{1,0},{0,1},{3,2},{2,3},{5,4},{4,5},{7,6},{6,7},{9,8},{8,9},{11,10... | collective-permute-start | bytes 3096584 | tf_op jit(solution)/shard_map/ppermute | solution.py:34
  64.5 17.0 %collective-permute-start.10 = (bf16[14,96,384]{2,1,0:T(8,128)(2,1)S(1)}, bf16[14,96,384]{2,1,0:T(8,128)(2,1)S(1)}, u32[]{:S(2)}, u32[]{:S(2)}) collective-permute-start(bf16[14,96,384]{2,1,0:T(8,128)(2,1)S(1)} %shard_map.130.refs_4_), channel_id=1, source_target_pairs={{8,0},{3,1},{10,2},{5,3},{12,4},{7,5},{14,6},{1,7},{16,8},{11,9},{... | collective-permute-start | bytes 3096584 | tf_op jit(solution)/shard_map/ppermute | solution.py:34
  66.9 14.6 %collective-permute-start.11 = (bf16[14,96,384]{2,1,0:T(8,128)(2,1)S(1)}, bf16[14,96,384]{2,1,0:T(8,128)(2,1)S(1)}, u32[]{:S(2)}, u32[]{:S(2)}) collective-permute-start(bf16[14,96,384]{2,1,0:T(8,128)(2,1)S(1)} %shard_map.130.refs_4_), channel_id=1, source_target_pairs={{24,0},{7,1},{26,2},{1,3},{28,4},{3,5},{30,6},{5,7},{0,8},{15,9},{... | collective-permute-start | bytes 3096584 | tf_op jit(solution)/shard_map/ppermute | solution.py:34
  66.9 14.6 %collective-permute-start.12 = (bf16[14,96,384]{2,1,0:T(8,128)(2,1)S(1)}, bf16[14,96,384]{2,1,0:T(8,128)(2,1)S(1)}, u32[]{:S(2)}, u32[]{:S(2)}) collective-permute-start(bf16[14,96,384]{2,1,0:T(8,128)(2,1)S(1)} %shard_map.130.refs_4_), channel_id=1, source_target_pairs={{224,0},{33,1},{226,2},{35,3},{228,4},{37,5},{230,6},{39,7},{232,8... | collective-permute-start | bytes 3096584 | tf_op jit(solution)/shard_map/ppermute | solution.py:34
  81.6 3.5 %collective-permute-start.19 = (bf16[6,1,32,384]{3,2,1,0:T(8,128)(2,1)S(1)}, bf16[6,1,32,384]{3,2,1,0:T(8,128)(2,1)S(1)}, u32[]{:S(2)}, u32[]{:S(2)}) collective-permute-start(bf16[6,1,32,384]{3,2,1,0:T(8,128)(2,1)S(1)} %get-tuple-element.80), channel_id=1, source_target_pairs={{1,0},{0,1},{3,2},{2,3},{5,4},{4,5},{7,6},{6,7},{9,8},{8,9},{11,10... | collective-permute-start | bytes 442376 | tf_op jit(solution)/shard_map/ppermute | solution.py:34
  82.6 6.7 %collective-permute-start.20 = (bf16[6,1,32,384]{3,2,1,0:T(8,128)(2,1)S(1)}, bf16[6,1,32,384]{3,2,1,0:T(8,128)(2,1)S(1)}, u32[]{:S(2)}, u32[]{:S(2)}) collective-permute-start(bf16[6,1,32,384]{3,2,1,0:T(8,128)(2,1)S(1)} %get-tuple-element.79), channel_id=1, source_target_pairs={{2,1},{1,2},{4,3},{3,4},{6,5},{5,6},{10,9},{9,10},{12,11},{11,12},... | collective-permute-start | bytes 442376 | tf_op jit(solution)/shard_map/ppermute | solution.py:34
  89.4 17.5 %collective-permute-start.22 = (bf16[14,96,384]{2,1,0:T(8,128)(2,1)S(1)}, bf16[14,96,384]{2,1,0:T(8,128)(2,1)S(1)}, u32[]{:S(2)}, u32[]{:S(2)}) collective-permute-start(bf16[14,96,384]{2,1,0:T(8,128)(2,1)S(1)} %collective-permute-done.10.refs_5_), channel_id=1, source_target_pairs={{1,0},{0,1},{3,2},{2,3},{5,4},{4,5},{7,6},{6,7},{9,8},{8,9},{11,10... | collective-permute-start | bytes 3096584 | tf_op jit(solution)/shard_map/ppermute | solution.py:34
  90.1 16.8 %collective-permute-start.23 = (bf16[14,96,384]{2,1,0:T(8,128)(2,1)S(1)}, bf16[14,96,384]{2,1,0:T(8,128)(2,1)S(1)}, u32[]{:S(2)}, u32[]{:S(2)}) collective-permute-start(bf16[14,96,384]{2,1,0:T(8,128)(2,1)S(1)} %collective-permute-done.11.refs_6_), channel_id=1, source_target_pairs={{1,0},{0,1},{3,2},{2,3},{5,4},{4,5},{7,6},{6,7},{9,8},{8,9},{11,10... | collective-permute-start | bytes 3096584 | tf_op jit(solution)/shard_map/ppermute | solution.py:34
  90.1 16.8 %collective-permute-start.24 = (bf16[14,96,384]{2,1,0:T(8,128)(2,1)S(1)}, bf16[14,96,384]{2,1,0:T(8,128)(2,1)S(1)}, u32[]{:S(2)}, u32[]{:S(2)}) collective-permute-start(bf16[14,96,384]{2,1,0:T(8,128)(2,1)S(1)} %collective-permute-done.12.refs_7_), channel_id=1, source_target_pairs={{1,0},{0,1},{3,2},{2,3},{5,4},{4,5},{7,6},{6,7},{9,8},{8,9},{11,10... | collective-permute-start | bytes 3096584 | tf_op jit(solution)/shard_map/ppermute | solution.py:34
  90.7 13.9 %collective-permute-start.21 = (bf16[2,6,32,384]{3,2,1,0:T(8,128)(2,1)S(1)}, bf16[2,6,32,384]{3,2,1,0:T(8,128)(2,1)S(1)}, u32[]{:S(2)}, u32[]{:S(2)}) collective-permute-start(bf16[2,6,32,384]{3,2,1,0:T(8,128)(2,1)S(1)} %pad_maximum_fusion.2), channel_id=1, source_target_pairs={{0,8},{1,9},{2,10},{3,11},{4,12},{5,13},{6,14},{7,15},{8,16},{9,17... | collective-permute-start | bytes 884744 | tf_op jit(solution)/shard_map/ppermute | solution.py:34
  (3 other events, 18.0 us)

commit v9 on v8

--- a/solution.py
+++ b/solution.py
@@ -15,7 +15,7 @@
 BUNDLE = 96
 ROUND = (0, 1, -1, 2)
 
-FETCH = np.array([[[4, 0], [1, 3], [-1, -3], [2, -2]], [[0, 4], [2, -2], [1, -3], [3, -1]]])
+FETCH = np.array([[0, 4], [2, -2], [1, -3], [3, -1]])
 
 
 def number(z, y, x, c):
@@ -37,9 +37,8 @@
 def z_source(which):
     def source(z, y, x, c):
         odd = z % 2
-        if c == 0:
-            return (z + int(FETCH[0, x, which]), y + 2 * odd - 1, x, c)
-        return (z - odd + int(FETCH[1, (x + 2 * odd) % NX, which]), y, x, c)
+        from_z = z - odd + int(FETCH[(x + 2 * odd) % NX, which])
+        return (from_z, y + 2 * odd - 1, x, c) if c == 0 else (from_z, y, x, c)
 
     return source
 
@@ -103,11 +102,12 @@
     aside = jnp.array((0, 1, -1, 0), jnp.int32)
     odd = z % 2
     at_z = z + jnp.array((0, 0, 0, 1), jnp.int32) * jnp.where(odd == 1, 1, -1)
-    piece_z = at_z[:, None, None] + table[0][(x + around) % NX][None, :, :]
+    at_x = x + around[None, :] + 2 * (at_z % 2)[:, None]
+    piece_z = (at_z - at_z % 2)[:, None, None] + table[at_x % NX]
     piece_y = (y + aside + 2 * (at_z % 2) - 1)[:, None, None]
     first = piece_z % NZ * NY + piece_y % NY
     at_z = z + jnp.array((0, 0, 0, 1), jnp.int32) * jnp.where(odd == 0, 1, -1)
-    piece_z = (at_z - at_z % 2)[:, None] + table[1][(x + aside + 2 * (at_z % 2)) % NX]
+    piece_z = (at_z - at_z % 2)[:, None] + table[(x + aside + 2 * (at_z % 2)) % NX]
     piece_y = y + around
     second = piece_z[:, None, :] % NZ * NY + piece_y[None, :, None] % NY
     ramp = jnp.arange(SHARD, dtype=jnp.int32)
@@ -159,15 +159,10 @@
     )(picks, acts.reshape(-1, C))
 
 
-def spread_halo_body(scalars, picks, ends, beside, across, _, out):
+def spread_halo_body(scalars, picks, ends, corners, beside, across, _, out):
     core = scalars[0]
     cells = jnp.concatenate(
-        [ends[:, 0:4].reshape(256, C)]
-        + [
-            rows[...].reshape(-1, C)
-            for rows in (ends.at[:, 4:5], beside, ends.at[:, 5:6], across)
-        ],
-        0,
+        [part[...].reshape(-1, C) for part in (ends, beside, corners, across)], 0
     )
     for half in range(2):
         for tap, part in enumerate(spread_cells(cells, picks[half])):
@@ -186,17 +181,17 @@
                 out[half, :, 5:6, :, lanes] = far
 
 
-def spread_halo(scalars, picks, ends, beside, across, spread):
+def spread_halo(scalars, picks, ends, corners, beside, across, spread):
     vmem = pl.BlockSpec(memory_space=pltpu.VMEM)
     return pl.pallas_call(
         spread_halo_body,
         out_shape=jax.ShapeDtypeStruct(spread.shape, spread.dtype),
-        in_specs=[pl.BlockSpec(memory_space=pltpu.SMEM)] + [vmem] * 5,
+        in_specs=[pl.BlockSpec(memory_space=pltpu.SMEM)] + [vmem] * 6,
         out_specs=vmem,
-        input_output_aliases={5: 0},
+        input_output_aliases={6: 0},
         compiler_params=pltpu.CompilerParams(vmem_limit_bytes=20 * 1024 * 1024),
         cost_estimate=pl.CostEstimate(flops=1000, bytes_accessed=1000, transcendentals=0),
-    )(scalars, picks, ends, beside, across, spread)
+    )(scalars, picks, ends, corners, beside, across, spread)
 
 
 def conv_body(
@@ -326,6 +321,11 @@
     return (z, y, x, 1 - c) if 0 <= x < NX else None
 
 
+def across_and_before(z, y, x, c):
+    place = across_chips(z, y, x, c)
+    return None if place is None else before_in_group(*place)
+
+
 def per_device(
     frames, clip_lengths, group_start, group_count, kernel_one, kernel_two, gain_one, gain_two
 ):
@@ -345,15 +345,16 @@
             jnp.where(first_core, acts[:, 0:1], acts[:, 3:4]),
         )
 
-    def with_rows(*arrays):
-        return jnp.concatenate([lax.dynamic_slice_in_dim(a, last, 2, 0) for a in arrays], 1)
+    def last_two(acts):
+        return lax.dynamic_slice_in_dim(acts, last, 2, 0)
 
     acts_one = norm_act(frames, gain_one)
     own = jnp.stack([own_half(kernel_one), own_half(kernel_two)])
     pieces = z_stage(own)
     inner, outer = sides(acts_one)
     beside, across = fetch(inner, sibling), fetch(outer, across_chips)
-    ends = fetch(with_rows(acts_one, beside, across), before_in_group)
+    ends = jnp.concatenate([last_two(acts_one), last_two(beside)], 1)
+    ends, corners = fetch(ends, before_in_group), fetch(last_two(outer), across_and_before)
     picks = make_picks(orders)
     pieces, picks, lag_weights, scalars = lax.optimization_barrier(
         (pieces, picks, lag_weights, scalars)
@@ -361,9 +362,12 @@
 
     opposite = fetch(pieces, small_source(2))
     after = fetch(pieces, small_source(1))
-    gated, ends = lax.optimization_barrier((pieces, ends))
+    gated, ends, corners, across = lax.optimization_barrier((pieces, ends, corners, across))
     parts = [pieces, after, fetch(gated, small_source(-1)), opposite]
-    spread = spread_halo(scalars, picks, ends, beside, across, spread_inner(picks, acts_one))
+    beside = jnp.concatenate([ends[:, 4:5], beside], 0)
+    spread = spread_halo(
+        scalars, picks, ends[:, 0:4], corners, beside, across, spread_inner(picks, acts_one)
+    )
     parts, spread = lax.optimization_barrier((parts, spread))
 
     one_bundle, two_bundle = join_rows(parts, 0), join_rows(parts, 1)
@@ -385,13 +389,19 @@
 
     two_bundles, acts_two = lax.optimization_barrier((two_bundles, acts_two))
     inner, outer = sides(acts_two)
-    across, beside = fetch(outer, across_chips), fetch(inner, sibling)
-    two_bundles, beside, across = lax.optimization_barrier((two_bundles, beside, across))
-    two_others += [fetch(b, sibling) for b in two_bundles[1:]]
-    ends = fetch(with_rows(acts_two, beside, across), before_in_group)
+    ends, corners, outer = lax.optimization_barrier((last_two(acts_two), last_two(outer), outer))
+    ends = fetch(ends, before_in_group)
+    across = fetch(outer, across_chips)
+    corners = fetch(corners, across_and_before)
+    two_others += [fetch(b, sibling) for b in two_bundles[1:3]]
     spread = spread_inner(picks, acts_two)
-    ends, spread = lax.optimization_barrier((ends, spread))
-    spread = spread_halo(scalars, picks, ends, beside, across, spread)
+    ends, corners, across, spread, two_others = lax.optimization_barrier(
+        (ends, corners, across, spread, two_others)
+    )
+    beside = fetch(jnp.concatenate([sides(ends)[0], inner], 0), sibling)
+    two_last, beside = lax.optimization_barrier((two_bundles[3], beside))
+    two_others.append(fetch(two_last, sibling))
+    spread = spread_halo(scalars, picks, ends, corners, beside, across, spread)
     result = conv(
         scalars, lag_weights, spread, frames.reshape(slots, 128, C), two_bundles, two_others,
         finish_add,

time: 121 us -> 118 us (0.975)
  waiting for transfers between devices: 48.5 us -> 35 us
  starting transfers between devices: 30.5 us -> 41 us
    ppermute x25 -> x27, waiting for transfers between devices: 48.5 us -> 35 us  [fetch(): return lax.ppermute(array, AXES, pairs)]
    ppermute x25 -> x27, starting transfers between devices: 30.5 us -> 41 us  [fetch(): return lax.ppermute(array, AXES, pairs)]
  transfers between devices with their start and end apart: 25 -> 27, of which waited for: 10 -> 12; matrix products, arithmetic and copies ran while one was open for 3% -> 4% of each run, Pallas kernels for 17% -> 17%
where the time goes in v9:
time: 118 us; the launch traced here: 117 us
  starting transfers between devices  41 us (35%)
  waiting for transfers between devices  35 us (30%)
  Pallas kernels  33.5 us (28%)
  local copies, waits for them, and re-layouts  3.38 us (3%)
  other arithmetic  2.34 us (2%)
  between operations  1.98 us (2%)
    ppermute x27, starting transfers between devices, fetch(): return lax.ppermute(array, AXES, pairs)  41 us
    ppermute x27, waiting for transfers between devices, fetch(): return lax.ppermute(array, AXES, pairs)  35 us
    pallas_call x2, Pallas kernels, conv(): pl.pallas_call(lambda *refs: conv_body(*refs, finish=finish), out_shape=j...  24.9 us
    pallas_call x2, Pallas kernels, spread_halo(): pl.pallas_call(spread_halo_body, out_shape=jax.ShapeDtypeStruct(spread.sh...  4.4 us
  transfers between devices with their start and end apart: 27, of which 12 were waited for; matrix products, arithmetic and copies ran while one was open for 4% of the time, Pallas kernels for 17%

profile of v9, /device:TPU:131, one launch (start us, length us, event | category | flops | bytes accessed | tf_op | source)
XLA Modules:
  0.0 117.2 jit_solution(13191290872013850161)
XLA Ops:
  0.0 1.1 constant_dynamic-slice_fusion.5
  1.2 1.3 %collective-permute-start.1 = (bf16[2,168,384]{2,1,0:T(8,128)(2,1)S(1)}, bf16[2,168,384]{2,1,0:T(8,128)(2,1)S(1)}, u32[]{:S(2)}, u32[]{:S(2)}) collective-permute-start(bf16[2,168,384]{2,1,0:T(8,128)(2,1)S(1)} %constant_dynamic-update-slice_fusion), channel_id=1, source_target_pairs={{152,0},{129,1},{218,2},{195,3},{188,4},{165,5},{254,6},{231,7},{1... | collective-permute-start | bytes 774152 | tf_op jit(solution)/shard_map/ppermute | solution.py:34
  2.5 4.3 %collective-permute-start = (bf16[2,168,384]{2,1,0:T(8,128)(2,1)S(1)}, bf16[2,168,384]{2,1,0:T(8,128)(2,1)S(1)}, u32[]{:S(2)}, u32[]{:S(2)}) collective-permute-start(bf16[2,168,384]{2,1,0:T(8,128)(2,1)S(1)} %constant_dynamic-update-slice_fusion), channel_id=1, source_target_pairs={{24,0},{1,1},{90,2},{67,3},{60,4},{37,5},{126,6},{103,7},{0,8},{9,... | collective-permute-start | bytes 774152 | tf_op jit(solution)/shard_map/ppermute | solution.py:34
  7.6 3.6 %collective-permute-start.6 = (bf16[6,1,32,384]{3,2,1,0:T(8,128)(2,1)S(1)}, bf16[6,1,32,384]{3,2,1,0:T(8,128)(2,1)S(1)}, u32[]{:S(2)}, u32[]{:S(2)}) collective-permute-start(bf16[6,1,32,384]{3,2,1,0:T(8,128)(2,1)S(1)} %get-tuple-element.93), channel_id=1, source_target_pairs={{2,1},{1,2},{4,3},{3,4},{6,5},{5,6},{10,9},{9,10},{12,11},{11,12},... | collective-permute-start | bytes 442376 | tf_op jit(solution)/shard_map/ppermute | solution.py:34
  11.8 3.0 %collective-permute-start.5 = (bf16[2,1,32,384]{3,2,1,0:T(8,128)(2,1)S(1)}, bf16[2,1,32,384]{3,2,1,0:T(8,128)(2,1)S(1)}, u32[]{:S(2)}, u32[]{:S(2)}) collective-permute-start(bf16[2,1,32,384]{3,2,1,0:T(8,128)(2,1)S(1)} %constant_dynamic-slice_fusion.2), channel_id=1, source_target_pairs={{2,9},{1,10},{4,11},{3,12},{6,13},{5,14},{10,17},{9,18},{12,19},{1... | collective-permute-start | bytes 147464 | tf_op jit(solution)/shard_map/ppermute | solution.py:34
  14.8 3.1 %collective-permute-start.3 = (bf16[6,1,32,384]{3,2,1,0:T(8,128)(2,1)S(1)}, bf16[6,1,32,384]{3,2,1,0:T(8,128)(2,1)S(1)}, u32[]{:S(2)}, u32[]{:S(2)}) collective-permute-start(bf16[6,1,32,384]{3,2,1,0:T(8,128)(2,1)S(1)} %get-tuple-element.94), channel_id=1, source_target_pairs={{1,0},{0,1},{3,2},{2,3},{5,4},{4,5},{7,6},{6,7},{9,8},{8,9},{11,10... | collective-permute-start | bytes 442376 | tf_op jit(solution)/shard_map/ppermute | solution.py:34
  22.1 1.9 %collective-permute-start.4 = (bf16[2,5,32,384]{3,2,1,0:T(8,128)(2,1)S(1)}, bf16[2,5,32,384]{3,2,1,0:T(8,128)(2,1)S(1)}, u32[]{:S(2)}, u32[]{:S(2)}) collective-permute-start(bf16[2,5,32,384]{3,2,1,0:T(8,128)(2,1)S(1)} %pad_maximum_fusion.1), channel_id=1, source_target_pairs={{0,8},{1,9},{2,10},{3,11},{4,12},{5,13},{6,14},{7,15},{8,16},{9,17... | collective-permute-start | bytes 737288 | tf_op jit(solution)/shard_map/ppermute | solution.py:34
  24.1 1.6 %shard_map.127.picks = bf16[2,384,384]{2,1,0:T(8,128)(2,1)} custom-call(s32[2,384]{1,0:T(2,128)} %pad_add_fusion.order), custom_call_target="tpu_custom_call" | custom-call | flops 1000 | bytes 1000 | tf_op jit(solution)/shard_map/pallas_call | solution.py:126
  25.8 4.0 %collective-permute-start.8 = (bf16[2,2,168,384]{3,2,1,0:T(8,128)(2,1)S(1)}, bf16[2,2,168,384]{3,2,1,0:T(8,128)(2,1)S(1)}, u32[]{:S(2)}, u32[]{:S(2)}) collective-permute-start(bf16[2,2,168,384]{3,2,1,0:T(8,128)(2,1)S(1)} %pad_maximum_fusion.refs_0_), channel_id=1, source_target_pairs={{4,0},{17,1},{6,2},{19,3},{0,4},{21,5},{2,6},{23,7},{12,8},{25,9},... | collective-permute-start | bytes 1548296 | tf_op jit(solution)/shard_map/ppermute | solution.py:34
  29.8 5.2 %collective-permute-done.4 = bf16[2,5,32,384]{3,2,1,0:T(8,128)(2,1)S(1)} collective-permute-done((bf16[2,5,32,384]{3,2,1,0:T(8,128)(2,1)S(1)}, bf16[2,5,32,384]{3,2,1,0:T(8,128)(2,1)S(1)}, u32[]{:S(2)}, u32[]{:S(2)}) %collective-permute-start.4) | collective-permute-done | bytes 245792 | tf_op jit(solution)/shard_map/ppermute | solution.py:34
  35.0 1.1 shard_map.128._
  36.2 2.1 %shard_map.129.refs_2_ = bf16[2,8,6,32,1152]{4,3,2,1,0:T(8,128)(2,1)S(1)} custom-call(s32[2]{0:T(128)S(1)} %pad_add_fusion.1.scalars.refs_0_, bf16[2,384,384]{2,1,0:T(8,128)(2,1)S(1)} %copy-done, bf16[2,4,32,384]{3,2,1,0:T(8,128)(2,1)S(1)} %slice.30.ends, bf16[2,1,32,384]{3,2,1,0:T(8,128)(2,1)S(1)} %collective-permute-done.5.corners, ...), custom_call_target="tpu_custom_call", output_to_operand_aliasing={{}: (6, {})} | custom-call | flops 1000 | bytes 1000 | tf_op jit(solution)/shard_map/pallas_call | solution.py:186
  38.3 2.3 %collective-permute-done.8.refs_3_ = bf16[2,2,168,384]{3,2,1,0:T(8,128)(2,1)S(1)} collective-permute-done((bf16[2,2,168,384]{3,2,1,0:T(8,128)(2,1)S(1)}, bf16[2,2,168,384]{3,2,1,0:T(8,128)(2,1)S(1)}, u32[]{:S(2)}, u32[]{:S(2)}) %collective-permute-start.8) | collective-permute-done | bytes 516128 | tf_op jit(solution)/shard_map/ppermute | solution.py:34
  40.6 1.9 %collective-permute-done.2.refs_1_ = bf16[2,2,168,384]{3,2,1,0:T(8,128)(2,1)S(1)} collective-permute-done((bf16[2,2,168,384]{3,2,1,0:T(8,128)(2,1)S(1)}, bf16[2,2,168,384]{3,2,1,0:T(8,128)(2,1)S(1)}, u32[]{:S(2)}, u32[]{:S(2)}) %collective-permute-start.2) | collective-permute-done | bytes 516128 | tf_op jit(solution)/shard_map/ppermute | solution.py:34
  42.6 3.5 %collective-permute-done.7.refs_2_ = bf16[2,2,168,384]{3,2,1,0:T(8,128)(2,1)S(1)} collective-permute-done((bf16[2,2,168,384]{3,2,1,0:T(8,128)(2,1)S(1)}, bf16[2,2,168,384]{3,2,1,0:T(8,128)(2,1)S(1)}, u32[]{:S(2)}, u32[]{:S(2)}) %collective-permute-start.7) | collective-permute-done | bytes 516128 | tf_op jit(solution)/shard_map/ppermute | solution.py:34
  47.1 0.6 collective-permute-start.16
  47.7 1.5 %collective-permute-start.14 = (bf16[14,96,384]{2,1,0:T(8,128)(2,1)S(1)}, bf16[14,96,384]{2,1,0:T(8,128)(2,1)S(1)}, u32[]{:S(2)}, u32[]{:S(2)}) collective-permute-start(bf16[14,96,384]{2,1,0:T(8,128)(2,1)S(1)} %shard_map.131.refs_4_), channel_id=1, source_target_pairs={{8,0},{3,1},{10,2},{5,3},{12,4},{7,5},{14,6},{1,7},{16,8},{11,9},{... | collective-permute-start | bytes 3096584 | tf_op jit(solution)/shard_map/ppermute | solution.py:34
  49.2 1.5 %collective-permute-done.10.refs_8_ = bf16[14,96,384]{2,1,0:T(8,128)(2,1)S(1)} collective-permute-done((bf16[14,96,384]{2,1,0:T(8,128)(2,1)S(1)}, bf16[14,96,384]{2,1,0:T(8,128)(2,1)S(1)}, u32[]{:S(2)}, u32[]{:S(2)}) %collective-permute-start.10) | collective-permute-done | bytes 1032224 | tf_op jit(solution)/shard_map/ppermute | solution.py:34
  50.7 10.2 %collective-permute-done.16.refs_7_ = bf16[14,96,384]{2,1,0:T(8,128)(2,1)S(1)} collective-permute-done((bf16[14,96,384]{2,1,0:T(8,128)(2,1)S(1)}, bf16[14,96,384]{2,1,0:T(8,128)(2,1)S(1)}, u32[]{:S(2)}, u32[]{:S(2)}) %collective-permute-start.16) | collective-permute-done | bytes 1032224 | tf_op jit(solution)/shard_map/ppermute | solution.py:34
  61.5 2.4 %collective-permute-start.17 = (bf16[14,96,384]{2,1,0:T(8,128)(2,1)S(1)}, bf16[14,96,384]{2,1,0:T(8,128)(2,1)S(1)}, u32[]{:S(2)}, u32[]{:S(2)}) collective-permute-start(bf16[14,96,384]{2,1,0:T(8,128)(2,1)S(1)} %collective-permute-done.14.refs_5_), channel_id=1, source_target_pairs={{1,0},{0,1},{3,2},{2,3},{5,4},{4,5},{7,6},{6,7},{9,8},{8,9},{11,10... | collective-permute-start | bytes 3096584 | tf_op jit(solution)/shard_map/ppermute | solution.py:34
  65.0 2.2 %collective-permute-start.12 = (bf16[14,96,384]{2,1,0:T(8,128)(2,1)S(1)}, bf16[14,96,384]{2,1,0:T(8,128)(2,1)S(1)}, u32[]{:S(2)}, u32[]{:S(2)}) collective-permute-start(bf16[14,96,384]{2,1,0:T(8,128)(2,1)S(1)} %shard_map.130.refs_4_), channel_id=1, source_target_pairs={{24,0},{7,1},{26,2},{1,3},{28,4},{3,5},{30,6},{5,7},{0,8},{15,9},{... | collective-permute-start | bytes 3096584 | tf_op jit(solution)/shard_map/ppermute | solution.py:34
  67.6 1.5 %collective-permute-done.19.refs_11_ = bf16[14,96,384]{2,1,0:T(8,128)(2,1)S(1)} collective-permute-done((bf16[14,96,384]{2,1,0:T(8,128)(2,1)S(1)}, bf16[14,96,384]{2,1,0:T(8,128)(2,1)S(1)}, u32[]{:S(2)}, u32[]{:S(2)}) %collective-permute-start.19) | collective-permute-done | bytes 1032224 | tf_op jit(solution)/shard_map/ppermute | solution.py:34
  69.1 12.3 %shard_map.132 = bf16[6,128,384]{2,1,0:T(8,128)(2,1)S(1)} custom-call(s32[2]{0:T(128)S(1)} %pad_add_fusion.1.scalars.refs_0_, f32[3,6]{1,0:T(4,128)S(1)} %add_convert_fusion.refs_1_, bf16[2,8,6,32,1152]{4,3,2,1,0:T(8,128)(2,1)S(1)} %shard_map.129.refs_2_, f32[1,384]{1,0:T(1,128)S(1)} %reshape.334.refs_3_, bf16[14,96,384]{2,1,0:T(8,128)(2,1)S(1)} %shard_map.131.refs_4_, ...), custom_call_target="tpu_custom_call" | custom-call | flops 1000 | bytes 1000 | tf_op jit(solution)/shard_map/pallas_call | solution.py:286
  81.4 1.2 %collective-permute-start.23 = (bf16[14,96,384]{2,1,0:T(8,128)(2,1)S(1)}, bf16[14,96,384]{2,1,0:T(8,128)(2,1)S(1)}, u32[]{:S(2)}, u32[]{:S(2)}) collective-permute-start(bf16[14,96,384]{2,1,0:T(8,128)(2,1)S(1)} %collective-permute-done.11.refs_5_), channel_id=1, source_target_pairs={{1,0},{0,1},{3,2},{2,3},{5,4},{4,5},{7,6},{6,7},{9,8},{8,9},{11,10... | collective-permute-start | bytes 3096584 | tf_op jit(solution)/shard_map/ppermute | solution.py:34
  82.7 3.0 %collective-permute-start.20 = (bf16[2,4,32,384]{3,2,1,0:T(8,128)(2,1)S(1)}, bf16[2,4,32,384]{3,2,1,0:T(8,128)(2,1)S(1)}, u32[]{:S(2)}, u32[]{:S(2)}) collective-permute-start(bf16[2,4,32,384]{3,2,1,0:T(8,128)(2,1)S(1)} %constant_dynamic-slice_fusion.1), channel_id=1, source_target_pairs={{0,8},{1,9},{2,10},{3,11},{4,12},{5,13},{6,14},{7,15},{8,16},{9,17... | collective-permute-start | bytes 589832 | tf_op jit(solution)/shard_map/ppermute | solution.py:34
  85.8 4.6 %collective-permute-start.22 = (bf16[6,1,32,384]{3,2,1,0:T(8,128)(2,1)S(1)}, bf16[6,1,32,384]{3,2,1,0:T(8,128)(2,1)S(1)}, u32[]{:S(2)}, u32[]{:S(2)}) collective-permute-start(bf16[6,1,32,384]{3,2,1,0:T(8,128)(2,1)S(1)} %get-tuple-element.72), channel_id=1, source_target_pairs={{2,1},{1,2},{4,3},{3,4},{6,5},{5,6},{10,9},{9,10},{12,11},{11,12},... | collective-permute-start | bytes 442376 | tf_op jit(solution)/shard_map/ppermute | solution.py:34
  90.4 2.4 %collective-permute-start.21 = (bf16[2,1,32,384]{3,2,1,0:T(8,128)(2,1)S(1)}, bf16[2,1,32,384]{3,2,1,0:T(8,128)(2,1)S(1)}, u32[]{:S(2)}, u32[]{:S(2)}) collective-permute-start(bf16[2,1,32,384]{3,2,1,0:T(8,128)(2,1)S(1)} %constant_dynamic-slice_fusion), channel_id=1, source_target_pairs={{2,9},{1,10},{4,11},{3,12},{6,13},{5,14},{10,17},{9,18},{12,19},{1... | collective-permute-start | bytes 147464 | tf_op jit(solution)/shard_map/ppermute | solution.py:34
  92.8 1.1 shard_map.133._
  93.9 6.2 %collective-permute-done.21.corners = bf16[2,1,32,384]{3,2,1,0:T(8,128)(2,1)S(1)} collective-permute-done((bf16[2,1,32,384]{3,2,1,0:T(8,128)(2,1)S(1)}, bf16[2,1,32,384]{3,2,1,0:T(8,128)(2,1)S(1)}, u32[]{:S(2)}, u32[]{:S(2)}) %collective-permute-start.21) | collective-permute-done | bytes 49184 | tf_op jit(solution)/shard_map/ppermute | solution.py:34
  100.2 1.4 %collective-permute-done.25.beside = bf16[8,1,32,384]{3,2,1,0:T(8,128)(2,1)S(1)} collective-permute-done((bf16[8,1,32,384]{3,2,1,0:T(8,128)(2,1)S(1)}, bf16[8,1,32,384]{3,2,1,0:T(8,128)(2,1)S(1)}, u32[]{:S(2)}, u32[]{:S(2)}) %collective-permute-start.25) | collective-permute-done | bytes 196640 | tf_op jit(solution)/shard_map/ppermute | solution.py:34
  101.8 2.3 %shard_map.134.refs_2_ = bf16[2,8,6,32,1152]{4,3,2,1,0:T(8,128)(2,1)S(1)} custom-call(s32[2]{0:T(128)S(1)} %pad_add_fusion.1.scalars.refs_0_, bf16[2,384,384]{2,1,0:T(8,128)(2,1)S(1)} %copy-done, bf16[2,4,32,384]{3,2,1,0:T(8,128)(2,1)S(1)} %collective-permute-done.20.ends, ...), custom_call_target="tpu_custom_call", output_to_operand_aliasing={{}: (6, {})} | custom-call | flops 1000 | bytes 1000 | tf_op jit(solution)/shard_map/pallas_call | solution.py:186
  104.3 12.7 %shard_map.135 = bf16[6,128,384]{2,1,0:T(8,128)(2,1)} custom-call(s32[2]{0:T(128)S(1)} %pad_add_fusion.1.scalars.refs_0_, f32[3,6]{1,0:T(4,128)S(1)} %add_convert_fusion.refs_1_, bf16[2,8,6,32,1152]{4,3,2,1,0:T(8,128)(2,1)S(1)} %shard_map.134.refs_2_, bf16[6,128,384]{2,1,0:T(8,128)(2,1)S(1)} %bitcast.30, bf16[14,96,384]{2,1,0:T(8,128)(2,1)S(1)} %shard_map.130.refs_4_, ...), custom_call_target="tpu_custom_call" | custom-call | flops 1000 | bytes 1000 | tf_op jit(solution)/shard_map/pallas_call | solution.py:286
  (101 shorter events, 8.2 us)
Async XLA Ops:
  1.2 24.5 %collective-permute-start.1 = (bf16[2,168,384]{2,1,0:T(8,128)(2,1)S(1)}, bf16[2,168,384]{2,1,0:T(8,128)(2,1)S(1)}, u32[]{:S(2)}, u32[]{:S(2)}) collective-permute-start(bf16[2,168,384]{2,1,0:T(8,128)(2,1)S(1)} %constant_dynamic-update-slice_fusion), channel_id=1, source_target_pairs={{152,0},{129,1},{218,2},{195,3},{188,4},{165,5},{254,6},{231,7},{1... | collective-permute-start | bytes 774152 | tf_op jit(solution)/shard_map/ppermute | solution.py:34
  2.5 23.2 %collective-permute-start = (bf16[2,168,384]{2,1,0:T(8,128)(2,1)S(1)}, bf16[2,168,384]{2,1,0:T(8,128)(2,1)S(1)}, u32[]{:S(2)}, u32[]{:S(2)}) collective-permute-start(bf16[2,168,384]{2,1,0:T(8,128)(2,1)S(1)} %constant_dynamic-update-slice_fusion), channel_id=1, source_target_pairs={{24,0},{1,1},{90,2},{67,3},{60,4},{37,5},{126,6},{103,7},{0,8},{9,... | collective-permute-start | bytes 774152 | tf_op jit(solution)/shard_map/ppermute | solution.py:34
  6.8 11.9 %copy-start.6 = (s32[4]{0:T(128)S(1)}, s32[4]{0:T(128)}, u32[]{:S(2)}) copy-start(s32[4]{0:T(128)} %constant.164.clone) | copy-start | bytes 52
  6.8 11.9 %copy-start.7 = (s32[4]{0:T(128)S(1)}, s32[4]{0:T(128)}, u32[]{:S(2)}) copy-start(s32[4]{0:T(128)} %constant.162.clone) | copy-start | bytes 52
  6.8 11.9 %copy-start.5 = (s32[4]{0:T(128)S(1)}, s32[4]{0:T(128)}, u32[]{:S(2)}) copy-start(s32[4]{0:T(128)} %constant.163.clone) | copy-start | bytes 52
  6.9 12.1 %copy-start.2 = (s32[4,2]{1,0:T(4,128)S(1)}, s32[4,2]{1,0:T(4,128)}, u32[]{:S(2)}) copy-start(s32[4,2]{1,0:T(4,128)} %constant.161.clone) | copy-start | bytes 100
  7.6 22.3 %collective-permute-start.6 = (bf16[6,1,32,384]{3,2,1,0:T(8,128)(2,1)S(1)}, bf16[6,1,32,384]{3,2,1,0:T(8,128)(2,1)S(1)}, u32[]{:S(2)}, u32[]{:S(2)}) collective-permute-start(bf16[6,1,32,384]{3,2,1,0:T(8,128)(2,1)S(1)} %get-tuple-element.93), channel_id=1, source_target_pairs={{2,1},{1,2},{4,3},{3,4},{6,5},{5,6},{10,9},{9,10},{12,11},{11,12},... | collective-permute-start | bytes 442376 | tf_op jit(solution)/shard_map/ppermute | solution.py:34
  11.8 18.0 %collective-permute-start.5 = (bf16[2,1,32,384]{3,2,1,0:T(8,128)(2,1)S(1)}, bf16[2,1,32,384]{3,2,1,0:T(8,128)(2,1)S(1)}, u32[]{:S(2)}, u32[]{:S(2)}) collective-permute-start(bf16[2,1,32,384]{3,2,1,0:T(8,128)(2,1)S(1)} %constant_dynamic-slice_fusion.2), channel_id=1, source_target_pairs={{2,9},{1,10},{4,11},{3,12},{6,13},{5,14},{10,17},{9,18},{12,19},{1... | collective-permute-start | bytes 147464 | tf_op jit(solution)/shard_map/ppermute | solution.py:34
  14.8 7.2 %collective-permute-start.3 = (bf16[6,1,32,384]{3,2,1,0:T(8,128)(2,1)S(1)}, bf16[6,1,32,384]{3,2,1,0:T(8,128)(2,1)S(1)}, u32[]{:S(2)}, u32[]{:S(2)}) collective-permute-start(bf16[6,1,32,384]{3,2,1,0:T(8,128)(2,1)S(1)} %get-tuple-element.94), channel_id=1, source_target_pairs={{1,0},{0,1},{3,2},{2,3},{5,4},{4,5},{7,6},{6,7},{9,8},{8,9},{11,10... | collective-permute-start | bytes 442376 | tf_op jit(solution)/shard_map/ppermute | solution.py:34
  22.1 12.9 %collective-permute-start.4 = (bf16[2,5,32,384]{3,2,1,0:T(8,128)(2,1)S(1)}, bf16[2,5,32,384]{3,2,1,0:T(8,128)(2,1)S(1)}, u32[]{:S(2)}, u32[]{:S(2)}) collective-permute-start(bf16[2,5,32,384]{3,2,1,0:T(8,128)(2,1)S(1)} %pad_maximum_fusion.1), channel_id=1, source_target_pairs={{0,8},{1,9},{2,10},{3,11},{4,12},{5,13},{6,14},{7,15},{8,16},{9,17... | collective-permute-start | bytes 737288 | tf_op jit(solution)/shard_map/ppermute | solution.py:34
  25.8 14.8 %collective-permute-start.8 = (bf16[2,2,168,384]{3,2,1,0:T(8,128)(2,1)S(1)}, bf16[2,2,168,384]{3,2,1,0:T(8,128)(2,1)S(1)}, u32[]{:S(2)}, u32[]{:S(2)}) collective-permute-start(bf16[2,2,168,384]{3,2,1,0:T(8,128)(2,1)S(1)} %pad_maximum_fusion.refs_0_), channel_id=1, source_target_pairs={{4,0},{17,1},{6,2},{19,3},{0,4},{21,5},{2,6},{23,7},{12,8},{25,9},... | collective-permute-start | bytes 1548296 | tf_op jit(solution)/shard_map/ppermute | solution.py:34
  29.8 12.7 %collective-permute-start.2 = (bf16[2,2,168,384]{3,2,1,0:T(8,128)(2,1)S(1)}, bf16[2,2,168,384]{3,2,1,0:T(8,128)(2,1)S(1)}, u32[]{:S(2)}, u32[]{:S(2)}) collective-permute-start(bf16[2,2,168,384]{3,2,1,0:T(8,128)(2,1)S(1)} %pad_maximum_fusion.refs_0_), channel_id=1, source_target_pairs={{2,0},{9,1},{4,2},{11,3},{6,4},{13,5},{0,6},{15,7},{10,8},{17,9},{... | collective-permute-start | bytes 1548296 | tf_op jit(solution)/shard_map/ppermute | solution.py:34
  35.0 11.0 %collective-permute-start.7 = (bf16[2,2,168,384]{3,2,1,0:T(8,128)(2,1)S(1)}, bf16[2,2,168,384]{3,2,1,0:T(8,128)(2,1)S(1)}, u32[]{:S(2)}, u32[]{:S(2)}) collective-permute-start(bf16[2,2,168,384]{3,2,1,0:T(8,128)(2,1)S(1)} %pad_maximum_fusion.refs_0_), channel_id=1, source_target_pairs={{6,0},{25,1},{0,2},{27,3},{2,4},{29,5},{4,6},{31,7},{14,8},{1,9},{... | collective-permute-start | bytes 1548296 | tf_op jit(solution)/shard_map/ppermute | solution.py:34
  46.3 20.9 %copy-start.4 = (f32[384]{0:T(512)S(1)}, f32[384]{0:T(512)}, u32[]{:S(2)}) copy-start(f32[384]{0:T(512)} %param.20) | copy-start | bytes 4612
  46.5 2.7 %collective-permute-start.9 = (bf16[14,96,384]{2,1,0:T(8,128)(2,1)S(1)}, bf16[14,96,384]{2,1,0:T(8,128)(2,1)S(1)}, u32[]{:S(2)}, u32[]{:S(2)}) collective-permute-start(bf16[14,96,384]{2,1,0:T(8,128)(2,1)S(1)} %shard_map.131.refs_4_), channel_id=1, source_target_pairs={{1,0},{0,1},{3,2},{2,3},{5,4},{4,5},{7,6},{6,7},{9,8},{8,9},{11,10... | collective-permute-start | bytes 3096584 | tf_op jit(solution)/shard_map/ppermute | solution.py:34
  46.6 4.1 %collective-permute-start.10 = (bf16[14,96,384]{2,1,0:T(8,128)(2,1)S(1)}, bf16[14,96,384]{2,1,0:T(8,128)(2,1)S(1)}, u32[]{:S(2)}, u32[]{:S(2)}) collective-permute-start(bf16[14,96,384]{2,1,0:T(8,128)(2,1)S(1)} %shard_map.130.refs_4_), channel_id=1, source_target_pairs={{1,0},{0,1},{3,2},{2,3},{5,4},{4,5},{7,6},{6,7},{9,8},{8,9},{11,10... | collective-permute-start | bytes 3096584 | tf_op jit(solution)/shard_map/ppermute | solution.py:34
  47.1 13.8 %collective-permute-start.16 = (bf16[14,96,384]{2,1,0:T(8,128)(2,1)S(1)}, bf16[14,96,384]{2,1,0:T(8,128)(2,1)S(1)}, u32[]{:S(2)}, u32[]{:S(2)}) collective-permute-start(bf16[14,96,384]{2,1,0:T(8,128)(2,1)S(1)} %shard_map.131.refs_4_), channel_id=1, source_target_pairs={{224,0},{33,1},{226,2},{35,3},{228,4},{37,5},{230,6},{39,7},{232,8... | collective-permute-start | bytes 3096584 | tf_op jit(solution)/shard_map/ppermute | solution.py:34
  47.7 13.8 %collective-permute-start.15 = (bf16[14,96,384]{2,1,0:T(8,128)(2,1)S(1)}, bf16[14,96,384]{2,1,0:T(8,128)(2,1)S(1)}, u32[]{:S(2)}, u32[]{:S(2)}) collective-permute-start(bf16[14,96,384]{2,1,0:T(8,128)(2,1)S(1)} %shard_map.131.refs_4_), channel_id=1, source_target_pairs={{24,0},{7,1},{26,2},{1,3},{28,4},{3,5},{30,6},{5,7},{0,8},{15,9},{... | collective-permute-start | bytes 3096584 | tf_op jit(solution)/shard_map/ppermute | solution.py:34
  47.7 13.8 %collective-permute-start.14 = (bf16[14,96,384]{2,1,0:T(8,128)(2,1)S(1)}, bf16[14,96,384]{2,1,0:T(8,128)(2,1)S(1)}, u32[]{:S(2)}, u32[]{:S(2)}) collective-permute-start(bf16[14,96,384]{2,1,0:T(8,128)(2,1)S(1)} %shard_map.131.refs_4_), channel_id=1, source_target_pairs={{8,0},{3,1},{10,2},{5,3},{12,4},{7,5},{14,6},{1,7},{16,8},{11,9},{... | collective-permute-start | bytes 3096584 | tf_op jit(solution)/shard_map/ppermute | solution.py:34
  61.5 5.7 %collective-permute-start.17 = (bf16[14,96,384]{2,1,0:T(8,128)(2,1)S(1)}, bf16[14,96,384]{2,1,0:T(8,128)(2,1)S(1)}, u32[]{:S(2)}, u32[]{:S(2)}) collective-permute-start(bf16[14,96,384]{2,1,0:T(8,128)(2,1)S(1)} %collective-permute-done.14.refs_5_), channel_id=1, source_target_pairs={{1,0},{0,1},{3,2},{2,3},{5,4},{4,5},{7,6},{6,7},{9,8},{8,9},{11,10... | collective-permute-start | bytes 3096584 | tf_op jit(solution)/shard_map/ppermute | solution.py:34
  63.9 3.7 %collective-permute-start.18 = (bf16[14,96,384]{2,1,0:T(8,128)(2,1)S(1)}, bf16[14,96,384]{2,1,0:T(8,128)(2,1)S(1)}, u32[]{:S(2)}, u32[]{:S(2)}) collective-permute-start(bf16[14,96,384]{2,1,0:T(8,128)(2,1)S(1)} %collective-permute-done.15.refs_6_), channel_id=1, source_target_pairs={{1,0},{0,1},{3,2},{2,3},{5,4},{4,5},{7,6},{6,7},{9,8},{8,9},{11,10... | collective-permute-start | bytes 3096584 | tf_op jit(solution)/shard_map/ppermute | solution.py:34
  63.9 5.2 %collective-permute-start.19 = (bf16[14,96,384]{2,1,0:T(8,128)(2,1)S(1)}, bf16[14,96,384]{2,1,0:T(8,128)(2,1)S(1)}, u32[]{:S(2)}, u32[]{:S(2)}) collective-permute-start(bf16[14,96,384]{2,1,0:T(8,128)(2,1)S(1)} %collective-permute-done.16.refs_7_), channel_id=1, source_target_pairs={{1,0},{0,1},{3,2},{2,3},{5,4},{4,5},{7,6},{6,7},{9,8},{8,9},{11,10... | collective-permute-start | bytes 3096584 | tf_op jit(solution)/shard_map/ppermute | solution.py:34
  64.4 17.0 %collective-permute-start.13 = (bf16[14,96,384]{2,1,0:T(8,128)(2,1)S(1)}, bf16[14,96,384]{2,1,0:T(8,128)(2,1)S(1)}, u32[]{:S(2)}, u32[]{:S(2)}) collective-permute-start(bf16[14,96,384]{2,1,0:T(8,128)(2,1)S(1)} %shard_map.130.refs_4_), channel_id=1, source_target_pairs={{224,0},{33,1},{226,2},{35,3},{228,4},{37,5},{230,6},{39,7},{232,8... | collective-permute-start | bytes 3096584 | tf_op jit(solution)/shard_map/ppermute | solution.py:34
  65.0 16.4 %collective-permute-start.12 = (bf16[14,96,384]{2,1,0:T(8,128)(2,1)S(1)}, bf16[14,96,384]{2,1,0:T(8,128)(2,1)S(1)}, u32[]{:S(2)}, u32[]{:S(2)}) collective-permute-start(bf16[14,96,384]{2,1,0:T(8,128)(2,1)S(1)} %shard_map.130.refs_4_), channel_id=1, source_target_pairs={{24,0},{7,1},{26,2},{1,3},{28,4},{3,5},{30,6},{5,7},{0,8},{15,9},{... | collective-permute-start | bytes 3096584 | tf_op jit(solution)/shard_map/ppermute | solution.py:34
  67.2 14.2 %collective-permute-start.11 = (bf16[14,96,384]{2,1,0:T(8,128)(2,1)S(1)}, bf16[14,96,384]{2,1,0:T(8,128)(2,1)S(1)}, u32[]{:S(2)}, u32[]{:S(2)}) collective-permute-start(bf16[14,96,384]{2,1,0:T(8,128)(2,1)S(1)} %shard_map.130.refs_4_), channel_id=1, source_target_pairs={{8,0},{3,1},{10,2},{5,3},{12,4},{7,5},{14,6},{1,7},{16,8},{11,9},{... | collective-permute-start | bytes 3096584 | tf_op jit(solution)/shard_map/ppermute | solution.py:34
  81.4 18.6 %collective-permute-start.23 = (bf16[14,96,384]{2,1,0:T(8,128)(2,1)S(1)}, bf16[14,96,384]{2,1,0:T(8,128)(2,1)S(1)}, u32[]{:S(2)}, u32[]{:S(2)}) collective-permute-start(bf16[14,96,384]{2,1,0:T(8,128)(2,1)S(1)} %collective-permute-done.11.refs_5_), channel_id=1, source_target_pairs={{1,0},{0,1},{3,2},{2,3},{5,4},{4,5},{7,6},{6,7},{9,8},{8,9},{11,10... | collective-permute-start | bytes 3096584 | tf_op jit(solution)/shard_map/ppermute | solution.py:34
  82.6 17.4 %collective-permute-start.24 = (bf16[14,96,384]{2,1,0:T(8,128)(2,1)S(1)}, bf16[14,96,384]{2,1,0:T(8,128)(2,1)S(1)}, u32[]{:S(2)}, u32[]{:S(2)}) collective-permute-start(bf16[14,96,384]{2,1,0:T(8,128)(2,1)S(1)} %collective-permute-done.12.refs_6_), channel_id=1, source_target_pairs={{1,0},{0,1},{3,2},{2,3},{5,4},{4,5},{7,6},{6,7},{9,8},{8,9},{11,10... | collective-permute-start | bytes 3096584 | tf_op jit(solution)/shard_map/ppermute | solution.py:34
  82.7 17.3 %collective-permute-start.20 = (bf16[2,4,32,384]{3,2,1,0:T(8,128)(2,1)S(1)}, bf16[2,4,32,384]{3,2,1,0:T(8,128)(2,1)S(1)}, u32[]{:S(2)}, u32[]{:S(2)}) collective-permute-start(bf16[2,4,32,384]{3,2,1,0:T(8,128)(2,1)S(1)} %constant_dynamic-slice_fusion.1), channel_id=1, source_target_pairs={{0,8},{1,9},{2,10},{3,11},{4,12},{5,13},{6,14},{7,15},{8,16},{9,17... | collective-permute-start | bytes 589832 | tf_op jit(solution)/shard_map/ppermute | solution.py:34
  85.8 14.3 %collective-permute-start.22 = (bf16[6,1,32,384]{3,2,1,0:T(8,128)(2,1)S(1)}, bf16[6,1,32,384]{3,2,1,0:T(8,128)(2,1)S(1)}, u32[]{:S(2)}, u32[]{:S(2)}) collective-permute-start(bf16[6,1,32,384]{3,2,1,0:T(8,128)(2,1)S(1)} %get-tuple-element.72), channel_id=1, source_target_pairs={{2,1},{1,2},{4,3},{3,4},{6,5},{5,6},{10,9},{9,10},{12,11},{11,12},... | collective-permute-start | bytes 442376 | tf_op jit(solution)/shard_map/ppermute | solution.py:34
  90.4 9.6 %collective-permute-start.21 = (bf16[2,1,32,384]{3,2,1,0:T(8,128)(2,1)S(1)}, bf16[2,1,32,384]{3,2,1,0:T(8,128)(2,1)S(1)}, u32[]{:S(2)}, u32[]{:S(2)}) collective-permute-start(bf16[2,1,32,384]{3,2,1,0:T(8,128)(2,1)S(1)} %constant_dynamic-slice_fusion), channel_id=1, source_target_pairs={{2,9},{1,10},{4,11},{3,12},{6,13},{5,14},{10,17},{9,18},{12,19},{1... | collective-permute-start | bytes 147464 | tf_op jit(solution)/shard_map/ppermute | solution.py:34
  100.1 1.5 %collective-permute-start.25 = (bf16[8,1,32,384]{3,2,1,0:T(8,128)(2,1)S(1)}, bf16[8,1,32,384]{3,2,1,0:T(8,128)(2,1)S(1)}, u32[]{:S(2)}, u32[]{:S(2)}) collective-permute-start(bf16[8,1,32,384]{3,2,1,0:T(8,128)(2,1)S(1)} %pad_maximum_fusion.3), channel_id=1, source_target_pairs={{1,0},{0,1},{3,2},{2,3},{5,4},{4,5},{7,6},{6,7},{9,8},{8,9},{11,10... | collective-permute-start | bytes 589832 | tf_op jit(solution)/shard_map/ppermute | solution.py:34
  101.7 2.6 %collective-permute-start.26 = (bf16[14,96,384]{2,1,0:T(8,128)(2,1)S(1)}, bf16[14,96,384]{2,1,0:T(8,128)(2,1)S(1)}, u32[]{:S(2)}, u32[]{:S(2)}) collective-permute-start(bf16[14,96,384]{2,1,0:T(8,128)(2,1)S(1)} %collective-permute-done.13.refs_7_), channel_id=1, source_target_pairs={{1,0},{0,1},{3,2},{2,3},{5,4},{4,5},{7,6},{6,7},{9,8},{8,9},{11,10... | collective-permute-start | bytes 3096584 | tf_op jit(solution)/shard_map/ppermute | solution.py:34
  (4 other events, 34.9 us)

commit v10 on v9

--- a/solution.py
+++ b/solution.py
@@ -159,10 +159,10 @@
     )(picks, acts.reshape(-1, C))
 
 
-def spread_halo_body(scalars, picks, ends, corners, beside, across, _, out):
+def spread_halo_body(scalars, picks, ends, beside, across, _, out):
     core = scalars[0]
     cells = jnp.concatenate(
-        [part[...].reshape(-1, C) for part in (ends, beside, corners, across)], 0
+        [part[...].reshape(-1, C) for part in (ends, beside, across)], 0
     )
     for half in range(2):
         for tap, part in enumerate(spread_cells(cells, picks[half])):
@@ -181,17 +181,17 @@
                 out[half, :, 5:6, :, lanes] = far
 
 
-def spread_halo(scalars, picks, ends, corners, beside, across, spread):
+def spread_halo(scalars, picks, ends, beside, across, spread):
     vmem = pl.BlockSpec(memory_space=pltpu.VMEM)
     return pl.pallas_call(
         spread_halo_body,
         out_shape=jax.ShapeDtypeStruct(spread.shape, spread.dtype),
-        in_specs=[pl.BlockSpec(memory_space=pltpu.SMEM)] + [vmem] * 6,
+        in_specs=[pl.BlockSpec(memory_space=pltpu.SMEM)] + [vmem] * 5,
         out_specs=vmem,
-        input_output_aliases={6: 0},
+        input_output_aliases={5: 0},
         compiler_params=pltpu.CompilerParams(vmem_limit_bytes=20 * 1024 * 1024),
         cost_estimate=pl.CostEstimate(flops=1000, bytes_accessed=1000, transcendentals=0),
-    )(scalars, picks, ends, corners, beside, across, spread)
+    )(scalars, picks, ends, beside, across, spread)
 
 
 def conv_body(
@@ -351,10 +351,7 @@
     acts_one = norm_act(frames, gain_one)
     own = jnp.stack([own_half(kernel_one), own_half(kernel_two)])
     pieces = z_stage(own)
-    inner, outer = sides(acts_one)
-    beside, across = fetch(inner, sibling), fetch(outer, across_chips)
-    ends = jnp.concatenate([last_two(acts_one), last_two(beside)], 1)
-    ends, corners = fetch(ends, before_in_group), fetch(last_two(outer), across_and_before)
+    ends = fetch(last_two(acts_one), before_in_group)
     picks = make_picks(orders)
     pieces, picks, lag_weights, scalars = lax.optimization_barrier(
         (pieces, picks, lag_weights, scalars)
@@ -362,23 +359,23 @@
 
     opposite = fetch(pieces, small_source(2))
     after = fetch(pieces, small_source(1))
-    gated, ends, corners, across = lax.optimization_barrier((pieces, ends, corners, across))
+    gated, ends = lax.optimization_barrier((pieces, ends))
     parts = [pieces, after, fetch(gated, small_source(-1)), opposite]
-    beside = jnp.concatenate([ends[:, 4:5], beside], 0)
-    spread = spread_halo(
-        scalars, picks, ends[:, 0:4], corners, beside, across, spread_inner(picks, acts_one)
-    )
-    parts, spread = lax.optimization_barrier((parts, spread))
+    inner, outer = sides(jnp.concatenate([ends, acts_one], 0))
+    across = fetch(outer, across_chips)
+    parts, across = lax.optimization_barrier((parts, across))
 
     one_bundle, two_bundle = join_rows(parts, 0), join_rows(parts, 1)
     one_bundles = bulk_stage(one_bundle)
     one_own, two_own = lax.optimization_barrier((one_bundle, two_bundle))
     one_others, two_others = [fetch(one_own, sibling)], [fetch(two_own, sibling)]
-    two_bundle, one_others, two_others = lax.optimization_barrier(
-        (two_bundle, one_others, two_others)
-    )
-    one_bundles, one_others, two_others = lax.optimization_barrier(
-        (one_bundles, one_others, two_others)
+    two_bundle, one_others, two_others, inner = lax.optimization_barrier(
+        (two_bundle, one_others, two_others, inner)
+    )
+    beside = fetch(inner, sibling)
+    spread = spread_halo(scalars, picks, ends, beside, across, spread_inner(picks, acts_one))
+    one_bundles, one_others, two_others, spread = lax.optimization_barrier(
+        (one_bundles, one_others, two_others, spread)
     )
     one_others += [fetch(b, sibling) for b in one_bundles[1:]]
 
@@ -401,7 +398,8 @@
     beside = fetch(jnp.concatenate([sides(ends)[0], inner], 0), sibling)
     two_last, beside = lax.optimization_barrier((two_bundles[3], beside))
     two_others.append(fetch(two_last, sibling))
-    spread = spread_halo(scalars, picks, ends, corners, beside, across, spread)
+    across = jnp.concatenate([corners, across], 0)
+    spread = spread_halo(scalars, picks, ends, beside, across, spread)
     result = conv(
         scalars, lag_weights, spread, frames.reshape(slots, 128, C), two_bundles, two_others,
         finish_add,

time: 118 us -> 116 us (0.983)
  starting transfers between devices: 41 us -> 36.5 us
  waiting for transfers between devices: 35 us -> 38 us
    ppermute x27 -> x26, starting transfers between devices: 41 us -> 36.5 us  [fetch(): return lax.ppermute(array, AXES, pairs)]
    ppermute x27 -> x26, waiting for transfers between devices: 35 us -> 38 us  [fetch(): return lax.ppermute(array, AXES, pairs)]
  transfers between devices with their start and end apart: 27 -> 26, of which waited for: 12 -> 13; matrix products, arithmetic and copies ran while one was open for 4% -> 4% of each run, Pallas kernels for 17% -> 18%
where the time goes in v10:
time: 116 us
  waiting for transfers between devices  38 us (33%)
  starting transfers between devices  36.5 us (31%)
  Pallas kernels  33.5 us (29%)
  local copies, waits for them, and re-layouts  3.34 us (3%)
  other arithmetic  2.34 us (2%)
  between operations  1.96 us (2%)
    ppermute x26, waiting for transfers between devices, fetch(): return lax.ppermute(array, AXES, pairs)  38 us
    ppermute x26, starting transfers between devices, fetch(): return lax.ppermute(array, AXES, pairs)  36.5 us
    pallas_call x2, Pallas kernels, conv(): pl.pallas_call(lambda *refs: conv_body(*refs, finish=finish), out_shape=j...  24.9 us
    pallas_call x2, Pallas kernels, spread_halo(): pl.pallas_call(spread_halo_body, out_shape=jax.ShapeDtypeStruct(spread.sh...  4.41 us
  transfers between devices with their start and end apart: 26, of which 13 were waited for; matrix products, arithmetic and copies ran while one was open for 4% of the time, Pallas kernels for 18%

profile of v10, /device:TPU:131, one launch (start us, length us, event | category | flops | bytes accessed | tf_op | source)
XLA Modules:
  0.0 115.7 jit_solution(13881194558798890337)
XLA Ops:
  0.0 1.1 constant_dynamic-slice_fusion.3
  1.3 2.1 %collective-permute-start = (bf16[2,168,384]{2,1,0:T(8,128)(2,1)S(1)}, bf16[2,168,384]{2,1,0:T(8,128)(2,1)S(1)}, u32[]{:S(2)}, u32[]{:S(2)}) collective-permute-start(bf16[2,168,384]{2,1,0:T(8,128)(2,1)S(1)} %constant_dynamic-update-slice_fusion), channel_id=1, source_target_pairs={{24,0},{1,1},{90,2},{67,3},{60,4},{37,5},{126,6},{103,7},{0,8},{9,... | collective-permute-start | bytes 774152 | tf_op jit(solution)/shard_map/ppermute | solution.py:34
  3.4 2.4 %collective-permute-start.1 = (bf16[2,168,384]{2,1,0:T(8,128)(2,1)S(1)}, bf16[2,168,384]{2,1,0:T(8,128)(2,1)S(1)}, u32[]{:S(2)}, u32[]{:S(2)}) collective-permute-start(bf16[2,168,384]{2,1,0:T(8,128)(2,1)S(1)} %constant_dynamic-update-slice_fusion), channel_id=1, source_target_pairs={{152,0},{129,1},{218,2},{195,3},{188,4},{165,5},{254,6},{231,7},{1... | collective-permute-start | bytes 774152 | tf_op jit(solution)/shard_map/ppermute | solution.py:34
  7.1 3.2 %collective-permute-start.3 = (bf16[2,4,32,384]{3,2,1,0:T(8,128)(2,1)S(1)}, bf16[2,4,32,384]{3,2,1,0:T(8,128)(2,1)S(1)}, u32[]{:S(2)}, u32[]{:S(2)}) collective-permute-start(bf16[2,4,32,384]{3,2,1,0:T(8,128)(2,1)S(1)} %constant_dynamic-slice_fusion.2), channel_id=1, source_target_pairs={{0,8},{1,9},{2,10},{3,11},{4,12},{5,13},{6,14},{7,15},{8,16},{9,17... | collective-permute-start | bytes 589832 | tf_op jit(solution)/shard_map/ppermute | solution.py:34
  13.8 0.6 pad_add_fusion.order
  14.5 1.6 %shard_map.127.picks = bf16[2,384,384]{2,1,0:T(8,128)(2,1)} custom-call(s32[2,384]{1,0:T(2,128)} %pad_add_fusion.order), custom_call_target="tpu_custom_call" | custom-call | flops 1000 | bytes 1000 | tf_op jit(solution)/shard_map/pallas_call | solution.py:126
  16.8 2.9 %collective-permute-start.2 = (bf16[2,2,168,384]{3,2,1,0:T(8,128)(2,1)S(1)}, bf16[2,2,168,384]{3,2,1,0:T(8,128)(2,1)S(1)}, u32[]{:S(2)}, u32[]{:S(2)}) collective-permute-start(bf16[2,2,168,384]{3,2,1,0:T(8,128)(2,1)S(1)} %pad_maximum_fusion.refs_0_), channel_id=1, source_target_pairs={{2,0},{9,1},{4,2},{11,3},{6,4},{13,5},{0,6},{15,7},{10,8},{17,9},{... | collective-permute-start | bytes 1548296 | tf_op jit(solution)/shard_map/ppermute | solution.py:34
  20.1 5.7 %collective-permute-done.3.ends = bf16[2,4,32,384]{3,2,1,0:T(8,128)(2,1)S(1)} collective-permute-done((bf16[2,4,32,384]{3,2,1,0:T(8,128)(2,1)S(1)}, bf16[2,4,32,384]{3,2,1,0:T(8,128)(2,1)S(1)}, u32[]{:S(2)}, u32[]{:S(2)}) %collective-permute-start.3) | collective-permute-done | bytes 196640 | tf_op jit(solution)/shard_map/ppermute | solution.py:34
  25.8 8.1 %collective-permute-start.6 = (bf16[8,1,32,384]{3,2,1,0:T(8,128)(2,1)S(1)}, bf16[8,1,32,384]{3,2,1,0:T(8,128)(2,1)S(1)}, u32[]{:S(2)}, u32[]{:S(2)}) collective-permute-start(bf16[8,1,32,384]{3,2,1,0:T(8,128)(2,1)S(1)} %broadcast_select_fusion.1), channel_id=1, source_target_pairs={{2,1},{1,2},{4,3},{3,4},{6,5},{5,6},{10,9},{9,10},{12,11},{11,12},... | collective-permute-start | bytes 589832 | tf_op jit(solution)/shard_map/ppermute | solution.py:34
  33.9 10.3 %collective-permute-done.6.across = bf16[8,1,32,384]{3,2,1,0:T(8,128)(2,1)S(1)} collective-permute-done((bf16[8,1,32,384]{3,2,1,0:T(8,128)(2,1)S(1)}, bf16[8,1,32,384]{3,2,1,0:T(8,128)(2,1)S(1)}, u32[]{:S(2)}, u32[]{:S(2)}) %collective-permute-start.6) | collective-permute-done | bytes 196640 | tf_op jit(solution)/shard_map/ppermute | solution.py:34
  44.6 2.7 %collective-permute-start.7 = (bf16[14,96,384]{2,1,0:T(8,128)(2,1)S(1)}, bf16[14,96,384]{2,1,0:T(8,128)(2,1)S(1)}, u32[]{:S(2)}, u32[]{:S(2)}) collective-permute-start(bf16[14,96,384]{2,1,0:T(8,128)(2,1)S(1)} %shard_map.129.refs_4_), channel_id=1, source_target_pairs={{1,0},{0,1},{3,2},{2,3},{5,4},{4,5},{7,6},{6,7},{9,8},{8,9},{11,10... | collective-permute-start | bytes 3096584 | tf_op jit(solution)/shard_map/ppermute | solution.py:34
  47.4 1.5 %collective-permute-start.13 = (bf16[14,96,384]{2,1,0:T(8,128)(2,1)S(1)}, bf16[14,96,384]{2,1,0:T(8,128)(2,1)S(1)}, u32[]{:S(2)}, u32[]{:S(2)}) collective-permute-start(bf16[14,96,384]{2,1,0:T(8,128)(2,1)S(1)} %shard_map.129.refs_4_), channel_id=1, source_target_pairs={{24,0},{7,1},{26,2},{1,3},{28,4},{3,5},{30,6},{5,7},{0,8},{15,9},{... | collective-permute-start | bytes 3096584 | tf_op jit(solution)/shard_map/ppermute | solution.py:34
  48.8 0.7 collective-permute-done.7.refs_8_
  49.5 1.5 %collective-permute-done.8.refs_8_ = bf16[14,96,384]{2,1,0:T(8,128)(2,1)S(1)} collective-permute-done((bf16[14,96,384]{2,1,0:T(8,128)(2,1)S(1)}, bf16[14,96,384]{2,1,0:T(8,128)(2,1)S(1)}, u32[]{:S(2)}, u32[]{:S(2)}) %collective-permute-start.8) | collective-permute-done | bytes 1032224 | tf_op jit(solution)/shard_map/ppermute | solution.py:34
  51.4 1.1 shard_map.130._
  52.5 2.1 %shard_map.131.refs_2_ = bf16[2,8,6,32,1152]{4,3,2,1,0:T(8,128)(2,1)S(1)} custom-call(s32[2]{0:T(128)S(1)} %pad_add_fusion.1.scalars.refs_0_, bf16[2,384,384]{2,1,0:T(8,128)(2,1)S(1)} %copy-done, bf16[2,4,32,384]{3,2,1,0:T(8,128)(2,1)S(1)} %collective-permute-done.3.ends, ...), custom_call_target="tpu_custom_call", output_to_operand_aliasing={{}: (5, {})} | custom-call | flops 1000 | bytes 1000 | tf_op jit(solution)/shard_map/pallas_call | solution.py:186
  54.6 6.5 %collective-permute-done.12.refs_5_ = bf16[14,96,384]{2,1,0:T(8,128)(2,1)S(1)} collective-permute-done((bf16[14,96,384]{2,1,0:T(8,128)(2,1)S(1)}, bf16[14,96,384]{2,1,0:T(8,128)(2,1)S(1)}, u32[]{:S(2)}, u32[]{:S(2)}) %collective-permute-start.12) | collective-permute-done | bytes 1032224 | tf_op jit(solution)/shard_map/ppermute | solution.py:34
  61.1 1.5 %collective-permute-done.14.refs_7_ = bf16[14,96,384]{2,1,0:T(8,128)(2,1)S(1)} collective-permute-done((bf16[14,96,384]{2,1,0:T(8,128)(2,1)S(1)}, bf16[14,96,384]{2,1,0:T(8,128)(2,1)S(1)}, u32[]{:S(2)}, u32[]{:S(2)}) %collective-permute-start.14) | collective-permute-done | bytes 1032224 | tf_op jit(solution)/shard_map/ppermute | solution.py:34
  62.6 3.0 %collective-permute-start.16 = (bf16[14,96,384]{2,1,0:T(8,128)(2,1)S(1)}, bf16[14,96,384]{2,1,0:T(8,128)(2,1)S(1)}, u32[]{:S(2)}, u32[]{:S(2)}) collective-permute-start(bf16[14,96,384]{2,1,0:T(8,128)(2,1)S(1)} %collective-permute-done.12.refs_5_), channel_id=1, source_target_pairs={{1,0},{0,1},{3,2},{2,3},{5,4},{4,5},{7,6},{6,7},{9,8},{8,9},{11,10... | collective-permute-start | bytes 3096584 | tf_op jit(solution)/shard_map/ppermute | solution.py:34
  66.1 1.0 collective-permute-start.10
  67.2 0.7 collective-permute-done.16.refs_9_
  67.9 1.5 %collective-permute-done.17.refs_10_ = bf16[14,96,384]{2,1,0:T(8,128)(2,1)S(1)} collective-permute-done((bf16[14,96,384]{2,1,0:T(8,128)(2,1)S(1)}, bf16[14,96,384]{2,1,0:T(8,128)(2,1)S(1)}, u32[]{:S(2)}, u32[]{:S(2)}) %collective-permute-start.17) | collective-permute-done | bytes 1032224 | tf_op jit(solution)/shard_map/ppermute | solution.py:34
  69.4 1.5 %collective-permute-done.18.refs_11_ = bf16[14,96,384]{2,1,0:T(8,128)(2,1)S(1)} collective-permute-done((bf16[14,96,384]{2,1,0:T(8,128)(2,1)S(1)}, bf16[14,96,384]{2,1,0:T(8,128)(2,1)S(1)}, u32[]{:S(2)}, u32[]{:S(2)}) %collective-permute-start.18) | collective-permute-done | bytes 1032224 | tf_op jit(solution)/shard_map/ppermute | solution.py:34
  70.9 12.3 %shard_map.132 = bf16[6,128,384]{2,1,0:T(8,128)(2,1)S(1)} custom-call(s32[2]{0:T(128)S(1)} %pad_add_fusion.1.scalars.refs_0_, f32[3,6]{1,0:T(4,128)S(1)} %add_convert_fusion.refs_1_, bf16[2,8,6,32,1152]{4,3,2,1,0:T(8,128)(2,1)S(1)} %shard_map.131.refs_2_, f32[1,384]{1,0:T(1,128)S(1)} %reshape.334.refs_3_, bf16[14,96,384]{2,1,0:T(8,128)(2,1)S(1)} %shard_map.129.refs_4_, ...), custom_call_target="tpu_custom_call" | custom-call | flops 1000 | bytes 1000 | tf_op jit(solution)/shard_map/pallas_call | solution.py:286
  83.8 1.9 %collective-permute-start.19 = (bf16[2,4,32,384]{3,2,1,0:T(8,128)(2,1)S(1)}, bf16[2,4,32,384]{3,2,1,0:T(8,128)(2,1)S(1)}, u32[]{:S(2)}, u32[]{:S(2)}) collective-permute-start(bf16[2,4,32,384]{3,2,1,0:T(8,128)(2,1)S(1)} %constant_dynamic-slice_fusion.1), channel_id=1, source_target_pairs={{0,8},{1,9},{2,10},{3,11},{4,12},{5,13},{6,14},{7,15},{8,16},{9,17... | collective-permute-start | bytes 589832 | tf_op jit(solution)/shard_map/ppermute | solution.py:34
  85.8 3.2 %collective-permute-start.21 = (bf16[6,1,32,384]{3,2,1,0:T(8,128)(2,1)S(1)}, bf16[6,1,32,384]{3,2,1,0:T(8,128)(2,1)S(1)}, u32[]{:S(2)}, u32[]{:S(2)}) collective-permute-start(bf16[6,1,32,384]{3,2,1,0:T(8,128)(2,1)S(1)} %get-tuple-element.72), channel_id=1, source_target_pairs={{2,1},{1,2},{4,3},{3,4},{6,5},{5,6},{10,9},{9,10},{12,11},{11,12},... | collective-permute-start | bytes 442376 | tf_op jit(solution)/shard_map/ppermute | solution.py:34
  89.0 2.4 %collective-permute-start.20 = (bf16[2,1,32,384]{3,2,1,0:T(8,128)(2,1)S(1)}, bf16[2,1,32,384]{3,2,1,0:T(8,128)(2,1)S(1)}, u32[]{:S(2)}, u32[]{:S(2)}) collective-permute-start(bf16[2,1,32,384]{3,2,1,0:T(8,128)(2,1)S(1)} %constant_dynamic-slice_fusion), channel_id=1, source_target_pairs={{2,9},{1,10},{4,11},{3,12},{6,13},{5,14},{10,17},{9,18},{12,19},{1... | collective-permute-start | bytes 147464 | tf_op jit(solution)/shard_map/ppermute | solution.py:34
  91.4 1.1 shard_map.133._
  92.5 6.1 %collective-permute-done.20 = bf16[2,1,32,384]{3,2,1,0:T(8,128)(2,1)S(1)} collective-permute-done((bf16[2,1,32,384]{3,2,1,0:T(8,128)(2,1)S(1)}, bf16[2,1,32,384]{3,2,1,0:T(8,128)(2,1)S(1)}, u32[]{:S(2)}, u32[]{:S(2)}) %collective-permute-start.20) | collective-permute-done | bytes 49184 | tf_op jit(solution)/shard_map/ppermute | solution.py:34
  98.8 1.4 %collective-permute-done.24.beside = bf16[8,1,32,384]{3,2,1,0:T(8,128)(2,1)S(1)} collective-permute-done((bf16[8,1,32,384]{3,2,1,0:T(8,128)(2,1)S(1)}, bf16[8,1,32,384]{3,2,1,0:T(8,128)(2,1)S(1)}, u32[]{:S(2)}, u32[]{:S(2)}) %collective-permute-start.24) | collective-permute-done | bytes 196640 | tf_op jit(solution)/shard_map/ppermute | solution.py:34
  100.4 2.3 %shard_map.134.refs_2_ = bf16[2,8,6,32,1152]{4,3,2,1,0:T(8,128)(2,1)S(1)} custom-call(s32[2]{0:T(128)S(1)} %pad_add_fusion.1.scalars.refs_0_, bf16[2,384,384]{2,1,0:T(8,128)(2,1)S(1)} %copy-done, bf16[2,4,32,384]{3,2,1,0:T(8,128)(2,1)S(1)} %collective-permute-done.19.ends, ...), custom_call_target="tpu_custom_call", output_to_operand_aliasing={{}: (5, {})} | custom-call | flops 1000 | bytes 1000 | tf_op jit(solution)/shard_map/pallas_call | solution.py:186
  102.8 12.7 %shard_map.135 = bf16[6,128,384]{2,1,0:T(8,128)(2,1)} custom-call(s32[2]{0:T(128)S(1)} %pad_add_fusion.1.scalars.refs_0_, f32[3,6]{1,0:T(4,128)S(1)} %add_convert_fusion.refs_1_, bf16[2,8,6,32,1152]{4,3,2,1,0:T(8,128)(2,1)S(1)} %shard_map.134.refs_2_, bf16[6,128,384]{2,1,0:T(8,128)(2,1)S(1)} %bitcast.31, bf16[14,96,384]{2,1,0:T(8,128)(2,1)S(1)} %shard_map.128.refs_4_, ...), custom_call_target="tpu_custom_call" | custom-call | flops 1000 | bytes 1000 | tf_op jit(solution)/shard_map/pallas_call | solution.py:286
  (95 shorter events, 7.2 us)
Async XLA Ops:
  1.2 9.1 %copy-start.6 = (s32[4]{0:T(128)S(1)}, s32[4]{0:T(128)}, u32[]{:S(2)}) copy-start(s32[4]{0:T(128)} %constant.162.clone) | copy-start | bytes 52
  1.3 9.1 %copy-start.7 = (s32[4]{0:T(128)S(1)}, s32[4]{0:T(128)}, u32[]{:S(2)}) copy-start(s32[4]{0:T(128)} %constant.164.clone) | copy-start | bytes 52
  1.3 9.2 %copy-start.5 = (s32[4]{0:T(128)S(1)}, s32[4]{0:T(128)}, u32[]{:S(2)}) copy-start(s32[4]{0:T(128)} %constant.163.clone) | copy-start | bytes 52
  1.3 9.4 %copy-start.2 = (s32[4,2]{1,0:T(4,128)S(1)}, s32[4,2]{1,0:T(4,128)}, u32[]{:S(2)}) copy-start(s32[4,2]{1,0:T(4,128)} %constant.161.clone) | copy-start | bytes 100
  1.3 15.4 %collective-permute-start = (bf16[2,168,384]{2,1,0:T(8,128)(2,1)S(1)}, bf16[2,168,384]{2,1,0:T(8,128)(2,1)S(1)}, u32[]{:S(2)}, u32[]{:S(2)}) collective-permute-start(bf16[2,168,384]{2,1,0:T(8,128)(2,1)S(1)} %constant_dynamic-update-slice_fusion), channel_id=1, source_target_pairs={{24,0},{1,1},{90,2},{67,3},{60,4},{37,5},{126,6},{103,7},{0,8},{9,... | collective-permute-start | bytes 774152 | tf_op jit(solution)/shard_map/ppermute | solution.py:34
  3.4 13.3 %collective-permute-start.1 = (bf16[2,168,384]{2,1,0:T(8,128)(2,1)S(1)}, bf16[2,168,384]{2,1,0:T(8,128)(2,1)S(1)}, u32[]{:S(2)}, u32[]{:S(2)}) collective-permute-start(bf16[2,168,384]{2,1,0:T(8,128)(2,1)S(1)} %constant_dynamic-update-slice_fusion), channel_id=1, source_target_pairs={{152,0},{129,1},{218,2},{195,3},{188,4},{165,5},{254,6},{231,7},{1... | collective-permute-start | bytes 774152 | tf_op jit(solution)/shard_map/ppermute | solution.py:34
  6.4 7.2 %copy-start.8 = (s32[3]{0:T(128)S(1)}, s32[3]{0:T(128)}, u32[]{:S(2)}) copy-start(s32[3]{0:T(128)} %param.14) | copy-start | bytes 40
  7.1 18.6 %collective-permute-start.3 = (bf16[2,4,32,384]{3,2,1,0:T(8,128)(2,1)S(1)}, bf16[2,4,32,384]{3,2,1,0:T(8,128)(2,1)S(1)}, u32[]{:S(2)}, u32[]{:S(2)}) collective-permute-start(bf16[2,4,32,384]{3,2,1,0:T(8,128)(2,1)S(1)} %constant_dynamic-slice_fusion.2), channel_id=1, source_target_pairs={{0,8},{1,9},{2,10},{3,11},{4,12},{5,13},{6,14},{7,15},{8,16},{9,17... | collective-permute-start | bytes 589832 | tf_op jit(solution)/shard_map/ppermute | solution.py:34
  16.8 27.4 %collective-permute-start.2 = (bf16[2,2,168,384]{3,2,1,0:T(8,128)(2,1)S(1)}, bf16[2,2,168,384]{3,2,1,0:T(8,128)(2,1)S(1)}, u32[]{:S(2)}, u32[]{:S(2)}) collective-permute-start(bf16[2,2,168,384]{3,2,1,0:T(8,128)(2,1)S(1)} %pad_maximum_fusion.refs_0_), channel_id=1, source_target_pairs={{2,0},{9,1},{4,2},{11,3},{6,4},{13,5},{0,6},{15,7},{10,8},{17,9},{... | collective-permute-start | bytes 1548296 | tf_op jit(solution)/shard_map/ppermute | solution.py:34
  19.7 24.5 %collective-permute-start.5 = (bf16[2,2,168,384]{3,2,1,0:T(8,128)(2,1)S(1)}, bf16[2,2,168,384]{3,2,1,0:T(8,128)(2,1)S(1)}, u32[]{:S(2)}, u32[]{:S(2)}) collective-permute-start(bf16[2,2,168,384]{3,2,1,0:T(8,128)(2,1)S(1)} %pad_maximum_fusion.refs_0_), channel_id=1, source_target_pairs={{4,0},{17,1},{6,2},{19,3},{0,4},{21,5},{2,6},{23,7},{12,8},{25,9},... | collective-permute-start | bytes 1548296 | tf_op jit(solution)/shard_map/ppermute | solution.py:34
  25.7 18.4 %collective-permute-start.4 = (bf16[2,2,168,384]{3,2,1,0:T(8,128)(2,1)S(1)}, bf16[2,2,168,384]{3,2,1,0:T(8,128)(2,1)S(1)}, u32[]{:S(2)}, u32[]{:S(2)}) collective-permute-start(bf16[2,2,168,384]{3,2,1,0:T(8,128)(2,1)S(1)} %pad_maximum_fusion.refs_0_), channel_id=1, source_target_pairs={{6,0},{25,1},{0,2},{27,3},{2,4},{29,5},{4,6},{31,7},{14,8},{1,9},{... | collective-permute-start | bytes 1548296 | tf_op jit(solution)/shard_map/ppermute | solution.py:34
  25.8 18.3 %collective-permute-start.6 = (bf16[8,1,32,384]{3,2,1,0:T(8,128)(2,1)S(1)}, bf16[8,1,32,384]{3,2,1,0:T(8,128)(2,1)S(1)}, u32[]{:S(2)}, u32[]{:S(2)}) collective-permute-start(bf16[8,1,32,384]{3,2,1,0:T(8,128)(2,1)S(1)} %broadcast_select_fusion.1), channel_id=1, source_target_pairs={{2,1},{1,2},{4,3},{3,4},{6,5},{5,6},{10,9},{9,10},{12,11},{11,12},... | collective-permute-start | bytes 589832 | tf_op jit(solution)/shard_map/ppermute | solution.py:34
  44.6 4.9 %collective-permute-start.7 = (bf16[14,96,384]{2,1,0:T(8,128)(2,1)S(1)}, bf16[14,96,384]{2,1,0:T(8,128)(2,1)S(1)}, u32[]{:S(2)}, u32[]{:S(2)}) collective-permute-start(bf16[14,96,384]{2,1,0:T(8,128)(2,1)S(1)} %shard_map.129.refs_4_), channel_id=1, source_target_pairs={{1,0},{0,1},{3,2},{2,3},{5,4},{4,5},{7,6},{6,7},{9,8},{8,9},{11,10... | collective-permute-start | bytes 3096584 | tf_op jit(solution)/shard_map/ppermute | solution.py:34
  47.3 3.7 %collective-permute-start.8 = (bf16[14,96,384]{2,1,0:T(8,128)(2,1)S(1)}, bf16[14,96,384]{2,1,0:T(8,128)(2,1)S(1)}, u32[]{:S(2)}, u32[]{:S(2)}) collective-permute-start(bf16[14,96,384]{2,1,0:T(8,128)(2,1)S(1)} %shard_map.128.refs_4_), channel_id=1, source_target_pairs={{1,0},{0,1},{3,2},{2,3},{5,4},{4,5},{7,6},{6,7},{9,8},{8,9},{11,10... | collective-permute-start | bytes 3096584 | tf_op jit(solution)/shard_map/ppermute | solution.py:34
  47.4 13.8 %collective-permute-start.12 = (bf16[14,96,384]{2,1,0:T(8,128)(2,1)S(1)}, bf16[14,96,384]{2,1,0:T(8,128)(2,1)S(1)}, u32[]{:S(2)}, u32[]{:S(2)}) collective-permute-start(bf16[14,96,384]{2,1,0:T(8,128)(2,1)S(1)} %shard_map.129.refs_4_), channel_id=1, source_target_pairs={{8,0},{3,1},{10,2},{5,3},{12,4},{7,5},{14,6},{1,7},{16,8},{11,9},{... | collective-permute-start | bytes 3096584 | tf_op jit(solution)/shard_map/ppermute | solution.py:34
  47.4 13.8 %collective-permute-start.13 = (bf16[14,96,384]{2,1,0:T(8,128)(2,1)S(1)}, bf16[14,96,384]{2,1,0:T(8,128)(2,1)S(1)}, u32[]{:S(2)}, u32[]{:S(2)}) collective-permute-start(bf16[14,96,384]{2,1,0:T(8,128)(2,1)S(1)} %shard_map.129.refs_4_), channel_id=1, source_target_pairs={{24,0},{7,1},{26,2},{1,3},{28,4},{3,5},{30,6},{5,7},{0,8},{15,9},{... | collective-permute-start | bytes 3096584 | tf_op jit(solution)/shard_map/ppermute | solution.py:34
  48.8 13.8 %collective-permute-start.14 = (bf16[14,96,384]{2,1,0:T(8,128)(2,1)S(1)}, bf16[14,96,384]{2,1,0:T(8,128)(2,1)S(1)}, u32[]{:S(2)}, u32[]{:S(2)}) collective-permute-start(bf16[14,96,384]{2,1,0:T(8,128)(2,1)S(1)} %shard_map.129.refs_4_), channel_id=1, source_target_pairs={{224,0},{33,1},{226,2},{35,3},{228,4},{37,5},{230,6},{39,7},{232,8... | collective-permute-start | bytes 3096584 | tf_op jit(solution)/shard_map/ppermute | solution.py:34
  51.0 1.5 %collective-permute-start.15 = (bf16[8,1,32,384]{3,2,1,0:T(8,128)(2,1)S(1)}, bf16[8,1,32,384]{3,2,1,0:T(8,128)(2,1)S(1)}, u32[]{:S(2)}, u32[]{:S(2)}) collective-permute-start(bf16[8,1,32,384]{3,2,1,0:T(8,128)(2,1)S(1)} %get-tuple-element.61), channel_id=1, source_target_pairs={{1,0},{0,1},{3,2},{2,3},{5,4},{4,5},{7,6},{6,7},{9,8},{8,9},{11,10... | collective-permute-start | bytes 589832 | tf_op jit(solution)/shard_map/ppermute | solution.py:34
  52.5 15.4 %copy-start.4 = (f32[384]{0:T(512)S(1)}, f32[384]{0:T(512)}, u32[]{:S(2)}) copy-start(f32[384]{0:T(512)} %param.20) | copy-start | bytes 4612
  62.6 5.3 %collective-permute-start.16 = (bf16[14,96,384]{2,1,0:T(8,128)(2,1)S(1)}, bf16[14,96,384]{2,1,0:T(8,128)(2,1)S(1)}, u32[]{:S(2)}, u32[]{:S(2)}) collective-permute-start(bf16[14,96,384]{2,1,0:T(8,128)(2,1)S(1)} %collective-permute-done.12.refs_5_), channel_id=1, source_target_pairs={{1,0},{0,1},{3,2},{2,3},{5,4},{4,5},{7,6},{6,7},{9,8},{8,9},{11,10... | collective-permute-start | bytes 3096584 | tf_op jit(solution)/shard_map/ppermute | solution.py:34
  65.6 3.7 %collective-permute-start.17 = (bf16[14,96,384]{2,1,0:T(8,128)(2,1)S(1)}, bf16[14,96,384]{2,1,0:T(8,128)(2,1)S(1)}, u32[]{:S(2)}, u32[]{:S(2)}) collective-permute-start(bf16[14,96,384]{2,1,0:T(8,128)(2,1)S(1)} %collective-permute-done.13.refs_6_), channel_id=1, source_target_pairs={{1,0},{0,1},{3,2},{2,3},{5,4},{4,5},{7,6},{6,7},{9,8},{8,9},{11,10... | collective-permute-start | bytes 3096584 | tf_op jit(solution)/shard_map/ppermute | solution.py:34
  65.6 5.2 %collective-permute-start.18 = (bf16[14,96,384]{2,1,0:T(8,128)(2,1)S(1)}, bf16[14,96,384]{2,1,0:T(8,128)(2,1)S(1)}, u32[]{:S(2)}, u32[]{:S(2)}) collective-permute-start(bf16[14,96,384]{2,1,0:T(8,128)(2,1)S(1)} %collective-permute-done.14.refs_7_), channel_id=1, source_target_pairs={{1,0},{0,1},{3,2},{2,3},{5,4},{4,5},{7,6},{6,7},{9,8},{8,9},{11,10... | collective-permute-start | bytes 3096584 | tf_op jit(solution)/shard_map/ppermute | solution.py:34
  66.1 17.0 %collective-permute-start.10 = (bf16[14,96,384]{2,1,0:T(8,128)(2,1)S(1)}, bf16[14,96,384]{2,1,0:T(8,128)(2,1)S(1)}, u32[]{:S(2)}, u32[]{:S(2)}) collective-permute-start(bf16[14,96,384]{2,1,0:T(8,128)(2,1)S(1)} %shard_map.128.refs_4_), channel_id=1, source_target_pairs={{24,0},{7,1},{26,2},{1,3},{28,4},{3,5},{30,6},{5,7},{0,8},{15,9},{... | collective-permute-start | bytes 3096584 | tf_op jit(solution)/shard_map/ppermute | solution.py:34
  67.2 16.0 %collective-permute-start.11 = (bf16[14,96,384]{2,1,0:T(8,128)(2,1)S(1)}, bf16[14,96,384]{2,1,0:T(8,128)(2,1)S(1)}, u32[]{:S(2)}, u32[]{:S(2)}) collective-permute-start(bf16[14,96,384]{2,1,0:T(8,128)(2,1)S(1)} %shard_map.128.refs_4_), channel_id=1, source_target_pairs={{224,0},{33,1},{226,2},{35,3},{228,4},{37,5},{230,6},{39,7},{232,8... | collective-permute-start | bytes 3096584 | tf_op jit(solution)/shard_map/ppermute | solution.py:34
  67.9 15.2 %collective-permute-start.9 = (bf16[14,96,384]{2,1,0:T(8,128)(2,1)S(1)}, bf16[14,96,384]{2,1,0:T(8,128)(2,1)S(1)}, u32[]{:S(2)}, u32[]{:S(2)}) collective-permute-start(bf16[14,96,384]{2,1,0:T(8,128)(2,1)S(1)} %shard_map.128.refs_4_), channel_id=1, source_target_pairs={{8,0},{3,1},{10,2},{5,3},{12,4},{7,5},{14,6},{1,7},{16,8},{11,9},{... | collective-permute-start | bytes 3096584 | tf_op jit(solution)/shard_map/ppermute | solution.py:34
  83.2 15.4 %collective-permute-start.22 = (bf16[14,96,384]{2,1,0:T(8,128)(2,1)S(1)}, bf16[14,96,384]{2,1,0:T(8,128)(2,1)S(1)}, u32[]{:S(2)}, u32[]{:S(2)}) collective-permute-start(bf16[14,96,384]{2,1,0:T(8,128)(2,1)S(1)} %collective-permute-done.9.refs_5_), channel_id=1, source_target_pairs={{1,0},{0,1},{3,2},{2,3},{5,4},{4,5},{7,6},{6,7},{9,8},{8,9},{11,10... | collective-permute-start | bytes 3096584 | tf_op jit(solution)/shard_map/ppermute | solution.py:34
  83.6 15.0 %collective-permute-start.23 = (bf16[14,96,384]{2,1,0:T(8,128)(2,1)S(1)}, bf16[14,96,384]{2,1,0:T(8,128)(2,1)S(1)}, u32[]{:S(2)}, u32[]{:S(2)}) collective-permute-start(bf16[14,96,384]{2,1,0:T(8,128)(2,1)S(1)} %collective-permute-done.10.refs_6_), channel_id=1, source_target_pairs={{1,0},{0,1},{3,2},{2,3},{5,4},{4,5},{7,6},{6,7},{9,8},{8,9},{11,10... | collective-permute-start | bytes 3096584 | tf_op jit(solution)/shard_map/ppermute | solution.py:34
  83.8 14.7 %collective-permute-start.19 = (bf16[2,4,32,384]{3,2,1,0:T(8,128)(2,1)S(1)}, bf16[2,4,32,384]{3,2,1,0:T(8,128)(2,1)S(1)}, u32[]{:S(2)}, u32[]{:S(2)}) collective-permute-start(bf16[2,4,32,384]{3,2,1,0:T(8,128)(2,1)S(1)} %constant_dynamic-slice_fusion.1), channel_id=1, source_target_pairs={{0,8},{1,9},{2,10},{3,11},{4,12},{5,13},{6,14},{7,15},{8,16},{9,17... | collective-permute-start | bytes 589832 | tf_op jit(solution)/shard_map/ppermute | solution.py:34
  85.8 12.8 %collective-permute-start.21 = (bf16[6,1,32,384]{3,2,1,0:T(8,128)(2,1)S(1)}, bf16[6,1,32,384]{3,2,1,0:T(8,128)(2,1)S(1)}, u32[]{:S(2)}, u32[]{:S(2)}) collective-permute-start(bf16[6,1,32,384]{3,2,1,0:T(8,128)(2,1)S(1)} %get-tuple-element.72), channel_id=1, source_target_pairs={{2,1},{1,2},{4,3},{3,4},{6,5},{5,6},{10,9},{9,10},{12,11},{11,12},... | collective-permute-start | bytes 442376 | tf_op jit(solution)/shard_map/ppermute | solution.py:34
  89.0 9.6 %collective-permute-start.20 = (bf16[2,1,32,384]{3,2,1,0:T(8,128)(2,1)S(1)}, bf16[2,1,32,384]{3,2,1,0:T(8,128)(2,1)S(1)}, u32[]{:S(2)}, u32[]{:S(2)}) collective-permute-start(bf16[2,1,32,384]{3,2,1,0:T(8,128)(2,1)S(1)} %constant_dynamic-slice_fusion), channel_id=1, source_target_pairs={{2,9},{1,10},{4,11},{3,12},{6,13},{5,14},{10,17},{9,18},{12,19},{1... | collective-permute-start | bytes 147464 | tf_op jit(solution)/shard_map/ppermute | solution.py:34
  98.7 1.5 %collective-permute-start.24 = (bf16[8,1,32,384]{3,2,1,0:T(8,128)(2,1)S(1)}, bf16[8,1,32,384]{3,2,1,0:T(8,128)(2,1)S(1)}, u32[]{:S(2)}, u32[]{:S(2)}) collective-permute-start(bf16[8,1,32,384]{3,2,1,0:T(8,128)(2,1)S(1)} %pad_maximum_fusion.3), channel_id=1, source_target_pairs={{1,0},{0,1},{3,2},{2,3},{5,4},{4,5},{7,6},{6,7},{9,8},{8,9},{11,10... | collective-permute-start | bytes 589832 | tf_op jit(solution)/shard_map/ppermute | solution.py:34
  100.2 2.6 %collective-permute-start.25 = (bf16[14,96,384]{2,1,0:T(8,128)(2,1)S(1)}, bf16[14,96,384]{2,1,0:T(8,128)(2,1)S(1)}, u32[]{:S(2)}, u32[]{:S(2)}) collective-permute-start(bf16[14,96,384]{2,1,0:T(8,128)(2,1)S(1)} %collective-permute-done.11.refs_7_), channel_id=1, source_target_pairs={{1,0},{0,1},{3,2},{2,3},{5,4},{4,5},{7,6},{6,7},{9,8},{8,9},{11,10... | collective-permute-start | bytes 3096584 | tf_op jit(solution)/shard_map/ppermute | solution.py:34
  (3 other events, 20.1 us)

commit v11 on v10

--- a/solution.py
+++ b/solution.py
@@ -223,45 +223,46 @@
 
     total[...] = jnp.zeros_like(total)
 
-    def window(half, lag, row, first, count):
-        block = spread[half, pl.ds(lag, frames), pl.ds(row, rows), :, pl.ds(C * first, C * count)]
-        return block.reshape(frames * rows * cols, C * count)
-
-    def add(lag, part):
-        part = part.reshape(frames, rows * cols, C)
+    def window(half, lag, row, long=frames, tall=rows, first=0, count=3):
+        block = spread[half, lag : lag + long, row : row + tall, :, C * first : C * (first + count)]
+        return block.reshape(long * tall * cols, C * count)
+
+    def taps(half, tap, lanes, count=3):
+        return weights[half, tap : tap + count, :, lanes].reshape(count * C, -1)
+
+    def times(cells, block):
+        return jnp.dot(cells, block, preferred_element_type=jnp.float32)
+
+    def add(lag, part, lanes):
         for f in range(frames):
-            total[f] += part[f] * lag_weights[lag, f]
-
-    def group(half, first_tap, index):
-        lag, row = index // 3, index % 3
-        block = weights[half, pl.ds(index * 3 - first_tap, 3)].reshape(3 * C, C)
-        add(lag, jnp.dot(window(half, lag, row, 0, 3), block, preferred_element_type=jnp.float32))
+            total[f, :, lanes] += part[f].reshape(rows * cols, -1) * lag_weights[lag, f]
+
+    low, high = slice(0, 256), slice(256, C)
+
+    def two_rows(half, lags, places, first_taps):
+        for lag, row, tap in zip(lags, places, first_taps):
+            part = times(window(half, lag, row), taps(half, tap, low))
+            add(lag, part.reshape(frames, rows, cols, 256), low)
+        more_frames, more_rows = lags[1] - lags[0], places[1] - places[0]
+        cells = window(half, lags[0], places[0], frames + more_frames, rows + more_rows)
+        block = jnp.concatenate([taps(half, tap, high) for tap in first_taps], 1)
+        part = times(cells, block).reshape(frames + more_frames, rows + more_rows, cols, 256)
+        add(lags[0], part[:frames, :rows, :, :128], high)
+        add(lags[1], part[more_frames:, more_rows:, :, 128:], high)
 
     for copy in copies(0, own):
         copy.wait()
-
-    @pl.loop(0, 4)
-    def _(index):
-        group(0, 0, index)
-
-    add(
-        1,
-        jnp.dot(
-            window(0, 1, 1, 0, 2),
-            weights[0, pl.ds(12, 2)].reshape(2 * C, C),
-            preferred_element_type=jnp.float32,
-        ),
-    )
+    two_rows(0, (0, 1), (0, 0), (0, 9))
+    two_rows(0, (0, 0), (1, 2), (3, 6))
+    everything = slice(0, C)
+    part = times(window(0, 1, 1, count=2), taps(0, 12, everything, 2))
+    add(1, part.reshape(frames, rows, cols, C), everything)
     for copy in copies(1, own):
         copy.wait()
-    add(
-        1,
-        jnp.dot(window(1, 1, 1, 2, 1), weights[1, 1], preferred_element_type=jnp.float32),
-    )
-
-    @pl.loop(5, 9)
-    def _(index):
-        group(1, 13, index)
+    part = times(window(1, 1, 1, first=2, count=1), taps(1, 1, everything, 1))
+    add(1, part.reshape(frames, rows, cols, C), everything)
+    two_rows(1, (1, 2), (2, 2), (2, 11))
+    two_rows(1, (2, 2), (0, 1), (5, 8))
 
     finish(scalars, total, tail, out)
 
@@ -351,19 +352,21 @@
     acts_one = norm_act(frames, gain_one)
     own = jnp.stack([own_half(kernel_one), own_half(kernel_two)])
     pieces = z_stage(own)
-    ends = fetch(last_two(acts_one), before_in_group)
+    inner, outer = sides(acts_one)
+    ends, across = fetch(last_two(acts_one), before_in_group), fetch(outer, across_chips)
     picks = make_picks(orders)
-    pieces, picks, lag_weights, scalars = lax.optimization_barrier(
-        (pieces, picks, lag_weights, scalars)
+    pieces, across, lag_weights, scalars = lax.optimization_barrier(
+        (pieces, across, lag_weights, scalars)
     )
 
     opposite = fetch(pieces, small_source(2))
     after = fetch(pieces, small_source(1))
     gated, ends = lax.optimization_barrier((pieces, ends))
     parts = [pieces, after, fetch(gated, small_source(-1)), opposite]
-    inner, outer = sides(jnp.concatenate([ends, acts_one], 0))
-    across = fetch(outer, across_chips)
-    parts, across = lax.optimization_barrier((parts, across))
+    inner, outer = jnp.concatenate([sides(ends)[0], inner], 0), sides(ends)[1]
+    corners = fetch(outer, across_chips)
+    parts, corners = lax.optimization_barrier((parts, corners))
+    across = jnp.concatenate([corners, across], 0)
 
     one_bundle, two_bundle = join_rows(parts, 0), join_rows(parts, 1)
     one_bundles = bulk_stage(one_bundle)

time: 116 us -> 116 us (level); the launches traced: 116 us -> 114 us
  waiting for transfers between devices: 38 us -> 27.7 us
  local copies, waits for them, and re-layouts: 3.34 us -> 9.07 us
  other arithmetic: 2.34 us -> 6.31 us
  Pallas kernels: 33.5 us -> 30.4 us
  starting transfers between devices: 36.5 us -> 39 us
    ppermute x26 -> x27, waiting for transfers between devices: 38 us -> 27.7 us  [fetch(): return lax.ppermute(array, AXES, pairs)]
    unnamed x19 -> x35, local copies, waits for them, and re-layouts: 0.07 us -> 4.78 us
    pallas_call x2, Pallas kernels: 24.9 us -> 21.1 us  [conv(): pl.pallas_call(lambda *refs: conv_body(*refs, finish=finish), out_shape=j...]
    ppermute x26 -> x27, starting transfers between devices: 36.5 us -> 39 us  [fetch(): return lax.ppermute(array, AXES, pairs)]
    mul x2, other arithmetic: 0.09 us -> 1.41 us  [channel_orders(): half.reshape(-1, 1) * SHARD + ramp]
  transfers between devices with their start and end apart: 26 -> 27, of which waited for: 13 -> 11; matrix products, arithmetic and copies ran while one was open for 4% -> 8% of each run, Pallas kernels for 18% -> 16%
where the time goes in v11:
time: 116 us; the launch traced here: 114 us
  starting transfers between devices  39 us (34%)
  Pallas kernels  30.4 us (26%)
  waiting for transfers between devices  27.7 us (24%)
  local copies, waits for them, and re-layouts  9.07 us (8%)
  other arithmetic  6.31 us (5%)
  between operations  1.96 us (2%)
    ppermute x27, starting transfers between devices, fetch(): return lax.ppermute(array, AXES, pairs)  39 us
    ppermute x27, waiting for transfers between devices, fetch(): return lax.ppermute(array, AXES, pairs)  27.7 us
    pallas_call x2, Pallas kernels, conv(): pl.pallas_call(lambda *refs: conv_body(*refs, finish=finish), out_shape=j...  21.1 us
    unnamed x35, local copies, waits for them, and re-layouts  4.78 us
    pallas_call x2, Pallas kernels, spread_halo(): pl.pallas_call(spread_halo_body, out_shape=jax.ShapeDtypeStruct(spread.sh...  4.18 us
  transfers between devices with their start and end apart: 27, of which 11 were waited for; matrix products, arithmetic and copies ran while one was open for 8% of the time, Pallas kernels for 16%

profile of v11, /device:TPU:131, one launch (start us, length us, event | category | flops | bytes accessed | tf_op | source)
XLA Modules:
  0.0 114.4 jit_solution(11841524839960320232)
XLA Ops:
  0.0 1.1 constant_dynamic-slice_fusion.3
  1.2 1.9 %collective-permute-start = (bf16[2,168,384]{2,1,0:T(8,128)(2,1)S(1)}, bf16[2,168,384]{2,1,0:T(8,128)(2,1)S(1)}, u32[]{:S(2)}, u32[]{:S(2)}) collective-permute-start(bf16[2,168,384]{2,1,0:T(8,128)(2,1)S(1)} %constant_dynamic-update-slice_fusion), channel_id=1, source_target_pairs={{24,0},{1,1},{90,2},{67,3},{60,4},{37,5},{126,6},{103,7},{0,8},{9,... | collective-permute-start | bytes 774152 | tf_op jit(solution)/shard_map/ppermute | solution.py:34
  3.2 2.4 %collective-permute-start.1 = (bf16[2,168,384]{2,1,0:T(8,128)(2,1)S(1)}, bf16[2,168,384]{2,1,0:T(8,128)(2,1)S(1)}, u32[]{:S(2)}, u32[]{:S(2)}) collective-permute-start(bf16[2,168,384]{2,1,0:T(8,128)(2,1)S(1)} %constant_dynamic-update-slice_fusion), channel_id=1, source_target_pairs={{152,0},{129,1},{218,2},{195,3},{188,4},{165,5},{254,6},{231,7},{1... | collective-permute-start | bytes 774152 | tf_op jit(solution)/shard_map/ppermute | solution.py:34
  7.0 4.8 %collective-permute-start.2 = (bf16[6,1,32,384]{3,2,1,0:T(8,128)(2,1)S(1)}, bf16[6,1,32,384]{3,2,1,0:T(8,128)(2,1)S(1)}, u32[]{:S(2)}, u32[]{:S(2)}) collective-permute-start(bf16[6,1,32,384]{3,2,1,0:T(8,128)(2,1)S(1)} %get-tuple-element.94), channel_id=1, source_target_pairs={{2,1},{1,2},{4,3},{3,4},{6,5},{5,6},{10,9},{9,10},{12,11},{11,12},... | collective-permute-start | bytes 442376 | tf_op jit(solution)/shard_map/ppermute | solution.py:34
  12.5 1.9 %collective-permute-start.4 = (bf16[2,4,32,384]{3,2,1,0:T(8,128)(2,1)S(1)}, bf16[2,4,32,384]{3,2,1,0:T(8,128)(2,1)S(1)}, u32[]{:S(2)}, u32[]{:S(2)}) collective-permute-start(bf16[2,4,32,384]{3,2,1,0:T(8,128)(2,1)S(1)} %constant_dynamic-slice_fusion.2), channel_id=1, source_target_pairs={{0,8},{1,9},{2,10},{3,11},{4,12},{5,13},{6,14},{7,15},{8,16},{9,17... | collective-permute-start | bytes 589832 | tf_op jit(solution)/shard_map/ppermute | solution.py:34
  17.5 2.0 %collective-permute-start.3 = (bf16[2,2,168,384]{3,2,1,0:T(8,128)(2,1)S(1)}, bf16[2,2,168,384]{3,2,1,0:T(8,128)(2,1)S(1)}, u32[]{:S(2)}, u32[]{:S(2)}) collective-permute-start(bf16[2,2,168,384]{3,2,1,0:T(8,128)(2,1)S(1)} %pad_maximum_fusion.refs_0_), channel_id=1, source_target_pairs={{2,0},{9,1},{4,2},{11,3},{6,4},{13,5},{0,6},{15,7},{10,8},{17,9},{... | collective-permute-start | bytes 1548296 | tf_op jit(solution)/shard_map/ppermute | solution.py:34
  19.8 7.0 %collective-permute-done.4.ends = bf16[2,4,32,384]{3,2,1,0:T(8,128)(2,1)S(1)} collective-permute-done((bf16[2,4,32,384]{3,2,1,0:T(8,128)(2,1)S(1)}, bf16[2,4,32,384]{3,2,1,0:T(8,128)(2,1)S(1)}, u32[]{:S(2)}, u32[]{:S(2)}) %collective-permute-start.4) | collective-permute-done | bytes 196640 | tf_op jit(solution)/shard_map/ppermute | solution.py:34
  28.3 6.6 %collective-permute-start.7 = (bf16[2,1,32,384]{3,2,1,0:T(8,128)(2,1)S(1)}, bf16[2,1,32,384]{3,2,1,0:T(8,128)(2,1)S(1)}, u32[]{:S(2)}, u32[]{:S(2)}) collective-permute-start(bf16[2,1,32,384]{3,2,1,0:T(8,128)(2,1)S(1)} %get-tuple-element.96), channel_id=1, source_target_pairs={{2,1},{1,2},{4,3},{3,4},{6,5},{5,6},{10,9},{9,10},{12,11},{11,12},... | collective-permute-start | bytes 147464 | tf_op jit(solution)/shard_map/ppermute | solution.py:34
  35.6 4.6 %collective-permute-done.7 = bf16[2,1,32,384]{3,2,1,0:T(8,128)(2,1)S(1)} collective-permute-done((bf16[2,1,32,384]{3,2,1,0:T(8,128)(2,1)S(1)}, bf16[2,1,32,384]{3,2,1,0:T(8,128)(2,1)S(1)}, u32[]{:S(2)}, u32[]{:S(2)}) %collective-permute-start.7) | collective-permute-done | bytes 49184 | tf_op jit(solution)/shard_map/ppermute | solution.py:34
  40.2 1.2 %shard_map.129.refs_4_ = bf16[14,96,384]{2,1,0:T(8,128)(2,1)} custom-call(bf16[2,2,168,384]{3,2,1,0:T(8,128)(2,1)S(1)} %pad_maximum_fusion.refs_0_, bf16[2,2,168,384]{3,2,1,0:T(8,128)(2,1)S(1)} %collective-permute-done.3.refs_1_, bf16[2,2,168,384]{3,2,1,0:T(8,128)(2,1)S(1)} %collective-permute-done.5.refs_2_, ...), custom_call_target="tpu_custom_call" | custom-call | bytes 2000000 | tf_op jit(solution)/shard_map/pallas_call | solution.py:83
  45.2 1.2 %collective-permute-start.8 = (bf16[14,96,384]{2,1,0:T(8,128)(2,1)}, bf16[14,96,384]{2,1,0:T(8,128)(2,1)}, u32[]{:S(2)}, u32[]{:S(2)}) collective-permute-start(bf16[14,96,384]{2,1,0:T(8,128)(2,1)} %shard_map.129.refs_4_), channel_id=1, source_target_pairs={{1,0},{0,1},{3,2},{2,3},{5,4},{4,5},{7,6},{6,7},{9,8},{8,9},{11,10... | collective-permute-start | bytes 3096584 | tf_op jit(solution)/shard_map/ppermute | solution.py:34
  46.6 1.5 %collective-permute-start.14 = (bf16[14,96,384]{2,1,0:T(8,128)(2,1)}, bf16[14,96,384]{2,1,0:T(8,128)(2,1)}, u32[]{:S(2)}, u32[]{:S(2)}) collective-permute-start(bf16[14,96,384]{2,1,0:T(8,128)(2,1)} %shard_map.129.refs_4_), channel_id=1, source_target_pairs={{24,0},{7,1},{26,2},{1,3},{28,4},{3,5},{30,6},{5,7},{0,8},{15,9},{... | collective-permute-start | bytes 3096584 | tf_op jit(solution)/shard_map/ppermute | solution.py:34
  52.5 1.6 %shard_map.127.picks = bf16[2,384,384]{2,1,0:T(8,128)(2,1)} custom-call(s32[2,384]{1,0:T(2,128)} %pad_add_fusion.order), custom_call_target="tpu_custom_call" | custom-call | flops 1000 | bytes 1000 | tf_op jit(solution)/shard_map/pallas_call | solution.py:126
  54.1 1.1 copy-done
  55.2 1.1 shard_map.130._
  56.3 2.1 %shard_map.131.refs_2_ = bf16[2,8,6,32,1152]{4,3,2,1,0:T(8,128)(2,1)S(1)} custom-call(s32[2]{0:T(128)S(1)} %pad_add_fusion.1.scalars.refs_0_, bf16[2,384,384]{2,1,0:T(8,128)(2,1)S(1)} %copy-done, bf16[2,4,32,384]{3,2,1,0:T(8,128)(2,1)S(1)} %collective-permute-done.4.ends, ...), custom_call_target="tpu_custom_call", output_to_operand_aliasing={{}: (5, {})} | custom-call | flops 1000 | bytes 1000 | tf_op jit(solution)/shard_map/pallas_call | solution.py:186
  58.4 2.3 %collective-permute-done.13.refs_5_ = bf16[14,96,384]{2,1,0:T(8,128)(2,1)} collective-permute-done((bf16[14,96,384]{2,1,0:T(8,128)(2,1)}, bf16[14,96,384]{2,1,0:T(8,128)(2,1)}, u32[]{:S(2)}, u32[]{:S(2)}) %collective-permute-start.13) | collective-permute-done | bytes 1032224 | tf_op jit(solution)/shard_map/ppermute | solution.py:34
  60.8 1.4 %collective-permute-done.15.refs_7_ = bf16[14,96,384]{2,1,0:T(8,128)(2,1)} collective-permute-done((bf16[14,96,384]{2,1,0:T(8,128)(2,1)}, bf16[14,96,384]{2,1,0:T(8,128)(2,1)}, u32[]{:S(2)}, u32[]{:S(2)}) %collective-permute-start.15) | collective-permute-done | bytes 1032224 | tf_op jit(solution)/shard_map/ppermute | solution.py:34
  62.2 3.0 %collective-permute-start.17 = (bf16[14,96,384]{2,1,0:T(8,128)(2,1)}, bf16[14,96,384]{2,1,0:T(8,128)(2,1)S(1)}, u32[]{:S(2)}, u32[]{:S(2)}) collective-permute-start(bf16[14,96,384]{2,1,0:T(8,128)(2,1)} %collective-permute-done.13.refs_5_), channel_id=1, source_target_pairs={{1,0},{0,1},{3,2},{2,3},{5,4},{4,5},{7,6},{6,7},{9,8},{8,9},{11,10... | collective-permute-start | bytes 3096584 | tf_op jit(solution)/shard_map/ppermute | solution.py:34
  65.7 1.5 %collective-permute-start.11 = (bf16[14,96,384]{2,1,0:T(8,128)(2,1)S(1)}, bf16[14,96,384]{2,1,0:T(8,128)(2,1)S(1)}, u32[]{:S(2)}, u32[]{:S(2)}) collective-permute-start(bf16[14,96,384]{2,1,0:T(8,128)(2,1)S(1)} %shard_map.128.refs_4_), channel_id=1, source_target_pairs={{24,0},{7,1},{26,2},{1,3},{28,4},{3,5},{30,6},{5,7},{0,8},{15,9},{... | collective-permute-start | bytes 3096584 | tf_op jit(solution)/shard_map/ppermute | solution.py:34
  67.7 1.5 %collective-permute-done.18.refs_10_ = bf16[14,96,384]{2,1,0:T(8,128)(2,1)S(1)} collective-permute-done((bf16[14,96,384]{2,1,0:T(8,128)(2,1)}, bf16[14,96,384]{2,1,0:T(8,128)(2,1)S(1)}, u32[]{:S(2)}, u32[]{:S(2)}) %collective-permute-start.18) | collective-permute-done | bytes 1032224 | tf_op jit(solution)/shard_map/ppermute | solution.py:34
  69.2 1.5 %collective-permute-done.19.refs_11_ = bf16[14,96,384]{2,1,0:T(8,128)(2,1)S(1)} collective-permute-done((bf16[14,96,384]{2,1,0:T(8,128)(2,1)}, bf16[14,96,384]{2,1,0:T(8,128)(2,1)S(1)}, u32[]{:S(2)}, u32[]{:S(2)}) %collective-permute-start.19) | collective-permute-done | bytes 1032224 | tf_op jit(solution)/shard_map/ppermute | solution.py:34
  70.7 10.3 %shard_map.132 = bf16[6,128,384]{2,1,0:T(8,128)(2,1)S(1)} custom-call(s32[2]{0:T(128)S(1)} %pad_add_fusion.1.scalars.refs_0_, f32[3,6]{1,0:T(4,128)S(1)} %add_convert_fusion.refs_1_, bf16[2,8,6,32,1152]{4,3,2,1,0:T(8,128)(2,1)S(1)} %shard_map.131.refs_2_, f32[1,384]{1,0:T(1,128)S(1)} %reshape.334.refs_3_, bf16[14,96,384]{2,1,0:T(8,128)(2,1)} %shard_map.129.refs_4_, ...), custom_call_target="tpu_custom_call" | custom-call | flops 1000 | bytes 1000 | tf_op jit(solution)/shard_map/pallas_call | solution.py:287
  81.5 2.4 %collective-permute-start.23 = (bf16[14,96,384]{2,1,0:T(8,128)(2,1)S(1)}, bf16[14,96,384]{2,1,0:T(8,128)(2,1)S(1)}, u32[]{:S(2)}, u32[]{:S(2)}) collective-permute-start(bf16[14,96,384]{2,1,0:T(8,128)(2,1)S(1)} %collective-permute-done.10.refs_5_), channel_id=1, source_target_pairs={{1,0},{0,1},{3,2},{2,3},{5,4},{4,5},{7,6},{6,7},{9,8},{8,9},{11,10... | collective-permute-start | bytes 3096584 | tf_op jit(solution)/shard_map/ppermute | solution.py:34
  84.0 1.9 %collective-permute-start.20 = (bf16[2,4,32,384]{3,2,1,0:T(8,128)(2,1)S(1)}, bf16[2,4,32,384]{3,2,1,0:T(8,128)(2,1)S(1)}, u32[]{:S(2)}, u32[]{:S(2)}) collective-permute-start(bf16[2,4,32,384]{3,2,1,0:T(8,128)(2,1)S(1)} %constant_dynamic-slice_fusion.1), channel_id=1, source_target_pairs={{0,8},{1,9},{2,10},{3,11},{4,12},{5,13},{6,14},{7,15},{8,16},{9,17... | collective-permute-start | bytes 589832 | tf_op jit(solution)/shard_map/ppermute | solution.py:34
  85.9 3.4 %collective-permute-start.22 = (bf16[6,1,32,384]{3,2,1,0:T(8,128)(2,1)S(1)}, bf16[6,1,32,384]{3,2,1,0:T(8,128)(2,1)S(1)}, u32[]{:S(2)}, u32[]{:S(2)}) collective-permute-start(bf16[6,1,32,384]{3,2,1,0:T(8,128)(2,1)S(1)} %get-tuple-element.72), channel_id=1, source_target_pairs={{2,1},{1,2},{4,3},{3,4},{6,5},{5,6},{10,9},{9,10},{12,11},{11,12},... | collective-permute-start | bytes 442376 | tf_op jit(solution)/shard_map/ppermute | solution.py:34
  89.4 1.9 %collective-permute-start.21 = (bf16[2,1,32,384]{3,2,1,0:T(8,128)(2,1)S(1)}, bf16[2,1,32,384]{3,2,1,0:T(8,128)(2,1)S(1)}, u32[]{:S(2)}, u32[]{:S(2)}) collective-permute-start(bf16[2,1,32,384]{3,2,1,0:T(8,128)(2,1)S(1)} %constant_dynamic-slice_fusion), channel_id=1, source_target_pairs={{2,9},{1,10},{4,11},{3,12},{6,13},{5,14},{10,17},{9,18},{12,19},{1... | collective-permute-start | bytes 147464 | tf_op jit(solution)/shard_map/ppermute | solution.py:34
  91.3 1.1 shard_map.133._
  92.4 6.6 %collective-permute-done.21 = bf16[2,1,32,384]{3,2,1,0:T(8,128)(2,1)S(1)} collective-permute-done((bf16[2,1,32,384]{3,2,1,0:T(8,128)(2,1)S(1)}, bf16[2,1,32,384]{3,2,1,0:T(8,128)(2,1)S(1)}, u32[]{:S(2)}, u32[]{:S(2)}) %collective-permute-start.21) | collective-permute-done | bytes 49184 | tf_op jit(solution)/shard_map/ppermute | solution.py:34
  99.4 1.4 %collective-permute-done.25.beside = bf16[8,1,32,384]{3,2,1,0:T(8,128)(2,1)S(1)} collective-permute-done((bf16[8,1,32,384]{3,2,1,0:T(8,128)(2,1)S(1)}, bf16[8,1,32,384]{3,2,1,0:T(8,128)(2,1)S(1)}, u32[]{:S(2)}, u32[]{:S(2)}) %collective-permute-start.25) | collective-permute-done | bytes 196640 | tf_op jit(solution)/shard_map/ppermute | solution.py:34
  101.0 2.1 %shard_map.134.refs_2_ = bf16[2,8,6,32,1152]{4,3,2,1,0:T(8,128)(2,1)S(1)} custom-call(s32[2]{0:T(128)S(1)} %pad_add_fusion.1.scalars.refs_0_, bf16[2,384,384]{2,1,0:T(8,128)(2,1)S(1)} %copy-done.1, bf16[2,4,32,384]{3,2,1,0:T(8,128)(2,1)S(1)} %collective-permute-done.20.ends, ...), custom_call_target="tpu_custom_call", output_to_operand_aliasing={{}: (5, {})} | custom-call | flops 1000 | bytes 1000 | tf_op jit(solution)/shard_map/pallas_call | solution.py:186
  103.5 10.8 %shard_map.135 = bf16[6,128,384]{2,1,0:T(8,128)(2,1)} custom-call(s32[2]{0:T(128)S(1)} %pad_add_fusion.1.scalars.refs_0_, f32[3,6]{1,0:T(4,128)S(1)} %add_convert_fusion.refs_1_, bf16[2,8,6,32,1152]{4,3,2,1,0:T(8,128)(2,1)S(1)} %shard_map.134.refs_2_, bf16[6,128,384]{2,1,0:T(8,128)(2,1)S(1)} %bitcast.30, bf16[14,96,384]{2,1,0:T(8,128)(2,1)S(1)} %shard_map.128.refs_4_, ...), custom_call_target="tpu_custom_call" | custom-call | flops 1000 | bytes 1000 | tf_op jit(solution)/shard_map/pallas_call | solution.py:287
  (115 shorter events, 17.2 us)
Async XLA Ops:
  1.2 16.2 %collective-permute-start = (bf16[2,168,384]{2,1,0:T(8,128)(2,1)S(1)}, bf16[2,168,384]{2,1,0:T(8,128)(2,1)S(1)}, u32[]{:S(2)}, u32[]{:S(2)}) collective-permute-start(bf16[2,168,384]{2,1,0:T(8,128)(2,1)S(1)} %constant_dynamic-update-slice_fusion), channel_id=1, source_target_pairs={{24,0},{1,1},{90,2},{67,3},{60,4},{37,5},{126,6},{103,7},{0,8},{9,... | collective-permute-start | bytes 774152 | tf_op jit(solution)/shard_map/ppermute | solution.py:34
  3.2 14.3 %collective-permute-start.1 = (bf16[2,168,384]{2,1,0:T(8,128)(2,1)S(1)}, bf16[2,168,384]{2,1,0:T(8,128)(2,1)S(1)}, u32[]{:S(2)}, u32[]{:S(2)}) collective-permute-start(bf16[2,168,384]{2,1,0:T(8,128)(2,1)S(1)} %constant_dynamic-update-slice_fusion), channel_id=1, source_target_pairs={{152,0},{129,1},{218,2},{195,3},{188,4},{165,5},{254,6},{231,7},{1... | collective-permute-start | bytes 774152 | tf_op jit(solution)/shard_map/ppermute | solution.py:34
  5.8 9.6 %copy-start.14 = (s32[4]{0:T(128)S(1)}, s32[4]{0:T(128)}, u32[]{:S(2)}) copy-start(s32[4]{0:T(128)} %constant.162.clone) | copy-start | bytes 52
  5.8 10.2 %copy-start.13 = (s32[4]{0:T(128)S(1)}, s32[4]{0:T(128)}, u32[]{:S(2)}) copy-start(s32[4]{0:T(128)} %constant.163.clone) | copy-start | bytes 52
  5.8 10.9 %copy-start.7 = (s32[4,2]{1,0:T(4,128)S(1)}, s32[4,2]{1,0:T(4,128)}, u32[]{:S(2)}) copy-start(s32[4,2]{1,0:T(4,128)} %constant.161.clone) | copy-start | bytes 100
  7.0 10.5 %collective-permute-start.2 = (bf16[6,1,32,384]{3,2,1,0:T(8,128)(2,1)S(1)}, bf16[6,1,32,384]{3,2,1,0:T(8,128)(2,1)S(1)}, u32[]{:S(2)}, u32[]{:S(2)}) collective-permute-start(bf16[6,1,32,384]{3,2,1,0:T(8,128)(2,1)S(1)} %get-tuple-element.94), channel_id=1, source_target_pairs={{2,1},{1,2},{4,3},{3,4},{6,5},{5,6},{10,9},{9,10},{12,11},{11,12},... | collective-permute-start | bytes 442376 | tf_op jit(solution)/shard_map/ppermute | solution.py:34
  12.5 14.3 %collective-permute-start.4 = (bf16[2,4,32,384]{3,2,1,0:T(8,128)(2,1)S(1)}, bf16[2,4,32,384]{3,2,1,0:T(8,128)(2,1)S(1)}, u32[]{:S(2)}, u32[]{:S(2)}) collective-permute-start(bf16[2,4,32,384]{3,2,1,0:T(8,128)(2,1)S(1)} %constant_dynamic-slice_fusion.2), channel_id=1, source_target_pairs={{0,8},{1,9},{2,10},{3,11},{4,12},{5,13},{6,14},{7,15},{8,16},{9,17... | collective-permute-start | bytes 589832 | tf_op jit(solution)/shard_map/ppermute | solution.py:34
  17.5 22.7 %collective-permute-start.3 = (bf16[2,2,168,384]{3,2,1,0:T(8,128)(2,1)S(1)}, bf16[2,2,168,384]{3,2,1,0:T(8,128)(2,1)S(1)}, u32[]{:S(2)}, u32[]{:S(2)}) collective-permute-start(bf16[2,2,168,384]{3,2,1,0:T(8,128)(2,1)S(1)} %pad_maximum_fusion.refs_0_), channel_id=1, source_target_pairs={{2,0},{9,1},{4,2},{11,3},{6,4},{13,5},{0,6},{15,7},{10,8},{17,9},{... | collective-permute-start | bytes 1548296 | tf_op jit(solution)/shard_map/ppermute | solution.py:34
  19.5 20.7 %collective-permute-start.6 = (bf16[2,2,168,384]{3,2,1,0:T(8,128)(2,1)S(1)}, bf16[2,2,168,384]{3,2,1,0:T(8,128)(2,1)S(1)}, u32[]{:S(2)}, u32[]{:S(2)}) collective-permute-start(bf16[2,2,168,384]{3,2,1,0:T(8,128)(2,1)S(1)} %pad_maximum_fusion.refs_0_), channel_id=1, source_target_pairs={{4,0},{17,1},{6,2},{19,3},{0,4},{21,5},{2,6},{23,7},{12,8},{25,9},... | collective-permute-start | bytes 1548296 | tf_op jit(solution)/shard_map/ppermute | solution.py:34
  26.8 13.4 %collective-permute-start.5 = (bf16[2,2,168,384]{3,2,1,0:T(8,128)(2,1)S(1)}, bf16[2,2,168,384]{3,2,1,0:T(8,128)(2,1)S(1)}, u32[]{:S(2)}, u32[]{:S(2)}) collective-permute-start(bf16[2,2,168,384]{3,2,1,0:T(8,128)(2,1)S(1)} %pad_maximum_fusion.refs_0_), channel_id=1, source_target_pairs={{6,0},{25,1},{0,2},{27,3},{2,4},{29,5},{4,6},{31,7},{14,8},{1,9},{... | collective-permute-start | bytes 1548296 | tf_op jit(solution)/shard_map/ppermute | solution.py:34
  28.3 11.9 %collective-permute-start.7 = (bf16[2,1,32,384]{3,2,1,0:T(8,128)(2,1)S(1)}, bf16[2,1,32,384]{3,2,1,0:T(8,128)(2,1)S(1)}, u32[]{:S(2)}, u32[]{:S(2)}) collective-permute-start(bf16[2,1,32,384]{3,2,1,0:T(8,128)(2,1)S(1)} %get-tuple-element.96), channel_id=1, source_target_pairs={{2,1},{1,2},{4,3},{3,4},{6,5},{5,6},{10,9},{9,10},{12,11},{11,12},... | collective-permute-start | bytes 147464 | tf_op jit(solution)/shard_map/ppermute | solution.py:34
  45.2 5.6 %collective-permute-start.8 = (bf16[14,96,384]{2,1,0:T(8,128)(2,1)}, bf16[14,96,384]{2,1,0:T(8,128)(2,1)}, u32[]{:S(2)}, u32[]{:S(2)}) collective-permute-start(bf16[14,96,384]{2,1,0:T(8,128)(2,1)} %shard_map.129.refs_4_), channel_id=1, source_target_pairs={{1,0},{0,1},{3,2},{2,3},{5,4},{4,5},{7,6},{6,7},{9,8},{8,9},{11,10... | collective-permute-start | bytes 3096584 | tf_op jit(solution)/shard_map/ppermute | solution.py:34
  46.5 4.4 %collective-permute-start.9 = (bf16[14,96,384]{2,1,0:T(8,128)(2,1)S(1)}, bf16[14,96,384]{2,1,0:T(8,128)(2,1)}, u32[]{:S(2)}, u32[]{:S(2)}) collective-permute-start(bf16[14,96,384]{2,1,0:T(8,128)(2,1)S(1)} %shard_map.128.refs_4_), channel_id=1, source_target_pairs={{1,0},{0,1},{3,2},{2,3},{5,4},{4,5},{7,6},{6,7},{9,8},{8,9},{11,10... | collective-permute-start | bytes 3096584 | tf_op jit(solution)/shard_map/ppermute | solution.py:34
  46.6 14.1 %collective-permute-start.13 = (bf16[14,96,384]{2,1,0:T(8,128)(2,1)}, bf16[14,96,384]{2,1,0:T(8,128)(2,1)}, u32[]{:S(2)}, u32[]{:S(2)}) collective-permute-start(bf16[14,96,384]{2,1,0:T(8,128)(2,1)} %shard_map.129.refs_4_), channel_id=1, source_target_pairs={{8,0},{3,1},{10,2},{5,3},{12,4},{7,5},{14,6},{1,7},{16,8},{11,9},{... | collective-permute-start | bytes 3096584 | tf_op jit(solution)/shard_map/ppermute | solution.py:34
  46.6 14.1 %collective-permute-start.14 = (bf16[14,96,384]{2,1,0:T(8,128)(2,1)}, bf16[14,96,384]{2,1,0:T(8,128)(2,1)}, u32[]{:S(2)}, u32[]{:S(2)}) collective-permute-start(bf16[14,96,384]{2,1,0:T(8,128)(2,1)} %shard_map.129.refs_4_), channel_id=1, source_target_pairs={{24,0},{7,1},{26,2},{1,3},{28,4},{3,5},{30,6},{5,7},{0,8},{15,9},{... | collective-permute-start | bytes 3096584 | tf_op jit(solution)/shard_map/ppermute | solution.py:34
  48.1 14.1 %collective-permute-start.15 = (bf16[14,96,384]{2,1,0:T(8,128)(2,1)}, bf16[14,96,384]{2,1,0:T(8,128)(2,1)}, u32[]{:S(2)}, u32[]{:S(2)}) collective-permute-start(bf16[14,96,384]{2,1,0:T(8,128)(2,1)} %shard_map.129.refs_4_), channel_id=1, source_target_pairs={{224,0},{33,1},{226,2},{35,3},{228,4},{37,5},{230,6},{39,7},{232,8... | collective-permute-start | bytes 3096584 | tf_op jit(solution)/shard_map/ppermute | solution.py:34
  50.8 5.5 %collective-permute-start.16 = (bf16[8,1,32,384]{3,2,1,0:T(8,128)(2,1)S(1)}, bf16[8,1,32,384]{3,2,1,0:T(8,128)(2,1)S(1)}, u32[]{:S(2)}, u32[]{:S(2)}) collective-permute-start(bf16[8,1,32,384]{3,2,1,0:T(8,128)(2,1)S(1)} %pad_maximum_fusion.1), channel_id=1, source_target_pairs={{1,0},{0,1},{3,2},{2,3},{5,4},{4,5},{7,6},{6,7},{9,8},{8,9},{11,10... | collective-permute-start | bytes 589832 | tf_op jit(solution)/shard_map/ppermute | solution.py:34
  56.3 11.4 %copy-start.11 = (f32[384]{0:T(512)S(1)}, f32[384]{0:T(512)}, u32[]{:S(2)}) copy-start(f32[384]{0:T(512)} %param.20) | copy-start | bytes 4612
  62.2 5.5 %collective-permute-start.17 = (bf16[14,96,384]{2,1,0:T(8,128)(2,1)}, bf16[14,96,384]{2,1,0:T(8,128)(2,1)S(1)}, u32[]{:S(2)}, u32[]{:S(2)}) collective-permute-start(bf16[14,96,384]{2,1,0:T(8,128)(2,1)} %collective-permute-done.13.refs_5_), channel_id=1, source_target_pairs={{1,0},{0,1},{3,2},{2,3},{5,4},{4,5},{7,6},{6,7},{9,8},{8,9},{11,10... | collective-permute-start | bytes 3096584 | tf_op jit(solution)/shard_map/ppermute | solution.py:34
  65.2 4.0 %collective-permute-start.18 = (bf16[14,96,384]{2,1,0:T(8,128)(2,1)}, bf16[14,96,384]{2,1,0:T(8,128)(2,1)S(1)}, u32[]{:S(2)}, u32[]{:S(2)}) collective-permute-start(bf16[14,96,384]{2,1,0:T(8,128)(2,1)} %collective-permute-done.14.refs_6_), channel_id=1, source_target_pairs={{1,0},{0,1},{3,2},{2,3},{5,4},{4,5},{7,6},{6,7},{9,8},{8,9},{11,10... | collective-permute-start | bytes 3096584 | tf_op jit(solution)/shard_map/ppermute | solution.py:34
  65.2 5.4 %collective-permute-start.19 = (bf16[14,96,384]{2,1,0:T(8,128)(2,1)}, bf16[14,96,384]{2,1,0:T(8,128)(2,1)S(1)}, u32[]{:S(2)}, u32[]{:S(2)}) collective-permute-start(bf16[14,96,384]{2,1,0:T(8,128)(2,1)} %collective-permute-done.15.refs_7_), channel_id=1, source_target_pairs={{1,0},{0,1},{3,2},{2,3},{5,4},{4,5},{7,6},{6,7},{9,8},{8,9},{11,10... | collective-permute-start | bytes 3096584 | tf_op jit(solution)/shard_map/ppermute | solution.py:34
  65.7 15.2 %collective-permute-start.10 = (bf16[14,96,384]{2,1,0:T(8,128)(2,1)S(1)}, bf16[14,96,384]{2,1,0:T(8,128)(2,1)S(1)}, u32[]{:S(2)}, u32[]{:S(2)}) collective-permute-start(bf16[14,96,384]{2,1,0:T(8,128)(2,1)S(1)} %shard_map.128.refs_4_), channel_id=1, source_target_pairs={{8,0},{3,1},{10,2},{5,3},{12,4},{7,5},{14,6},{1,7},{16,8},{11,9},{... | collective-permute-start | bytes 3096584 | tf_op jit(solution)/shard_map/ppermute | solution.py:34
  65.7 15.3 %collective-permute-start.11 = (bf16[14,96,384]{2,1,0:T(8,128)(2,1)S(1)}, bf16[14,96,384]{2,1,0:T(8,128)(2,1)S(1)}, u32[]{:S(2)}, u32[]{:S(2)}) collective-permute-start(bf16[14,96,384]{2,1,0:T(8,128)(2,1)S(1)} %shard_map.128.refs_4_), channel_id=1, source_target_pairs={{24,0},{7,1},{26,2},{1,3},{28,4},{3,5},{30,6},{5,7},{0,8},{15,9},{... | collective-permute-start | bytes 3096584 | tf_op jit(solution)/shard_map/ppermute | solution.py:34
  67.7 13.8 %collective-permute-start.12 = (bf16[14,96,384]{2,1,0:T(8,128)(2,1)S(1)}, bf16[14,96,384]{2,1,0:T(8,128)(2,1)S(1)}, u32[]{:S(2)}, u32[]{:S(2)}) collective-permute-start(bf16[14,96,384]{2,1,0:T(8,128)(2,1)S(1)} %shard_map.128.refs_4_), channel_id=1, source_target_pairs={{224,0},{33,1},{226,2},{35,3},{228,4},{37,5},{230,6},{39,7},{232,8... | collective-permute-start | bytes 3096584 | tf_op jit(solution)/shard_map/ppermute | solution.py:34
  81.0 10.3 %copy-start.1 = (bf16[2,384,384]{2,1,0:T(8,128)(2,1)S(1)}, bf16[2,384,384]{2,1,0:T(8,128)(2,1)}, u32[]{:S(2)}) copy-start(bf16[2,384,384]{2,1,0:T(8,128)(2,1)} %shard_map.127.picks) | copy-start | bytes 1769476
  81.5 17.6 %collective-permute-start.23 = (bf16[14,96,384]{2,1,0:T(8,128)(2,1)S(1)}, bf16[14,96,384]{2,1,0:T(8,128)(2,1)S(1)}, u32[]{:S(2)}, u32[]{:S(2)}) collective-permute-start(bf16[14,96,384]{2,1,0:T(8,128)(2,1)S(1)} %collective-permute-done.10.refs_5_), channel_id=1, source_target_pairs={{1,0},{0,1},{3,2},{2,3},{5,4},{4,5},{7,6},{6,7},{9,8},{8,9},{11,10... | collective-permute-start | bytes 3096584 | tf_op jit(solution)/shard_map/ppermute | solution.py:34
  83.9 15.1 %collective-permute-start.24 = (bf16[14,96,384]{2,1,0:T(8,128)(2,1)S(1)}, bf16[14,96,384]{2,1,0:T(8,128)(2,1)S(1)}, u32[]{:S(2)}, u32[]{:S(2)}) collective-permute-start(bf16[14,96,384]{2,1,0:T(8,128)(2,1)S(1)} %collective-permute-done.11.refs_6_), channel_id=1, source_target_pairs={{1,0},{0,1},{3,2},{2,3},{5,4},{4,5},{7,6},{6,7},{9,8},{8,9},{11,10... | collective-permute-start | bytes 3096584 | tf_op jit(solution)/shard_map/ppermute | solution.py:34
  84.0 15.0 %collective-permute-start.20 = (bf16[2,4,32,384]{3,2,1,0:T(8,128)(2,1)S(1)}, bf16[2,4,32,384]{3,2,1,0:T(8,128)(2,1)S(1)}, u32[]{:S(2)}, u32[]{:S(2)}) collective-permute-start(bf16[2,4,32,384]{3,2,1,0:T(8,128)(2,1)S(1)} %constant_dynamic-slice_fusion.1), channel_id=1, source_target_pairs={{0,8},{1,9},{2,10},{3,11},{4,12},{5,13},{6,14},{7,15},{8,16},{9,17... | collective-permute-start | bytes 589832 | tf_op jit(solution)/shard_map/ppermute | solution.py:34
  85.9 13.1 %collective-permute-start.22 = (bf16[6,1,32,384]{3,2,1,0:T(8,128)(2,1)S(1)}, bf16[6,1,32,384]{3,2,1,0:T(8,128)(2,1)S(1)}, u32[]{:S(2)}, u32[]{:S(2)}) collective-permute-start(bf16[6,1,32,384]{3,2,1,0:T(8,128)(2,1)S(1)} %get-tuple-element.72), channel_id=1, source_target_pairs={{2,1},{1,2},{4,3},{3,4},{6,5},{5,6},{10,9},{9,10},{12,11},{11,12},... | collective-permute-start | bytes 442376 | tf_op jit(solution)/shard_map/ppermute | solution.py:34
  89.4 9.6 %collective-permute-start.21 = (bf16[2,1,32,384]{3,2,1,0:T(8,128)(2,1)S(1)}, bf16[2,1,32,384]{3,2,1,0:T(8,128)(2,1)S(1)}, u32[]{:S(2)}, u32[]{:S(2)}) collective-permute-start(bf16[2,1,32,384]{3,2,1,0:T(8,128)(2,1)S(1)} %constant_dynamic-slice_fusion), channel_id=1, source_target_pairs={{2,9},{1,10},{4,11},{3,12},{6,13},{5,14},{10,17},{9,18},{12,19},{1... | collective-permute-start | bytes 147464 | tf_op jit(solution)/shard_map/ppermute | solution.py:34
  99.1 1.8 %collective-permute-start.25 = (bf16[8,1,32,384]{3,2,1,0:T(8,128)(2,1)S(1)}, bf16[8,1,32,384]{3,2,1,0:T(8,128)(2,1)S(1)}, u32[]{:S(2)}, u32[]{:S(2)}) collective-permute-start(bf16[8,1,32,384]{3,2,1,0:T(8,128)(2,1)S(1)} %pad_maximum_fusion.3), channel_id=1, source_target_pairs={{1,0},{0,1},{3,2},{2,3},{5,4},{4,5},{7,6},{6,7},{9,8},{8,9},{11,10... | collective-permute-start | bytes 589832 | tf_op jit(solution)/shard_map/ppermute | solution.py:34
  100.8 2.6 %collective-permute-start.26 = (bf16[14,96,384]{2,1,0:T(8,128)(2,1)S(1)}, bf16[14,96,384]{2,1,0:T(8,128)(2,1)S(1)}, u32[]{:S(2)}, u32[]{:S(2)}) collective-permute-start(bf16[14,96,384]{2,1,0:T(8,128)(2,1)S(1)} %collective-permute-done.12.refs_7_), channel_id=1, source_target_pairs={{1,0},{0,1},{3,2},{2,3},{5,4},{4,5},{7,6},{6,7},{9,8},{8,9},{11,10... | collective-permute-start | bytes 3096584 | tf_op jit(solution)/shard_map/ppermute | solution.py:34
  (12 other events, 41.5 us)

commit v12 on v11

--- a/solution.py
+++ b/solution.py
@@ -154,7 +154,7 @@
         out_shape=jax.ShapeDtypeStruct((2, 8, 6, 32, 3 * C), jnp.bfloat16),
         in_specs=[vmem] * 2,
         out_specs=vmem,
-        compiler_params=pltpu.CompilerParams(vmem_limit_bytes=20 * 1024 * 1024),
+        compiler_params=pltpu.CompilerParams(vmem_limit_bytes=16 * 1024 * 1024),
         cost_estimate=pl.CostEstimate(flops=1000, bytes_accessed=1000, transcendentals=0),
     )(picks, acts.reshape(-1, C))
 
@@ -189,7 +189,7 @@
         in_specs=[pl.BlockSpec(memory_space=pltpu.SMEM)] + [vmem] * 5,
         out_specs=vmem,
         input_output_aliases={5: 0},
-        compiler_params=pltpu.CompilerParams(vmem_limit_bytes=20 * 1024 * 1024),
+        compiler_params=pltpu.CompilerParams(vmem_limit_bytes=16 * 1024 * 1024),
         cost_estimate=pl.CostEstimate(flops=1000, bytes_accessed=1000, transcendentals=0),
     )(scalars, picks, ends, beside, across, spread)
 
@@ -294,7 +294,7 @@
             pltpu.VMEM((6, 128, C), jnp.float32),
             pltpu.SemaphoreType.DMA((2, 4)),
         ],
-        compiler_params=pltpu.CompilerParams(vmem_limit_bytes=26 * 1024 * 1024),
+        compiler_params=pltpu.CompilerParams(vmem_limit_bytes=22 * 1024 * 1024),
         cost_estimate=pl.CostEstimate(flops=1000, bytes_accessed=1000, transcendentals=0),
     )(scalars, lag_weights, spread, tail, *own, *got)
 

time: 116 us -> 116 us (level)
  no operation moved by 1% of the time
where the time goes in v12:
time: 116 us; the launch traced here: 114 us
  starting transfers between devices  39 us (34%)
  Pallas kernels  30.4 us (26%)
  waiting for transfers between devices  27.7 us (24%)
  local copies, waits for them, and re-layouts  9.07 us (8%)
  other arithmetic  6.31 us (5%)
  between operations  1.95 us (2%)
    ppermute x27, starting transfers between devices, fetch(): return lax.ppermute(array, AXES, pairs)  39 us
    ppermute x27, waiting for transfers between devices, fetch(): return lax.ppermute(array, AXES, pairs)  27.7 us
    pallas_call x2, Pallas kernels, conv(): pl.pallas_call(lambda *refs: conv_body(*refs, finish=finish), out_shape=j...  21.1 us
    unnamed x35, local copies, waits for them, and re-layouts  4.78 us
    pallas_call x2, Pallas kernels, spread_halo(): pl.pallas_call(spread_halo_body, out_shape=jax.ShapeDtypeStruct(spread.sh...  4.18 us
  transfers between devices with their start and end apart: 27, of which 11 were waited for; matrix products, arithmetic and copies ran while one was open for 8% of the time, Pallas kernels for 16%

profile of v12, /device:TPU:131, one launch (start us, length us, event | category | flops | bytes accessed | tf_op | source)
XLA Modules:
  0.0 114.4 jit_solution(224443711936297975)
XLA Ops:
  0.0 1.1 constant_dynamic-slice_fusion.3
  1.2 1.9 %collective-permute-start = (bf16[2,168,384]{2,1,0:T(8,128)(2,1)S(1)}, bf16[2,168,384]{2,1,0:T(8,128)(2,1)S(1)}, u32[]{:S(2)}, u32[]{:S(2)}) collective-permute-start(bf16[2,168,384]{2,1,0:T(8,128)(2,1)S(1)} %constant_dynamic-update-slice_fusion), channel_id=1, source_target_pairs={{24,0},{1,1},{90,2},{67,3},{60,4},{37,5},{126,6},{103,7},{0,8},{9,... | collective-permute-start | bytes 774152 | tf_op jit(solution)/shard_map/ppermute | solution.py:34
  3.2 2.4 %collective-permute-start.1 = (bf16[2,168,384]{2,1,0:T(8,128)(2,1)S(1)}, bf16[2,168,384]{2,1,0:T(8,128)(2,1)S(1)}, u32[]{:S(2)}, u32[]{:S(2)}) collective-permute-start(bf16[2,168,384]{2,1,0:T(8,128)(2,1)S(1)} %constant_dynamic-update-slice_fusion), channel_id=1, source_target_pairs={{152,0},{129,1},{218,2},{195,3},{188,4},{165,5},{254,6},{231,7},{1... | collective-permute-start | bytes 774152 | tf_op jit(solution)/shard_map/ppermute | solution.py:34
  7.0 4.8 %collective-permute-start.2 = (bf16[6,1,32,384]{3,2,1,0:T(8,128)(2,1)S(1)}, bf16[6,1,32,384]{3,2,1,0:T(8,128)(2,1)S(1)}, u32[]{:S(2)}, u32[]{:S(2)}) collective-permute-start(bf16[6,1,32,384]{3,2,1,0:T(8,128)(2,1)S(1)} %get-tuple-element.94), channel_id=1, source_target_pairs={{2,1},{1,2},{4,3},{3,4},{6,5},{5,6},{10,9},{9,10},{12,11},{11,12},... | collective-permute-start | bytes 442376 | tf_op jit(solution)/shard_map/ppermute | solution.py:34
  12.5 1.9 %collective-permute-start.4 = (bf16[2,4,32,384]{3,2,1,0:T(8,128)(2,1)S(1)}, bf16[2,4,32,384]{3,2,1,0:T(8,128)(2,1)S(1)}, u32[]{:S(2)}, u32[]{:S(2)}) collective-permute-start(bf16[2,4,32,384]{3,2,1,0:T(8,128)(2,1)S(1)} %constant_dynamic-slice_fusion.2), channel_id=1, source_target_pairs={{0,8},{1,9},{2,10},{3,11},{4,12},{5,13},{6,14},{7,15},{8,16},{9,17... | collective-permute-start | bytes 589832 | tf_op jit(solution)/shard_map/ppermute | solution.py:34
  17.5 2.0 %collective-permute-start.3 = (bf16[2,2,168,384]{3,2,1,0:T(8,128)(2,1)S(1)}, bf16[2,2,168,384]{3,2,1,0:T(8,128)(2,1)S(1)}, u32[]{:S(2)}, u32[]{:S(2)}) collective-permute-start(bf16[2,2,168,384]{3,2,1,0:T(8,128)(2,1)S(1)} %pad_maximum_fusion.refs_0_), channel_id=1, source_target_pairs={{2,0},{9,1},{4,2},{11,3},{6,4},{13,5},{0,6},{15,7},{10,8},{17,9},{... | collective-permute-start | bytes 1548296 | tf_op jit(solution)/shard_map/ppermute | solution.py:34
  19.8 7.0 %collective-permute-done.4.ends = bf16[2,4,32,384]{3,2,1,0:T(8,128)(2,1)S(1)} collective-permute-done((bf16[2,4,32,384]{3,2,1,0:T(8,128)(2,1)S(1)}, bf16[2,4,32,384]{3,2,1,0:T(8,128)(2,1)S(1)}, u32[]{:S(2)}, u32[]{:S(2)}) %collective-permute-start.4) | collective-permute-done | bytes 196640 | tf_op jit(solution)/shard_map/ppermute | solution.py:34
  28.3 6.6 %collective-permute-start.7 = (bf16[2,1,32,384]{3,2,1,0:T(8,128)(2,1)S(1)}, bf16[2,1,32,384]{3,2,1,0:T(8,128)(2,1)S(1)}, u32[]{:S(2)}, u32[]{:S(2)}) collective-permute-start(bf16[2,1,32,384]{3,2,1,0:T(8,128)(2,1)S(1)} %get-tuple-element.96), channel_id=1, source_target_pairs={{2,1},{1,2},{4,3},{3,4},{6,5},{5,6},{10,9},{9,10},{12,11},{11,12},... | collective-permute-start | bytes 147464 | tf_op jit(solution)/shard_map/ppermute | solution.py:34
  35.6 4.6 %collective-permute-done.7 = bf16[2,1,32,384]{3,2,1,0:T(8,128)(2,1)S(1)} collective-permute-done((bf16[2,1,32,384]{3,2,1,0:T(8,128)(2,1)S(1)}, bf16[2,1,32,384]{3,2,1,0:T(8,128)(2,1)S(1)}, u32[]{:S(2)}, u32[]{:S(2)}) %collective-permute-start.7) | collective-permute-done | bytes 49184 | tf_op jit(solution)/shard_map/ppermute | solution.py:34
  40.2 1.2 %shard_map.129.refs_4_ = bf16[14,96,384]{2,1,0:T(8,128)(2,1)} custom-call(bf16[2,2,168,384]{3,2,1,0:T(8,128)(2,1)S(1)} %pad_maximum_fusion.refs_0_, bf16[2,2,168,384]{3,2,1,0:T(8,128)(2,1)S(1)} %collective-permute-done.3.refs_1_, bf16[2,2,168,384]{3,2,1,0:T(8,128)(2,1)S(1)} %collective-permute-done.5.refs_2_, ...), custom_call_target="tpu_custom_call" | custom-call | bytes 2000000 | tf_op jit(solution)/shard_map/pallas_call | solution.py:83
  45.2 1.2 %collective-permute-start.8 = (bf16[14,96,384]{2,1,0:T(8,128)(2,1)}, bf16[14,96,384]{2,1,0:T(8,128)(2,1)}, u32[]{:S(2)}, u32[]{:S(2)}) collective-permute-start(bf16[14,96,384]{2,1,0:T(8,128)(2,1)} %shard_map.129.refs_4_), channel_id=1, source_target_pairs={{1,0},{0,1},{3,2},{2,3},{5,4},{4,5},{7,6},{6,7},{9,8},{8,9},{11,10... | collective-permute-start | bytes 3096584 | tf_op jit(solution)/shard_map/ppermute | solution.py:34
  46.6 1.5 %collective-permute-start.14 = (bf16[14,96,384]{2,1,0:T(8,128)(2,1)}, bf16[14,96,384]{2,1,0:T(8,128)(2,1)}, u32[]{:S(2)}, u32[]{:S(2)}) collective-permute-start(bf16[14,96,384]{2,1,0:T(8,128)(2,1)} %shard_map.129.refs_4_), channel_id=1, source_target_pairs={{24,0},{7,1},{26,2},{1,3},{28,4},{3,5},{30,6},{5,7},{0,8},{15,9},{... | collective-permute-start | bytes 3096584 | tf_op jit(solution)/shard_map/ppermute | solution.py:34
  52.5 1.6 %shard_map.127.picks = bf16[2,384,384]{2,1,0:T(8,128)(2,1)} custom-call(s32[2,384]{1,0:T(2,128)} %pad_add_fusion.order), custom_call_target="tpu_custom_call" | custom-call | flops 1000 | bytes 1000 | tf_op jit(solution)/shard_map/pallas_call | solution.py:126
  54.1 1.1 copy-done
  55.2 1.1 shard_map.130._
  56.3 2.1 %shard_map.131.refs_2_ = bf16[2,8,6,32,1152]{4,3,2,1,0:T(8,128)(2,1)S(1)} custom-call(s32[2]{0:T(128)S(1)} %pad_add_fusion.1.scalars.refs_0_, bf16[2,384,384]{2,1,0:T(8,128)(2,1)S(1)} %copy-done, bf16[2,4,32,384]{3,2,1,0:T(8,128)(2,1)S(1)} %collective-permute-done.4.ends, ...), custom_call_target="tpu_custom_call", output_to_operand_aliasing={{}: (5, {})} | custom-call | flops 1000 | bytes 1000 | tf_op jit(solution)/shard_map/pallas_call | solution.py:186
  58.4 2.3 %collective-permute-done.13.refs_5_ = bf16[14,96,384]{2,1,0:T(8,128)(2,1)} collective-permute-done((bf16[14,96,384]{2,1,0:T(8,128)(2,1)}, bf16[14,96,384]{2,1,0:T(8,128)(2,1)}, u32[]{:S(2)}, u32[]{:S(2)}) %collective-permute-start.13) | collective-permute-done | bytes 1032224 | tf_op jit(solution)/shard_map/ppermute | solution.py:34
  60.8 1.4 %collective-permute-done.15.refs_7_ = bf16[14,96,384]{2,1,0:T(8,128)(2,1)} collective-permute-done((bf16[14,96,384]{2,1,0:T(8,128)(2,1)}, bf16[14,96,384]{2,1,0:T(8,128)(2,1)}, u32[]{:S(2)}, u32[]{:S(2)}) %collective-permute-start.15) | collective-permute-done | bytes 1032224 | tf_op jit(solution)/shard_map/ppermute | solution.py:34
  62.2 3.0 %collective-permute-start.17 = (bf16[14,96,384]{2,1,0:T(8,128)(2,1)}, bf16[14,96,384]{2,1,0:T(8,128)(2,1)S(1)}, u32[]{:S(2)}, u32[]{:S(2)}) collective-permute-start(bf16[14,96,384]{2,1,0:T(8,128)(2,1)} %collective-permute-done.13.refs_5_), channel_id=1, source_target_pairs={{1,0},{0,1},{3,2},{2,3},{5,4},{4,5},{7,6},{6,7},{9,8},{8,9},{11,10... | collective-permute-start | bytes 3096584 | tf_op jit(solution)/shard_map/ppermute | solution.py:34
  65.7 1.5 %collective-permute-start.11 = (bf16[14,96,384]{2,1,0:T(8,128)(2,1)S(1)}, bf16[14,96,384]{2,1,0:T(8,128)(2,1)S(1)}, u32[]{:S(2)}, u32[]{:S(2)}) collective-permute-start(bf16[14,96,384]{2,1,0:T(8,128)(2,1)S(1)} %shard_map.128.refs_4_), channel_id=1, source_target_pairs={{24,0},{7,1},{26,2},{1,3},{28,4},{3,5},{30,6},{5,7},{0,8},{15,9},{... | collective-permute-start | bytes 3096584 | tf_op jit(solution)/shard_map/ppermute | solution.py:34
  67.7 1.5 %collective-permute-done.18.refs_10_ = bf16[14,96,384]{2,1,0:T(8,128)(2,1)S(1)} collective-permute-done((bf16[14,96,384]{2,1,0:T(8,128)(2,1)}, bf16[14,96,384]{2,1,0:T(8,128)(2,1)S(1)}, u32[]{:S(2)}, u32[]{:S(2)}) %collective-permute-start.18) | collective-permute-done | bytes 1032224 | tf_op jit(solution)/shard_map/ppermute | solution.py:34
  69.2 1.5 %collective-permute-done.19.refs_11_ = bf16[14,96,384]{2,1,0:T(8,128)(2,1)S(1)} collective-permute-done((bf16[14,96,384]{2,1,0:T(8,128)(2,1)}, bf16[14,96,384]{2,1,0:T(8,128)(2,1)S(1)}, u32[]{:S(2)}, u32[]{:S(2)}) %collective-permute-start.19) | collective-permute-done | bytes 1032224 | tf_op jit(solution)/shard_map/ppermute | solution.py:34
  70.7 10.3 %shard_map.132 = bf16[6,128,384]{2,1,0:T(8,128)(2,1)S(1)} custom-call(s32[2]{0:T(128)S(1)} %pad_add_fusion.1.scalars.refs_0_, f32[3,6]{1,0:T(4,128)S(1)} %add_convert_fusion.refs_1_, bf16[2,8,6,32,1152]{4,3,2,1,0:T(8,128)(2,1)S(1)} %shard_map.131.refs_2_, f32[1,384]{1,0:T(1,128)S(1)} %reshape.334.refs_3_, bf16[14,96,384]{2,1,0:T(8,128)(2,1)} %shard_map.129.refs_4_, ...), custom_call_target="tpu_custom_call" | custom-call | flops 1000 | bytes 1000 | tf_op jit(solution)/shard_map/pallas_call | solution.py:287
  81.5 2.4 %collective-permute-start.23 = (bf16[14,96,384]{2,1,0:T(8,128)(2,1)S(1)}, bf16[14,96,384]{2,1,0:T(8,128)(2,1)S(1)}, u32[]{:S(2)}, u32[]{:S(2)}) collective-permute-start(bf16[14,96,384]{2,1,0:T(8,128)(2,1)S(1)} %collective-permute-done.10.refs_5_), channel_id=1, source_target_pairs={{1,0},{0,1},{3,2},{2,3},{5,4},{4,5},{7,6},{6,7},{9,8},{8,9},{11,10... | collective-permute-start | bytes 3096584 | tf_op jit(solution)/shard_map/ppermute | solution.py:34
  84.0 1.9 %collective-permute-start.20 = (bf16[2,4,32,384]{3,2,1,0:T(8,128)(2,1)S(1)}, bf16[2,4,32,384]{3,2,1,0:T(8,128)(2,1)S(1)}, u32[]{:S(2)}, u32[]{:S(2)}) collective-permute-start(bf16[2,4,32,384]{3,2,1,0:T(8,128)(2,1)S(1)} %constant_dynamic-slice_fusion.1), channel_id=1, source_target_pairs={{0,8},{1,9},{2,10},{3,11},{4,12},{5,13},{6,14},{7,15},{8,16},{9,17... | collective-permute-start | bytes 589832 | tf_op jit(solution)/shard_map/ppermute | solution.py:34
  85.9 3.4 %collective-permute-start.22 = (bf16[6,1,32,384]{3,2,1,0:T(8,128)(2,1)S(1)}, bf16[6,1,32,384]{3,2,1,0:T(8,128)(2,1)S(1)}, u32[]{:S(2)}, u32[]{:S(2)}) collective-permute-start(bf16[6,1,32,384]{3,2,1,0:T(8,128)(2,1)S(1)} %get-tuple-element.72), channel_id=1, source_target_pairs={{2,1},{1,2},{4,3},{3,4},{6,5},{5,6},{10,9},{9,10},{12,11},{11,12},... | collective-permute-start | bytes 442376 | tf_op jit(solution)/shard_map/ppermute | solution.py:34
  89.4 1.9 %collective-permute-start.21 = (bf16[2,1,32,384]{3,2,1,0:T(8,128)(2,1)S(1)}, bf16[2,1,32,384]{3,2,1,0:T(8,128)(2,1)S(1)}, u32[]{:S(2)}, u32[]{:S(2)}) collective-permute-start(bf16[2,1,32,384]{3,2,1,0:T(8,128)(2,1)S(1)} %constant_dynamic-slice_fusion), channel_id=1, source_target_pairs={{2,9},{1,10},{4,11},{3,12},{6,13},{5,14},{10,17},{9,18},{12,19},{1... | collective-permute-start | bytes 147464 | tf_op jit(solution)/shard_map/ppermute | solution.py:34
  91.3 1.1 shard_map.133._
  92.4 6.6 %collective-permute-done.21 = bf16[2,1,32,384]{3,2,1,0:T(8,128)(2,1)S(1)} collective-permute-done((bf16[2,1,32,384]{3,2,1,0:T(8,128)(2,1)S(1)}, bf16[2,1,32,384]{3,2,1,0:T(8,128)(2,1)S(1)}, u32[]{:S(2)}, u32[]{:S(2)}) %collective-permute-start.21) | collective-permute-done | bytes 49184 | tf_op jit(solution)/shard_map/ppermute | solution.py:34
  99.4 1.4 %collective-permute-done.25.beside = bf16[8,1,32,384]{3,2,1,0:T(8,128)(2,1)S(1)} collective-permute-done((bf16[8,1,32,384]{3,2,1,0:T(8,128)(2,1)S(1)}, bf16[8,1,32,384]{3,2,1,0:T(8,128)(2,1)S(1)}, u32[]{:S(2)}, u32[]{:S(2)}) %collective-permute-start.25) | collective-permute-done | bytes 196640 | tf_op jit(solution)/shard_map/ppermute | solution.py:34
  101.0 2.1 %shard_map.134.refs_2_ = bf16[2,8,6,32,1152]{4,3,2,1,0:T(8,128)(2,1)S(1)} custom-call(s32[2]{0:T(128)S(1)} %pad_add_fusion.1.scalars.refs_0_, bf16[2,384,384]{2,1,0:T(8,128)(2,1)S(1)} %copy-done.1, bf16[2,4,32,384]{3,2,1,0:T(8,128)(2,1)S(1)} %collective-permute-done.20.ends, ...), custom_call_target="tpu_custom_call", output_to_operand_aliasing={{}: (5, {})} | custom-call | flops 1000 | bytes 1000 | tf_op jit(solution)/shard_map/pallas_call | solution.py:186
  103.5 10.8 %shard_map.135 = bf16[6,128,384]{2,1,0:T(8,128)(2,1)} custom-call(s32[2]{0:T(128)S(1)} %pad_add_fusion.1.scalars.refs_0_, f32[3,6]{1,0:T(4,128)S(1)} %add_convert_fusion.refs_1_, bf16[2,8,6,32,1152]{4,3,2,1,0:T(8,128)(2,1)S(1)} %shard_map.134.refs_2_, bf16[6,128,384]{2,1,0:T(8,128)(2,1)S(1)} %bitcast.30, bf16[14,96,384]{2,1,0:T(8,128)(2,1)S(1)} %shard_map.128.refs_4_, ...), custom_call_target="tpu_custom_call" | custom-call | flops 1000 | bytes 1000 | tf_op jit(solution)/shard_map/pallas_call | solution.py:287
  (115 shorter events, 17.2 us)
Async XLA Ops:
  1.2 16.2 %collective-permute-start = (bf16[2,168,384]{2,1,0:T(8,128)(2,1)S(1)}, bf16[2,168,384]{2,1,0:T(8,128)(2,1)S(1)}, u32[]{:S(2)}, u32[]{:S(2)}) collective-permute-start(bf16[2,168,384]{2,1,0:T(8,128)(2,1)S(1)} %constant_dynamic-update-slice_fusion), channel_id=1, source_target_pairs={{24,0},{1,1},{90,2},{67,3},{60,4},{37,5},{126,6},{103,7},{0,8},{9,... | collective-permute-start | bytes 774152 | tf_op jit(solution)/shard_map/ppermute | solution.py:34
  3.2 14.3 %collective-permute-start.1 = (bf16[2,168,384]{2,1,0:T(8,128)(2,1)S(1)}, bf16[2,168,384]{2,1,0:T(8,128)(2,1)S(1)}, u32[]{:S(2)}, u32[]{:S(2)}) collective-permute-start(bf16[2,168,384]{2,1,0:T(8,128)(2,1)S(1)} %constant_dynamic-update-slice_fusion), channel_id=1, source_target_pairs={{152,0},{129,1},{218,2},{195,3},{188,4},{165,5},{254,6},{231,7},{1... | collective-permute-start | bytes 774152 | tf_op jit(solution)/shard_map/ppermute | solution.py:34
  5.8 9.6 %copy-start.14 = (s32[4]{0:T(128)S(1)}, s32[4]{0:T(128)}, u32[]{:S(2)}) copy-start(s32[4]{0:T(128)} %constant.162.clone) | copy-start | bytes 52
  5.8 10.2 %copy-start.13 = (s32[4]{0:T(128)S(1)}, s32[4]{0:T(128)}, u32[]{:S(2)}) copy-start(s32[4]{0:T(128)} %constant.163.clone) | copy-start | bytes 52
  5.8 10.9 %copy-start.7 = (s32[4,2]{1,0:T(4,128)S(1)}, s32[4,2]{1,0:T(4,128)}, u32[]{:S(2)}) copy-start(s32[4,2]{1,0:T(4,128)} %constant.161.clone) | copy-start | bytes 100
  7.0 10.5 %collective-permute-start.2 = (bf16[6,1,32,384]{3,2,1,0:T(8,128)(2,1)S(1)}, bf16[6,1,32,384]{3,2,1,0:T(8,128)(2,1)S(1)}, u32[]{:S(2)}, u32[]{:S(2)}) collective-permute-start(bf16[6,1,32,384]{3,2,1,0:T(8,128)(2,1)S(1)} %get-tuple-element.94), channel_id=1, source_target_pairs={{2,1},{1,2},{4,3},{3,4},{6,5},{5,6},{10,9},{9,10},{12,11},{11,12},... | collective-permute-start | bytes 442376 | tf_op jit(solution)/shard_map/ppermute | solution.py:34
  12.5 14.3 %collective-permute-start.4 = (bf16[2,4,32,384]{3,2,1,0:T(8,128)(2,1)S(1)}, bf16[2,4,32,384]{3,2,1,0:T(8,128)(2,1)S(1)}, u32[]{:S(2)}, u32[]{:S(2)}) collective-permute-start(bf16[2,4,32,384]{3,2,1,0:T(8,128)(2,1)S(1)} %constant_dynamic-slice_fusion.2), channel_id=1, source_target_pairs={{0,8},{1,9},{2,10},{3,11},{4,12},{5,13},{6,14},{7,15},{8,16},{9,17... | collective-permute-start | bytes 589832 | tf_op jit(solution)/shard_map/ppermute | solution.py:34
  17.5 22.7 %collective-permute-start.3 = (bf16[2,2,168,384]{3,2,1,0:T(8,128)(2,1)S(1)}, bf16[2,2,168,384]{3,2,1,0:T(8,128)(2,1)S(1)}, u32[]{:S(2)}, u32[]{:S(2)}) collective-permute-start(bf16[2,2,168,384]{3,2,1,0:T(8,128)(2,1)S(1)} %pad_maximum_fusion.refs_0_), channel_id=1, source_target_pairs={{2,0},{9,1},{4,2},{11,3},{6,4},{13,5},{0,6},{15,7},{10,8},{17,9},{... | collective-permute-start | bytes 1548296 | tf_op jit(solution)/shard_map/ppermute | solution.py:34
  19.5 20.7 %collective-permute-start.6 = (bf16[2,2,168,384]{3,2,1,0:T(8,128)(2,1)S(1)}, bf16[2,2,168,384]{3,2,1,0:T(8,128)(2,1)S(1)}, u32[]{:S(2)}, u32[]{:S(2)}) collective-permute-start(bf16[2,2,168,384]{3,2,1,0:T(8,128)(2,1)S(1)} %pad_maximum_fusion.refs_0_), channel_id=1, source_target_pairs={{4,0},{17,1},{6,2},{19,3},{0,4},{21,5},{2,6},{23,7},{12,8},{25,9},... | collective-permute-start | bytes 1548296 | tf_op jit(solution)/shard_map/ppermute | solution.py:34
  26.8 13.4 %collective-permute-start.5 = (bf16[2,2,168,384]{3,2,1,0:T(8,128)(2,1)S(1)}, bf16[2,2,168,384]{3,2,1,0:T(8,128)(2,1)S(1)}, u32[]{:S(2)}, u32[]{:S(2)}) collective-permute-start(bf16[2,2,168,384]{3,2,1,0:T(8,128)(2,1)S(1)} %pad_maximum_fusion.refs_0_), channel_id=1, source_target_pairs={{6,0},{25,1},{0,2},{27,3},{2,4},{29,5},{4,6},{31,7},{14,8},{1,9},{... | collective-permute-start | bytes 1548296 | tf_op jit(solution)/shard_map/ppermute | solution.py:34
  28.3 11.9 %collective-permute-start.7 = (bf16[2,1,32,384]{3,2,1,0:T(8,128)(2,1)S(1)}, bf16[2,1,32,384]{3,2,1,0:T(8,128)(2,1)S(1)}, u32[]{:S(2)}, u32[]{:S(2)}) collective-permute-start(bf16[2,1,32,384]{3,2,1,0:T(8,128)(2,1)S(1)} %get-tuple-element.96), channel_id=1, source_target_pairs={{2,1},{1,2},{4,3},{3,4},{6,5},{5,6},{10,9},{9,10},{12,11},{11,12},... | collective-permute-start | bytes 147464 | tf_op jit(solution)/shard_map/ppermute | solution.py:34
  45.2 5.6 %collective-permute-start.8 = (bf16[14,96,384]{2,1,0:T(8,128)(2,1)}, bf16[14,96,384]{2,1,0:T(8,128)(2,1)}, u32[]{:S(2)}, u32[]{:S(2)}) collective-permute-start(bf16[14,96,384]{2,1,0:T(8,128)(2,1)} %shard_map.129.refs_4_), channel_id=1, source_target_pairs={{1,0},{0,1},{3,2},{2,3},{5,4},{4,5},{7,6},{6,7},{9,8},{8,9},{11,10... | collective-permute-start | bytes 3096584 | tf_op jit(solution)/shard_map/ppermute | solution.py:34
  46.5 4.4 %collective-permute-start.9 = (bf16[14,96,384]{2,1,0:T(8,128)(2,1)S(1)}, bf16[14,96,384]{2,1,0:T(8,128)(2,1)}, u32[]{:S(2)}, u32[]{:S(2)}) collective-permute-start(bf16[14,96,384]{2,1,0:T(8,128)(2,1)S(1)} %shard_map.128.refs_4_), channel_id=1, source_target_pairs={{1,0},{0,1},{3,2},{2,3},{5,4},{4,5},{7,6},{6,7},{9,8},{8,9},{11,10... | collective-permute-start | bytes 3096584 | tf_op jit(solution)/shard_map/ppermute | solution.py:34
  46.6 14.1 %collective-permute-start.13 = (bf16[14,96,384]{2,1,0:T(8,128)(2,1)}, bf16[14,96,384]{2,1,0:T(8,128)(2,1)}, u32[]{:S(2)}, u32[]{:S(2)}) collective-permute-start(bf16[14,96,384]{2,1,0:T(8,128)(2,1)} %shard_map.129.refs_4_), channel_id=1, source_target_pairs={{8,0},{3,1},{10,2},{5,3},{12,4},{7,5},{14,6},{1,7},{16,8},{11,9},{... | collective-permute-start | bytes 3096584 | tf_op jit(solution)/shard_map/ppermute | solution.py:34
  46.6 14.1 %collective-permute-start.14 = (bf16[14,96,384]{2,1,0:T(8,128)(2,1)}, bf16[14,96,384]{2,1,0:T(8,128)(2,1)}, u32[]{:S(2)}, u32[]{:S(2)}) collective-permute-start(bf16[14,96,384]{2,1,0:T(8,128)(2,1)} %shard_map.129.refs_4_), channel_id=1, source_target_pairs={{24,0},{7,1},{26,2},{1,3},{28,4},{3,5},{30,6},{5,7},{0,8},{15,9},{... | collective-permute-start | bytes 3096584 | tf_op jit(solution)/shard_map/ppermute | solution.py:34
  48.1 14.1 %collective-permute-start.15 = (bf16[14,96,384]{2,1,0:T(8,128)(2,1)}, bf16[14,96,384]{2,1,0:T(8,128)(2,1)}, u32[]{:S(2)}, u32[]{:S(2)}) collective-permute-start(bf16[14,96,384]{2,1,0:T(8,128)(2,1)} %shard_map.129.refs_4_), channel_id=1, source_target_pairs={{224,0},{33,1},{226,2},{35,3},{228,4},{37,5},{230,6},{39,7},{232,8... | collective-permute-start | bytes 3096584 | tf_op jit(solution)/shard_map/ppermute | solution.py:34
  50.8 5.5 %collective-permute-start.16 = (bf16[8,1,32,384]{3,2,1,0:T(8,128)(2,1)S(1)}, bf16[8,1,32,384]{3,2,1,0:T(8,128)(2,1)S(1)}, u32[]{:S(2)}, u32[]{:S(2)}) collective-permute-start(bf16[8,1,32,384]{3,2,1,0:T(8,128)(2,1)S(1)} %pad_maximum_fusion.1), channel_id=1, source_target_pairs={{1,0},{0,1},{3,2},{2,3},{5,4},{4,5},{7,6},{6,7},{9,8},{8,9},{11,10... | collective-permute-start | bytes 589832 | tf_op jit(solution)/shard_map/ppermute | solution.py:34
  56.3 11.4 %copy-start.11 = (f32[384]{0:T(512)S(1)}, f32[384]{0:T(512)}, u32[]{:S(2)}) copy-start(f32[384]{0:T(512)} %param.20) | copy-start | bytes 4612
  62.2 5.5 %collective-permute-start.17 = (bf16[14,96,384]{2,1,0:T(8,128)(2,1)}, bf16[14,96,384]{2,1,0:T(8,128)(2,1)S(1)}, u32[]{:S(2)}, u32[]{:S(2)}) collective-permute-start(bf16[14,96,384]{2,1,0:T(8,128)(2,1)} %collective-permute-done.13.refs_5_), channel_id=1, source_target_pairs={{1,0},{0,1},{3,2},{2,3},{5,4},{4,5},{7,6},{6,7},{9,8},{8,9},{11,10... | collective-permute-start | bytes 3096584 | tf_op jit(solution)/shard_map/ppermute | solution.py:34
  65.2 4.0 %collective-permute-start.18 = (bf16[14,96,384]{2,1,0:T(8,128)(2,1)}, bf16[14,96,384]{2,1,0:T(8,128)(2,1)S(1)}, u32[]{:S(2)}, u32[]{:S(2)}) collective-permute-start(bf16[14,96,384]{2,1,0:T(8,128)(2,1)} %collective-permute-done.14.refs_6_), channel_id=1, source_target_pairs={{1,0},{0,1},{3,2},{2,3},{5,4},{4,5},{7,6},{6,7},{9,8},{8,9},{11,10... | collective-permute-start | bytes 3096584 | tf_op jit(solution)/shard_map/ppermute | solution.py:34
  65.2 5.4 %collective-permute-start.19 = (bf16[14,96,384]{2,1,0:T(8,128)(2,1)}, bf16[14,96,384]{2,1,0:T(8,128)(2,1)S(1)}, u32[]{:S(2)}, u32[]{:S(2)}) collective-permute-start(bf16[14,96,384]{2,1,0:T(8,128)(2,1)} %collective-permute-done.15.refs_7_), channel_id=1, source_target_pairs={{1,0},{0,1},{3,2},{2,3},{5,4},{4,5},{7,6},{6,7},{9,8},{8,9},{11,10... | collective-permute-start | bytes 3096584 | tf_op jit(solution)/shard_map/ppermute | solution.py:34
  65.7 15.2 %collective-permute-start.10 = (bf16[14,96,384]{2,1,0:T(8,128)(2,1)S(1)}, bf16[14,96,384]{2,1,0:T(8,128)(2,1)S(1)}, u32[]{:S(2)}, u32[]{:S(2)}) collective-permute-start(bf16[14,96,384]{2,1,0:T(8,128)(2,1)S(1)} %shard_map.128.refs_4_), channel_id=1, source_target_pairs={{8,0},{3,1},{10,2},{5,3},{12,4},{7,5},{14,6},{1,7},{16,8},{11,9},{... | collective-permute-start | bytes 3096584 | tf_op jit(solution)/shard_map/ppermute | solution.py:34
  65.7 15.3 %collective-permute-start.11 = (bf16[14,96,384]{2,1,0:T(8,128)(2,1)S(1)}, bf16[14,96,384]{2,1,0:T(8,128)(2,1)S(1)}, u32[]{:S(2)}, u32[]{:S(2)}) collective-permute-start(bf16[14,96,384]{2,1,0:T(8,128)(2,1)S(1)} %shard_map.128.refs_4_), channel_id=1, source_target_pairs={{24,0},{7,1},{26,2},{1,3},{28,4},{3,5},{30,6},{5,7},{0,8},{15,9},{... | collective-permute-start | bytes 3096584 | tf_op jit(solution)/shard_map/ppermute | solution.py:34
  67.7 13.8 %collective-permute-start.12 = (bf16[14,96,384]{2,1,0:T(8,128)(2,1)S(1)}, bf16[14,96,384]{2,1,0:T(8,128)(2,1)S(1)}, u32[]{:S(2)}, u32[]{:S(2)}) collective-permute-start(bf16[14,96,384]{2,1,0:T(8,128)(2,1)S(1)} %shard_map.128.refs_4_), channel_id=1, source_target_pairs={{224,0},{33,1},{226,2},{35,3},{228,4},{37,5},{230,6},{39,7},{232,8... | collective-permute-start | bytes 3096584 | tf_op jit(solution)/shard_map/ppermute | solution.py:34
  81.0 10.3 %copy-start.1 = (bf16[2,384,384]{2,1,0:T(8,128)(2,1)S(1)}, bf16[2,384,384]{2,1,0:T(8,128)(2,1)}, u32[]{:S(2)}) copy-start(bf16[2,384,384]{2,1,0:T(8,128)(2,1)} %shard_map.127.picks) | copy-start | bytes 1769476
  81.5 17.6 %collective-permute-start.23 = (bf16[14,96,384]{2,1,0:T(8,128)(2,1)S(1)}, bf16[14,96,384]{2,1,0:T(8,128)(2,1)S(1)}, u32[]{:S(2)}, u32[]{:S(2)}) collective-permute-start(bf16[14,96,384]{2,1,0:T(8,128)(2,1)S(1)} %collective-permute-done.10.refs_5_), channel_id=1, source_target_pairs={{1,0},{0,1},{3,2},{2,3},{5,4},{4,5},{7,6},{6,7},{9,8},{8,9},{11,10... | collective-permute-start | bytes 3096584 | tf_op jit(solution)/shard_map/ppermute | solution.py:34
  83.9 15.1 %collective-permute-start.24 = (bf16[14,96,384]{2,1,0:T(8,128)(2,1)S(1)}, bf16[14,96,384]{2,1,0:T(8,128)(2,1)S(1)}, u32[]{:S(2)}, u32[]{:S(2)}) collective-permute-start(bf16[14,96,384]{2,1,0:T(8,128)(2,1)S(1)} %collective-permute-done.11.refs_6_), channel_id=1, source_target_pairs={{1,0},{0,1},{3,2},{2,3},{5,4},{4,5},{7,6},{6,7},{9,8},{8,9},{11,10... | collective-permute-start | bytes 3096584 | tf_op jit(solution)/shard_map/ppermute | solution.py:34
  84.0 15.0 %collective-permute-start.20 = (bf16[2,4,32,384]{3,2,1,0:T(8,128)(2,1)S(1)}, bf16[2,4,32,384]{3,2,1,0:T(8,128)(2,1)S(1)}, u32[]{:S(2)}, u32[]{:S(2)}) collective-permute-start(bf16[2,4,32,384]{3,2,1,0:T(8,128)(2,1)S(1)} %constant_dynamic-slice_fusion.1), channel_id=1, source_target_pairs={{0,8},{1,9},{2,10},{3,11},{4,12},{5,13},{6,14},{7,15},{8,16},{9,17... | collective-permute-start | bytes 589832 | tf_op jit(solution)/shard_map/ppermute | solution.py:34
  85.9 13.1 %collective-permute-start.22 = (bf16[6,1,32,384]{3,2,1,0:T(8,128)(2,1)S(1)}, bf16[6,1,32,384]{3,2,1,0:T(8,128)(2,1)S(1)}, u32[]{:S(2)}, u32[]{:S(2)}) collective-permute-start(bf16[6,1,32,384]{3,2,1,0:T(8,128)(2,1)S(1)} %get-tuple-element.72), channel_id=1, source_target_pairs={{2,1},{1,2},{4,3},{3,4},{6,5},{5,6},{10,9},{9,10},{12,11},{11,12},... | collective-permute-start | bytes 442376 | tf_op jit(solution)/shard_map/ppermute | solution.py:34
  89.4 9.6 %collective-permute-start.21 = (bf16[2,1,32,384]{3,2,1,0:T(8,128)(2,1)S(1)}, bf16[2,1,32,384]{3,2,1,0:T(8,128)(2,1)S(1)}, u32[]{:S(2)}, u32[]{:S(2)}) collective-permute-start(bf16[2,1,32,384]{3,2,1,0:T(8,128)(2,1)S(1)} %constant_dynamic-slice_fusion), channel_id=1, source_target_pairs={{2,9},{1,10},{4,11},{3,12},{6,13},{5,14},{10,17},{9,18},{12,19},{1... | collective-permute-start | bytes 147464 | tf_op jit(solution)/shard_map/ppermute | solution.py:34
  99.1 1.8 %collective-permute-start.25 = (bf16[8,1,32,384]{3,2,1,0:T(8,128)(2,1)S(1)}, bf16[8,1,32,384]{3,2,1,0:T(8,128)(2,1)S(1)}, u32[]{:S(2)}, u32[]{:S(2)}) collective-permute-start(bf16[8,1,32,384]{3,2,1,0:T(8,128)(2,1)S(1)} %pad_maximum_fusion.3), channel_id=1, source_target_pairs={{1,0},{0,1},{3,2},{2,3},{5,4},{4,5},{7,6},{6,7},{9,8},{8,9},{11,10... | collective-permute-start | bytes 589832 | tf_op jit(solution)/shard_map/ppermute | solution.py:34
  100.8 2.6 %collective-permute-start.26 = (bf16[14,96,384]{2,1,0:T(8,128)(2,1)S(1)}, bf16[14,96,384]{2,1,0:T(8,128)(2,1)S(1)}, u32[]{:S(2)}, u32[]{:S(2)}) collective-permute-start(bf16[14,96,384]{2,1,0:T(8,128)(2,1)S(1)} %collective-permute-done.12.refs_7_), channel_id=1, source_target_pairs={{1,0},{0,1},{3,2},{2,3},{5,4},{4,5},{7,6},{6,7},{9,8},{8,9},{11,10... | collective-permute-start | bytes 3096584 | tf_op jit(solution)/shard_map/ppermute | solution.py:34
  (12 other events, 41.5 us)

commit v13 on v11

--- a/solution.py
+++ b/solution.py
@@ -352,21 +352,19 @@
     acts_one = norm_act(frames, gain_one)
     own = jnp.stack([own_half(kernel_one), own_half(kernel_two)])
     pieces = z_stage(own)
-    inner, outer = sides(acts_one)
-    ends, across = fetch(last_two(acts_one), before_in_group), fetch(outer, across_chips)
+    ends = fetch(last_two(acts_one), before_in_group)
     picks = make_picks(orders)
-    pieces, across, lag_weights, scalars = lax.optimization_barrier(
-        (pieces, across, lag_weights, scalars)
+    pieces, picks, lag_weights, scalars = lax.optimization_barrier(
+        (pieces, picks, lag_weights, scalars)
     )
 
     opposite = fetch(pieces, small_source(2))
     after = fetch(pieces, small_source(1))
     gated, ends = lax.optimization_barrier((pieces, ends))
     parts = [pieces, after, fetch(gated, small_source(-1)), opposite]
-    inner, outer = jnp.concatenate([sides(ends)[0], inner], 0), sides(ends)[1]
-    corners = fetch(outer, across_chips)
-    parts, corners = lax.optimization_barrier((parts, corners))
-    across = jnp.concatenate([corners, across], 0)
+    inner, outer = sides(jnp.concatenate([ends, acts_one], 0))
+    across = fetch(outer, across_chips)
+    parts, across = lax.optimization_barrier((parts, across))
 
     one_bundle, two_bundle = join_rows(parts, 0), join_rows(parts, 1)
     one_bundles = bulk_stage(one_bundle)

time: 116 us -> 114 us (0.983)
  waiting for transfers between devices: 27.7 us -> 38.6 us
  local copies, waits for them, and re-layouts: 9.07 us -> 3.34 us
  other arithmetic: 6.31 us -> 2.34 us
  Pallas kernels: 30.4 us -> 28.2 us
    ppermute x27 -> x26, waiting for transfers between devices: 27.7 us -> 38.6 us  [fetch(): return lax.ppermute(array, AXES, pairs)]
    unnamed x35 -> x19, local copies, waits for them, and re-layouts: 4.78 us -> 0.07 us
    mul x2, other arithmetic: 1.41 us -> 0.09 us  [channel_orders(): half.reshape(-1, 1) * SHARD + ramp]
    pallas_call x2, Pallas kernels: 21.1 us -> 19.8 us  [conv(): pl.pallas_call(lambda *refs: conv_body(*refs, finish=finish), out_shape=j...]
    ppermute x27 -> x26, starting transfers between devices: 39 us -> 38.2 us  [fetch(): return lax.ppermute(array, AXES, pairs)]
  transfers between devices with their start and end apart: 27 -> 26, of which waited for: 11 -> 15; matrix products, arithmetic and copies ran while one was open for 8% -> 4% of each run, Pallas kernels for 16% -> 16%
where the time goes in v13:
time: 114 us; the launch traced here: 113 us
  waiting for transfers between devices  38.6 us (34%)
  starting transfers between devices  38.2 us (34%)
  Pallas kernels  28.2 us (25%)
  local copies, waits for them, and re-layouts  3.34 us (3%)
  other arithmetic  2.34 us (2%)
  between operations  1.95 us (2%)
    ppermute x26, waiting for transfers between devices, fetch(): return lax.ppermute(array, AXES, pairs)  38.6 us
    ppermute x26, starting transfers between devices, fetch(): return lax.ppermute(array, AXES, pairs)  38.2 us
    pallas_call x2, Pallas kernels, conv(): pl.pallas_call(lambda *refs: conv_body(*refs, finish=finish), out_shape=j...  19.8 us
    pallas_call x2, Pallas kernels, spread_halo(): pl.pallas_call(spread_halo_body, out_shape=jax.ShapeDtypeStruct(spread.sh...  4.2 us
  transfers between devices with their start and end apart: 26, of which 15 were waited for; matrix products, arithmetic and copies ran while one was open for 4% of the time, Pallas kernels for 16%

profile of v13, /device:TPU:131, one launch (start us, length us, event | category | flops | bytes accessed | tf_op | source)
XLA Modules:
  0.0 112.6 jit_solution(18227793312332853418)
XLA Ops:
  0.0 1.1 constant_dynamic-slice_fusion.3
  1.3 2.1 %collective-permute-start = (bf16[2,168,384]{2,1,0:T(8,128)(2,1)S(1)}, bf16[2,168,384]{2,1,0:T(8,128)(2,1)S(1)}, u32[]{:S(2)}, u32[]{:S(2)}) collective-permute-start(bf16[2,168,384]{2,1,0:T(8,128)(2,1)S(1)} %constant_dynamic-update-slice_fusion), channel_id=1, source_target_pairs={{24,0},{1,1},{90,2},{67,3},{60,4},{37,5},{126,6},{103,7},{0,8},{9,... | collective-permute-start | bytes 774152 | tf_op jit(solution)/shard_map/ppermute | solution.py:34
  3.4 2.4 %collective-permute-start.1 = (bf16[2,168,384]{2,1,0:T(8,128)(2,1)S(1)}, bf16[2,168,384]{2,1,0:T(8,128)(2,1)S(1)}, u32[]{:S(2)}, u32[]{:S(2)}) collective-permute-start(bf16[2,168,384]{2,1,0:T(8,128)(2,1)S(1)} %constant_dynamic-update-slice_fusion), channel_id=1, source_target_pairs={{152,0},{129,1},{218,2},{195,3},{188,4},{165,5},{254,6},{231,7},{1... | collective-permute-start | bytes 774152 | tf_op jit(solution)/shard_map/ppermute | solution.py:34
  7.1 3.2 %collective-permute-start.3 = (bf16[2,4,32,384]{3,2,1,0:T(8,128)(2,1)S(1)}, bf16[2,4,32,384]{3,2,1,0:T(8,128)(2,1)S(1)}, u32[]{:S(2)}, u32[]{:S(2)}) collective-permute-start(bf16[2,4,32,384]{3,2,1,0:T(8,128)(2,1)S(1)} %constant_dynamic-slice_fusion.2), channel_id=1, source_target_pairs={{0,8},{1,9},{2,10},{3,11},{4,12},{5,13},{6,14},{7,15},{8,16},{9,17... | collective-permute-start | bytes 589832 | tf_op jit(solution)/shard_map/ppermute | solution.py:34
  14.5 1.6 %shard_map.127.picks = bf16[2,384,384]{2,1,0:T(8,128)(2,1)} custom-call(s32[2,384]{1,0:T(2,128)} %pad_add_fusion.order), custom_call_target="tpu_custom_call" | custom-call | flops 1000 | bytes 1000 | tf_op jit(solution)/shard_map/pallas_call | solution.py:126
  16.8 2.9 %collective-permute-start.2 = (bf16[2,2,168,384]{3,2,1,0:T(8,128)(2,1)S(1)}, bf16[2,2,168,384]{3,2,1,0:T(8,128)(2,1)S(1)}, u32[]{:S(2)}, u32[]{:S(2)}) collective-permute-start(bf16[2,2,168,384]{3,2,1,0:T(8,128)(2,1)S(1)} %pad_maximum_fusion.refs_0_), channel_id=1, source_target_pairs={{2,0},{9,1},{4,2},{11,3},{6,4},{13,5},{0,6},{15,7},{10,8},{17,9},{... | collective-permute-start | bytes 1548296 | tf_op jit(solution)/shard_map/ppermute | solution.py:34
  20.1 5.7 %collective-permute-done.3.ends = bf16[2,4,32,384]{3,2,1,0:T(8,128)(2,1)S(1)} collective-permute-done((bf16[2,4,32,384]{3,2,1,0:T(8,128)(2,1)S(1)}, bf16[2,4,32,384]{3,2,1,0:T(8,128)(2,1)S(1)}, u32[]{:S(2)}, u32[]{:S(2)}) %collective-permute-start.3) | collective-permute-done | bytes 196640 | tf_op jit(solution)/shard_map/ppermute | solution.py:34
  25.8 8.1 %collective-permute-start.6 = (bf16[8,1,32,384]{3,2,1,0:T(8,128)(2,1)S(1)}, bf16[8,1,32,384]{3,2,1,0:T(8,128)(2,1)S(1)}, u32[]{:S(2)}, u32[]{:S(2)}) collective-permute-start(bf16[8,1,32,384]{3,2,1,0:T(8,128)(2,1)S(1)} %broadcast_select_fusion.1), channel_id=1, source_target_pairs={{2,1},{1,2},{4,3},{3,4},{6,5},{5,6},{10,9},{9,10},{12,11},{11,12},... | collective-permute-start | bytes 589832 | tf_op jit(solution)/shard_map/ppermute | solution.py:34
  33.9 10.3 %collective-permute-done.6.across = bf16[8,1,32,384]{3,2,1,0:T(8,128)(2,1)S(1)} collective-permute-done((bf16[8,1,32,384]{3,2,1,0:T(8,128)(2,1)S(1)}, bf16[8,1,32,384]{3,2,1,0:T(8,128)(2,1)S(1)}, u32[]{:S(2)}, u32[]{:S(2)}) %collective-permute-start.6) | collective-permute-done | bytes 196640 | tf_op jit(solution)/shard_map/ppermute | solution.py:34
  44.6 2.7 %collective-permute-start.7 = (bf16[14,96,384]{2,1,0:T(8,128)(2,1)S(1)}, bf16[14,96,384]{2,1,0:T(8,128)(2,1)S(1)}, u32[]{:S(2)}, u32[]{:S(2)}) collective-permute-start(bf16[14,96,384]{2,1,0:T(8,128)(2,1)S(1)} %shard_map.129.refs_4_), channel_id=1, source_target_pairs={{1,0},{0,1},{3,2},{2,3},{5,4},{4,5},{7,6},{6,7},{9,8},{8,9},{11,10... | collective-permute-start | bytes 3096584 | tf_op jit(solution)/shard_map/ppermute | solution.py:34
  47.4 1.5 %collective-permute-start.13 = (bf16[14,96,384]{2,1,0:T(8,128)(2,1)S(1)}, bf16[14,96,384]{2,1,0:T(8,128)(2,1)S(1)}, u32[]{:S(2)}, u32[]{:S(2)}) collective-permute-start(bf16[14,96,384]{2,1,0:T(8,128)(2,1)S(1)} %shard_map.129.refs_4_), channel_id=1, source_target_pairs={{24,0},{7,1},{26,2},{1,3},{28,4},{3,5},{30,6},{5,7},{0,8},{15,9},{... | collective-permute-start | bytes 3096584 | tf_op jit(solution)/shard_map/ppermute | solution.py:34
  49.5 1.5 %collective-permute-done.8.refs_8_ = bf16[14,96,384]{2,1,0:T(8,128)(2,1)S(1)} collective-permute-done((bf16[14,96,384]{2,1,0:T(8,128)(2,1)S(1)}, bf16[14,96,384]{2,1,0:T(8,128)(2,1)S(1)}, u32[]{:S(2)}, u32[]{:S(2)}) %collective-permute-start.8) | collective-permute-done | bytes 1032224 | tf_op jit(solution)/shard_map/ppermute | solution.py:34
  51.4 1.1 shard_map.130._
  52.5 2.1 %shard_map.131.refs_2_ = bf16[2,8,6,32,1152]{4,3,2,1,0:T(8,128)(2,1)S(1)} custom-call(s32[2]{0:T(128)S(1)} %pad_add_fusion.1.scalars.refs_0_, bf16[2,384,384]{2,1,0:T(8,128)(2,1)S(1)} %copy-done, bf16[2,4,32,384]{3,2,1,0:T(8,128)(2,1)S(1)} %collective-permute-done.3.ends, ...), custom_call_target="tpu_custom_call", output_to_operand_aliasing={{}: (5, {})} | custom-call | flops 1000 | bytes 1000 | tf_op jit(solution)/shard_map/pallas_call | solution.py:186
  54.6 6.5 %collective-permute-done.12.refs_5_ = bf16[14,96,384]{2,1,0:T(8,128)(2,1)S(1)} collective-permute-done((bf16[14,96,384]{2,1,0:T(8,128)(2,1)S(1)}, bf16[14,96,384]{2,1,0:T(8,128)(2,1)S(1)}, u32[]{:S(2)}, u32[]{:S(2)}) %collective-permute-start.12) | collective-permute-done | bytes 1032224 | tf_op jit(solution)/shard_map/ppermute | solution.py:34
  61.1 1.5 %collective-permute-done.14.refs_7_ = bf16[14,96,384]{2,1,0:T(8,128)(2,1)S(1)} collective-permute-done((bf16[14,96,384]{2,1,0:T(8,128)(2,1)S(1)}, bf16[14,96,384]{2,1,0:T(8,128)(2,1)S(1)}, u32[]{:S(2)}, u32[]{:S(2)}) %collective-permute-start.14) | collective-permute-done | bytes 1032224 | tf_op jit(solution)/shard_map/ppermute | solution.py:34
  62.6 3.0 %collective-permute-start.16 = (bf16[14,96,384]{2,1,0:T(8,128)(2,1)S(1)}, bf16[14,96,384]{2,1,0:T(8,128)(2,1)S(1)}, u32[]{:S(2)}, u32[]{:S(2)}) collective-permute-start(bf16[14,96,384]{2,1,0:T(8,128)(2,1)S(1)} %collective-permute-done.12.refs_5_), channel_id=1, source_target_pairs={{1,0},{0,1},{3,2},{2,3},{5,4},{4,5},{7,6},{6,7},{9,8},{8,9},{11,10... | collective-permute-start | bytes 3096584 | tf_op jit(solution)/shard_map/ppermute | solution.py:34
  66.1 1.0 collective-permute-start.10
  67.2 0.7 collective-permute-done.16.refs_9_
  67.9 1.5 %collective-permute-done.17.refs_10_ = bf16[14,96,384]{2,1,0:T(8,128)(2,1)S(1)} collective-permute-done((bf16[14,96,384]{2,1,0:T(8,128)(2,1)S(1)}, bf16[14,96,384]{2,1,0:T(8,128)(2,1)S(1)}, u32[]{:S(2)}, u32[]{:S(2)}) %collective-permute-start.17) | collective-permute-done | bytes 1032224 | tf_op jit(solution)/shard_map/ppermute | solution.py:34
  69.4 1.5 %collective-permute-done.18.refs_11_ = bf16[14,96,384]{2,1,0:T(8,128)(2,1)S(1)} collective-permute-done((bf16[14,96,384]{2,1,0:T(8,128)(2,1)S(1)}, bf16[14,96,384]{2,1,0:T(8,128)(2,1)S(1)}, u32[]{:S(2)}, u32[]{:S(2)}) %collective-permute-start.18) | collective-permute-done | bytes 1032224 | tf_op jit(solution)/shard_map/ppermute | solution.py:34
  70.9 9.7 %shard_map.132 = bf16[6,128,384]{2,1,0:T(8,128)(2,1)S(1)} custom-call(s32[2]{0:T(128)S(1)} %pad_add_fusion.1.scalars.refs_0_, f32[3,6]{1,0:T(4,128)S(1)} %add_convert_fusion.refs_1_, bf16[2,8,6,32,1152]{4,3,2,1,0:T(8,128)(2,1)S(1)} %shard_map.131.refs_2_, f32[1,384]{1,0:T(1,128)S(1)} %reshape.334.refs_3_, bf16[14,96,384]{2,1,0:T(8,128)(2,1)S(1)} %shard_map.129.refs_4_, ...), custom_call_target="tpu_custom_call" | custom-call | flops 1000 | bytes 1000 | tf_op jit(solution)/shard_map/pallas_call | solution.py:287
  80.9 0.7 collective-permute-done.9.refs_5_
  81.7 1.2 %collective-permute-start.22 = (bf16[14,96,384]{2,1,0:T(8,128)(2,1)S(1)}, bf16[14,96,384]{2,1,0:T(8,128)(2,1)S(1)}, u32[]{:S(2)}, u32[]{:S(2)}) collective-permute-start(bf16[14,96,384]{2,1,0:T(8,128)(2,1)S(1)} %collective-permute-done.9.refs_5_), channel_id=1, source_target_pairs={{1,0},{0,1},{3,2},{2,3},{5,4},{4,5},{7,6},{6,7},{9,8},{8,9},{11,10... | collective-permute-start | bytes 3096584 | tf_op jit(solution)/shard_map/ppermute | solution.py:34
  83.0 1.9 %collective-permute-start.19 = (bf16[2,4,32,384]{3,2,1,0:T(8,128)(2,1)S(1)}, bf16[2,4,32,384]{3,2,1,0:T(8,128)(2,1)S(1)}, u32[]{:S(2)}, u32[]{:S(2)}) collective-permute-start(bf16[2,4,32,384]{3,2,1,0:T(8,128)(2,1)S(1)} %constant_dynamic-slice_fusion.1), channel_id=1, source_target_pairs={{0,8},{1,9},{2,10},{3,11},{4,12},{5,13},{6,14},{7,15},{8,16},{9,17... | collective-permute-start | bytes 589832 | tf_op jit(solution)/shard_map/ppermute | solution.py:34
  84.9 3.3 %collective-permute-start.21 = (bf16[6,1,32,384]{3,2,1,0:T(8,128)(2,1)S(1)}, bf16[6,1,32,384]{3,2,1,0:T(8,128)(2,1)S(1)}, u32[]{:S(2)}, u32[]{:S(2)}) collective-permute-start(bf16[6,1,32,384]{3,2,1,0:T(8,128)(2,1)S(1)} %get-tuple-element.72), channel_id=1, source_target_pairs={{2,1},{1,2},{4,3},{3,4},{6,5},{5,6},{10,9},{9,10},{12,11},{11,12},... | collective-permute-start | bytes 442376 | tf_op jit(solution)/shard_map/ppermute | solution.py:34
  88.2 3.1 %collective-permute-start.20 = (bf16[2,1,32,384]{3,2,1,0:T(8,128)(2,1)S(1)}, bf16[2,1,32,384]{3,2,1,0:T(8,128)(2,1)S(1)}, u32[]{:S(2)}, u32[]{:S(2)}) collective-permute-start(bf16[2,1,32,384]{3,2,1,0:T(8,128)(2,1)S(1)} %constant_dynamic-slice_fusion), channel_id=1, source_target_pairs={{2,9},{1,10},{4,11},{3,12},{6,13},{5,14},{10,17},{9,18},{12,19},{1... | collective-permute-start | bytes 147464 | tf_op jit(solution)/shard_map/ppermute | solution.py:34
  91.4 1.1 shard_map.133._
  92.5 5.4 %collective-permute-done.20 = bf16[2,1,32,384]{3,2,1,0:T(8,128)(2,1)S(1)} collective-permute-done((bf16[2,1,32,384]{3,2,1,0:T(8,128)(2,1)S(1)}, bf16[2,1,32,384]{3,2,1,0:T(8,128)(2,1)S(1)}, u32[]{:S(2)}, u32[]{:S(2)}) %collective-permute-start.20) | collective-permute-done | bytes 49184 | tf_op jit(solution)/shard_map/ppermute | solution.py:34
  98.3 1.4 %collective-permute-done.24.beside = bf16[8,1,32,384]{3,2,1,0:T(8,128)(2,1)S(1)} collective-permute-done((bf16[8,1,32,384]{3,2,1,0:T(8,128)(2,1)S(1)}, bf16[8,1,32,384]{3,2,1,0:T(8,128)(2,1)S(1)}, u32[]{:S(2)}, u32[]{:S(2)}) %collective-permute-start.24) | collective-permute-done | bytes 196640 | tf_op jit(solution)/shard_map/ppermute | solution.py:34
  99.9 2.1 %shard_map.134.refs_2_ = bf16[2,8,6,32,1152]{4,3,2,1,0:T(8,128)(2,1)S(1)} custom-call(s32[2]{0:T(128)S(1)} %pad_add_fusion.1.scalars.refs_0_, bf16[2,384,384]{2,1,0:T(8,128)(2,1)S(1)} %copy-done, bf16[2,4,32,384]{3,2,1,0:T(8,128)(2,1)S(1)} %collective-permute-done.19.ends, ...), custom_call_target="tpu_custom_call", output_to_operand_aliasing={{}: (5, {})} | custom-call | flops 1000 | bytes 1000 | tf_op jit(solution)/shard_map/pallas_call | solution.py:186
  102.3 10.1 %shard_map.135 = bf16[6,128,384]{2,1,0:T(8,128)(2,1)} custom-call(s32[2]{0:T(128)S(1)} %pad_add_fusion.1.scalars.refs_0_, f32[3,6]{1,0:T(4,128)S(1)} %add_convert_fusion.refs_1_, bf16[2,8,6,32,1152]{4,3,2,1,0:T(8,128)(2,1)S(1)} %shard_map.134.refs_2_, bf16[6,128,384]{2,1,0:T(8,128)(2,1)S(1)} %bitcast.31, bf16[14,96,384]{2,1,0:T(8,128)(2,1)S(1)} %shard_map.128.refs_4_, ...), custom_call_target="tpu_custom_call" | custom-call | flops 1000 | bytes 1000 | tf_op jit(solution)/shard_map/pallas_call | solution.py:287
  (95 shorter events, 8.7 us)
Async XLA Ops:
  1.2 9.1 %copy-start.6 = (s32[4]{0:T(128)S(1)}, s32[4]{0:T(128)}, u32[]{:S(2)}) copy-start(s32[4]{0:T(128)} %constant.162.clone) | copy-start | bytes 52
  1.3 9.1 %copy-start.7 = (s32[4]{0:T(128)S(1)}, s32[4]{0:T(128)}, u32[]{:S(2)}) copy-start(s32[4]{0:T(128)} %constant.164.clone) | copy-start | bytes 52
  1.3 9.2 %copy-start.5 = (s32[4]{0:T(128)S(1)}, s32[4]{0:T(128)}, u32[]{:S(2)}) copy-start(s32[4]{0:T(128)} %constant.163.clone) | copy-start | bytes 52
  1.3 9.4 %copy-start.2 = (s32[4,2]{1,0:T(4,128)S(1)}, s32[4,2]{1,0:T(4,128)}, u32[]{:S(2)}) copy-start(s32[4,2]{1,0:T(4,128)} %constant.161.clone) | copy-start | bytes 100
  1.3 15.4 %collective-permute-start = (bf16[2,168,384]{2,1,0:T(8,128)(2,1)S(1)}, bf16[2,168,384]{2,1,0:T(8,128)(2,1)S(1)}, u32[]{:S(2)}, u32[]{:S(2)}) collective-permute-start(bf16[2,168,384]{2,1,0:T(8,128)(2,1)S(1)} %constant_dynamic-update-slice_fusion), channel_id=1, source_target_pairs={{24,0},{1,1},{90,2},{67,3},{60,4},{37,5},{126,6},{103,7},{0,8},{9,... | collective-permute-start | bytes 774152 | tf_op jit(solution)/shard_map/ppermute | solution.py:34
  3.4 13.3 %collective-permute-start.1 = (bf16[2,168,384]{2,1,0:T(8,128)(2,1)S(1)}, bf16[2,168,384]{2,1,0:T(8,128)(2,1)S(1)}, u32[]{:S(2)}, u32[]{:S(2)}) collective-permute-start(bf16[2,168,384]{2,1,0:T(8,128)(2,1)S(1)} %constant_dynamic-update-slice_fusion), channel_id=1, source_target_pairs={{152,0},{129,1},{218,2},{195,3},{188,4},{165,5},{254,6},{231,7},{1... | collective-permute-start | bytes 774152 | tf_op jit(solution)/shard_map/ppermute | solution.py:34
  6.4 7.2 %copy-start.8 = (s32[3]{0:T(128)S(1)}, s32[3]{0:T(128)}, u32[]{:S(2)}) copy-start(s32[3]{0:T(128)} %param.14) | copy-start | bytes 40
  7.1 18.6 %collective-permute-start.3 = (bf16[2,4,32,384]{3,2,1,0:T(8,128)(2,1)S(1)}, bf16[2,4,32,384]{3,2,1,0:T(8,128)(2,1)S(1)}, u32[]{:S(2)}, u32[]{:S(2)}) collective-permute-start(bf16[2,4,32,384]{3,2,1,0:T(8,128)(2,1)S(1)} %constant_dynamic-slice_fusion.2), channel_id=1, source_target_pairs={{0,8},{1,9},{2,10},{3,11},{4,12},{5,13},{6,14},{7,15},{8,16},{9,17... | collective-permute-start | bytes 589832 | tf_op jit(solution)/shard_map/ppermute | solution.py:34
  16.8 27.4 %collective-permute-start.2 = (bf16[2,2,168,384]{3,2,1,0:T(8,128)(2,1)S(1)}, bf16[2,2,168,384]{3,2,1,0:T(8,128)(2,1)S(1)}, u32[]{:S(2)}, u32[]{:S(2)}) collective-permute-start(bf16[2,2,168,384]{3,2,1,0:T(8,128)(2,1)S(1)} %pad_maximum_fusion.refs_0_), channel_id=1, source_target_pairs={{2,0},{9,1},{4,2},{11,3},{6,4},{13,5},{0,6},{15,7},{10,8},{17,9},{... | collective-permute-start | bytes 1548296 | tf_op jit(solution)/shard_map/ppermute | solution.py:34
  19.7 24.5 %collective-permute-start.5 = (bf16[2,2,168,384]{3,2,1,0:T(8,128)(2,1)S(1)}, bf16[2,2,168,384]{3,2,1,0:T(8,128)(2,1)S(1)}, u32[]{:S(2)}, u32[]{:S(2)}) collective-permute-start(bf16[2,2,168,384]{3,2,1,0:T(8,128)(2,1)S(1)} %pad_maximum_fusion.refs_0_), channel_id=1, source_target_pairs={{4,0},{17,1},{6,2},{19,3},{0,4},{21,5},{2,6},{23,7},{12,8},{25,9},... | collective-permute-start | bytes 1548296 | tf_op jit(solution)/shard_map/ppermute | solution.py:34
  25.7 18.4 %collective-permute-start.4 = (bf16[2,2,168,384]{3,2,1,0:T(8,128)(2,1)S(1)}, bf16[2,2,168,384]{3,2,1,0:T(8,128)(2,1)S(1)}, u32[]{:S(2)}, u32[]{:S(2)}) collective-permute-start(bf16[2,2,168,384]{3,2,1,0:T(8,128)(2,1)S(1)} %pad_maximum_fusion.refs_0_), channel_id=1, source_target_pairs={{6,0},{25,1},{0,2},{27,3},{2,4},{29,5},{4,6},{31,7},{14,8},{1,9},{... | collective-permute-start | bytes 1548296 | tf_op jit(solution)/shard_map/ppermute | solution.py:34
  25.8 18.3 %collective-permute-start.6 = (bf16[8,1,32,384]{3,2,1,0:T(8,128)(2,1)S(1)}, bf16[8,1,32,384]{3,2,1,0:T(8,128)(2,1)S(1)}, u32[]{:S(2)}, u32[]{:S(2)}) collective-permute-start(bf16[8,1,32,384]{3,2,1,0:T(8,128)(2,1)S(1)} %broadcast_select_fusion.1), channel_id=1, source_target_pairs={{2,1},{1,2},{4,3},{3,4},{6,5},{5,6},{10,9},{9,10},{12,11},{11,12},... | collective-permute-start | bytes 589832 | tf_op jit(solution)/shard_map/ppermute | solution.py:34
  44.6 4.9 %collective-permute-start.7 = (bf16[14,96,384]{2,1,0:T(8,128)(2,1)S(1)}, bf16[14,96,384]{2,1,0:T(8,128)(2,1)S(1)}, u32[]{:S(2)}, u32[]{:S(2)}) collective-permute-start(bf16[14,96,384]{2,1,0:T(8,128)(2,1)S(1)} %shard_map.129.refs_4_), channel_id=1, source_target_pairs={{1,0},{0,1},{3,2},{2,3},{5,4},{4,5},{7,6},{6,7},{9,8},{8,9},{11,10... | collective-permute-start | bytes 3096584 | tf_op jit(solution)/shard_map/ppermute | solution.py:34
  47.3 3.7 %collective-permute-start.8 = (bf16[14,96,384]{2,1,0:T(8,128)(2,1)S(1)}, bf16[14,96,384]{2,1,0:T(8,128)(2,1)S(1)}, u32[]{:S(2)}, u32[]{:S(2)}) collective-permute-start(bf16[14,96,384]{2,1,0:T(8,128)(2,1)S(1)} %shard_map.128.refs_4_), channel_id=1, source_target_pairs={{1,0},{0,1},{3,2},{2,3},{5,4},{4,5},{7,6},{6,7},{9,8},{8,9},{11,10... | collective-permute-start | bytes 3096584 | tf_op jit(solution)/shard_map/ppermute | solution.py:34
  47.4 13.8 %collective-permute-start.12 = (bf16[14,96,384]{2,1,0:T(8,128)(2,1)S(1)}, bf16[14,96,384]{2,1,0:T(8,128)(2,1)S(1)}, u32[]{:S(2)}, u32[]{:S(2)}) collective-permute-start(bf16[14,96,384]{2,1,0:T(8,128)(2,1)S(1)} %shard_map.129.refs_4_), channel_id=1, source_target_pairs={{8,0},{3,1},{10,2},{5,3},{12,4},{7,5},{14,6},{1,7},{16,8},{11,9},{... | collective-permute-start | bytes 3096584 | tf_op jit(solution)/shard_map/ppermute | solution.py:34
  47.4 13.8 %collective-permute-start.13 = (bf16[14,96,384]{2,1,0:T(8,128)(2,1)S(1)}, bf16[14,96,384]{2,1,0:T(8,128)(2,1)S(1)}, u32[]{:S(2)}, u32[]{:S(2)}) collective-permute-start(bf16[14,96,384]{2,1,0:T(8,128)(2,1)S(1)} %shard_map.129.refs_4_), channel_id=1, source_target_pairs={{24,0},{7,1},{26,2},{1,3},{28,4},{3,5},{30,6},{5,7},{0,8},{15,9},{... | collective-permute-start | bytes 3096584 | tf_op jit(solution)/shard_map/ppermute | solution.py:34
  48.8 13.8 %collective-permute-start.14 = (bf16[14,96,384]{2,1,0:T(8,128)(2,1)S(1)}, bf16[14,96,384]{2,1,0:T(8,128)(2,1)S(1)}, u32[]{:S(2)}, u32[]{:S(2)}) collective-permute-start(bf16[14,96,384]{2,1,0:T(8,128)(2,1)S(1)} %shard_map.129.refs_4_), channel_id=1, source_target_pairs={{224,0},{33,1},{226,2},{35,3},{228,4},{37,5},{230,6},{39,7},{232,8... | collective-permute-start | bytes 3096584 | tf_op jit(solution)/shard_map/ppermute | solution.py:34
  51.0 1.5 %collective-permute-start.15 = (bf16[8,1,32,384]{3,2,1,0:T(8,128)(2,1)S(1)}, bf16[8,1,32,384]{3,2,1,0:T(8,128)(2,1)S(1)}, u32[]{:S(2)}, u32[]{:S(2)}) collective-permute-start(bf16[8,1,32,384]{3,2,1,0:T(8,128)(2,1)S(1)} %get-tuple-element.61), channel_id=1, source_target_pairs={{1,0},{0,1},{3,2},{2,3},{5,4},{4,5},{7,6},{6,7},{9,8},{8,9},{11,10... | collective-permute-start | bytes 589832 | tf_op jit(solution)/shard_map/ppermute | solution.py:34
  52.5 15.4 %copy-start.4 = (f32[384]{0:T(512)S(1)}, f32[384]{0:T(512)}, u32[]{:S(2)}) copy-start(f32[384]{0:T(512)} %param.20) | copy-start | bytes 4612
  62.6 5.3 %collective-permute-start.16 = (bf16[14,96,384]{2,1,0:T(8,128)(2,1)S(1)}, bf16[14,96,384]{2,1,0:T(8,128)(2,1)S(1)}, u32[]{:S(2)}, u32[]{:S(2)}) collective-permute-start(bf16[14,96,384]{2,1,0:T(8,128)(2,1)S(1)} %collective-permute-done.12.refs_5_), channel_id=1, source_target_pairs={{1,0},{0,1},{3,2},{2,3},{5,4},{4,5},{7,6},{6,7},{9,8},{8,9},{11,10... | collective-permute-start | bytes 3096584 | tf_op jit(solution)/shard_map/ppermute | solution.py:34
  65.6 3.7 %collective-permute-start.17 = (bf16[14,96,384]{2,1,0:T(8,128)(2,1)S(1)}, bf16[14,96,384]{2,1,0:T(8,128)(2,1)S(1)}, u32[]{:S(2)}, u32[]{:S(2)}) collective-permute-start(bf16[14,96,384]{2,1,0:T(8,128)(2,1)S(1)} %collective-permute-done.13.refs_6_), channel_id=1, source_target_pairs={{1,0},{0,1},{3,2},{2,3},{5,4},{4,5},{7,6},{6,7},{9,8},{8,9},{11,10... | collective-permute-start | bytes 3096584 | tf_op jit(solution)/shard_map/ppermute | solution.py:34
  65.6 5.2 %collective-permute-start.18 = (bf16[14,96,384]{2,1,0:T(8,128)(2,1)S(1)}, bf16[14,96,384]{2,1,0:T(8,128)(2,1)S(1)}, u32[]{:S(2)}, u32[]{:S(2)}) collective-permute-start(bf16[14,96,384]{2,1,0:T(8,128)(2,1)S(1)} %collective-permute-done.14.refs_7_), channel_id=1, source_target_pairs={{1,0},{0,1},{3,2},{2,3},{5,4},{4,5},{7,6},{6,7},{9,8},{8,9},{11,10... | collective-permute-start | bytes 3096584 | tf_op jit(solution)/shard_map/ppermute | solution.py:34
  66.1 14.4 %collective-permute-start.10 = (bf16[14,96,384]{2,1,0:T(8,128)(2,1)S(1)}, bf16[14,96,384]{2,1,0:T(8,128)(2,1)S(1)}, u32[]{:S(2)}, u32[]{:S(2)}) collective-permute-start(bf16[14,96,384]{2,1,0:T(8,128)(2,1)S(1)} %shard_map.128.refs_4_), channel_id=1, source_target_pairs={{24,0},{7,1},{26,2},{1,3},{28,4},{3,5},{30,6},{5,7},{0,8},{15,9},{... | collective-permute-start | bytes 3096584 | tf_op jit(solution)/shard_map/ppermute | solution.py:34
  67.2 13.8 %collective-permute-start.11 = (bf16[14,96,384]{2,1,0:T(8,128)(2,1)S(1)}, bf16[14,96,384]{2,1,0:T(8,128)(2,1)S(1)}, u32[]{:S(2)}, u32[]{:S(2)}) collective-permute-start(bf16[14,96,384]{2,1,0:T(8,128)(2,1)S(1)} %shard_map.128.refs_4_), channel_id=1, source_target_pairs={{224,0},{33,1},{226,2},{35,3},{228,4},{37,5},{230,6},{39,7},{232,8... | collective-permute-start | bytes 3096584 | tf_op jit(solution)/shard_map/ppermute | solution.py:34
  67.9 13.8 %collective-permute-start.9 = (bf16[14,96,384]{2,1,0:T(8,128)(2,1)S(1)}, bf16[14,96,384]{2,1,0:T(8,128)(2,1)S(1)}, u32[]{:S(2)}, u32[]{:S(2)}) collective-permute-start(bf16[14,96,384]{2,1,0:T(8,128)(2,1)S(1)} %shard_map.128.refs_4_), channel_id=1, source_target_pairs={{8,0},{3,1},{10,2},{5,3},{12,4},{7,5},{14,6},{1,7},{16,8},{11,9},{... | collective-permute-start | bytes 3096584 | tf_op jit(solution)/shard_map/ppermute | solution.py:34
  81.7 16.2 %collective-permute-start.22 = (bf16[14,96,384]{2,1,0:T(8,128)(2,1)S(1)}, bf16[14,96,384]{2,1,0:T(8,128)(2,1)S(1)}, u32[]{:S(2)}, u32[]{:S(2)}) collective-permute-start(bf16[14,96,384]{2,1,0:T(8,128)(2,1)S(1)} %collective-permute-done.9.refs_5_), channel_id=1, source_target_pairs={{1,0},{0,1},{3,2},{2,3},{5,4},{4,5},{7,6},{6,7},{9,8},{8,9},{11,10... | collective-permute-start | bytes 3096584 | tf_op jit(solution)/shard_map/ppermute | solution.py:34
  82.9 15.0 %collective-permute-start.23 = (bf16[14,96,384]{2,1,0:T(8,128)(2,1)S(1)}, bf16[14,96,384]{2,1,0:T(8,128)(2,1)S(1)}, u32[]{:S(2)}, u32[]{:S(2)}) collective-permute-start(bf16[14,96,384]{2,1,0:T(8,128)(2,1)S(1)} %collective-permute-done.10.refs_6_), channel_id=1, source_target_pairs={{1,0},{0,1},{3,2},{2,3},{5,4},{4,5},{7,6},{6,7},{9,8},{8,9},{11,10... | collective-permute-start | bytes 3096584 | tf_op jit(solution)/shard_map/ppermute | solution.py:34
  83.0 14.9 %collective-permute-start.19 = (bf16[2,4,32,384]{3,2,1,0:T(8,128)(2,1)S(1)}, bf16[2,4,32,384]{3,2,1,0:T(8,128)(2,1)S(1)}, u32[]{:S(2)}, u32[]{:S(2)}) collective-permute-start(bf16[2,4,32,384]{3,2,1,0:T(8,128)(2,1)S(1)} %constant_dynamic-slice_fusion.1), channel_id=1, source_target_pairs={{0,8},{1,9},{2,10},{3,11},{4,12},{5,13},{6,14},{7,15},{8,16},{9,17... | collective-permute-start | bytes 589832 | tf_op jit(solution)/shard_map/ppermute | solution.py:34
  84.9 12.9 %collective-permute-start.21 = (bf16[6,1,32,384]{3,2,1,0:T(8,128)(2,1)S(1)}, bf16[6,1,32,384]{3,2,1,0:T(8,128)(2,1)S(1)}, u32[]{:S(2)}, u32[]{:S(2)}) collective-permute-start(bf16[6,1,32,384]{3,2,1,0:T(8,128)(2,1)S(1)} %get-tuple-element.72), channel_id=1, source_target_pairs={{2,1},{1,2},{4,3},{3,4},{6,5},{5,6},{10,9},{9,10},{12,11},{11,12},... | collective-permute-start | bytes 442376 | tf_op jit(solution)/shard_map/ppermute | solution.py:34
  88.2 9.6 %collective-permute-start.20 = (bf16[2,1,32,384]{3,2,1,0:T(8,128)(2,1)S(1)}, bf16[2,1,32,384]{3,2,1,0:T(8,128)(2,1)S(1)}, u32[]{:S(2)}, u32[]{:S(2)}) collective-permute-start(bf16[2,1,32,384]{3,2,1,0:T(8,128)(2,1)S(1)} %constant_dynamic-slice_fusion), channel_id=1, source_target_pairs={{2,9},{1,10},{4,11},{3,12},{6,13},{5,14},{10,17},{9,18},{12,19},{1... | collective-permute-start | bytes 147464 | tf_op jit(solution)/shard_map/ppermute | solution.py:34
  97.9 1.8 %collective-permute-start.24 = (bf16[8,1,32,384]{3,2,1,0:T(8,128)(2,1)S(1)}, bf16[8,1,32,384]{3,2,1,0:T(8,128)(2,1)S(1)}, u32[]{:S(2)}, u32[]{:S(2)}) collective-permute-start(bf16[8,1,32,384]{3,2,1,0:T(8,128)(2,1)S(1)} %pad_maximum_fusion.3), channel_id=1, source_target_pairs={{1,0},{0,1},{3,2},{2,3},{5,4},{4,5},{7,6},{6,7},{9,8},{8,9},{11,10... | collective-permute-start | bytes 589832 | tf_op jit(solution)/shard_map/ppermute | solution.py:34
  99.7 2.6 %collective-permute-start.25 = (bf16[14,96,384]{2,1,0:T(8,128)(2,1)S(1)}, bf16[14,96,384]{2,1,0:T(8,128)(2,1)S(1)}, u32[]{:S(2)}, u32[]{:S(2)}) collective-permute-start(bf16[14,96,384]{2,1,0:T(8,128)(2,1)S(1)} %collective-permute-done.11.refs_7_), channel_id=1, source_target_pairs={{1,0},{0,1},{3,2},{2,3},{5,4},{4,5},{7,6},{6,7},{9,8},{8,9},{11,10... | collective-permute-start | bytes 3096584 | tf_op jit(solution)/shard_map/ppermute | solution.py:34
  (3 other events, 20.1 us)

commit v14 on v13

--- a/solution.py
+++ b/solution.py
@@ -385,20 +385,19 @@
         scalars, lag_weights, spread, gain_two.reshape(1, C), one_bundles, one_others, finish_norm
     ).reshape(frames.shape)
 
-    two_bundles, acts_two = lax.optimization_barrier((two_bundles, acts_two))
     inner, outer = sides(acts_two)
     ends, corners, outer = lax.optimization_barrier((last_two(acts_two), last_two(outer), outer))
     ends = fetch(ends, before_in_group)
     across = fetch(outer, across_chips)
     corners = fetch(corners, across_and_before)
-    two_others += [fetch(b, sibling) for b in two_bundles[1:3]]
     spread = spread_inner(picks, acts_two)
-    ends, corners, across, spread, two_others = lax.optimization_barrier(
-        (ends, corners, across, spread, two_others)
+    ends, corners, across, spread, two_bundles = lax.optimization_barrier(
+        (ends, corners, across, spread, two_bundles)
     )
     beside = fetch(jnp.concatenate([sides(ends)[0], inner], 0), sibling)
-    two_last, beside = lax.optimization_barrier((two_bundles[3], beside))
-    two_others.append(fetch(two_last, sibling))
+    two_others.append(fetch(two_bundles[1], sibling))
+    two_last, beside = lax.optimization_barrier((two_bundles[2:], beside))
+    two_others += [fetch(b, sibling) for b in two_last]
     across = jnp.concatenate([corners, across], 0)
     spread = spread_halo(scalars, picks, ends, beside, across, spread)
     result = conv(

time: 114 us -> 112 us (0.982)
  starting transfers between devices: 38.2 us -> 36.8 us
    ppermute x26, starting transfers between devices: 38.2 us -> 36.8 us  [fetch(): return lax.ppermute(array, AXES, pairs)]
  transfers between devices with their start and end apart: 26 -> 26, of which waited for: 15 -> 14; matrix products, arithmetic and copies ran while one was open for 4% -> 4% of each run, Pallas kernels for 16% -> 16%
where the time goes in v14:
time: 112 us
  waiting for transfers between devices  39.1 us (35%)
  starting transfers between devices  36.8 us (33%)
  Pallas kernels  28.1 us (25%)
  local copies, waits for them, and re-layouts  3.34 us (3%)
  other arithmetic  2.34 us (2%)
  between operations  1.96 us (2%)
    ppermute x26, waiting for transfers between devices, fetch(): return lax.ppermute(array, AXES, pairs)  39.1 us
    ppermute x26, starting transfers between devices, fetch(): return lax.ppermute(array, AXES, pairs)  36.8 us
    pallas_call x2, Pallas kernels, conv(): pl.pallas_call(lambda *refs: conv_body(*refs, finish=finish), out_shape=j...  19.8 us
    pallas_call x2, Pallas kernels, spread_halo(): pl.pallas_call(spread_halo_body, out_shape=jax.ShapeDtypeStruct(spread.sh...  4.19 us
  transfers between devices with their start and end apart: 26, of which 14 were waited for; matrix products, arithmetic and copies ran while one was open for 4% of the time, Pallas kernels for 16%

profile of v14, /device:TPU:131, one launch (start us, length us, event | category | flops | bytes accessed | tf_op | source)
XLA Modules:
  0.0 111.7 jit_solution(8807138412309968513)
XLA Ops:
  0.0 1.1 constant_dynamic-slice_fusion.3
  1.3 2.1 %collective-permute-start = (bf16[2,168,384]{2,1,0:T(8,128)(2,1)S(1)}, bf16[2,168,384]{2,1,0:T(8,128)(2,1)S(1)}, u32[]{:S(2)}, u32[]{:S(2)}) collective-permute-start(bf16[2,168,384]{2,1,0:T(8,128)(2,1)S(1)} %constant_dynamic-update-slice_fusion), channel_id=1, source_target_pairs={{24,0},{1,1},{90,2},{67,3},{60,4},{37,5},{126,6},{103,7},{0,8},{9,... | collective-permute-start | bytes 774152 | tf_op jit(solution)/shard_map/ppermute | solution.py:34
  3.4 2.4 %collective-permute-start.1 = (bf16[2,168,384]{2,1,0:T(8,128)(2,1)S(1)}, bf16[2,168,384]{2,1,0:T(8,128)(2,1)S(1)}, u32[]{:S(2)}, u32[]{:S(2)}) collective-permute-start(bf16[2,168,384]{2,1,0:T(8,128)(2,1)S(1)} %constant_dynamic-update-slice_fusion), channel_id=1, source_target_pairs={{152,0},{129,1},{218,2},{195,3},{188,4},{165,5},{254,6},{231,7},{1... | collective-permute-start | bytes 774152 | tf_op jit(solution)/shard_map/ppermute | solution.py:34
  7.1 3.2 %collective-permute-start.3 = (bf16[2,4,32,384]{3,2,1,0:T(8,128)(2,1)S(1)}, bf16[2,4,32,384]{3,2,1,0:T(8,128)(2,1)S(1)}, u32[]{:S(2)}, u32[]{:S(2)}) collective-permute-start(bf16[2,4,32,384]{3,2,1,0:T(8,128)(2,1)S(1)} %constant_dynamic-slice_fusion.2), channel_id=1, source_target_pairs={{0,8},{1,9},{2,10},{3,11},{4,12},{5,13},{6,14},{7,15},{8,16},{9,17... | collective-permute-start | bytes 589832 | tf_op jit(solution)/shard_map/ppermute | solution.py:34
  13.8 0.6 pad_add_fusion.order
  14.5 1.6 %shard_map.127.picks = bf16[2,384,384]{2,1,0:T(8,128)(2,1)} custom-call(s32[2,384]{1,0:T(2,128)} %pad_add_fusion.order), custom_call_target="tpu_custom_call" | custom-call | flops 1000 | bytes 1000 | tf_op jit(solution)/shard_map/pallas_call | solution.py:126
  16.8 2.9 %collective-permute-start.2 = (bf16[2,2,168,384]{3,2,1,0:T(8,128)(2,1)S(1)}, bf16[2,2,168,384]{3,2,1,0:T(8,128)(2,1)S(1)}, u32[]{:S(2)}, u32[]{:S(2)}) collective-permute-start(bf16[2,2,168,384]{3,2,1,0:T(8,128)(2,1)S(1)} %pad_maximum_fusion.refs_0_), channel_id=1, source_target_pairs={{2,0},{9,1},{4,2},{11,3},{6,4},{13,5},{0,6},{15,7},{10,8},{17,9},{... | collective-permute-start | bytes 1548296 | tf_op jit(solution)/shard_map/ppermute | solution.py:34
  20.1 5.7 %collective-permute-done.3.ends = bf16[2,4,32,384]{3,2,1,0:T(8,128)(2,1)S(1)} collective-permute-done((bf16[2,4,32,384]{3,2,1,0:T(8,128)(2,1)S(1)}, bf16[2,4,32,384]{3,2,1,0:T(8,128)(2,1)S(1)}, u32[]{:S(2)}, u32[]{:S(2)}) %collective-permute-start.3) | collective-permute-done | bytes 196640 | tf_op jit(solution)/shard_map/ppermute | solution.py:34
  25.8 8.1 %collective-permute-start.6 = (bf16[8,1,32,384]{3,2,1,0:T(8,128)(2,1)S(1)}, bf16[8,1,32,384]{3,2,1,0:T(8,128)(2,1)S(1)}, u32[]{:S(2)}, u32[]{:S(2)}) collective-permute-start(bf16[8,1,32,384]{3,2,1,0:T(8,128)(2,1)S(1)} %broadcast_select_fusion.1), channel_id=1, source_target_pairs={{2,1},{1,2},{4,3},{3,4},{6,5},{5,6},{10,9},{9,10},{12,11},{11,12},... | collective-permute-start | bytes 589832 | tf_op jit(solution)/shard_map/ppermute | solution.py:34
  33.9 10.3 %collective-permute-done.6.across = bf16[8,1,32,384]{3,2,1,0:T(8,128)(2,1)S(1)} collective-permute-done((bf16[8,1,32,384]{3,2,1,0:T(8,128)(2,1)S(1)}, bf16[8,1,32,384]{3,2,1,0:T(8,128)(2,1)S(1)}, u32[]{:S(2)}, u32[]{:S(2)}) %collective-permute-start.6) | collective-permute-done | bytes 196640 | tf_op jit(solution)/shard_map/ppermute | solution.py:34
  44.6 2.7 %collective-permute-start.10 = (bf16[14,96,384]{2,1,0:T(8,128)(2,1)S(1)}, bf16[14,96,384]{2,1,0:T(8,128)(2,1)S(1)}, u32[]{:S(2)}, u32[]{:S(2)}) collective-permute-start(bf16[14,96,384]{2,1,0:T(8,128)(2,1)S(1)} %shard_map.128.refs_4_), channel_id=1, source_target_pairs={{1,0},{0,1},{3,2},{2,3},{5,4},{4,5},{7,6},{6,7},{9,8},{8,9},{11,10... | collective-permute-start | bytes 3096584 | tf_op jit(solution)/shard_map/ppermute | solution.py:34
  47.4 1.5 %collective-permute-start.8 = (bf16[14,96,384]{2,1,0:T(8,128)(2,1)S(1)}, bf16[14,96,384]{2,1,0:T(8,128)(2,1)S(1)}, u32[]{:S(2)}, u32[]{:S(2)}) collective-permute-start(bf16[14,96,384]{2,1,0:T(8,128)(2,1)S(1)} %shard_map.128.refs_4_), channel_id=1, source_target_pairs={{24,0},{7,1},{26,2},{1,3},{28,4},{3,5},{30,6},{5,7},{0,8},{15,9},{... | collective-permute-start | bytes 3096584 | tf_op jit(solution)/shard_map/ppermute | solution.py:34
  48.8 0.7 collective-permute-done.10.refs_8_
  49.5 1.5 %collective-permute-done.11.refs_8_ = bf16[14,96,384]{2,1,0:T(8,128)(2,1)S(1)} collective-permute-done((bf16[14,96,384]{2,1,0:T(8,128)(2,1)S(1)}, bf16[14,96,384]{2,1,0:T(8,128)(2,1)S(1)}, u32[]{:S(2)}, u32[]{:S(2)}) %collective-permute-start.11) | collective-permute-done | bytes 1032224 | tf_op jit(solution)/shard_map/ppermute | solution.py:34
  51.4 1.1 shard_map.130._
  52.5 2.1 %shard_map.131.refs_2_ = bf16[2,8,6,32,1152]{4,3,2,1,0:T(8,128)(2,1)S(1)} custom-call(s32[2]{0:T(128)S(1)} %pad_add_fusion.1.scalars.refs_0_, bf16[2,384,384]{2,1,0:T(8,128)(2,1)S(1)} %copy-done, bf16[2,4,32,384]{3,2,1,0:T(8,128)(2,1)S(1)} %collective-permute-done.3.ends, ...), custom_call_target="tpu_custom_call", output_to_operand_aliasing={{}: (5, {})} | custom-call | flops 1000 | bytes 1000 | tf_op jit(solution)/shard_map/pallas_call | solution.py:186
  54.6 6.5 %collective-permute-done.7.refs_5_ = bf16[14,96,384]{2,1,0:T(8,128)(2,1)S(1)} collective-permute-done((bf16[14,96,384]{2,1,0:T(8,128)(2,1)S(1)}, bf16[14,96,384]{2,1,0:T(8,128)(2,1)S(1)}, u32[]{:S(2)}, u32[]{:S(2)}) %collective-permute-start.7) | collective-permute-done | bytes 1032224 | tf_op jit(solution)/shard_map/ppermute | solution.py:34
  61.1 1.5 %collective-permute-done.9.refs_7_ = bf16[14,96,384]{2,1,0:T(8,128)(2,1)S(1)} collective-permute-done((bf16[14,96,384]{2,1,0:T(8,128)(2,1)S(1)}, bf16[14,96,384]{2,1,0:T(8,128)(2,1)S(1)}, u32[]{:S(2)}, u32[]{:S(2)}) %collective-permute-start.9) | collective-permute-done | bytes 1032224 | tf_op jit(solution)/shard_map/ppermute | solution.py:34
  62.6 3.0 %collective-permute-start.13 = (bf16[14,96,384]{2,1,0:T(8,128)(2,1)S(1)}, bf16[14,96,384]{2,1,0:T(8,128)(2,1)S(1)}, u32[]{:S(2)}, u32[]{:S(2)}) collective-permute-start(bf16[14,96,384]{2,1,0:T(8,128)(2,1)S(1)} %collective-permute-done.7.refs_5_), channel_id=1, source_target_pairs={{1,0},{0,1},{3,2},{2,3},{5,4},{4,5},{7,6},{6,7},{9,8},{8,9},{11,10... | collective-permute-start | bytes 3096584 | tf_op jit(solution)/shard_map/ppermute | solution.py:34
  66.2 1.5 %collective-permute-start.20 = (bf16[14,96,384]{2,1,0:T(8,128)(2,1)S(1)}, bf16[14,96,384]{2,1,0:T(8,128)(2,1)S(1)}, u32[]{:S(2)}, u32[]{:S(2)}) collective-permute-start(bf16[14,96,384]{2,1,0:T(8,128)(2,1)S(1)} %shard_map.129.refs_4_), channel_id=1, source_target_pairs={{24,0},{7,1},{26,2},{1,3},{28,4},{3,5},{30,6},{5,7},{0,8},{15,9},{... | collective-permute-start | bytes 3096584 | tf_op jit(solution)/shard_map/ppermute | solution.py:34
  67.9 1.5 %collective-permute-done.14.refs_10_ = bf16[14,96,384]{2,1,0:T(8,128)(2,1)S(1)} collective-permute-done((bf16[14,96,384]{2,1,0:T(8,128)(2,1)S(1)}, bf16[14,96,384]{2,1,0:T(8,128)(2,1)S(1)}, u32[]{:S(2)}, u32[]{:S(2)}) %collective-permute-start.14) | collective-permute-done | bytes 1032224 | tf_op jit(solution)/shard_map/ppermute | solution.py:34
  69.4 1.5 %collective-permute-done.15.refs_11_ = bf16[14,96,384]{2,1,0:T(8,128)(2,1)S(1)} collective-permute-done((bf16[14,96,384]{2,1,0:T(8,128)(2,1)S(1)}, bf16[14,96,384]{2,1,0:T(8,128)(2,1)S(1)}, u32[]{:S(2)}, u32[]{:S(2)}) %collective-permute-start.15) | collective-permute-done | bytes 1032224 | tf_op jit(solution)/shard_map/ppermute | solution.py:34
  70.9 9.7 %shard_map.132 = bf16[6,128,384]{2,1,0:T(8,128)(2,1)S(1)} custom-call(s32[2]{0:T(128)S(1)} %pad_add_fusion.1.scalars.refs_0_, f32[3,6]{1,0:T(4,128)S(1)} %add_convert_fusion.refs_1_, bf16[2,8,6,32,1152]{4,3,2,1,0:T(8,128)(2,1)S(1)} %shard_map.131.refs_2_, f32[1,384]{1,0:T(1,128)S(1)} %reshape.331.refs_3_, bf16[14,96,384]{2,1,0:T(8,128)(2,1)S(1)} %shard_map.128.refs_4_, ...), custom_call_target="tpu_custom_call" | custom-call | flops 1000 | bytes 1000 | tf_op jit(solution)/shard_map/pallas_call | solution.py:287
  80.6 1.9 %collective-permute-start.16 = (bf16[2,4,32,384]{3,2,1,0:T(8,128)(2,1)S(1)}, bf16[2,4,32,384]{3,2,1,0:T(8,128)(2,1)S(1)}, u32[]{:S(2)}, u32[]{:S(2)}) collective-permute-start(bf16[2,4,32,384]{3,2,1,0:T(8,128)(2,1)S(1)} %constant_dynamic-slice_fusion.1), channel_id=1, source_target_pairs={{0,8},{1,9},{2,10},{3,11},{4,12},{5,13},{6,14},{7,15},{8,16},{9,17... | collective-permute-start | bytes 589832 | tf_op jit(solution)/shard_map/ppermute | solution.py:34
  82.6 3.2 %collective-permute-start.18 = (bf16[6,1,32,384]{3,2,1,0:T(8,128)(2,1)S(1)}, bf16[6,1,32,384]{3,2,1,0:T(8,128)(2,1)S(1)}, u32[]{:S(2)}, u32[]{:S(2)}) collective-permute-start(bf16[6,1,32,384]{3,2,1,0:T(8,128)(2,1)S(1)} %get-tuple-element.67), channel_id=1, source_target_pairs={{2,1},{1,2},{4,3},{3,4},{6,5},{5,6},{10,9},{9,10},{12,11},{11,12},... | collective-permute-start | bytes 442376 | tf_op jit(solution)/shard_map/ppermute | solution.py:34
  85.7 1.9 %collective-permute-start.17 = (bf16[2,1,32,384]{3,2,1,0:T(8,128)(2,1)S(1)}, bf16[2,1,32,384]{3,2,1,0:T(8,128)(2,1)S(1)}, u32[]{:S(2)}, u32[]{:S(2)}) collective-permute-start(bf16[2,1,32,384]{3,2,1,0:T(8,128)(2,1)S(1)} %constant_dynamic-slice_fusion), channel_id=1, source_target_pairs={{2,9},{1,10},{4,11},{3,12},{6,13},{5,14},{10,17},{9,18},{12,19},{1... | collective-permute-start | bytes 147464 | tf_op jit(solution)/shard_map/ppermute | solution.py:34
  87.7 1.1 shard_map.133._
  88.8 6.6 %collective-permute-done.17 = bf16[2,1,32,384]{3,2,1,0:T(8,128)(2,1)S(1)} collective-permute-done((bf16[2,1,32,384]{3,2,1,0:T(8,128)(2,1)S(1)}, bf16[2,1,32,384]{3,2,1,0:T(8,128)(2,1)S(1)}, u32[]{:S(2)}, u32[]{:S(2)}) %collective-permute-start.17) | collective-permute-done | bytes 49184 | tf_op jit(solution)/shard_map/ppermute | solution.py:34
  96.0 0.9 collective-permute-done.22.beside
  97.5 2.1 %shard_map.134.refs_2_ = bf16[2,8,6,32,1152]{4,3,2,1,0:T(8,128)(2,1)S(1)} custom-call(s32[2]{0:T(128)S(1)} %pad_add_fusion.1.scalars.refs_0_, bf16[2,384,384]{2,1,0:T(8,128)(2,1)S(1)} %copy-done, bf16[2,4,32,384]{3,2,1,0:T(8,128)(2,1)S(1)} %collective-permute-done.16.ends, ...), custom_call_target="tpu_custom_call", output_to_operand_aliasing={{}: (5, {})} | custom-call | flops 1000 | bytes 1000 | tf_op jit(solution)/shard_map/pallas_call | solution.py:186
  99.9 1.5 %collective-permute-done.25.refs_11_ = bf16[14,96,384]{2,1,0:T(8,128)(2,1)S(1)} collective-permute-done((bf16[14,96,384]{2,1,0:T(8,128)(2,1)S(1)}, bf16[14,96,384]{2,1,0:T(8,128)(2,1)S(1)}, u32[]{:S(2)}, u32[]{:S(2)}) %collective-permute-start.25) | collective-permute-done | bytes 1032224 | tf_op jit(solution)/shard_map/ppermute | solution.py:34
  101.4 10.1 %shard_map.135 = bf16[6,128,384]{2,1,0:T(8,128)(2,1)} custom-call(s32[2]{0:T(128)S(1)} %pad_add_fusion.1.scalars.refs_0_, f32[3,6]{1,0:T(4,128)S(1)} %add_convert_fusion.refs_1_, bf16[2,8,6,32,1152]{4,3,2,1,0:T(8,128)(2,1)S(1)} %shard_map.134.refs_2_, bf16[6,128,384]{2,1,0:T(8,128)(2,1)S(1)} %bitcast.31, bf16[14,96,384]{2,1,0:T(8,128)(2,1)S(1)} %shard_map.129.refs_4_, ...), custom_call_target="tpu_custom_call" | custom-call | flops 1000 | bytes 1000 | tf_op jit(solution)/shard_map/pallas_call | solution.py:287
  (95 shorter events, 7.9 us)
Async XLA Ops:
  1.2 9.1 %copy-start.6 = (s32[4]{0:T(128)S(1)}, s32[4]{0:T(128)}, u32[]{:S(2)}) copy-start(s32[4]{0:T(128)} %constant.162.clone) | copy-start | bytes 52
  1.3 9.1 %copy-start.7 = (s32[4]{0:T(128)S(1)}, s32[4]{0:T(128)}, u32[]{:S(2)}) copy-start(s32[4]{0:T(128)} %constant.164.clone) | copy-start | bytes 52
  1.3 9.2 %copy-start.5 = (s32[4]{0:T(128)S(1)}, s32[4]{0:T(128)}, u32[]{:S(2)}) copy-start(s32[4]{0:T(128)} %constant.163.clone) | copy-start | bytes 52
  1.3 9.4 %copy-start.2 = (s32[4,2]{1,0:T(4,128)S(1)}, s32[4,2]{1,0:T(4,128)}, u32[]{:S(2)}) copy-start(s32[4,2]{1,0:T(4,128)} %constant.161.clone) | copy-start | bytes 100
  1.3 15.4 %collective-permute-start = (bf16[2,168,384]{2,1,0:T(8,128)(2,1)S(1)}, bf16[2,168,384]{2,1,0:T(8,128)(2,1)S(1)}, u32[]{:S(2)}, u32[]{:S(2)}) collective-permute-start(bf16[2,168,384]{2,1,0:T(8,128)(2,1)S(1)} %constant_dynamic-update-slice_fusion), channel_id=1, source_target_pairs={{24,0},{1,1},{90,2},{67,3},{60,4},{37,5},{126,6},{103,7},{0,8},{9,... | collective-permute-start | bytes 774152 | tf_op jit(solution)/shard_map/ppermute | solution.py:34
  3.4 13.3 %collective-permute-start.1 = (bf16[2,168,384]{2,1,0:T(8,128)(2,1)S(1)}, bf16[2,168,384]{2,1,0:T(8,128)(2,1)S(1)}, u32[]{:S(2)}, u32[]{:S(2)}) collective-permute-start(bf16[2,168,384]{2,1,0:T(8,128)(2,1)S(1)} %constant_dynamic-update-slice_fusion), channel_id=1, source_target_pairs={{152,0},{129,1},{218,2},{195,3},{188,4},{165,5},{254,6},{231,7},{1... | collective-permute-start | bytes 774152 | tf_op jit(solution)/shard_map/ppermute | solution.py:34
  6.4 7.2 %copy-start.8 = (s32[3]{0:T(128)S(1)}, s32[3]{0:T(128)}, u32[]{:S(2)}) copy-start(s32[3]{0:T(128)} %param.14) | copy-start | bytes 40
  7.1 18.6 %collective-permute-start.3 = (bf16[2,4,32,384]{3,2,1,0:T(8,128)(2,1)S(1)}, bf16[2,4,32,384]{3,2,1,0:T(8,128)(2,1)S(1)}, u32[]{:S(2)}, u32[]{:S(2)}) collective-permute-start(bf16[2,4,32,384]{3,2,1,0:T(8,128)(2,1)S(1)} %constant_dynamic-slice_fusion.2), channel_id=1, source_target_pairs={{0,8},{1,9},{2,10},{3,11},{4,12},{5,13},{6,14},{7,15},{8,16},{9,17... | collective-permute-start | bytes 589832 | tf_op jit(solution)/shard_map/ppermute | solution.py:34
  16.8 27.4 %collective-permute-start.2 = (bf16[2,2,168,384]{3,2,1,0:T(8,128)(2,1)S(1)}, bf16[2,2,168,384]{3,2,1,0:T(8,128)(2,1)S(1)}, u32[]{:S(2)}, u32[]{:S(2)}) collective-permute-start(bf16[2,2,168,384]{3,2,1,0:T(8,128)(2,1)S(1)} %pad_maximum_fusion.refs_0_), channel_id=1, source_target_pairs={{2,0},{9,1},{4,2},{11,3},{6,4},{13,5},{0,6},{15,7},{10,8},{17,9},{... | collective-permute-start | bytes 1548296 | tf_op jit(solution)/shard_map/ppermute | solution.py:34
  19.7 24.5 %collective-permute-start.5 = (bf16[2,2,168,384]{3,2,1,0:T(8,128)(2,1)S(1)}, bf16[2,2,168,384]{3,2,1,0:T(8,128)(2,1)S(1)}, u32[]{:S(2)}, u32[]{:S(2)}) collective-permute-start(bf16[2,2,168,384]{3,2,1,0:T(8,128)(2,1)S(1)} %pad_maximum_fusion.refs_0_), channel_id=1, source_target_pairs={{4,0},{17,1},{6,2},{19,3},{0,4},{21,5},{2,6},{23,7},{12,8},{25,9},... | collective-permute-start | bytes 1548296 | tf_op jit(solution)/shard_map/ppermute | solution.py:34
  25.7 18.4 %collective-permute-start.4 = (bf16[2,2,168,384]{3,2,1,0:T(8,128)(2,1)S(1)}, bf16[2,2,168,384]{3,2,1,0:T(8,128)(2,1)S(1)}, u32[]{:S(2)}, u32[]{:S(2)}) collective-permute-start(bf16[2,2,168,384]{3,2,1,0:T(8,128)(2,1)S(1)} %pad_maximum_fusion.refs_0_), channel_id=1, source_target_pairs={{6,0},{25,1},{0,2},{27,3},{2,4},{29,5},{4,6},{31,7},{14,8},{1,9},{... | collective-permute-start | bytes 1548296 | tf_op jit(solution)/shard_map/ppermute | solution.py:34
  25.8 18.3 %collective-permute-start.6 = (bf16[8,1,32,384]{3,2,1,0:T(8,128)(2,1)S(1)}, bf16[8,1,32,384]{3,2,1,0:T(8,128)(2,1)S(1)}, u32[]{:S(2)}, u32[]{:S(2)}) collective-permute-start(bf16[8,1,32,384]{3,2,1,0:T(8,128)(2,1)S(1)} %broadcast_select_fusion.1), channel_id=1, source_target_pairs={{2,1},{1,2},{4,3},{3,4},{6,5},{5,6},{10,9},{9,10},{12,11},{11,12},... | collective-permute-start | bytes 589832 | tf_op jit(solution)/shard_map/ppermute | solution.py:34
  44.6 4.9 %collective-permute-start.10 = (bf16[14,96,384]{2,1,0:T(8,128)(2,1)S(1)}, bf16[14,96,384]{2,1,0:T(8,128)(2,1)S(1)}, u32[]{:S(2)}, u32[]{:S(2)}) collective-permute-start(bf16[14,96,384]{2,1,0:T(8,128)(2,1)S(1)} %shard_map.128.refs_4_), channel_id=1, source_target_pairs={{1,0},{0,1},{3,2},{2,3},{5,4},{4,5},{7,6},{6,7},{9,8},{8,9},{11,10... | collective-permute-start | bytes 3096584 | tf_op jit(solution)/shard_map/ppermute | solution.py:34
  47.3 3.7 %collective-permute-start.11 = (bf16[14,96,384]{2,1,0:T(8,128)(2,1)S(1)}, bf16[14,96,384]{2,1,0:T(8,128)(2,1)S(1)}, u32[]{:S(2)}, u32[]{:S(2)}) collective-permute-start(bf16[14,96,384]{2,1,0:T(8,128)(2,1)S(1)} %shard_map.129.refs_4_), channel_id=1, source_target_pairs={{1,0},{0,1},{3,2},{2,3},{5,4},{4,5},{7,6},{6,7},{9,8},{8,9},{11,10... | collective-permute-start | bytes 3096584 | tf_op jit(solution)/shard_map/ppermute | solution.py:34
  47.4 13.8 %collective-permute-start.7 = (bf16[14,96,384]{2,1,0:T(8,128)(2,1)S(1)}, bf16[14,96,384]{2,1,0:T(8,128)(2,1)S(1)}, u32[]{:S(2)}, u32[]{:S(2)}) collective-permute-start(bf16[14,96,384]{2,1,0:T(8,128)(2,1)S(1)} %shard_map.128.refs_4_), channel_id=1, source_target_pairs={{8,0},{3,1},{10,2},{5,3},{12,4},{7,5},{14,6},{1,7},{16,8},{11,9},{... | collective-permute-start | bytes 3096584 | tf_op jit(solution)/shard_map/ppermute | solution.py:34
  47.4 13.8 %collective-permute-start.8 = (bf16[14,96,384]{2,1,0:T(8,128)(2,1)S(1)}, bf16[14,96,384]{2,1,0:T(8,128)(2,1)S(1)}, u32[]{:S(2)}, u32[]{:S(2)}) collective-permute-start(bf16[14,96,384]{2,1,0:T(8,128)(2,1)S(1)} %shard_map.128.refs_4_), channel_id=1, source_target_pairs={{24,0},{7,1},{26,2},{1,3},{28,4},{3,5},{30,6},{5,7},{0,8},{15,9},{... | collective-permute-start | bytes 3096584 | tf_op jit(solution)/shard_map/ppermute | solution.py:34
  48.8 13.8 %collective-permute-start.9 = (bf16[14,96,384]{2,1,0:T(8,128)(2,1)S(1)}, bf16[14,96,384]{2,1,0:T(8,128)(2,1)S(1)}, u32[]{:S(2)}, u32[]{:S(2)}) collective-permute-start(bf16[14,96,384]{2,1,0:T(8,128)(2,1)S(1)} %shard_map.128.refs_4_), channel_id=1, source_target_pairs={{224,0},{33,1},{226,2},{35,3},{228,4},{37,5},{230,6},{39,7},{232,8... | collective-permute-start | bytes 3096584 | tf_op jit(solution)/shard_map/ppermute | solution.py:34
  51.0 1.5 %collective-permute-start.12 = (bf16[8,1,32,384]{3,2,1,0:T(8,128)(2,1)S(1)}, bf16[8,1,32,384]{3,2,1,0:T(8,128)(2,1)S(1)}, u32[]{:S(2)}, u32[]{:S(2)}) collective-permute-start(bf16[8,1,32,384]{3,2,1,0:T(8,128)(2,1)S(1)} %get-tuple-element.57), channel_id=1, source_target_pairs={{1,0},{0,1},{3,2},{2,3},{5,4},{4,5},{7,6},{6,7},{9,8},{8,9},{11,10... | collective-permute-start | bytes 589832 | tf_op jit(solution)/shard_map/ppermute | solution.py:34
  52.5 15.4 %copy-start.4 = (f32[384]{0:T(512)S(1)}, f32[384]{0:T(512)}, u32[]{:S(2)}) copy-start(f32[384]{0:T(512)} %param.20) | copy-start | bytes 4612
  62.6 5.3 %collective-permute-start.13 = (bf16[14,96,384]{2,1,0:T(8,128)(2,1)S(1)}, bf16[14,96,384]{2,1,0:T(8,128)(2,1)S(1)}, u32[]{:S(2)}, u32[]{:S(2)}) collective-permute-start(bf16[14,96,384]{2,1,0:T(8,128)(2,1)S(1)} %collective-permute-done.7.refs_5_), channel_id=1, source_target_pairs={{1,0},{0,1},{3,2},{2,3},{5,4},{4,5},{7,6},{6,7},{9,8},{8,9},{11,10... | collective-permute-start | bytes 3096584 | tf_op jit(solution)/shard_map/ppermute | solution.py:34
  65.6 3.7 %collective-permute-start.14 = (bf16[14,96,384]{2,1,0:T(8,128)(2,1)S(1)}, bf16[14,96,384]{2,1,0:T(8,128)(2,1)S(1)}, u32[]{:S(2)}, u32[]{:S(2)}) collective-permute-start(bf16[14,96,384]{2,1,0:T(8,128)(2,1)S(1)} %collective-permute-done.8.refs_6_), channel_id=1, source_target_pairs={{1,0},{0,1},{3,2},{2,3},{5,4},{4,5},{7,6},{6,7},{9,8},{8,9},{11,10... | collective-permute-start | bytes 3096584 | tf_op jit(solution)/shard_map/ppermute | solution.py:34
  65.6 5.2 %collective-permute-start.15 = (bf16[14,96,384]{2,1,0:T(8,128)(2,1)S(1)}, bf16[14,96,384]{2,1,0:T(8,128)(2,1)S(1)}, u32[]{:S(2)}, u32[]{:S(2)}) collective-permute-start(bf16[14,96,384]{2,1,0:T(8,128)(2,1)S(1)} %collective-permute-done.9.refs_7_), channel_id=1, source_target_pairs={{1,0},{0,1},{3,2},{2,3},{5,4},{4,5},{7,6},{6,7},{9,8},{8,9},{11,10... | collective-permute-start | bytes 3096584 | tf_op jit(solution)/shard_map/ppermute | solution.py:34
  66.1 19.6 %collective-permute-start.19 = (bf16[14,96,384]{2,1,0:T(8,128)(2,1)S(1)}, bf16[14,96,384]{2,1,0:T(8,128)(2,1)S(1)}, u32[]{:S(2)}, u32[]{:S(2)}) collective-permute-start(bf16[14,96,384]{2,1,0:T(8,128)(2,1)S(1)} %shard_map.129.refs_4_), channel_id=1, source_target_pairs={{8,0},{3,1},{10,2},{5,3},{12,4},{7,5},{14,6},{1,7},{16,8},{11,9},{... | collective-permute-start | bytes 3096584 | tf_op jit(solution)/shard_map/ppermute | solution.py:34
  66.2 22.6 %collective-permute-start.20 = (bf16[14,96,384]{2,1,0:T(8,128)(2,1)S(1)}, bf16[14,96,384]{2,1,0:T(8,128)(2,1)S(1)}, u32[]{:S(2)}, u32[]{:S(2)}) collective-permute-start(bf16[14,96,384]{2,1,0:T(8,128)(2,1)S(1)} %shard_map.129.refs_4_), channel_id=1, source_target_pairs={{24,0},{7,1},{26,2},{1,3},{28,4},{3,5},{30,6},{5,7},{0,8},{15,9},{... | collective-permute-start | bytes 3096584 | tf_op jit(solution)/shard_map/ppermute | solution.py:34
  67.9 20.9 %collective-permute-start.21 = (bf16[14,96,384]{2,1,0:T(8,128)(2,1)S(1)}, bf16[14,96,384]{2,1,0:T(8,128)(2,1)S(1)}, u32[]{:S(2)}, u32[]{:S(2)}) collective-permute-start(bf16[14,96,384]{2,1,0:T(8,128)(2,1)S(1)} %shard_map.129.refs_4_), channel_id=1, source_target_pairs={{224,0},{33,1},{226,2},{35,3},{228,4},{37,5},{230,6},{39,7},{232,8... | collective-permute-start | bytes 3096584 | tf_op jit(solution)/shard_map/ppermute | solution.py:34
  80.6 14.7 %collective-permute-start.16 = (bf16[2,4,32,384]{3,2,1,0:T(8,128)(2,1)S(1)}, bf16[2,4,32,384]{3,2,1,0:T(8,128)(2,1)S(1)}, u32[]{:S(2)}, u32[]{:S(2)}) collective-permute-start(bf16[2,4,32,384]{3,2,1,0:T(8,128)(2,1)S(1)} %constant_dynamic-slice_fusion.1), channel_id=1, source_target_pairs={{0,8},{1,9},{2,10},{3,11},{4,12},{5,13},{6,14},{7,15},{8,16},{9,17... | collective-permute-start | bytes 589832 | tf_op jit(solution)/shard_map/ppermute | solution.py:34
  82.6 12.8 %collective-permute-start.18 = (bf16[6,1,32,384]{3,2,1,0:T(8,128)(2,1)S(1)}, bf16[6,1,32,384]{3,2,1,0:T(8,128)(2,1)S(1)}, u32[]{:S(2)}, u32[]{:S(2)}) collective-permute-start(bf16[6,1,32,384]{3,2,1,0:T(8,128)(2,1)S(1)} %get-tuple-element.67), channel_id=1, source_target_pairs={{2,1},{1,2},{4,3},{3,4},{6,5},{5,6},{10,9},{9,10},{12,11},{11,12},... | collective-permute-start | bytes 442376 | tf_op jit(solution)/shard_map/ppermute | solution.py:34
  85.7 9.6 %collective-permute-start.17 = (bf16[2,1,32,384]{3,2,1,0:T(8,128)(2,1)S(1)}, bf16[2,1,32,384]{3,2,1,0:T(8,128)(2,1)S(1)}, u32[]{:S(2)}, u32[]{:S(2)}) collective-permute-start(bf16[2,1,32,384]{3,2,1,0:T(8,128)(2,1)S(1)} %constant_dynamic-slice_fusion), channel_id=1, source_target_pairs={{2,9},{1,10},{4,11},{3,12},{6,13},{5,14},{10,17},{9,18},{12,19},{1... | collective-permute-start | bytes 147464 | tf_op jit(solution)/shard_map/ppermute | solution.py:34
  95.4 1.5 %collective-permute-start.22 = (bf16[8,1,32,384]{3,2,1,0:T(8,128)(2,1)S(1)}, bf16[8,1,32,384]{3,2,1,0:T(8,128)(2,1)S(1)}, u32[]{:S(2)}, u32[]{:S(2)}) collective-permute-start(bf16[8,1,32,384]{3,2,1,0:T(8,128)(2,1)S(1)} %pad_maximum_fusion.3), channel_id=1, source_target_pairs={{1,0},{0,1},{3,2},{2,3},{5,4},{4,5},{7,6},{6,7},{9,8},{8,9},{11,10... | collective-permute-start | bytes 589832 | tf_op jit(solution)/shard_map/ppermute | solution.py:34
  95.5 4.1 %collective-permute-start.23 = (bf16[14,96,384]{2,1,0:T(8,128)(2,1)S(1)}, bf16[14,96,384]{2,1,0:T(8,128)(2,1)S(1)}, u32[]{:S(2)}, u32[]{:S(2)}) collective-permute-start(bf16[14,96,384]{2,1,0:T(8,128)(2,1)S(1)} %collective-permute-done.19.refs_5_), channel_id=1, source_target_pairs={{1,0},{0,1},{3,2},{2,3},{5,4},{4,5},{7,6},{6,7},{9,8},{8,9},{11,10... | collective-permute-start | bytes 3096584 | tf_op jit(solution)/shard_map/ppermute | solution.py:34
  97.0 3.0 %collective-permute-start.24 = (bf16[14,96,384]{2,1,0:T(8,128)(2,1)S(1)}, bf16[14,96,384]{2,1,0:T(8,128)(2,1)S(1)}, u32[]{:S(2)}, u32[]{:S(2)}) collective-permute-start(bf16[14,96,384]{2,1,0:T(8,128)(2,1)S(1)} %collective-permute-done.20.refs_6_), channel_id=1, source_target_pairs={{1,0},{0,1},{3,2},{2,3},{5,4},{4,5},{7,6},{6,7},{9,8},{8,9},{11,10... | collective-permute-start | bytes 3096584 | tf_op jit(solution)/shard_map/ppermute | solution.py:34
  97.1 4.3 %collective-permute-start.25 = (bf16[14,96,384]{2,1,0:T(8,128)(2,1)S(1)}, bf16[14,96,384]{2,1,0:T(8,128)(2,1)S(1)}, u32[]{:S(2)}, u32[]{:S(2)}) collective-permute-start(bf16[14,96,384]{2,1,0:T(8,128)(2,1)S(1)} %collective-permute-done.21.refs_7_), channel_id=1, source_target_pairs={{1,0},{0,1},{3,2},{2,3},{5,4},{4,5},{7,6},{6,7},{9,8},{8,9},{11,10... | collective-permute-start | bytes 3096584 | tf_op jit(solution)/shard_map/ppermute | solution.py:34
  (3 other events, 20.1 us)

commit v15 on v14

--- a/solution.py
+++ b/solution.py
@@ -389,6 +389,7 @@
     ends, corners, outer = lax.optimization_barrier((last_two(acts_two), last_two(outer), outer))
     ends = fetch(ends, before_in_group)
     across = fetch(outer, across_chips)
+    corners, two_bundles = lax.optimization_barrier((corners, two_bundles))
     corners = fetch(corners, across_and_before)
     spread = spread_inner(picks, acts_two)
     ends, corners, across, spread, two_bundles = lax.optimization_barrier(

time: 112 us -> 112 us (level)
  no operation moved by 1% of the time
where the time goes in v15:
time: 112 us
  waiting for transfers between devices  39.2 us (35%)
  starting transfers between devices  36.8 us (33%)
  Pallas kernels  28.1 us (25%)
  local copies, waits for them, and re-layouts  3.34 us (3%)
  other arithmetic  2.34 us (2%)
  between operations  1.96 us (2%)
    ppermute x26, waiting for transfers between devices, fetch(): return lax.ppermute(array, AXES, pairs)  39.2 us
    ppermute x26, starting transfers between devices, fetch(): return lax.ppermute(array, AXES, pairs)  36.8 us
    pallas_call x2, Pallas kernels, conv(): pl.pallas_call(lambda *refs: conv_body(*refs, finish=finish), out_shape=j...  19.8 us
    pallas_call x2, Pallas kernels, spread_halo(): pl.pallas_call(spread_halo_body, out_shape=jax.ShapeDtypeStruct(spread.sh...  4.19 us
  transfers between devices with their start and end apart: 26, of which 14 were waited for; matrix products, arithmetic and copies ran while one was open for 4% of the time, Pallas kernels for 16%

profile of v15, /device:TPU:131, one launch (start us, length us, event | category | flops | bytes accessed | tf_op | source)
XLA Modules:
  0.0 111.7 jit_solution(9612754857426862131)
XLA Ops:
  0.0 1.1 constant_dynamic-slice_fusion.3
  1.3 2.1 %collective-permute-start = (bf16[2,168,384]{2,1,0:T(8,128)(2,1)S(1)}, bf16[2,168,384]{2,1,0:T(8,128)(2,1)S(1)}, u32[]{:S(2)}, u32[]{:S(2)}) collective-permute-start(bf16[2,168,384]{2,1,0:T(8,128)(2,1)S(1)} %constant_dynamic-update-slice_fusion), channel_id=1, source_target_pairs={{24,0},{1,1},{90,2},{67,3},{60,4},{37,5},{126,6},{103,7},{0,8},{9,... | collective-permute-start | bytes 774152 | tf_op jit(solution)/shard_map/ppermute | solution.py:34
  3.4 2.4 %collective-permute-start.1 = (bf16[2,168,384]{2,1,0:T(8,128)(2,1)S(1)}, bf16[2,168,384]{2,1,0:T(8,128)(2,1)S(1)}, u32[]{:S(2)}, u32[]{:S(2)}) collective-permute-start(bf16[2,168,384]{2,1,0:T(8,128)(2,1)S(1)} %constant_dynamic-update-slice_fusion), channel_id=1, source_target_pairs={{152,0},{129,1},{218,2},{195,3},{188,4},{165,5},{254,6},{231,7},{1... | collective-permute-start | bytes 774152 | tf_op jit(solution)/shard_map/ppermute | solution.py:34
  7.1 3.2 %collective-permute-start.3 = (bf16[2,4,32,384]{3,2,1,0:T(8,128)(2,1)S(1)}, bf16[2,4,32,384]{3,2,1,0:T(8,128)(2,1)S(1)}, u32[]{:S(2)}, u32[]{:S(2)}) collective-permute-start(bf16[2,4,32,384]{3,2,1,0:T(8,128)(2,1)S(1)} %constant_dynamic-slice_fusion.2), channel_id=1, source_target_pairs={{0,8},{1,9},{2,10},{3,11},{4,12},{5,13},{6,14},{7,15},{8,16},{9,17... | collective-permute-start | bytes 589832 | tf_op jit(solution)/shard_map/ppermute | solution.py:34
  13.8 0.6 pad_add_fusion.order
  14.5 1.6 %shard_map.127.picks = bf16[2,384,384]{2,1,0:T(8,128)(2,1)} custom-call(s32[2,384]{1,0:T(2,128)} %pad_add_fusion.order), custom_call_target="tpu_custom_call" | custom-call | flops 1000 | bytes 1000 | tf_op jit(solution)/shard_map/pallas_call | solution.py:126
  16.8 2.9 %collective-permute-start.2 = (bf16[2,2,168,384]{3,2,1,0:T(8,128)(2,1)S(1)}, bf16[2,2,168,384]{3,2,1,0:T(8,128)(2,1)S(1)}, u32[]{:S(2)}, u32[]{:S(2)}) collective-permute-start(bf16[2,2,168,384]{3,2,1,0:T(8,128)(2,1)S(1)} %pad_maximum_fusion.refs_0_), channel_id=1, source_target_pairs={{2,0},{9,1},{4,2},{11,3},{6,4},{13,5},{0,6},{15,7},{10,8},{17,9},{... | collective-permute-start | bytes 1548296 | tf_op jit(solution)/shard_map/ppermute | solution.py:34
  20.1 5.7 %collective-permute-done.3.ends = bf16[2,4,32,384]{3,2,1,0:T(8,128)(2,1)S(1)} collective-permute-done((bf16[2,4,32,384]{3,2,1,0:T(8,128)(2,1)S(1)}, bf16[2,4,32,384]{3,2,1,0:T(8,128)(2,1)S(1)}, u32[]{:S(2)}, u32[]{:S(2)}) %collective-permute-start.3) | collective-permute-done | bytes 196640 | tf_op jit(solution)/shard_map/ppermute | solution.py:34
  25.8 8.1 %collective-permute-start.6 = (bf16[8,1,32,384]{3,2,1,0:T(8,128)(2,1)S(1)}, bf16[8,1,32,384]{3,2,1,0:T(8,128)(2,1)S(1)}, u32[]{:S(2)}, u32[]{:S(2)}) collective-permute-start(bf16[8,1,32,384]{3,2,1,0:T(8,128)(2,1)S(1)} %broadcast_select_fusion.1), channel_id=1, source_target_pairs={{2,1},{1,2},{4,3},{3,4},{6,5},{5,6},{10,9},{9,10},{12,11},{11,12},... | collective-permute-start | bytes 589832 | tf_op jit(solution)/shard_map/ppermute | solution.py:34
  33.9 10.3 %collective-permute-done.6.across = bf16[8,1,32,384]{3,2,1,0:T(8,128)(2,1)S(1)} collective-permute-done((bf16[8,1,32,384]{3,2,1,0:T(8,128)(2,1)S(1)}, bf16[8,1,32,384]{3,2,1,0:T(8,128)(2,1)S(1)}, u32[]{:S(2)}, u32[]{:S(2)}) %collective-permute-start.6) | collective-permute-done | bytes 196640 | tf_op jit(solution)/shard_map/ppermute | solution.py:34
  44.6 2.7 %collective-permute-start.10 = (bf16[14,96,384]{2,1,0:T(8,128)(2,1)S(1)}, bf16[14,96,384]{2,1,0:T(8,128)(2,1)S(1)}, u32[]{:S(2)}, u32[]{:S(2)}) collective-permute-start(bf16[14,96,384]{2,1,0:T(8,128)(2,1)S(1)} %shard_map.128.refs_4_), channel_id=1, source_target_pairs={{1,0},{0,1},{3,2},{2,3},{5,4},{4,5},{7,6},{6,7},{9,8},{8,9},{11,10... | collective-permute-start | bytes 3096584 | tf_op jit(solution)/shard_map/ppermute | solution.py:34
  47.4 1.5 %collective-permute-start.8 = (bf16[14,96,384]{2,1,0:T(8,128)(2,1)S(1)}, bf16[14,96,384]{2,1,0:T(8,128)(2,1)S(1)}, u32[]{:S(2)}, u32[]{:S(2)}) collective-permute-start(bf16[14,96,384]{2,1,0:T(8,128)(2,1)S(1)} %shard_map.128.refs_4_), channel_id=1, source_target_pairs={{24,0},{7,1},{26,2},{1,3},{28,4},{3,5},{30,6},{5,7},{0,8},{15,9},{... | collective-permute-start | bytes 3096584 | tf_op jit(solution)/shard_map/ppermute | solution.py:34
  48.8 0.7 collective-permute-done.10.refs_8_
  49.5 1.5 %collective-permute-done.11.refs_8_ = bf16[14,96,384]{2,1,0:T(8,128)(2,1)S(1)} collective-permute-done((bf16[14,96,384]{2,1,0:T(8,128)(2,1)S(1)}, bf16[14,96,384]{2,1,0:T(8,128)(2,1)S(1)}, u32[]{:S(2)}, u32[]{:S(2)}) %collective-permute-start.11) | collective-permute-done | bytes 1032224 | tf_op jit(solution)/shard_map/ppermute | solution.py:34
  51.4 1.1 shard_map.130._
  52.5 2.1 %shard_map.131.refs_2_ = bf16[2,8,6,32,1152]{4,3,2,1,0:T(8,128)(2,1)S(1)} custom-call(s32[2]{0:T(128)S(1)} %pad_add_fusion.1.scalars.refs_0_, bf16[2,384,384]{2,1,0:T(8,128)(2,1)S(1)} %copy-done, bf16[2,4,32,384]{3,2,1,0:T(8,128)(2,1)S(1)} %collective-permute-done.3.ends, ...), custom_call_target="tpu_custom_call", output_to_operand_aliasing={{}: (5, {})} | custom-call | flops 1000 | bytes 1000 | tf_op jit(solution)/shard_map/pallas_call | solution.py:186
  54.6 6.5 %collective-permute-done.7.refs_5_ = bf16[14,96,384]{2,1,0:T(8,128)(2,1)S(1)} collective-permute-done((bf16[14,96,384]{2,1,0:T(8,128)(2,1)S(1)}, bf16[14,96,384]{2,1,0:T(8,128)(2,1)S(1)}, u32[]{:S(2)}, u32[]{:S(2)}) %collective-permute-start.7) | collective-permute-done | bytes 1032224 | tf_op jit(solution)/shard_map/ppermute | solution.py:34
  61.1 1.5 %collective-permute-done.9.refs_7_ = bf16[14,96,384]{2,1,0:T(8,128)(2,1)S(1)} collective-permute-done((bf16[14,96,384]{2,1,0:T(8,128)(2,1)S(1)}, bf16[14,96,384]{2,1,0:T(8,128)(2,1)S(1)}, u32[]{:S(2)}, u32[]{:S(2)}) %collective-permute-start.9) | collective-permute-done | bytes 1032224 | tf_op jit(solution)/shard_map/ppermute | solution.py:34
  62.6 3.0 %collective-permute-start.13 = (bf16[14,96,384]{2,1,0:T(8,128)(2,1)S(1)}, bf16[14,96,384]{2,1,0:T(8,128)(2,1)S(1)}, u32[]{:S(2)}, u32[]{:S(2)}) collective-permute-start(bf16[14,96,384]{2,1,0:T(8,128)(2,1)S(1)} %collective-permute-done.7.refs_5_), channel_id=1, source_target_pairs={{1,0},{0,1},{3,2},{2,3},{5,4},{4,5},{7,6},{6,7},{9,8},{8,9},{11,10... | collective-permute-start | bytes 3096584 | tf_op jit(solution)/shard_map/ppermute | solution.py:34
  66.2 1.5 %collective-permute-start.18 = (bf16[14,96,384]{2,1,0:T(8,128)(2,1)S(1)}, bf16[14,96,384]{2,1,0:T(8,128)(2,1)S(1)}, u32[]{:S(2)}, u32[]{:S(2)}) collective-permute-start(bf16[14,96,384]{2,1,0:T(8,128)(2,1)S(1)} %shard_map.129.refs_4_), channel_id=1, source_target_pairs={{24,0},{7,1},{26,2},{1,3},{28,4},{3,5},{30,6},{5,7},{0,8},{15,9},{... | collective-permute-start | bytes 3096584 | tf_op jit(solution)/shard_map/ppermute | solution.py:34
  67.9 1.5 %collective-permute-done.14.refs_10_ = bf16[14,96,384]{2,1,0:T(8,128)(2,1)S(1)} collective-permute-done((bf16[14,96,384]{2,1,0:T(8,128)(2,1)S(1)}, bf16[14,96,384]{2,1,0:T(8,128)(2,1)S(1)}, u32[]{:S(2)}, u32[]{:S(2)}) %collective-permute-start.14) | collective-permute-done | bytes 1032224 | tf_op jit(solution)/shard_map/ppermute | solution.py:34
  69.4 1.5 %collective-permute-done.15.refs_11_ = bf16[14,96,384]{2,1,0:T(8,128)(2,1)S(1)} collective-permute-done((bf16[14,96,384]{2,1,0:T(8,128)(2,1)S(1)}, bf16[14,96,384]{2,1,0:T(8,128)(2,1)S(1)}, u32[]{:S(2)}, u32[]{:S(2)}) %collective-permute-start.15) | collective-permute-done | bytes 1032224 | tf_op jit(solution)/shard_map/ppermute | solution.py:34
  70.9 9.7 %shard_map.132 = bf16[6,128,384]{2,1,0:T(8,128)(2,1)S(1)} custom-call(s32[2]{0:T(128)S(1)} %pad_add_fusion.1.scalars.refs_0_, f32[3,6]{1,0:T(4,128)S(1)} %add_convert_fusion.refs_1_, bf16[2,8,6,32,1152]{4,3,2,1,0:T(8,128)(2,1)S(1)} %shard_map.131.refs_2_, f32[1,384]{1,0:T(1,128)S(1)} %reshape.331.refs_3_, bf16[14,96,384]{2,1,0:T(8,128)(2,1)S(1)} %shard_map.128.refs_4_, ...), custom_call_target="tpu_custom_call" | custom-call | flops 1000 | bytes 1000 | tf_op jit(solution)/shard_map/pallas_call | solution.py:287
  80.6 1.9 %collective-permute-start.16 = (bf16[2,4,32,384]{3,2,1,0:T(8,128)(2,1)S(1)}, bf16[2,4,32,384]{3,2,1,0:T(8,128)(2,1)S(1)}, u32[]{:S(2)}, u32[]{:S(2)}) collective-permute-start(bf16[2,4,32,384]{3,2,1,0:T(8,128)(2,1)S(1)} %constant_dynamic-slice_fusion.1), channel_id=1, source_target_pairs={{0,8},{1,9},{2,10},{3,11},{4,12},{5,13},{6,14},{7,15},{8,16},{9,17... | collective-permute-start | bytes 589832 | tf_op jit(solution)/shard_map/ppermute | solution.py:34
  82.6 3.2 %collective-permute-start.21 = (bf16[6,1,32,384]{3,2,1,0:T(8,128)(2,1)S(1)}, bf16[6,1,32,384]{3,2,1,0:T(8,128)(2,1)S(1)}, u32[]{:S(2)}, u32[]{:S(2)}) collective-permute-start(bf16[6,1,32,384]{3,2,1,0:T(8,128)(2,1)S(1)} %get-tuple-element.74), channel_id=1, source_target_pairs={{2,1},{1,2},{4,3},{3,4},{6,5},{5,6},{10,9},{9,10},{12,11},{11,12},... | collective-permute-start | bytes 442376 | tf_op jit(solution)/shard_map/ppermute | solution.py:34
  85.8 1.9 %collective-permute-start.20 = (bf16[2,1,32,384]{3,2,1,0:T(8,128)(2,1)S(1)}, bf16[2,1,32,384]{3,2,1,0:T(8,128)(2,1)S(1)}, u32[]{:S(2)}, u32[]{:S(2)}) collective-permute-start(bf16[2,1,32,384]{3,2,1,0:T(8,128)(2,1)S(1)} %constant_dynamic-slice_fusion), channel_id=1, source_target_pairs={{2,9},{1,10},{4,11},{3,12},{6,13},{5,14},{10,17},{9,18},{12,19},{1... | collective-permute-start | bytes 147464 | tf_op jit(solution)/shard_map/ppermute | solution.py:34
  87.7 1.1 shard_map.133._
  88.8 6.6 %collective-permute-done.20 = bf16[2,1,32,384]{3,2,1,0:T(8,128)(2,1)S(1)} collective-permute-done((bf16[2,1,32,384]{3,2,1,0:T(8,128)(2,1)S(1)}, bf16[2,1,32,384]{3,2,1,0:T(8,128)(2,1)S(1)}, u32[]{:S(2)}, u32[]{:S(2)}) %collective-permute-start.20) | collective-permute-done | bytes 49184 | tf_op jit(solution)/shard_map/ppermute | solution.py:34
  96.0 0.9 collective-permute-done.22.beside
  97.5 2.1 %shard_map.134.refs_2_ = bf16[2,8,6,32,1152]{4,3,2,1,0:T(8,128)(2,1)S(1)} custom-call(s32[2]{0:T(128)S(1)} %pad_add_fusion.1.scalars.refs_0_, bf16[2,384,384]{2,1,0:T(8,128)(2,1)S(1)} %copy-done, bf16[2,4,32,384]{3,2,1,0:T(8,128)(2,1)S(1)} %collective-permute-done.16.ends, ...), custom_call_target="tpu_custom_call", output_to_operand_aliasing={{}: (5, {})} | custom-call | flops 1000 | bytes 1000 | tf_op jit(solution)/shard_map/pallas_call | solution.py:186
  99.9 1.5 %collective-permute-done.25.refs_11_ = bf16[14,96,384]{2,1,0:T(8,128)(2,1)S(1)} collective-permute-done((bf16[14,96,384]{2,1,0:T(8,128)(2,1)S(1)}, bf16[14,96,384]{2,1,0:T(8,128)(2,1)S(1)}, u32[]{:S(2)}, u32[]{:S(2)}) %collective-permute-start.25) | collective-permute-done | bytes 1032224 | tf_op jit(solution)/shard_map/ppermute | solution.py:34
  101.4 10.1 %shard_map.135 = bf16[6,128,384]{2,1,0:T(8,128)(2,1)} custom-call(s32[2]{0:T(128)S(1)} %pad_add_fusion.1.scalars.refs_0_, f32[3,6]{1,0:T(4,128)S(1)} %add_convert_fusion.refs_1_, bf16[2,8,6,32,1152]{4,3,2,1,0:T(8,128)(2,1)S(1)} %shard_map.134.refs_2_, bf16[6,128,384]{2,1,0:T(8,128)(2,1)S(1)} %bitcast.31, bf16[14,96,384]{2,1,0:T(8,128)(2,1)S(1)} %shard_map.129.refs_4_, ...), custom_call_target="tpu_custom_call" | custom-call | flops 1000 | bytes 1000 | tf_op jit(solution)/shard_map/pallas_call | solution.py:287
  (95 shorter events, 7.9 us)
Async XLA Ops:
  1.2 9.1 %copy-start.6 = (s32[4]{0:T(128)S(1)}, s32[4]{0:T(128)}, u32[]{:S(2)}) copy-start(s32[4]{0:T(128)} %constant.162.clone) | copy-start | bytes 52
  1.3 9.1 %copy-start.7 = (s32[4]{0:T(128)S(1)}, s32[4]{0:T(128)}, u32[]{:S(2)}) copy-start(s32[4]{0:T(128)} %constant.164.clone) | copy-start | bytes 52
  1.3 9.2 %copy-start.5 = (s32[4]{0:T(128)S(1)}, s32[4]{0:T(128)}, u32[]{:S(2)}) copy-start(s32[4]{0:T(128)} %constant.163.clone) | copy-start | bytes 52
  1.3 9.4 %copy-start.2 = (s32[4,2]{1,0:T(4,128)S(1)}, s32[4,2]{1,0:T(4,128)}, u32[]{:S(2)}) copy-start(s32[4,2]{1,0:T(4,128)} %constant.161.clone) | copy-start | bytes 100
  1.3 15.4 %collective-permute-start = (bf16[2,168,384]{2,1,0:T(8,128)(2,1)S(1)}, bf16[2,168,384]{2,1,0:T(8,128)(2,1)S(1)}, u32[]{:S(2)}, u32[]{:S(2)}) collective-permute-start(bf16[2,168,384]{2,1,0:T(8,128)(2,1)S(1)} %constant_dynamic-update-slice_fusion), channel_id=1, source_target_pairs={{24,0},{1,1},{90,2},{67,3},{60,4},{37,5},{126,6},{103,7},{0,8},{9,... | collective-permute-start | bytes 774152 | tf_op jit(solution)/shard_map/ppermute | solution.py:34
  3.4 13.3 %collective-permute-start.1 = (bf16[2,168,384]{2,1,0:T(8,128)(2,1)S(1)}, bf16[2,168,384]{2,1,0:T(8,128)(2,1)S(1)}, u32[]{:S(2)}, u32[]{:S(2)}) collective-permute-start(bf16[2,168,384]{2,1,0:T(8,128)(2,1)S(1)} %constant_dynamic-update-slice_fusion), channel_id=1, source_target_pairs={{152,0},{129,1},{218,2},{195,3},{188,4},{165,5},{254,6},{231,7},{1... | collective-permute-start | bytes 774152 | tf_op jit(solution)/shard_map/ppermute | solution.py:34
  6.4 7.2 %copy-start.8 = (s32[3]{0:T(128)S(1)}, s32[3]{0:T(128)}, u32[]{:S(2)}) copy-start(s32[3]{0:T(128)} %param.14) | copy-start | bytes 40
  7.1 18.6 %collective-permute-start.3 = (bf16[2,4,32,384]{3,2,1,0:T(8,128)(2,1)S(1)}, bf16[2,4,32,384]{3,2,1,0:T(8,128)(2,1)S(1)}, u32[]{:S(2)}, u32[]{:S(2)}) collective-permute-start(bf16[2,4,32,384]{3,2,1,0:T(8,128)(2,1)S(1)} %constant_dynamic-slice_fusion.2), channel_id=1, source_target_pairs={{0,8},{1,9},{2,10},{3,11},{4,12},{5,13},{6,14},{7,15},{8,16},{9,17... | collective-permute-start | bytes 589832 | tf_op jit(solution)/shard_map/ppermute | solution.py:34
  16.8 27.4 %collective-permute-start.2 = (bf16[2,2,168,384]{3,2,1,0:T(8,128)(2,1)S(1)}, bf16[2,2,168,384]{3,2,1,0:T(8,128)(2,1)S(1)}, u32[]{:S(2)}, u32[]{:S(2)}) collective-permute-start(bf16[2,2,168,384]{3,2,1,0:T(8,128)(2,1)S(1)} %pad_maximum_fusion.refs_0_), channel_id=1, source_target_pairs={{2,0},{9,1},{4,2},{11,3},{6,4},{13,5},{0,6},{15,7},{10,8},{17,9},{... | collective-permute-start | bytes 1548296 | tf_op jit(solution)/shard_map/ppermute | solution.py:34
  19.7 24.5 %collective-permute-start.5 = (bf16[2,2,168,384]{3,2,1,0:T(8,128)(2,1)S(1)}, bf16[2,2,168,384]{3,2,1,0:T(8,128)(2,1)S(1)}, u32[]{:S(2)}, u32[]{:S(2)}) collective-permute-start(bf16[2,2,168,384]{3,2,1,0:T(8,128)(2,1)S(1)} %pad_maximum_fusion.refs_0_), channel_id=1, source_target_pairs={{4,0},{17,1},{6,2},{19,3},{0,4},{21,5},{2,6},{23,7},{12,8},{25,9},... | collective-permute-start | bytes 1548296 | tf_op jit(solution)/shard_map/ppermute | solution.py:34
  25.7 18.4 %collective-permute-start.4 = (bf16[2,2,168,384]{3,2,1,0:T(8,128)(2,1)S(1)}, bf16[2,2,168,384]{3,2,1,0:T(8,128)(2,1)S(1)}, u32[]{:S(2)}, u32[]{:S(2)}) collective-permute-start(bf16[2,2,168,384]{3,2,1,0:T(8,128)(2,1)S(1)} %pad_maximum_fusion.refs_0_), channel_id=1, source_target_pairs={{6,0},{25,1},{0,2},{27,3},{2,4},{29,5},{4,6},{31,7},{14,8},{1,9},{... | collective-permute-start | bytes 1548296 | tf_op jit(solution)/shard_map/ppermute | solution.py:34
  25.8 18.3 %collective-permute-start.6 = (bf16[8,1,32,384]{3,2,1,0:T(8,128)(2,1)S(1)}, bf16[8,1,32,384]{3,2,1,0:T(8,128)(2,1)S(1)}, u32[]{:S(2)}, u32[]{:S(2)}) collective-permute-start(bf16[8,1,32,384]{3,2,1,0:T(8,128)(2,1)S(1)} %broadcast_select_fusion.1), channel_id=1, source_target_pairs={{2,1},{1,2},{4,3},{3,4},{6,5},{5,6},{10,9},{9,10},{12,11},{11,12},... | collective-permute-start | bytes 589832 | tf_op jit(solution)/shard_map/ppermute | solution.py:34
  44.6 4.9 %collective-permute-start.10 = (bf16[14,96,384]{2,1,0:T(8,128)(2,1)S(1)}, bf16[14,96,384]{2,1,0:T(8,128)(2,1)S(1)}, u32[]{:S(2)}, u32[]{:S(2)}) collective-permute-start(bf16[14,96,384]{2,1,0:T(8,128)(2,1)S(1)} %shard_map.128.refs_4_), channel_id=1, source_target_pairs={{1,0},{0,1},{3,2},{2,3},{5,4},{4,5},{7,6},{6,7},{9,8},{8,9},{11,10... | collective-permute-start | bytes 3096584 | tf_op jit(solution)/shard_map/ppermute | solution.py:34
  47.3 3.7 %collective-permute-start.11 = (bf16[14,96,384]{2,1,0:T(8,128)(2,1)S(1)}, bf16[14,96,384]{2,1,0:T(8,128)(2,1)S(1)}, u32[]{:S(2)}, u32[]{:S(2)}) collective-permute-start(bf16[14,96,384]{2,1,0:T(8,128)(2,1)S(1)} %shard_map.129.refs_4_), channel_id=1, source_target_pairs={{1,0},{0,1},{3,2},{2,3},{5,4},{4,5},{7,6},{6,7},{9,8},{8,9},{11,10... | collective-permute-start | bytes 3096584 | tf_op jit(solution)/shard_map/ppermute | solution.py:34
  47.4 13.8 %collective-permute-start.7 = (bf16[14,96,384]{2,1,0:T(8,128)(2,1)S(1)}, bf16[14,96,384]{2,1,0:T(8,128)(2,1)S(1)}, u32[]{:S(2)}, u32[]{:S(2)}) collective-permute-start(bf16[14,96,384]{2,1,0:T(8,128)(2,1)S(1)} %shard_map.128.refs_4_), channel_id=1, source_target_pairs={{8,0},{3,1},{10,2},{5,3},{12,4},{7,5},{14,6},{1,7},{16,8},{11,9},{... | collective-permute-start | bytes 3096584 | tf_op jit(solution)/shard_map/ppermute | solution.py:34
  47.4 13.8 %collective-permute-start.8 = (bf16[14,96,384]{2,1,0:T(8,128)(2,1)S(1)}, bf16[14,96,384]{2,1,0:T(8,128)(2,1)S(1)}, u32[]{:S(2)}, u32[]{:S(2)}) collective-permute-start(bf16[14,96,384]{2,1,0:T(8,128)(2,1)S(1)} %shard_map.128.refs_4_), channel_id=1, source_target_pairs={{24,0},{7,1},{26,2},{1,3},{28,4},{3,5},{30,6},{5,7},{0,8},{15,9},{... | collective-permute-start | bytes 3096584 | tf_op jit(solution)/shard_map/ppermute | solution.py:34
  48.8 13.8 %collective-permute-start.9 = (bf16[14,96,384]{2,1,0:T(8,128)(2,1)S(1)}, bf16[14,96,384]{2,1,0:T(8,128)(2,1)S(1)}, u32[]{:S(2)}, u32[]{:S(2)}) collective-permute-start(bf16[14,96,384]{2,1,0:T(8,128)(2,1)S(1)} %shard_map.128.refs_4_), channel_id=1, source_target_pairs={{224,0},{33,1},{226,2},{35,3},{228,4},{37,5},{230,6},{39,7},{232,8... | collective-permute-start | bytes 3096584 | tf_op jit(solution)/shard_map/ppermute | solution.py:34
  51.0 1.5 %collective-permute-start.12 = (bf16[8,1,32,384]{3,2,1,0:T(8,128)(2,1)S(1)}, bf16[8,1,32,384]{3,2,1,0:T(8,128)(2,1)S(1)}, u32[]{:S(2)}, u32[]{:S(2)}) collective-permute-start(bf16[8,1,32,384]{3,2,1,0:T(8,128)(2,1)S(1)} %get-tuple-element.62), channel_id=1, source_target_pairs={{1,0},{0,1},{3,2},{2,3},{5,4},{4,5},{7,6},{6,7},{9,8},{8,9},{11,10... | collective-permute-start | bytes 589832 | tf_op jit(solution)/shard_map/ppermute | solution.py:34
  52.5 15.4 %copy-start.4 = (f32[384]{0:T(512)S(1)}, f32[384]{0:T(512)}, u32[]{:S(2)}) copy-start(f32[384]{0:T(512)} %param.20) | copy-start | bytes 4612
  62.6 5.3 %collective-permute-start.13 = (bf16[14,96,384]{2,1,0:T(8,128)(2,1)S(1)}, bf16[14,96,384]{2,1,0:T(8,128)(2,1)S(1)}, u32[]{:S(2)}, u32[]{:S(2)}) collective-permute-start(bf16[14,96,384]{2,1,0:T(8,128)(2,1)S(1)} %collective-permute-done.7.refs_5_), channel_id=1, source_target_pairs={{1,0},{0,1},{3,2},{2,3},{5,4},{4,5},{7,6},{6,7},{9,8},{8,9},{11,10... | collective-permute-start | bytes 3096584 | tf_op jit(solution)/shard_map/ppermute | solution.py:34
  65.6 3.7 %collective-permute-start.14 = (bf16[14,96,384]{2,1,0:T(8,128)(2,1)S(1)}, bf16[14,96,384]{2,1,0:T(8,128)(2,1)S(1)}, u32[]{:S(2)}, u32[]{:S(2)}) collective-permute-start(bf16[14,96,384]{2,1,0:T(8,128)(2,1)S(1)} %collective-permute-done.8.refs_6_), channel_id=1, source_target_pairs={{1,0},{0,1},{3,2},{2,3},{5,4},{4,5},{7,6},{6,7},{9,8},{8,9},{11,10... | collective-permute-start | bytes 3096584 | tf_op jit(solution)/shard_map/ppermute | solution.py:34
  65.6 5.2 %collective-permute-start.15 = (bf16[14,96,384]{2,1,0:T(8,128)(2,1)S(1)}, bf16[14,96,384]{2,1,0:T(8,128)(2,1)S(1)}, u32[]{:S(2)}, u32[]{:S(2)}) collective-permute-start(bf16[14,96,384]{2,1,0:T(8,128)(2,1)S(1)} %collective-permute-done.9.refs_7_), channel_id=1, source_target_pairs={{1,0},{0,1},{3,2},{2,3},{5,4},{4,5},{7,6},{6,7},{9,8},{8,9},{11,10... | collective-permute-start | bytes 3096584 | tf_op jit(solution)/shard_map/ppermute | solution.py:34
  66.1 19.6 %collective-permute-start.17 = (bf16[14,96,384]{2,1,0:T(8,128)(2,1)S(1)}, bf16[14,96,384]{2,1,0:T(8,128)(2,1)S(1)}, u32[]{:S(2)}, u32[]{:S(2)}) collective-permute-start(bf16[14,96,384]{2,1,0:T(8,128)(2,1)S(1)} %shard_map.129.refs_4_), channel_id=1, source_target_pairs={{8,0},{3,1},{10,2},{5,3},{12,4},{7,5},{14,6},{1,7},{16,8},{11,9},{... | collective-permute-start | bytes 3096584 | tf_op jit(solution)/shard_map/ppermute | solution.py:34
  66.2 19.6 %collective-permute-start.18 = (bf16[14,96,384]{2,1,0:T(8,128)(2,1)S(1)}, bf16[14,96,384]{2,1,0:T(8,128)(2,1)S(1)}, u32[]{:S(2)}, u32[]{:S(2)}) collective-permute-start(bf16[14,96,384]{2,1,0:T(8,128)(2,1)S(1)} %shard_map.129.refs_4_), channel_id=1, source_target_pairs={{24,0},{7,1},{26,2},{1,3},{28,4},{3,5},{30,6},{5,7},{0,8},{15,9},{... | collective-permute-start | bytes 3096584 | tf_op jit(solution)/shard_map/ppermute | solution.py:34
  67.9 17.9 %collective-permute-start.19 = (bf16[14,96,384]{2,1,0:T(8,128)(2,1)S(1)}, bf16[14,96,384]{2,1,0:T(8,128)(2,1)S(1)}, u32[]{:S(2)}, u32[]{:S(2)}) collective-permute-start(bf16[14,96,384]{2,1,0:T(8,128)(2,1)S(1)} %shard_map.129.refs_4_), channel_id=1, source_target_pairs={{224,0},{33,1},{226,2},{35,3},{228,4},{37,5},{230,6},{39,7},{232,8... | collective-permute-start | bytes 3096584 | tf_op jit(solution)/shard_map/ppermute | solution.py:34
  80.6 14.8 %collective-permute-start.16 = (bf16[2,4,32,384]{3,2,1,0:T(8,128)(2,1)S(1)}, bf16[2,4,32,384]{3,2,1,0:T(8,128)(2,1)S(1)}, u32[]{:S(2)}, u32[]{:S(2)}) collective-permute-start(bf16[2,4,32,384]{3,2,1,0:T(8,128)(2,1)S(1)} %constant_dynamic-slice_fusion.1), channel_id=1, source_target_pairs={{0,8},{1,9},{2,10},{3,11},{4,12},{5,13},{6,14},{7,15},{8,16},{9,17... | collective-permute-start | bytes 589832 | tf_op jit(solution)/shard_map/ppermute | solution.py:34
  82.6 12.8 %collective-permute-start.21 = (bf16[6,1,32,384]{3,2,1,0:T(8,128)(2,1)S(1)}, bf16[6,1,32,384]{3,2,1,0:T(8,128)(2,1)S(1)}, u32[]{:S(2)}, u32[]{:S(2)}) collective-permute-start(bf16[6,1,32,384]{3,2,1,0:T(8,128)(2,1)S(1)} %get-tuple-element.74), channel_id=1, source_target_pairs={{2,1},{1,2},{4,3},{3,4},{6,5},{5,6},{10,9},{9,10},{12,11},{11,12},... | collective-permute-start | bytes 442376 | tf_op jit(solution)/shard_map/ppermute | solution.py:34
  85.8 9.6 %collective-permute-start.20 = (bf16[2,1,32,384]{3,2,1,0:T(8,128)(2,1)S(1)}, bf16[2,1,32,384]{3,2,1,0:T(8,128)(2,1)S(1)}, u32[]{:S(2)}, u32[]{:S(2)}) collective-permute-start(bf16[2,1,32,384]{3,2,1,0:T(8,128)(2,1)S(1)} %constant_dynamic-slice_fusion), channel_id=1, source_target_pairs={{2,9},{1,10},{4,11},{3,12},{6,13},{5,14},{10,17},{9,18},{12,19},{1... | collective-permute-start | bytes 147464 | tf_op jit(solution)/shard_map/ppermute | solution.py:34
  95.5 1.5 %collective-permute-start.22 = (bf16[8,1,32,384]{3,2,1,0:T(8,128)(2,1)S(1)}, bf16[8,1,32,384]{3,2,1,0:T(8,128)(2,1)S(1)}, u32[]{:S(2)}, u32[]{:S(2)}) collective-permute-start(bf16[8,1,32,384]{3,2,1,0:T(8,128)(2,1)S(1)} %pad_maximum_fusion.3), channel_id=1, source_target_pairs={{1,0},{0,1},{3,2},{2,3},{5,4},{4,5},{7,6},{6,7},{9,8},{8,9},{11,10... | collective-permute-start | bytes 589832 | tf_op jit(solution)/shard_map/ppermute | solution.py:34
  95.6 4.1 %collective-permute-start.23 = (bf16[14,96,384]{2,1,0:T(8,128)(2,1)S(1)}, bf16[14,96,384]{2,1,0:T(8,128)(2,1)S(1)}, u32[]{:S(2)}, u32[]{:S(2)}) collective-permute-start(bf16[14,96,384]{2,1,0:T(8,128)(2,1)S(1)} %collective-permute-done.17.refs_5_), channel_id=1, source_target_pairs={{1,0},{0,1},{3,2},{2,3},{5,4},{4,5},{7,6},{6,7},{9,8},{8,9},{11,10... | collective-permute-start | bytes 3096584 | tf_op jit(solution)/shard_map/ppermute | solution.py:34
  97.0 3.0 %collective-permute-start.24 = (bf16[14,96,384]{2,1,0:T(8,128)(2,1)S(1)}, bf16[14,96,384]{2,1,0:T(8,128)(2,1)S(1)}, u32[]{:S(2)}, u32[]{:S(2)}) collective-permute-start(bf16[14,96,384]{2,1,0:T(8,128)(2,1)S(1)} %collective-permute-done.18.refs_6_), channel_id=1, source_target_pairs={{1,0},{0,1},{3,2},{2,3},{5,4},{4,5},{7,6},{6,7},{9,8},{8,9},{11,10... | collective-permute-start | bytes 3096584 | tf_op jit(solution)/shard_map/ppermute | solution.py:34
  97.1 4.3 %collective-permute-start.25 = (bf16[14,96,384]{2,1,0:T(8,128)(2,1)S(1)}, bf16[14,96,384]{2,1,0:T(8,128)(2,1)S(1)}, u32[]{:S(2)}, u32[]{:S(2)}) collective-permute-start(bf16[14,96,384]{2,1,0:T(8,128)(2,1)S(1)} %collective-permute-done.19.refs_7_), channel_id=1, source_target_pairs={{1,0},{0,1},{3,2},{2,3},{5,4},{4,5},{7,6},{6,7},{9,8},{8,9},{11,10... | collective-permute-start | bytes 3096584 | tf_op jit(solution)/shard_map/ppermute | solution.py:34
  (3 other events, 20.1 us)

commit v16 on v15

--- a/solution.py
+++ b/solution.py
@@ -360,8 +360,7 @@
 
     opposite = fetch(pieces, small_source(2))
     after = fetch(pieces, small_source(1))
-    gated, ends = lax.optimization_barrier((pieces, ends))
-    parts = [pieces, after, fetch(gated, small_source(-1)), opposite]
+    parts = [pieces, after, fetch(pieces, small_source(-1)), opposite]
     inner, outer = sides(jnp.concatenate([ends, acts_one], 0))
     across = fetch(outer, across_chips)
     parts, across = lax.optimization_barrier((parts, across))

time: 112 us -> 111 us (level)
  waiting for transfers between devices: 39.2 us -> 34.8 us
  starting transfers between devices: 36.8 us -> 39.9 us
    ppermute x26, waiting for transfers between devices: 39.2 us -> 34.8 us  [fetch(): return lax.ppermute(array, AXES, pairs)]
    ppermute x26, starting transfers between devices: 36.8 us -> 39.9 us  [fetch(): return lax.ppermute(array, AXES, pairs)]
  transfers between devices with their start and end apart: 26 -> 26, of which waited for: 14 -> 11; matrix products, arithmetic and copies ran while one was open for 4% -> 4% of each run, Pallas kernels for 16% -> 16%
where the time goes in v16:
time: 111 us
  starting transfers between devices  39.9 us (36%)
  waiting for transfers between devices  34.8 us (31%)
  Pallas kernels  28.1 us (25%)
  local copies, waits for them, and re-layouts  3.34 us (3%)
  other arithmetic  2.34 us (2%)
  between operations  2 us (2%)
    ppermute x26, starting transfers between devices, fetch(): return lax.ppermute(array, AXES, pairs)  39.9 us
    ppermute x26, waiting for transfers between devices, fetch(): return lax.ppermute(array, AXES, pairs)  34.8 us
    pallas_call x2, Pallas kernels, conv(): pl.pallas_call(lambda *refs: conv_body(*refs, finish=finish), out_shape=j...  19.8 us
    pallas_call x2, Pallas kernels, spread_halo(): pl.pallas_call(spread_halo_body, out_shape=jax.ShapeDtypeStruct(spread.sh...  4.18 us
  transfers between devices with their start and end apart: 26, of which 11 were waited for; matrix products, arithmetic and copies ran while one was open for 4% of the time, Pallas kernels for 16%

profile of v16, /device:TPU:131, one launch (start us, length us, event | category | flops | bytes accessed | tf_op | source)
XLA Modules:
  0.0 110.5 jit_solution(2133811300555097573)
XLA Ops:
  0.0 1.1 constant_dynamic-slice_fusion.3
  1.3 2.1 %collective-permute-start = (bf16[2,168,384]{2,1,0:T(8,128)(2,1)S(1)}, bf16[2,168,384]{2,1,0:T(8,128)(2,1)S(1)}, u32[]{:S(2)}, u32[]{:S(2)}) collective-permute-start(bf16[2,168,384]{2,1,0:T(8,128)(2,1)S(1)} %constant_dynamic-update-slice_fusion), channel_id=1, source_target_pairs={{24,0},{1,1},{90,2},{67,3},{60,4},{37,5},{126,6},{103,7},{0,8},{9,... | collective-permute-start | bytes 774152 | tf_op jit(solution)/shard_map/ppermute | solution.py:34
  3.4 2.4 %collective-permute-start.1 = (bf16[2,168,384]{2,1,0:T(8,128)(2,1)S(1)}, bf16[2,168,384]{2,1,0:T(8,128)(2,1)S(1)}, u32[]{:S(2)}, u32[]{:S(2)}) collective-permute-start(bf16[2,168,384]{2,1,0:T(8,128)(2,1)S(1)} %constant_dynamic-update-slice_fusion), channel_id=1, source_target_pairs={{152,0},{129,1},{218,2},{195,3},{188,4},{165,5},{254,6},{231,7},{1... | collective-permute-start | bytes 774152 | tf_op jit(solution)/shard_map/ppermute | solution.py:34
  7.1 3.2 %collective-permute-start.5 = (bf16[2,4,32,384]{3,2,1,0:T(8,128)(2,1)S(1)}, bf16[2,4,32,384]{3,2,1,0:T(8,128)(2,1)S(1)}, u32[]{:S(2)}, u32[]{:S(2)}) collective-permute-start(bf16[2,4,32,384]{3,2,1,0:T(8,128)(2,1)S(1)} %constant_dynamic-slice_fusion.2), channel_id=1, source_target_pairs={{0,8},{1,9},{2,10},{3,11},{4,12},{5,13},{6,14},{7,15},{8,16},{9,17... | collective-permute-start | bytes 589832 | tf_op jit(solution)/shard_map/ppermute | solution.py:34
  10.6 0.6 gather_fusion
  12.0 0.6 gather_fusion.1
  13.8 0.6 pad_add_fusion.order
  14.5 1.6 %shard_map.127.picks = bf16[2,384,384]{2,1,0:T(8,128)(2,1)} custom-call(s32[2,384]{1,0:T(2,128)} %pad_add_fusion.order), custom_call_target="tpu_custom_call" | custom-call | flops 1000 | bytes 1000 | tf_op jit(solution)/shard_map/pallas_call | solution.py:126
  16.2 0.5 collective-permute-done
  16.8 2.9 %collective-permute-start.2 = (bf16[2,2,168,384]{3,2,1,0:T(8,128)(2,1)S(1)}, bf16[2,2,168,384]{3,2,1,0:T(8,128)(2,1)S(1)}, u32[]{:S(2)}, u32[]{:S(2)}) collective-permute-start(bf16[2,2,168,384]{3,2,1,0:T(8,128)(2,1)S(1)} %pad_maximum_fusion.refs_0_), channel_id=1, source_target_pairs={{2,0},{9,1},{4,2},{11,3},{6,4},{13,5},{0,6},{15,7},{10,8},{17,9},{... | collective-permute-start | bytes 1548296 | tf_op jit(solution)/shard_map/ppermute | solution.py:34
  19.7 1.6 %collective-permute-start.4 = (bf16[2,2,168,384]{3,2,1,0:T(8,128)(2,1)S(1)}, bf16[2,2,168,384]{3,2,1,0:T(8,128)(2,1)S(1)}, u32[]{:S(2)}, u32[]{:S(2)}) collective-permute-start(bf16[2,2,168,384]{3,2,1,0:T(8,128)(2,1)S(1)} %pad_maximum_fusion.refs_0_), channel_id=1, source_target_pairs={{4,0},{17,1},{6,2},{19,3},{0,4},{21,5},{2,6},{23,7},{12,8},{25,9},... | collective-permute-start | bytes 1548296 | tf_op jit(solution)/shard_map/ppermute | solution.py:34
  21.4 3.6 %collective-permute-done.5.ends = bf16[2,4,32,384]{3,2,1,0:T(8,128)(2,1)S(1)} collective-permute-done((bf16[2,4,32,384]{3,2,1,0:T(8,128)(2,1)S(1)}, bf16[2,4,32,384]{3,2,1,0:T(8,128)(2,1)S(1)}, u32[]{:S(2)}, u32[]{:S(2)}) %collective-permute-start.5) | collective-permute-done | bytes 196640 | tf_op jit(solution)/shard_map/ppermute | solution.py:34
  25.1 6.8 %collective-permute-start.6 = (bf16[8,1,32,384]{3,2,1,0:T(8,128)(2,1)S(1)}, bf16[8,1,32,384]{3,2,1,0:T(8,128)(2,1)S(1)}, u32[]{:S(2)}, u32[]{:S(2)}) collective-permute-start(bf16[8,1,32,384]{3,2,1,0:T(8,128)(2,1)S(1)} %broadcast_select_fusion.1), channel_id=1, source_target_pairs={{2,1},{1,2},{4,3},{3,4},{6,5},{5,6},{10,9},{9,10},{12,11},{11,12},... | collective-permute-start | bytes 589832 | tf_op jit(solution)/shard_map/ppermute | solution.py:34
  31.9 10.4 %collective-permute-done.6.across = bf16[8,1,32,384]{3,2,1,0:T(8,128)(2,1)S(1)} collective-permute-done((bf16[8,1,32,384]{3,2,1,0:T(8,128)(2,1)S(1)}, bf16[8,1,32,384]{3,2,1,0:T(8,128)(2,1)S(1)}, u32[]{:S(2)}, u32[]{:S(2)}) %collective-permute-start.6) | collective-permute-done | bytes 196640 | tf_op jit(solution)/shard_map/ppermute | solution.py:34
  43.2 4.1 %collective-permute-start.7 = (bf16[14,96,384]{2,1,0:T(8,128)(2,1)S(1)}, bf16[14,96,384]{2,1,0:T(8,128)(2,1)S(1)}, u32[]{:S(2)}, u32[]{:S(2)}) collective-permute-start(bf16[14,96,384]{2,1,0:T(8,128)(2,1)S(1)} %shard_map.128.refs_4_), channel_id=1, source_target_pairs={{8,0},{3,1},{10,2},{5,3},{12,4},{7,5},{14,6},{1,7},{16,8},{11,9},{... | collective-permute-start | bytes 3096584 | tf_op jit(solution)/shard_map/ppermute | solution.py:34
  47.5 1.1 shard_map.130._
  48.9 2.1 %shard_map.131.refs_2_ = bf16[2,8,6,32,1152]{4,3,2,1,0:T(8,128)(2,1)S(1)} custom-call(s32[2]{0:T(128)S(1)} %pad_add_fusion.1.scalars.refs_0_, bf16[2,384,384]{2,1,0:T(8,128)(2,1)S(1)} %copy-done, bf16[2,4,32,384]{3,2,1,0:T(8,128)(2,1)S(1)} %collective-permute-done.5.ends, ...), custom_call_target="tpu_custom_call", output_to_operand_aliasing={{}: (5, {})} | custom-call | flops 1000 | bytes 1000 | tf_op jit(solution)/shard_map/pallas_call | solution.py:186
  51.0 7.9 %collective-permute-done.7.refs_5_ = bf16[14,96,384]{2,1,0:T(8,128)(2,1)S(1)} collective-permute-done((bf16[14,96,384]{2,1,0:T(8,128)(2,1)S(1)}, bf16[14,96,384]{2,1,0:T(8,128)(2,1)S(1)}, u32[]{:S(2)}, u32[]{:S(2)}) %collective-permute-start.7) | collective-permute-done | bytes 1032224 | tf_op jit(solution)/shard_map/ppermute | solution.py:34
  58.9 2.1 %collective-permute-done.8.refs_6_ = bf16[14,96,384]{2,1,0:T(8,128)(2,1)S(1)} collective-permute-done((bf16[14,96,384]{2,1,0:T(8,128)(2,1)S(1)}, bf16[14,96,384]{2,1,0:T(8,128)(2,1)S(1)}, u32[]{:S(2)}, u32[]{:S(2)}) %collective-permute-start.8) | collective-permute-done | bytes 1032224 | tf_op jit(solution)/shard_map/ppermute | solution.py:34
  61.9 4.2 %collective-permute-start.17 = (bf16[14,96,384]{2,1,0:T(8,128)(2,1)S(1)}, bf16[14,96,384]{2,1,0:T(8,128)(2,1)S(1)}, u32[]{:S(2)}, u32[]{:S(2)}) collective-permute-start(bf16[14,96,384]{2,1,0:T(8,128)(2,1)S(1)} %shard_map.129.refs_4_), channel_id=1, source_target_pairs={{8,0},{3,1},{10,2},{5,3},{12,4},{7,5},{14,6},{1,7},{16,8},{11,9},{... | collective-permute-start | bytes 3096584 | tf_op jit(solution)/shard_map/ppermute | solution.py:34
  66.1 0.5 collective-permute-done.15.refs_11_
  66.6 9.7 %shard_map.132 = bf16[6,128,384]{2,1,0:T(8,128)(2,1)S(1)} custom-call(s32[2]{0:T(128)S(1)} %pad_add_fusion.1.scalars.refs_0_, f32[3,6]{1,0:T(4,128)S(1)} %add_convert_fusion.refs_1_, bf16[2,8,6,32,1152]{4,3,2,1,0:T(8,128)(2,1)S(1)} %shard_map.131.refs_2_, f32[1,384]{1,0:T(1,128)S(1)} %reshape.331.refs_3_, bf16[14,96,384]{2,1,0:T(8,128)(2,1)S(1)} %shard_map.128.refs_4_, ...), custom_call_target="tpu_custom_call" | custom-call | flops 1000 | bytes 1000 | tf_op jit(solution)/shard_map/pallas_call | solution.py:287
  76.4 1.9 %collective-permute-start.16 = (bf16[2,4,32,384]{3,2,1,0:T(8,128)(2,1)S(1)}, bf16[2,4,32,384]{3,2,1,0:T(8,128)(2,1)S(1)}, u32[]{:S(2)}, u32[]{:S(2)}) collective-permute-start(bf16[2,4,32,384]{3,2,1,0:T(8,128)(2,1)S(1)} %constant_dynamic-slice_fusion.1), channel_id=1, source_target_pairs={{0,8},{1,9},{2,10},{3,11},{4,12},{5,13},{6,14},{7,15},{8,16},{9,17... | collective-permute-start | bytes 589832 | tf_op jit(solution)/shard_map/ppermute | solution.py:34
  78.3 4.4 %collective-permute-start.21 = (bf16[6,1,32,384]{3,2,1,0:T(8,128)(2,1)S(1)}, bf16[6,1,32,384]{3,2,1,0:T(8,128)(2,1)S(1)}, u32[]{:S(2)}, u32[]{:S(2)}) collective-permute-start(bf16[6,1,32,384]{3,2,1,0:T(8,128)(2,1)S(1)} %get-tuple-element.70), channel_id=1, source_target_pairs={{2,1},{1,2},{4,3},{3,4},{6,5},{5,6},{10,9},{9,10},{12,11},{11,12},... | collective-permute-start | bytes 442376 | tf_op jit(solution)/shard_map/ppermute | solution.py:34
  82.8 1.9 %collective-permute-start.20 = (bf16[2,1,32,384]{3,2,1,0:T(8,128)(2,1)S(1)}, bf16[2,1,32,384]{3,2,1,0:T(8,128)(2,1)S(1)}, u32[]{:S(2)}, u32[]{:S(2)}) collective-permute-start(bf16[2,1,32,384]{3,2,1,0:T(8,128)(2,1)S(1)} %constant_dynamic-slice_fusion), channel_id=1, source_target_pairs={{2,9},{1,10},{4,11},{3,12},{6,13},{5,14},{10,17},{9,18},{12,19},{1... | collective-permute-start | bytes 147464 | tf_op jit(solution)/shard_map/ppermute | solution.py:34
  84.7 1.1 shard_map.133._
  85.8 6.6 %collective-permute-done.20 = bf16[2,1,32,384]{3,2,1,0:T(8,128)(2,1)S(1)} collective-permute-done((bf16[2,1,32,384]{3,2,1,0:T(8,128)(2,1)S(1)}, bf16[2,1,32,384]{3,2,1,0:T(8,128)(2,1)S(1)}, u32[]{:S(2)}, u32[]{:S(2)}) %collective-permute-start.20) | collective-permute-done | bytes 49184 | tf_op jit(solution)/shard_map/ppermute | solution.py:34
  92.4 2.2 %collective-permute-start.22 = (bf16[8,1,32,384]{3,2,1,0:T(8,128)(2,1)S(1)}, bf16[8,1,32,384]{3,2,1,0:T(8,128)(2,1)S(1)}, u32[]{:S(2)}, u32[]{:S(2)}) collective-permute-start(bf16[8,1,32,384]{3,2,1,0:T(8,128)(2,1)S(1)} %pad_maximum_fusion.3), channel_id=1, source_target_pairs={{1,0},{0,1},{3,2},{2,3},{5,4},{4,5},{7,6},{6,7},{9,8},{8,9},{11,10... | collective-permute-start | bytes 589832 | tf_op jit(solution)/shard_map/ppermute | solution.py:34
  94.7 1.0 collective-permute-done.22.beside
  96.2 2.1 %shard_map.134.refs_2_ = bf16[2,8,6,32,1152]{4,3,2,1,0:T(8,128)(2,1)S(1)} custom-call(s32[2]{0:T(128)S(1)} %pad_add_fusion.1.scalars.refs_0_, bf16[2,384,384]{2,1,0:T(8,128)(2,1)S(1)} %copy-done, bf16[2,4,32,384]{3,2,1,0:T(8,128)(2,1)S(1)} %collective-permute-done.16.ends, ...), custom_call_target="tpu_custom_call", output_to_operand_aliasing={{}: (5, {})} | custom-call | flops 1000 | bytes 1000 | tf_op jit(solution)/shard_map/pallas_call | solution.py:186
  98.7 1.5 %collective-permute-done.25.refs_11_ = bf16[14,96,384]{2,1,0:T(8,128)(2,1)S(1)} collective-permute-done((bf16[14,96,384]{2,1,0:T(8,128)(2,1)S(1)}, bf16[14,96,384]{2,1,0:T(8,128)(2,1)S(1)}, u32[]{:S(2)}, u32[]{:S(2)}) %collective-permute-start.25) | collective-permute-done | bytes 1032224 | tf_op jit(solution)/shard_map/ppermute | solution.py:34
  100.2 10.1 %shard_map.135 = bf16[6,128,384]{2,1,0:T(8,128)(2,1)} custom-call(s32[2]{0:T(128)S(1)} %pad_add_fusion.1.scalars.refs_0_, f32[3,6]{1,0:T(4,128)S(1)} %add_convert_fusion.refs_1_, bf16[2,8,6,32,1152]{4,3,2,1,0:T(8,128)(2,1)S(1)} %shard_map.134.refs_2_, bf16[6,128,384]{2,1,0:T(8,128)(2,1)S(1)} %bitcast.31, bf16[14,96,384]{2,1,0:T(8,128)(2,1)S(1)} %shard_map.129.refs_4_, ...), custom_call_target="tpu_custom_call" | custom-call | flops 1000 | bytes 1000 | tf_op jit(solution)/shard_map/pallas_call | solution.py:287
  (95 shorter events, 6.2 us)
Async XLA Ops:
  1.2 9.1 %copy-start.6 = (s32[4]{0:T(128)S(1)}, s32[4]{0:T(128)}, u32[]{:S(2)}) copy-start(s32[4]{0:T(128)} %constant.162.clone) | copy-start | bytes 52
  1.3 9.1 %copy-start.7 = (s32[4]{0:T(128)S(1)}, s32[4]{0:T(128)}, u32[]{:S(2)}) copy-start(s32[4]{0:T(128)} %constant.164.clone) | copy-start | bytes 52
  1.3 9.2 %copy-start.5 = (s32[4]{0:T(128)S(1)}, s32[4]{0:T(128)}, u32[]{:S(2)}) copy-start(s32[4]{0:T(128)} %constant.163.clone) | copy-start | bytes 52
  1.3 9.4 %copy-start.2 = (s32[4,2]{1,0:T(4,128)S(1)}, s32[4,2]{1,0:T(4,128)}, u32[]{:S(2)}) copy-start(s32[4,2]{1,0:T(4,128)} %constant.161.clone) | copy-start | bytes 100
  1.3 15.4 %collective-permute-start = (bf16[2,168,384]{2,1,0:T(8,128)(2,1)S(1)}, bf16[2,168,384]{2,1,0:T(8,128)(2,1)S(1)}, u32[]{:S(2)}, u32[]{:S(2)}) collective-permute-start(bf16[2,168,384]{2,1,0:T(8,128)(2,1)S(1)} %constant_dynamic-update-slice_fusion), channel_id=1, source_target_pairs={{24,0},{1,1},{90,2},{67,3},{60,4},{37,5},{126,6},{103,7},{0,8},{9,... | collective-permute-start | bytes 774152 | tf_op jit(solution)/shard_map/ppermute | solution.py:34
  3.4 13.3 %collective-permute-start.1 = (bf16[2,168,384]{2,1,0:T(8,128)(2,1)S(1)}, bf16[2,168,384]{2,1,0:T(8,128)(2,1)S(1)}, u32[]{:S(2)}, u32[]{:S(2)}) collective-permute-start(bf16[2,168,384]{2,1,0:T(8,128)(2,1)S(1)} %constant_dynamic-update-slice_fusion), channel_id=1, source_target_pairs={{152,0},{129,1},{218,2},{195,3},{188,4},{165,5},{254,6},{231,7},{1... | collective-permute-start | bytes 774152 | tf_op jit(solution)/shard_map/ppermute | solution.py:34
  6.4 7.2 %copy-start.8 = (s32[3]{0:T(128)S(1)}, s32[3]{0:T(128)}, u32[]{:S(2)}) copy-start(s32[3]{0:T(128)} %param.14) | copy-start | bytes 40
  7.1 17.8 %collective-permute-start.5 = (bf16[2,4,32,384]{3,2,1,0:T(8,128)(2,1)S(1)}, bf16[2,4,32,384]{3,2,1,0:T(8,128)(2,1)S(1)}, u32[]{:S(2)}, u32[]{:S(2)}) collective-permute-start(bf16[2,4,32,384]{3,2,1,0:T(8,128)(2,1)S(1)} %constant_dynamic-slice_fusion.2), channel_id=1, source_target_pairs={{0,8},{1,9},{2,10},{3,11},{4,12},{5,13},{6,14},{7,15},{8,16},{9,17... | collective-permute-start | bytes 589832 | tf_op jit(solution)/shard_map/ppermute | solution.py:34
  16.8 25.5 %collective-permute-start.2 = (bf16[2,2,168,384]{3,2,1,0:T(8,128)(2,1)S(1)}, bf16[2,2,168,384]{3,2,1,0:T(8,128)(2,1)S(1)}, u32[]{:S(2)}, u32[]{:S(2)}) collective-permute-start(bf16[2,2,168,384]{3,2,1,0:T(8,128)(2,1)S(1)} %pad_maximum_fusion.refs_0_), channel_id=1, source_target_pairs={{2,0},{9,1},{4,2},{11,3},{6,4},{13,5},{0,6},{15,7},{10,8},{17,9},{... | collective-permute-start | bytes 1548296 | tf_op jit(solution)/shard_map/ppermute | solution.py:34
  19.7 22.5 %collective-permute-start.3 = (bf16[2,2,168,384]{3,2,1,0:T(8,128)(2,1)S(1)}, bf16[2,2,168,384]{3,2,1,0:T(8,128)(2,1)S(1)}, u32[]{:S(2)}, u32[]{:S(2)}) collective-permute-start(bf16[2,2,168,384]{3,2,1,0:T(8,128)(2,1)S(1)} %pad_maximum_fusion.refs_0_), channel_id=1, source_target_pairs={{6,0},{25,1},{0,2},{27,3},{2,4},{29,5},{4,6},{31,7},{14,8},{1,9},{... | collective-permute-start | bytes 1548296 | tf_op jit(solution)/shard_map/ppermute | solution.py:34
  19.7 22.5 %collective-permute-start.4 = (bf16[2,2,168,384]{3,2,1,0:T(8,128)(2,1)S(1)}, bf16[2,2,168,384]{3,2,1,0:T(8,128)(2,1)S(1)}, u32[]{:S(2)}, u32[]{:S(2)}) collective-permute-start(bf16[2,2,168,384]{3,2,1,0:T(8,128)(2,1)S(1)} %pad_maximum_fusion.refs_0_), channel_id=1, source_target_pairs={{4,0},{17,1},{6,2},{19,3},{0,4},{21,5},{2,6},{23,7},{12,8},{25,9},... | collective-permute-start | bytes 1548296 | tf_op jit(solution)/shard_map/ppermute | solution.py:34
  25.1 17.1 %collective-permute-start.6 = (bf16[8,1,32,384]{3,2,1,0:T(8,128)(2,1)S(1)}, bf16[8,1,32,384]{3,2,1,0:T(8,128)(2,1)S(1)}, u32[]{:S(2)}, u32[]{:S(2)}) collective-permute-start(bf16[8,1,32,384]{3,2,1,0:T(8,128)(2,1)S(1)} %broadcast_select_fusion.1), channel_id=1, source_target_pairs={{2,1},{1,2},{4,3},{3,4},{6,5},{5,6},{10,9},{9,10},{12,11},{11,12},... | collective-permute-start | bytes 589832 | tf_op jit(solution)/shard_map/ppermute | solution.py:34
  42.6 4.7 %collective-permute-start.10 = (bf16[14,96,384]{2,1,0:T(8,128)(2,1)S(1)}, bf16[14,96,384]{2,1,0:T(8,128)(2,1)S(1)}, u32[]{:S(2)}, u32[]{:S(2)}) collective-permute-start(bf16[14,96,384]{2,1,0:T(8,128)(2,1)S(1)} %shard_map.128.refs_4_), channel_id=1, source_target_pairs={{1,0},{0,1},{3,2},{2,3},{5,4},{4,5},{7,6},{6,7},{9,8},{8,9},{11,10... | collective-permute-start | bytes 3096584 | tf_op jit(solution)/shard_map/ppermute | solution.py:34
  43.0 4.3 %collective-permute-start.11 = (bf16[14,96,384]{2,1,0:T(8,128)(2,1)S(1)}, bf16[14,96,384]{2,1,0:T(8,128)(2,1)S(1)}, u32[]{:S(2)}, u32[]{:S(2)}) collective-permute-start(bf16[14,96,384]{2,1,0:T(8,128)(2,1)S(1)} %shard_map.129.refs_4_), channel_id=1, source_target_pairs={{1,0},{0,1},{3,2},{2,3},{5,4},{4,5},{7,6},{6,7},{9,8},{8,9},{11,10... | collective-permute-start | bytes 3096584 | tf_op jit(solution)/shard_map/ppermute | solution.py:34
  43.2 15.6 %collective-permute-start.7 = (bf16[14,96,384]{2,1,0:T(8,128)(2,1)S(1)}, bf16[14,96,384]{2,1,0:T(8,128)(2,1)S(1)}, u32[]{:S(2)}, u32[]{:S(2)}) collective-permute-start(bf16[14,96,384]{2,1,0:T(8,128)(2,1)S(1)} %shard_map.128.refs_4_), channel_id=1, source_target_pairs={{8,0},{3,1},{10,2},{5,3},{12,4},{7,5},{14,6},{1,7},{16,8},{11,9},{... | collective-permute-start | bytes 3096584 | tf_op jit(solution)/shard_map/ppermute | solution.py:34
  47.3 13.7 %collective-permute-start.8 = (bf16[14,96,384]{2,1,0:T(8,128)(2,1)S(1)}, bf16[14,96,384]{2,1,0:T(8,128)(2,1)S(1)}, u32[]{:S(2)}, u32[]{:S(2)}) collective-permute-start(bf16[14,96,384]{2,1,0:T(8,128)(2,1)S(1)} %shard_map.128.refs_4_), channel_id=1, source_target_pairs={{24,0},{7,1},{26,2},{1,3},{28,4},{3,5},{30,6},{5,7},{0,8},{15,9},{... | collective-permute-start | bytes 3096584 | tf_op jit(solution)/shard_map/ppermute | solution.py:34
  47.3 13.7 %collective-permute-start.9 = (bf16[14,96,384]{2,1,0:T(8,128)(2,1)S(1)}, bf16[14,96,384]{2,1,0:T(8,128)(2,1)S(1)}, u32[]{:S(2)}, u32[]{:S(2)}) collective-permute-start(bf16[14,96,384]{2,1,0:T(8,128)(2,1)S(1)} %shard_map.128.refs_4_), channel_id=1, source_target_pairs={{224,0},{33,1},{226,2},{35,3},{228,4},{37,5},{230,6},{39,7},{232,8... | collective-permute-start | bytes 3096584 | tf_op jit(solution)/shard_map/ppermute | solution.py:34
  47.3 1.5 %collective-permute-start.12 = (bf16[8,1,32,384]{3,2,1,0:T(8,128)(2,1)S(1)}, bf16[8,1,32,384]{3,2,1,0:T(8,128)(2,1)S(1)}, u32[]{:S(2)}, u32[]{:S(2)}) collective-permute-start(bf16[8,1,32,384]{3,2,1,0:T(8,128)(2,1)S(1)} %get-tuple-element.58), channel_id=1, source_target_pairs={{1,0},{0,1},{3,2},{2,3},{5,4},{4,5},{7,6},{6,7},{9,8},{8,9},{11,10... | collective-permute-start | bytes 589832 | tf_op jit(solution)/shard_map/ppermute | solution.py:34
  48.5 17.6 %copy-start.4 = (f32[384]{0:T(512)S(1)}, f32[384]{0:T(512)}, u32[]{:S(2)}) copy-start(f32[384]{0:T(512)} %param.20) | copy-start | bytes 4612
  61.0 5.1 %collective-permute-start.13 = (bf16[14,96,384]{2,1,0:T(8,128)(2,1)S(1)}, bf16[14,96,384]{2,1,0:T(8,128)(2,1)S(1)}, u32[]{:S(2)}, u32[]{:S(2)}) collective-permute-start(bf16[14,96,384]{2,1,0:T(8,128)(2,1)S(1)} %collective-permute-done.7.refs_5_), channel_id=1, source_target_pairs={{1,0},{0,1},{3,2},{2,3},{5,4},{4,5},{7,6},{6,7},{9,8},{8,9},{11,10... | collective-permute-start | bytes 3096584 | tf_op jit(solution)/shard_map/ppermute | solution.py:34
  61.4 4.7 %collective-permute-start.14 = (bf16[14,96,384]{2,1,0:T(8,128)(2,1)S(1)}, bf16[14,96,384]{2,1,0:T(8,128)(2,1)S(1)}, u32[]{:S(2)}, u32[]{:S(2)}) collective-permute-start(bf16[14,96,384]{2,1,0:T(8,128)(2,1)S(1)} %collective-permute-done.8.refs_6_), channel_id=1, source_target_pairs={{1,0},{0,1},{3,2},{2,3},{5,4},{4,5},{7,6},{6,7},{9,8},{8,9},{11,10... | collective-permute-start | bytes 3096584 | tf_op jit(solution)/shard_map/ppermute | solution.py:34
  61.5 5.1 %collective-permute-start.15 = (bf16[14,96,384]{2,1,0:T(8,128)(2,1)S(1)}, bf16[14,96,384]{2,1,0:T(8,128)(2,1)S(1)}, u32[]{:S(2)}, u32[]{:S(2)}) collective-permute-start(bf16[14,96,384]{2,1,0:T(8,128)(2,1)S(1)} %collective-permute-done.9.refs_7_), channel_id=1, source_target_pairs={{1,0},{0,1},{3,2},{2,3},{5,4},{4,5},{7,6},{6,7},{9,8},{8,9},{11,10... | collective-permute-start | bytes 3096584 | tf_op jit(solution)/shard_map/ppermute | solution.py:34
  61.9 20.8 %collective-permute-start.17 = (bf16[14,96,384]{2,1,0:T(8,128)(2,1)S(1)}, bf16[14,96,384]{2,1,0:T(8,128)(2,1)S(1)}, u32[]{:S(2)}, u32[]{:S(2)}) collective-permute-start(bf16[14,96,384]{2,1,0:T(8,128)(2,1)S(1)} %shard_map.129.refs_4_), channel_id=1, source_target_pairs={{8,0},{3,1},{10,2},{5,3},{12,4},{7,5},{14,6},{1,7},{16,8},{11,9},{... | collective-permute-start | bytes 3096584 | tf_op jit(solution)/shard_map/ppermute | solution.py:34
  66.1 16.6 %collective-permute-start.18 = (bf16[14,96,384]{2,1,0:T(8,128)(2,1)S(1)}, bf16[14,96,384]{2,1,0:T(8,128)(2,1)S(1)}, u32[]{:S(2)}, u32[]{:S(2)}) collective-permute-start(bf16[14,96,384]{2,1,0:T(8,128)(2,1)S(1)} %shard_map.129.refs_4_), channel_id=1, source_target_pairs={{24,0},{7,1},{26,2},{1,3},{28,4},{3,5},{30,6},{5,7},{0,8},{15,9},{... | collective-permute-start | bytes 3096584 | tf_op jit(solution)/shard_map/ppermute | solution.py:34
  66.1 16.6 %collective-permute-start.19 = (bf16[14,96,384]{2,1,0:T(8,128)(2,1)S(1)}, bf16[14,96,384]{2,1,0:T(8,128)(2,1)S(1)}, u32[]{:S(2)}, u32[]{:S(2)}) collective-permute-start(bf16[14,96,384]{2,1,0:T(8,128)(2,1)S(1)} %shard_map.129.refs_4_), channel_id=1, source_target_pairs={{224,0},{33,1},{226,2},{35,3},{228,4},{37,5},{230,6},{39,7},{232,8... | collective-permute-start | bytes 3096584 | tf_op jit(solution)/shard_map/ppermute | solution.py:34
  76.4 16.0 %collective-permute-start.16 = (bf16[2,4,32,384]{3,2,1,0:T(8,128)(2,1)S(1)}, bf16[2,4,32,384]{3,2,1,0:T(8,128)(2,1)S(1)}, u32[]{:S(2)}, u32[]{:S(2)}) collective-permute-start(bf16[2,4,32,384]{3,2,1,0:T(8,128)(2,1)S(1)} %constant_dynamic-slice_fusion.1), channel_id=1, source_target_pairs={{0,8},{1,9},{2,10},{3,11},{4,12},{5,13},{6,14},{7,15},{8,16},{9,17... | collective-permute-start | bytes 589832 | tf_op jit(solution)/shard_map/ppermute | solution.py:34
  78.3 14.0 %collective-permute-start.21 = (bf16[6,1,32,384]{3,2,1,0:T(8,128)(2,1)S(1)}, bf16[6,1,32,384]{3,2,1,0:T(8,128)(2,1)S(1)}, u32[]{:S(2)}, u32[]{:S(2)}) collective-permute-start(bf16[6,1,32,384]{3,2,1,0:T(8,128)(2,1)S(1)} %get-tuple-element.70), channel_id=1, source_target_pairs={{2,1},{1,2},{4,3},{3,4},{6,5},{5,6},{10,9},{9,10},{12,11},{11,12},... | collective-permute-start | bytes 442376 | tf_op jit(solution)/shard_map/ppermute | solution.py:34
  82.8 9.6 %collective-permute-start.20 = (bf16[2,1,32,384]{3,2,1,0:T(8,128)(2,1)S(1)}, bf16[2,1,32,384]{3,2,1,0:T(8,128)(2,1)S(1)}, u32[]{:S(2)}, u32[]{:S(2)}) collective-permute-start(bf16[2,1,32,384]{3,2,1,0:T(8,128)(2,1)S(1)} %constant_dynamic-slice_fusion), channel_id=1, source_target_pairs={{2,9},{1,10},{4,11},{3,12},{6,13},{5,14},{10,17},{9,18},{12,19},{1... | collective-permute-start | bytes 147464 | tf_op jit(solution)/shard_map/ppermute | solution.py:34
  92.4 3.3 %collective-permute-start.22 = (bf16[8,1,32,384]{3,2,1,0:T(8,128)(2,1)S(1)}, bf16[8,1,32,384]{3,2,1,0:T(8,128)(2,1)S(1)}, u32[]{:S(2)}, u32[]{:S(2)}) collective-permute-start(bf16[8,1,32,384]{3,2,1,0:T(8,128)(2,1)S(1)} %pad_maximum_fusion.3), channel_id=1, source_target_pairs={{1,0},{0,1},{3,2},{2,3},{5,4},{4,5},{7,6},{6,7},{9,8},{8,9},{11,10... | collective-permute-start | bytes 589832 | tf_op jit(solution)/shard_map/ppermute | solution.py:34
  94.6 3.7 %collective-permute-start.23 = (bf16[14,96,384]{2,1,0:T(8,128)(2,1)S(1)}, bf16[14,96,384]{2,1,0:T(8,128)(2,1)S(1)}, u32[]{:S(2)}, u32[]{:S(2)}) collective-permute-start(bf16[14,96,384]{2,1,0:T(8,128)(2,1)S(1)} %collective-permute-done.17.refs_5_), channel_id=1, source_target_pairs={{1,0},{0,1},{3,2},{2,3},{5,4},{4,5},{7,6},{6,7},{9,8},{8,9},{11,10... | collective-permute-start | bytes 3096584 | tf_op jit(solution)/shard_map/ppermute | solution.py:34
  95.7 3.0 %collective-permute-start.24 = (bf16[14,96,384]{2,1,0:T(8,128)(2,1)S(1)}, bf16[14,96,384]{2,1,0:T(8,128)(2,1)S(1)}, u32[]{:S(2)}, u32[]{:S(2)}) collective-permute-start(bf16[14,96,384]{2,1,0:T(8,128)(2,1)S(1)} %collective-permute-done.18.refs_6_), channel_id=1, source_target_pairs={{1,0},{0,1},{3,2},{2,3},{5,4},{4,5},{7,6},{6,7},{9,8},{8,9},{11,10... | collective-permute-start | bytes 3096584 | tf_op jit(solution)/shard_map/ppermute | solution.py:34
  96.1 4.1 %collective-permute-start.25 = (bf16[14,96,384]{2,1,0:T(8,128)(2,1)S(1)}, bf16[14,96,384]{2,1,0:T(8,128)(2,1)S(1)}, u32[]{:S(2)}, u32[]{:S(2)}) collective-permute-start(bf16[14,96,384]{2,1,0:T(8,128)(2,1)S(1)} %collective-permute-done.19.refs_7_), channel_id=1, source_target_pairs={{1,0},{0,1},{3,2},{2,3},{5,4},{4,5},{7,6},{6,7},{9,8},{8,9},{11,10... | collective-permute-start | bytes 3096584 | tf_op jit(solution)/shard_map/ppermute | solution.py:34
  (3 other events, 18.1 us)

commit v17 on v16

--- a/solution.py
+++ b/solution.py
@@ -116,7 +116,7 @@
 
 def picks_body(order, out):
     for half in range(2):
-        out[half] = (
+        out[:, C * half : C * (half + 1)] = (
             lax.broadcasted_iota(jnp.int32, (C, C), 0) == order[half : half + 1, :]
         ).astype(jnp.bfloat16)
 
@@ -125,26 +125,28 @@
     vmem = pl.BlockSpec(memory_space=pltpu.VMEM)
     return pl.pallas_call(
         picks_body,
-        out_shape=jax.ShapeDtypeStruct((2, C, C), jnp.bfloat16),
+        out_shape=jax.ShapeDtypeStruct((C, 2 * C), jnp.bfloat16),
         in_specs=[vmem],
         out_specs=vmem,
         cost_estimate=pl.CostEstimate(flops=1000, bytes_accessed=1000, transcendentals=0),
     )(orders)
 
 
-def spread_cells(cells, pick):
+def spread_cells(cells, picks):
     rows = cells.shape[0]
-    plain = jnp.dot(cells, pick, preferred_element_type=jnp.float32)
+    both = jnp.dot(cells, picks, preferred_element_type=jnp.float32)
     col = lax.broadcasted_iota(jnp.int32, (rows, C), 0) % 32
-    before = jnp.where(col == 0, 0.0, pltpu.roll(plain, 1, 0))
-    after = jnp.where(col == 31, 0.0, pltpu.roll(plain, rows - 1, 0))
-    return [part.astype(jnp.bfloat16) for part in (before, plain, after)]
+    for half in range(2):
+        plain = both[:, C * half : C * (half + 1)]
+        before = jnp.where(col == 0, 0.0, pltpu.roll(plain, 1, 0))
+        after = jnp.where(col == 31, 0.0, pltpu.roll(plain, rows - 1, 0))
+        for tap, part in enumerate((before, plain, after)):
+            yield half, tap, part.astype(jnp.bfloat16)
 
 
 def spread_inner_body(picks, acts, out):
-    for half in range(2):
-        for tap, part in enumerate(spread_cells(acts[...], picks[half])):
-            out[half, 2:8, 1:5, :, C * tap : C * (tap + 1)] = part.reshape(6, 4, 32, C)
+    for half, tap, part in spread_cells(acts[...], picks[...]):
+        out[half, 2:8, 1:5, :, C * tap : C * (tap + 1)] = part.reshape(6, 4, 32, C)
 
 
 def spread_inner(picks, acts):
@@ -164,21 +166,20 @@
     cells = jnp.concatenate(
         [part[...].reshape(-1, C) for part in (ends, beside, across)], 0
     )
-    for half in range(2):
-        for tap, part in enumerate(spread_cells(cells, picks[half])):
-            lanes = slice(C * tap, C * (tap + 1))
-            out[half, 0:2, 1:5, :, lanes] = part[0:256].reshape(2, 4, 32, C)
-            near, far = part[256:512].reshape(8, 1, 32, C), part[512:768].reshape(8, 1, 32, C)
-
-            @pl.when(core == 0)
-            def _():
-                out[half, :, 0:1, :, lanes] = far
-                out[half, :, 5:6, :, lanes] = near
-
-            @pl.when(core == 1)
-            def _():
-                out[half, :, 0:1, :, lanes] = near
-                out[half, :, 5:6, :, lanes] = far
+    for half, tap, part in spread_cells(cells, picks[...]):
+        lanes = slice(C * tap, C * (tap + 1))
+        out[half, 0:2, 1:5, :, lanes] = part[0:256].reshape(2, 4, 32, C)
+        near, far = part[256:512].reshape(8, 1, 32, C), part[512:768].reshape(8, 1, 32, C)
+
+        @pl.when(core == 0)
+        def _():
+            out[half, :, 0:1, :, lanes] = far
+            out[half, :, 5:6, :, lanes] = near
+
+        @pl.when(core == 1)
+        def _():
+            out[half, :, 0:1, :, lanes] = near
+            out[half, :, 5:6, :, lanes] = far
 
 
 def spread_halo(scalars, picks, ends, beside, across, spread):

time: 111 us -> 111 us (level)
  transfers between devices with their start and end apart: 26 -> 26, of which waited for: 11 -> 11; matrix products, arithmetic and copies ran while one was open for 4% -> 4% of each run, Pallas kernels for 16% -> 15%
where the time goes in v17:
time: 111 us
  starting transfers between devices  39.9 us (36%)
  waiting for transfers between devices  35.4 us (32%)
  Pallas kernels  27.6 us (25%)
  local copies, waits for them, and re-layouts  3.34 us (3%)
  other arithmetic  2.34 us (2%)
  between operations  2 us (2%)
    ppermute x26, starting transfers between devices, fetch(): return lax.ppermute(array, AXES, pairs)  39.9 us
    ppermute x26, waiting for transfers between devices, fetch(): return lax.ppermute(array, AXES, pairs)  35.4 us
    pallas_call x2, Pallas kernels, conv(): pl.pallas_call(lambda *refs: conv_body(*refs, finish=finish), out_shape=j...  19.8 us
    pallas_call x2, Pallas kernels, spread_halo(): pl.pallas_call(spread_halo_body, out_shape=jax.ShapeDtypeStruct(spread.sh...  3.88 us
  transfers between devices with their start and end apart: 26, of which 11 were waited for; matrix products, arithmetic and copies ran while one was open for 4% of the time, Pallas kernels for 15%

profile of v17, /device:TPU:131, one launch (start us, length us, event | category | flops | bytes accessed | tf_op | source)
XLA Modules:
  0.0 110.5 jit_solution(12640664590670580892)
XLA Ops:
  0.0 1.1 constant_dynamic-slice_fusion.3
  1.3 2.1 %collective-permute-start = (bf16[2,168,384]{2,1,0:T(8,128)(2,1)S(1)}, bf16[2,168,384]{2,1,0:T(8,128)(2,1)S(1)}, u32[]{:S(2)}, u32[]{:S(2)}) collective-permute-start(bf16[2,168,384]{2,1,0:T(8,128)(2,1)S(1)} %constant_dynamic-update-slice_fusion), channel_id=1, source_target_pairs={{24,0},{1,1},{90,2},{67,3},{60,4},{37,5},{126,6},{103,7},{0,8},{9,... | collective-permute-start | bytes 774152 | tf_op jit(solution)/shard_map/ppermute | solution.py:34
  3.4 2.4 %collective-permute-start.1 = (bf16[2,168,384]{2,1,0:T(8,128)(2,1)S(1)}, bf16[2,168,384]{2,1,0:T(8,128)(2,1)S(1)}, u32[]{:S(2)}, u32[]{:S(2)}) collective-permute-start(bf16[2,168,384]{2,1,0:T(8,128)(2,1)S(1)} %constant_dynamic-update-slice_fusion), channel_id=1, source_target_pairs={{152,0},{129,1},{218,2},{195,3},{188,4},{165,5},{254,6},{231,7},{1... | collective-permute-start | bytes 774152 | tf_op jit(solution)/shard_map/ppermute | solution.py:34
  7.1 3.2 %collective-permute-start.5 = (bf16[2,4,32,384]{3,2,1,0:T(8,128)(2,1)S(1)}, bf16[2,4,32,384]{3,2,1,0:T(8,128)(2,1)S(1)}, u32[]{:S(2)}, u32[]{:S(2)}) collective-permute-start(bf16[2,4,32,384]{3,2,1,0:T(8,128)(2,1)S(1)} %constant_dynamic-slice_fusion.2), channel_id=1, source_target_pairs={{0,8},{1,9},{2,10},{3,11},{4,12},{5,13},{6,14},{7,15},{8,16},{9,17... | collective-permute-start | bytes 589832 | tf_op jit(solution)/shard_map/ppermute | solution.py:34
  10.6 0.6 gather_fusion
  12.0 0.6 gather_fusion.1
  13.8 0.6 pad_add_fusion.order
  14.5 1.6 %shard_map.127.picks = bf16[384,768]{1,0:T(8,128)(2,1)} custom-call(s32[2,384]{1,0:T(2,128)} %pad_add_fusion.order), custom_call_target="tpu_custom_call" | custom-call | flops 1000 | bytes 1000 | tf_op jit(solution)/shard_map/pallas_call | solution.py:126
  16.8 2.9 %collective-permute-start.2 = (bf16[2,2,168,384]{3,2,1,0:T(8,128)(2,1)S(1)}, bf16[2,2,168,384]{3,2,1,0:T(8,128)(2,1)S(1)}, u32[]{:S(2)}, u32[]{:S(2)}) collective-permute-start(bf16[2,2,168,384]{3,2,1,0:T(8,128)(2,1)S(1)} %pad_maximum_fusion.refs_0_), channel_id=1, source_target_pairs={{2,0},{9,1},{4,2},{11,3},{6,4},{13,5},{0,6},{15,7},{10,8},{17,9},{... | collective-permute-start | bytes 1548296 | tf_op jit(solution)/shard_map/ppermute | solution.py:34
  19.7 1.6 %collective-permute-start.4 = (bf16[2,2,168,384]{3,2,1,0:T(8,128)(2,1)S(1)}, bf16[2,2,168,384]{3,2,1,0:T(8,128)(2,1)S(1)}, u32[]{:S(2)}, u32[]{:S(2)}) collective-permute-start(bf16[2,2,168,384]{3,2,1,0:T(8,128)(2,1)S(1)} %pad_maximum_fusion.refs_0_), channel_id=1, source_target_pairs={{4,0},{17,1},{6,2},{19,3},{0,4},{21,5},{2,6},{23,7},{12,8},{25,9},... | collective-permute-start | bytes 1548296 | tf_op jit(solution)/shard_map/ppermute | solution.py:34
  21.4 3.6 %collective-permute-done.5.ends = bf16[2,4,32,384]{3,2,1,0:T(8,128)(2,1)S(1)} collective-permute-done((bf16[2,4,32,384]{3,2,1,0:T(8,128)(2,1)S(1)}, bf16[2,4,32,384]{3,2,1,0:T(8,128)(2,1)S(1)}, u32[]{:S(2)}, u32[]{:S(2)}) %collective-permute-start.5) | collective-permute-done | bytes 196640 | tf_op jit(solution)/shard_map/ppermute | solution.py:34
  25.1 6.8 %collective-permute-start.6 = (bf16[8,1,32,384]{3,2,1,0:T(8,128)(2,1)S(1)}, bf16[8,1,32,384]{3,2,1,0:T(8,128)(2,1)S(1)}, u32[]{:S(2)}, u32[]{:S(2)}) collective-permute-start(bf16[8,1,32,384]{3,2,1,0:T(8,128)(2,1)S(1)} %broadcast_select_fusion.1), channel_id=1, source_target_pairs={{2,1},{1,2},{4,3},{3,4},{6,5},{5,6},{10,9},{9,10},{12,11},{11,12},... | collective-permute-start | bytes 589832 | tf_op jit(solution)/shard_map/ppermute | solution.py:34
  31.9 10.4 %collective-permute-done.6.across = bf16[8,1,32,384]{3,2,1,0:T(8,128)(2,1)S(1)} collective-permute-done((bf16[8,1,32,384]{3,2,1,0:T(8,128)(2,1)S(1)}, bf16[8,1,32,384]{3,2,1,0:T(8,128)(2,1)S(1)}, u32[]{:S(2)}, u32[]{:S(2)}) %collective-permute-start.6) | collective-permute-done | bytes 196640 | tf_op jit(solution)/shard_map/ppermute | solution.py:34
  43.2 4.1 %collective-permute-start.7 = (bf16[14,96,384]{2,1,0:T(8,128)(2,1)S(1)}, bf16[14,96,384]{2,1,0:T(8,128)(2,1)S(1)}, u32[]{:S(2)}, u32[]{:S(2)}) collective-permute-start(bf16[14,96,384]{2,1,0:T(8,128)(2,1)S(1)} %shard_map.128.refs_4_), channel_id=1, source_target_pairs={{8,0},{3,1},{10,2},{5,3},{12,4},{7,5},{14,6},{1,7},{16,8},{11,9},{... | collective-permute-start | bytes 3096584 | tf_op jit(solution)/shard_map/ppermute | solution.py:34
  47.5 0.9 shard_map.130._
  48.9 1.9 %shard_map.131.refs_2_ = bf16[2,8,6,32,1152]{4,3,2,1,0:T(8,128)(2,1)S(1)} custom-call(s32[2]{0:T(128)S(1)} %pad_add_fusion.1.scalars.refs_0_, bf16[384,768]{1,0:T(8,128)(2,1)S(1)} %copy-done, bf16[2,4,32,384]{3,2,1,0:T(8,128)(2,1)S(1)} %collective-permute-done.5.ends, ...), custom_call_target="tpu_custom_call", output_to_operand_aliasing={{}: (5, {})} | custom-call | flops 1000 | bytes 1000 | tf_op jit(solution)/shard_map/pallas_call | solution.py:187
  50.8 8.1 %collective-permute-done.7.refs_5_ = bf16[14,96,384]{2,1,0:T(8,128)(2,1)S(1)} collective-permute-done((bf16[14,96,384]{2,1,0:T(8,128)(2,1)S(1)}, bf16[14,96,384]{2,1,0:T(8,128)(2,1)S(1)}, u32[]{:S(2)}, u32[]{:S(2)}) %collective-permute-start.7) | collective-permute-done | bytes 1032224 | tf_op jit(solution)/shard_map/ppermute | solution.py:34
  58.9 2.1 %collective-permute-done.8.refs_6_ = bf16[14,96,384]{2,1,0:T(8,128)(2,1)S(1)} collective-permute-done((bf16[14,96,384]{2,1,0:T(8,128)(2,1)S(1)}, bf16[14,96,384]{2,1,0:T(8,128)(2,1)S(1)}, u32[]{:S(2)}, u32[]{:S(2)}) %collective-permute-start.8) | collective-permute-done | bytes 1032224 | tf_op jit(solution)/shard_map/ppermute | solution.py:34
  61.9 4.2 %collective-permute-start.17 = (bf16[14,96,384]{2,1,0:T(8,128)(2,1)S(1)}, bf16[14,96,384]{2,1,0:T(8,128)(2,1)S(1)}, u32[]{:S(2)}, u32[]{:S(2)}) collective-permute-start(bf16[14,96,384]{2,1,0:T(8,128)(2,1)S(1)} %shard_map.129.refs_4_), channel_id=1, source_target_pairs={{8,0},{3,1},{10,2},{5,3},{12,4},{7,5},{14,6},{1,7},{16,8},{11,9},{... | collective-permute-start | bytes 3096584 | tf_op jit(solution)/shard_map/ppermute | solution.py:34
  66.1 0.5 collective-permute-done.15.refs_11_
  66.6 9.7 %shard_map.132 = bf16[6,128,384]{2,1,0:T(8,128)(2,1)S(1)} custom-call(s32[2]{0:T(128)S(1)} %pad_add_fusion.1.scalars.refs_0_, f32[3,6]{1,0:T(4,128)S(1)} %add_convert_fusion.refs_1_, bf16[2,8,6,32,1152]{4,3,2,1,0:T(8,128)(2,1)S(1)} %shard_map.131.refs_2_, f32[1,384]{1,0:T(1,128)S(1)} %reshape.331.refs_3_, bf16[14,96,384]{2,1,0:T(8,128)(2,1)S(1)} %shard_map.128.refs_4_, ...), custom_call_target="tpu_custom_call" | custom-call | flops 1000 | bytes 1000 | tf_op jit(solution)/shard_map/pallas_call | solution.py:288
  76.4 1.9 %collective-permute-start.16 = (bf16[2,4,32,384]{3,2,1,0:T(8,128)(2,1)S(1)}, bf16[2,4,32,384]{3,2,1,0:T(8,128)(2,1)S(1)}, u32[]{:S(2)}, u32[]{:S(2)}) collective-permute-start(bf16[2,4,32,384]{3,2,1,0:T(8,128)(2,1)S(1)} %constant_dynamic-slice_fusion.1), channel_id=1, source_target_pairs={{0,8},{1,9},{2,10},{3,11},{4,12},{5,13},{6,14},{7,15},{8,16},{9,17... | collective-permute-start | bytes 589832 | tf_op jit(solution)/shard_map/ppermute | solution.py:34
  78.3 4.4 %collective-permute-start.21 = (bf16[6,1,32,384]{3,2,1,0:T(8,128)(2,1)S(1)}, bf16[6,1,32,384]{3,2,1,0:T(8,128)(2,1)S(1)}, u32[]{:S(2)}, u32[]{:S(2)}) collective-permute-start(bf16[6,1,32,384]{3,2,1,0:T(8,128)(2,1)S(1)} %get-tuple-element.70), channel_id=1, source_target_pairs={{2,1},{1,2},{4,3},{3,4},{6,5},{5,6},{10,9},{9,10},{12,11},{11,12},... | collective-permute-start | bytes 442376 | tf_op jit(solution)/shard_map/ppermute | solution.py:34
  82.7 1.9 %collective-permute-start.20 = (bf16[2,1,32,384]{3,2,1,0:T(8,128)(2,1)S(1)}, bf16[2,1,32,384]{3,2,1,0:T(8,128)(2,1)S(1)}, u32[]{:S(2)}, u32[]{:S(2)}) collective-permute-start(bf16[2,1,32,384]{3,2,1,0:T(8,128)(2,1)S(1)} %constant_dynamic-slice_fusion), channel_id=1, source_target_pairs={{2,9},{1,10},{4,11},{3,12},{6,13},{5,14},{10,17},{9,18},{12,19},{1... | collective-permute-start | bytes 147464 | tf_op jit(solution)/shard_map/ppermute | solution.py:34
  84.7 0.9 shard_map.133._
  85.6 6.8 %collective-permute-done.20 = bf16[2,1,32,384]{3,2,1,0:T(8,128)(2,1)S(1)} collective-permute-done((bf16[2,1,32,384]{3,2,1,0:T(8,128)(2,1)S(1)}, bf16[2,1,32,384]{3,2,1,0:T(8,128)(2,1)S(1)}, u32[]{:S(2)}, u32[]{:S(2)}) %collective-permute-start.20) | collective-permute-done | bytes 49184 | tf_op jit(solution)/shard_map/ppermute | solution.py:34
  92.4 2.2 %collective-permute-start.22 = (bf16[8,1,32,384]{3,2,1,0:T(8,128)(2,1)S(1)}, bf16[8,1,32,384]{3,2,1,0:T(8,128)(2,1)S(1)}, u32[]{:S(2)}, u32[]{:S(2)}) collective-permute-start(bf16[8,1,32,384]{3,2,1,0:T(8,128)(2,1)S(1)} %pad_maximum_fusion.3), channel_id=1, source_target_pairs={{1,0},{0,1},{3,2},{2,3},{5,4},{4,5},{7,6},{6,7},{9,8},{8,9},{11,10... | collective-permute-start | bytes 589832 | tf_op jit(solution)/shard_map/ppermute | solution.py:34
  94.7 1.0 collective-permute-done.22.beside
  96.2 1.9 %shard_map.134.refs_2_ = bf16[2,8,6,32,1152]{4,3,2,1,0:T(8,128)(2,1)S(1)} custom-call(s32[2]{0:T(128)S(1)} %pad_add_fusion.1.scalars.refs_0_, bf16[384,768]{1,0:T(8,128)(2,1)S(1)} %copy-done, bf16[2,4,32,384]{3,2,1,0:T(8,128)(2,1)S(1)} %collective-permute-done.16.ends, ...), custom_call_target="tpu_custom_call", output_to_operand_aliasing={{}: (5, {})} | custom-call | flops 1000 | bytes 1000 | tf_op jit(solution)/shard_map/pallas_call | solution.py:187
  98.2 0.5 collective-permute-done.24.refs_10_
  98.7 1.5 %collective-permute-done.25.refs_11_ = bf16[14,96,384]{2,1,0:T(8,128)(2,1)S(1)} collective-permute-done((bf16[14,96,384]{2,1,0:T(8,128)(2,1)S(1)}, bf16[14,96,384]{2,1,0:T(8,128)(2,1)S(1)}, u32[]{:S(2)}, u32[]{:S(2)}) %collective-permute-start.25) | collective-permute-done | bytes 1032224 | tf_op jit(solution)/shard_map/ppermute | solution.py:34
  100.2 10.1 %shard_map.135 = bf16[6,128,384]{2,1,0:T(8,128)(2,1)} custom-call(s32[2]{0:T(128)S(1)} %pad_add_fusion.1.scalars.refs_0_, f32[3,6]{1,0:T(4,128)S(1)} %add_convert_fusion.refs_1_, bf16[2,8,6,32,1152]{4,3,2,1,0:T(8,128)(2,1)S(1)} %shard_map.134.refs_2_, bf16[6,128,384]{2,1,0:T(8,128)(2,1)S(1)} %bitcast.31, bf16[14,96,384]{2,1,0:T(8,128)(2,1)S(1)} %shard_map.129.refs_4_, ...), custom_call_target="tpu_custom_call" | custom-call | flops 1000 | bytes 1000 | tf_op jit(solution)/shard_map/pallas_call | solution.py:288
  (95 shorter events, 6.5 us)
Async XLA Ops:
  1.2 9.1 %copy-start.6 = (s32[4]{0:T(128)S(1)}, s32[4]{0:T(128)}, u32[]{:S(2)}) copy-start(s32[4]{0:T(128)} %constant.162.clone) | copy-start | bytes 52
  1.3 9.1 %copy-start.7 = (s32[4]{0:T(128)S(1)}, s32[4]{0:T(128)}, u32[]{:S(2)}) copy-start(s32[4]{0:T(128)} %constant.164.clone) | copy-start | bytes 52
  1.3 9.2 %copy-start.5 = (s32[4]{0:T(128)S(1)}, s32[4]{0:T(128)}, u32[]{:S(2)}) copy-start(s32[4]{0:T(128)} %constant.163.clone) | copy-start | bytes 52
  1.3 9.4 %copy-start.2 = (s32[4,2]{1,0:T(4,128)S(1)}, s32[4,2]{1,0:T(4,128)}, u32[]{:S(2)}) copy-start(s32[4,2]{1,0:T(4,128)} %constant.161.clone) | copy-start | bytes 100
  1.3 15.4 %collective-permute-start = (bf16[2,168,384]{2,1,0:T(8,128)(2,1)S(1)}, bf16[2,168,384]{2,1,0:T(8,128)(2,1)S(1)}, u32[]{:S(2)}, u32[]{:S(2)}) collective-permute-start(bf16[2,168,384]{2,1,0:T(8,128)(2,1)S(1)} %constant_dynamic-update-slice_fusion), channel_id=1, source_target_pairs={{24,0},{1,1},{90,2},{67,3},{60,4},{37,5},{126,6},{103,7},{0,8},{9,... | collective-permute-start | bytes 774152 | tf_op jit(solution)/shard_map/ppermute | solution.py:34
  3.4 13.3 %collective-permute-start.1 = (bf16[2,168,384]{2,1,0:T(8,128)(2,1)S(1)}, bf16[2,168,384]{2,1,0:T(8,128)(2,1)S(1)}, u32[]{:S(2)}, u32[]{:S(2)}) collective-permute-start(bf16[2,168,384]{2,1,0:T(8,128)(2,1)S(1)} %constant_dynamic-update-slice_fusion), channel_id=1, source_target_pairs={{152,0},{129,1},{218,2},{195,3},{188,4},{165,5},{254,6},{231,7},{1... | collective-permute-start | bytes 774152 | tf_op jit(solution)/shard_map/ppermute | solution.py:34
  6.4 7.2 %copy-start.8 = (s32[3]{0:T(128)S(1)}, s32[3]{0:T(128)}, u32[]{:S(2)}) copy-start(s32[3]{0:T(128)} %param.14) | copy-start | bytes 40
  7.1 17.8 %collective-permute-start.5 = (bf16[2,4,32,384]{3,2,1,0:T(8,128)(2,1)S(1)}, bf16[2,4,32,384]{3,2,1,0:T(8,128)(2,1)S(1)}, u32[]{:S(2)}, u32[]{:S(2)}) collective-permute-start(bf16[2,4,32,384]{3,2,1,0:T(8,128)(2,1)S(1)} %constant_dynamic-slice_fusion.2), channel_id=1, source_target_pairs={{0,8},{1,9},{2,10},{3,11},{4,12},{5,13},{6,14},{7,15},{8,16},{9,17... | collective-permute-start | bytes 589832 | tf_op jit(solution)/shard_map/ppermute | solution.py:34
  16.8 25.5 %collective-permute-start.2 = (bf16[2,2,168,384]{3,2,1,0:T(8,128)(2,1)S(1)}, bf16[2,2,168,384]{3,2,1,0:T(8,128)(2,1)S(1)}, u32[]{:S(2)}, u32[]{:S(2)}) collective-permute-start(bf16[2,2,168,384]{3,2,1,0:T(8,128)(2,1)S(1)} %pad_maximum_fusion.refs_0_), channel_id=1, source_target_pairs={{2,0},{9,1},{4,2},{11,3},{6,4},{13,5},{0,6},{15,7},{10,8},{17,9},{... | collective-permute-start | bytes 1548296 | tf_op jit(solution)/shard_map/ppermute | solution.py:34
  19.7 22.5 %collective-permute-start.3 = (bf16[2,2,168,384]{3,2,1,0:T(8,128)(2,1)S(1)}, bf16[2,2,168,384]{3,2,1,0:T(8,128)(2,1)S(1)}, u32[]{:S(2)}, u32[]{:S(2)}) collective-permute-start(bf16[2,2,168,384]{3,2,1,0:T(8,128)(2,1)S(1)} %pad_maximum_fusion.refs_0_), channel_id=1, source_target_pairs={{6,0},{25,1},{0,2},{27,3},{2,4},{29,5},{4,6},{31,7},{14,8},{1,9},{... | collective-permute-start | bytes 1548296 | tf_op jit(solution)/shard_map/ppermute | solution.py:34
  19.7 22.5 %collective-permute-start.4 = (bf16[2,2,168,384]{3,2,1,0:T(8,128)(2,1)S(1)}, bf16[2,2,168,384]{3,2,1,0:T(8,128)(2,1)S(1)}, u32[]{:S(2)}, u32[]{:S(2)}) collective-permute-start(bf16[2,2,168,384]{3,2,1,0:T(8,128)(2,1)S(1)} %pad_maximum_fusion.refs_0_), channel_id=1, source_target_pairs={{4,0},{17,1},{6,2},{19,3},{0,4},{21,5},{2,6},{23,7},{12,8},{25,9},... | collective-permute-start | bytes 1548296 | tf_op jit(solution)/shard_map/ppermute | solution.py:34
  25.1 17.1 %collective-permute-start.6 = (bf16[8,1,32,384]{3,2,1,0:T(8,128)(2,1)S(1)}, bf16[8,1,32,384]{3,2,1,0:T(8,128)(2,1)S(1)}, u32[]{:S(2)}, u32[]{:S(2)}) collective-permute-start(bf16[8,1,32,384]{3,2,1,0:T(8,128)(2,1)S(1)} %broadcast_select_fusion.1), channel_id=1, source_target_pairs={{2,1},{1,2},{4,3},{3,4},{6,5},{5,6},{10,9},{9,10},{12,11},{11,12},... | collective-permute-start | bytes 589832 | tf_op jit(solution)/shard_map/ppermute | solution.py:34
  42.6 4.7 %collective-permute-start.10 = (bf16[14,96,384]{2,1,0:T(8,128)(2,1)S(1)}, bf16[14,96,384]{2,1,0:T(8,128)(2,1)S(1)}, u32[]{:S(2)}, u32[]{:S(2)}) collective-permute-start(bf16[14,96,384]{2,1,0:T(8,128)(2,1)S(1)} %shard_map.128.refs_4_), channel_id=1, source_target_pairs={{1,0},{0,1},{3,2},{2,3},{5,4},{4,5},{7,6},{6,7},{9,8},{8,9},{11,10... | collective-permute-start | bytes 3096584 | tf_op jit(solution)/shard_map/ppermute | solution.py:34
  43.0 4.3 %collective-permute-start.11 = (bf16[14,96,384]{2,1,0:T(8,128)(2,1)S(1)}, bf16[14,96,384]{2,1,0:T(8,128)(2,1)S(1)}, u32[]{:S(2)}, u32[]{:S(2)}) collective-permute-start(bf16[14,96,384]{2,1,0:T(8,128)(2,1)S(1)} %shard_map.129.refs_4_), channel_id=1, source_target_pairs={{1,0},{0,1},{3,2},{2,3},{5,4},{4,5},{7,6},{6,7},{9,8},{8,9},{11,10... | collective-permute-start | bytes 3096584 | tf_op jit(solution)/shard_map/ppermute | solution.py:34
  43.2 15.6 %collective-permute-start.7 = (bf16[14,96,384]{2,1,0:T(8,128)(2,1)S(1)}, bf16[14,96,384]{2,1,0:T(8,128)(2,1)S(1)}, u32[]{:S(2)}, u32[]{:S(2)}) collective-permute-start(bf16[14,96,384]{2,1,0:T(8,128)(2,1)S(1)} %shard_map.128.refs_4_), channel_id=1, source_target_pairs={{8,0},{3,1},{10,2},{5,3},{12,4},{7,5},{14,6},{1,7},{16,8},{11,9},{... | collective-permute-start | bytes 3096584 | tf_op jit(solution)/shard_map/ppermute | solution.py:34
  47.3 13.7 %collective-permute-start.8 = (bf16[14,96,384]{2,1,0:T(8,128)(2,1)S(1)}, bf16[14,96,384]{2,1,0:T(8,128)(2,1)S(1)}, u32[]{:S(2)}, u32[]{:S(2)}) collective-permute-start(bf16[14,96,384]{2,1,0:T(8,128)(2,1)S(1)} %shard_map.128.refs_4_), channel_id=1, source_target_pairs={{24,0},{7,1},{26,2},{1,3},{28,4},{3,5},{30,6},{5,7},{0,8},{15,9},{... | collective-permute-start | bytes 3096584 | tf_op jit(solution)/shard_map/ppermute | solution.py:34
  47.3 13.7 %collective-permute-start.9 = (bf16[14,96,384]{2,1,0:T(8,128)(2,1)S(1)}, bf16[14,96,384]{2,1,0:T(8,128)(2,1)S(1)}, u32[]{:S(2)}, u32[]{:S(2)}) collective-permute-start(bf16[14,96,384]{2,1,0:T(8,128)(2,1)S(1)} %shard_map.128.refs_4_), channel_id=1, source_target_pairs={{224,0},{33,1},{226,2},{35,3},{228,4},{37,5},{230,6},{39,7},{232,8... | collective-permute-start | bytes 3096584 | tf_op jit(solution)/shard_map/ppermute | solution.py:34
  47.3 1.5 %collective-permute-start.12 = (bf16[8,1,32,384]{3,2,1,0:T(8,128)(2,1)S(1)}, bf16[8,1,32,384]{3,2,1,0:T(8,128)(2,1)S(1)}, u32[]{:S(2)}, u32[]{:S(2)}) collective-permute-start(bf16[8,1,32,384]{3,2,1,0:T(8,128)(2,1)S(1)} %get-tuple-element.58), channel_id=1, source_target_pairs={{1,0},{0,1},{3,2},{2,3},{5,4},{4,5},{7,6},{6,7},{9,8},{8,9},{11,10... | collective-permute-start | bytes 589832 | tf_op jit(solution)/shard_map/ppermute | solution.py:34
  48.4 17.7 %copy-start.4 = (f32[384]{0:T(512)S(1)}, f32[384]{0:T(512)}, u32[]{:S(2)}) copy-start(f32[384]{0:T(512)} %param.20) | copy-start | bytes 4612
  61.0 5.1 %collective-permute-start.13 = (bf16[14,96,384]{2,1,0:T(8,128)(2,1)S(1)}, bf16[14,96,384]{2,1,0:T(8,128)(2,1)S(1)}, u32[]{:S(2)}, u32[]{:S(2)}) collective-permute-start(bf16[14,96,384]{2,1,0:T(8,128)(2,1)S(1)} %collective-permute-done.7.refs_5_), channel_id=1, source_target_pairs={{1,0},{0,1},{3,2},{2,3},{5,4},{4,5},{7,6},{6,7},{9,8},{8,9},{11,10... | collective-permute-start | bytes 3096584 | tf_op jit(solution)/shard_map/ppermute | solution.py:34
  61.4 4.7 %collective-permute-start.14 = (bf16[14,96,384]{2,1,0:T(8,128)(2,1)S(1)}, bf16[14,96,384]{2,1,0:T(8,128)(2,1)S(1)}, u32[]{:S(2)}, u32[]{:S(2)}) collective-permute-start(bf16[14,96,384]{2,1,0:T(8,128)(2,1)S(1)} %collective-permute-done.8.refs_6_), channel_id=1, source_target_pairs={{1,0},{0,1},{3,2},{2,3},{5,4},{4,5},{7,6},{6,7},{9,8},{8,9},{11,10... | collective-permute-start | bytes 3096584 | tf_op jit(solution)/shard_map/ppermute | solution.py:34
  61.5 5.1 %collective-permute-start.15 = (bf16[14,96,384]{2,1,0:T(8,128)(2,1)S(1)}, bf16[14,96,384]{2,1,0:T(8,128)(2,1)S(1)}, u32[]{:S(2)}, u32[]{:S(2)}) collective-permute-start(bf16[14,96,384]{2,1,0:T(8,128)(2,1)S(1)} %collective-permute-done.9.refs_7_), channel_id=1, source_target_pairs={{1,0},{0,1},{3,2},{2,3},{5,4},{4,5},{7,6},{6,7},{9,8},{8,9},{11,10... | collective-permute-start | bytes 3096584 | tf_op jit(solution)/shard_map/ppermute | solution.py:34
  61.9 20.8 %collective-permute-start.17 = (bf16[14,96,384]{2,1,0:T(8,128)(2,1)S(1)}, bf16[14,96,384]{2,1,0:T(8,128)(2,1)S(1)}, u32[]{:S(2)}, u32[]{:S(2)}) collective-permute-start(bf16[14,96,384]{2,1,0:T(8,128)(2,1)S(1)} %shard_map.129.refs_4_), channel_id=1, source_target_pairs={{8,0},{3,1},{10,2},{5,3},{12,4},{7,5},{14,6},{1,7},{16,8},{11,9},{... | collective-permute-start | bytes 3096584 | tf_op jit(solution)/shard_map/ppermute | solution.py:34
  66.1 16.6 %collective-permute-start.18 = (bf16[14,96,384]{2,1,0:T(8,128)(2,1)S(1)}, bf16[14,96,384]{2,1,0:T(8,128)(2,1)S(1)}, u32[]{:S(2)}, u32[]{:S(2)}) collective-permute-start(bf16[14,96,384]{2,1,0:T(8,128)(2,1)S(1)} %shard_map.129.refs_4_), channel_id=1, source_target_pairs={{24,0},{7,1},{26,2},{1,3},{28,4},{3,5},{30,6},{5,7},{0,8},{15,9},{... | collective-permute-start | bytes 3096584 | tf_op jit(solution)/shard_map/ppermute | solution.py:34
  66.1 16.6 %collective-permute-start.19 = (bf16[14,96,384]{2,1,0:T(8,128)(2,1)S(1)}, bf16[14,96,384]{2,1,0:T(8,128)(2,1)S(1)}, u32[]{:S(2)}, u32[]{:S(2)}) collective-permute-start(bf16[14,96,384]{2,1,0:T(8,128)(2,1)S(1)} %shard_map.129.refs_4_), channel_id=1, source_target_pairs={{224,0},{33,1},{226,2},{35,3},{228,4},{37,5},{230,6},{39,7},{232,8... | collective-permute-start | bytes 3096584 | tf_op jit(solution)/shard_map/ppermute | solution.py:34
  76.4 16.0 %collective-permute-start.16 = (bf16[2,4,32,384]{3,2,1,0:T(8,128)(2,1)S(1)}, bf16[2,4,32,384]{3,2,1,0:T(8,128)(2,1)S(1)}, u32[]{:S(2)}, u32[]{:S(2)}) collective-permute-start(bf16[2,4,32,384]{3,2,1,0:T(8,128)(2,1)S(1)} %constant_dynamic-slice_fusion.1), channel_id=1, source_target_pairs={{0,8},{1,9},{2,10},{3,11},{4,12},{5,13},{6,14},{7,15},{8,16},{9,17... | collective-permute-start | bytes 589832 | tf_op jit(solution)/shard_map/ppermute | solution.py:34
  78.3 14.0 %collective-permute-start.21 = (bf16[6,1,32,384]{3,2,1,0:T(8,128)(2,1)S(1)}, bf16[6,1,32,384]{3,2,1,0:T(8,128)(2,1)S(1)}, u32[]{:S(2)}, u32[]{:S(2)}) collective-permute-start(bf16[6,1,32,384]{3,2,1,0:T(8,128)(2,1)S(1)} %get-tuple-element.70), channel_id=1, source_target_pairs={{2,1},{1,2},{4,3},{3,4},{6,5},{5,6},{10,9},{9,10},{12,11},{11,12},... | collective-permute-start | bytes 442376 | tf_op jit(solution)/shard_map/ppermute | solution.py:34
  82.7 9.6 %collective-permute-start.20 = (bf16[2,1,32,384]{3,2,1,0:T(8,128)(2,1)S(1)}, bf16[2,1,32,384]{3,2,1,0:T(8,128)(2,1)S(1)}, u32[]{:S(2)}, u32[]{:S(2)}) collective-permute-start(bf16[2,1,32,384]{3,2,1,0:T(8,128)(2,1)S(1)} %constant_dynamic-slice_fusion), channel_id=1, source_target_pairs={{2,9},{1,10},{4,11},{3,12},{6,13},{5,14},{10,17},{9,18},{12,19},{1... | collective-permute-start | bytes 147464 | tf_op jit(solution)/shard_map/ppermute | solution.py:34
  92.4 3.3 %collective-permute-start.22 = (bf16[8,1,32,384]{3,2,1,0:T(8,128)(2,1)S(1)}, bf16[8,1,32,384]{3,2,1,0:T(8,128)(2,1)S(1)}, u32[]{:S(2)}, u32[]{:S(2)}) collective-permute-start(bf16[8,1,32,384]{3,2,1,0:T(8,128)(2,1)S(1)} %pad_maximum_fusion.3), channel_id=1, source_target_pairs={{1,0},{0,1},{3,2},{2,3},{5,4},{4,5},{7,6},{6,7},{9,8},{8,9},{11,10... | collective-permute-start | bytes 589832 | tf_op jit(solution)/shard_map/ppermute | solution.py:34
  94.6 3.6 %collective-permute-start.23 = (bf16[14,96,384]{2,1,0:T(8,128)(2,1)S(1)}, bf16[14,96,384]{2,1,0:T(8,128)(2,1)S(1)}, u32[]{:S(2)}, u32[]{:S(2)}) collective-permute-start(bf16[14,96,384]{2,1,0:T(8,128)(2,1)S(1)} %collective-permute-done.17.refs_5_), channel_id=1, source_target_pairs={{1,0},{0,1},{3,2},{2,3},{5,4},{4,5},{7,6},{6,7},{9,8},{8,9},{11,10... | collective-permute-start | bytes 3096584 | tf_op jit(solution)/shard_map/ppermute | solution.py:34
  95.7 3.0 %collective-permute-start.24 = (bf16[14,96,384]{2,1,0:T(8,128)(2,1)S(1)}, bf16[14,96,384]{2,1,0:T(8,128)(2,1)S(1)}, u32[]{:S(2)}, u32[]{:S(2)}) collective-permute-start(bf16[14,96,384]{2,1,0:T(8,128)(2,1)S(1)} %collective-permute-done.18.refs_6_), channel_id=1, source_target_pairs={{1,0},{0,1},{3,2},{2,3},{5,4},{4,5},{7,6},{6,7},{9,8},{8,9},{11,10... | collective-permute-start | bytes 3096584 | tf_op jit(solution)/shard_map/ppermute | solution.py:34
  96.1 4.1 %collective-permute-start.25 = (bf16[14,96,384]{2,1,0:T(8,128)(2,1)S(1)}, bf16[14,96,384]{2,1,0:T(8,128)(2,1)S(1)}, u32[]{:S(2)}, u32[]{:S(2)}) collective-permute-start(bf16[14,96,384]{2,1,0:T(8,128)(2,1)S(1)} %collective-permute-done.19.refs_7_), channel_id=1, source_target_pairs={{1,0},{0,1},{3,2},{2,3},{5,4},{4,5},{7,6},{6,7},{9,8},{8,9},{11,10... | collective-permute-start | bytes 3096584 | tf_op jit(solution)/shard_map/ppermute | solution.py:34
  (3 other events, 18.1 us)
